TPU v7x, 32 devices: a whole 2x2x4 slice. The times are simulated.
32 devices in a mesh: sp: 8 (over z, y), tp: 4 (over x, core).
Axes of the slice: x: 2, y: 2, z: 4, core: 2. Of those that a mesh axis runs over, the one named last changes fastest.
Arguments:
- patches: bfloat16 [4, 96, 768, 256], P(None, 'sp', 'tp'), may hold values from -6 to 6
- present: int32 [4, 768], P(None, 'tp'), may hold values from 0 to 1, as said below
- first_gain: float32 [768], P('tp'), may hold values from 0.1 to 1.9
- first_shift: float32 [768], P('tp'), may hold values from -3 to 3
- filter_inner: bfloat16 [2, 8, 96, 96], P(None, 'tp'), may hold values from -0.4375 to 0.4375
- inner_bias: float32 [2, 8, 96], P(None, 'tp'), may hold values from -3 to 3
- filter_outer: bfloat16 [2, 8, 96, 96], P(None, 'tp'), may hold values from -0.4375 to 0.4375
- outer_bias: float32 [2, 8, 96], P(None, 'tp'), may hold values from -3 to 3
- second_gain: float32 [768], P('tp'), may hold values from 0.1 to 1.9
- second_shift: float32 [768], P('tp'), may hold values from -3 to 3
- expand_weight: bfloat16 [768, 3072], P(None, 'tp'), may hold values from -0.21875 to 0.21875
- expand_bias: float32 [3072], P('tp'), may hold values from -3 to 3
- project_weight: bfloat16 [3072, 768], P('tp'), may hold values from -0.109375 to 0.109375
- project_bias: float32 [768], P('tp'), may hold values from -3 to 3
- cotangent: bfloat16 [4, 96, 768, 256], P(None, 'sp', 'tp'), may hold values from -6 to 6
Outputs:
- result: float32 [4, 96, 768, 256], P(None, 'sp', 'tp')
- patches_grad: float32 [4, 96, 768, 256], P(None, 'sp', 'tp')
- first_gain_grad: float32 [768], replicated
- first_shift_grad: float32 [768], replicated
- filter_inner_grad: float32 [2, 8, 96, 96], P(None, 'tp', 'sp')
- inner_bias_grad: float32 [2, 8, 96], P(None, 'tp', 'sp')
- filter_outer_grad: float32 [2, 8, 96, 96], P(None, 'tp', 'sp')
- outer_bias_grad: float32 [2, 8, 96], P(None, 'tp', 'sp')
- second_gain_grad: float32 [768], replicated
- second_shift_grad: float32 [768], replicated
- expand_weight_grad: float32 [768, 3072], P('sp', 'tp')
- expand_bias_grad: float32 [3072], replicated
- project_weight_grad: float32 [3072, 768], P('tp', 'sp')
- project_bias_grad: float32 [768], replicated
- shrink_share: float32 [], replicated
Inputs may be any that keep to these rules, and one draw needn't show every extreme that they name: 1 marks a feature present in the snapshot, 0 an absent one.
All inputs are finite; a program needn't handle non-finite values.
Results may differ from a plain program's by a relative error of at most 0.008.
The roundings to bfloat16 on the way count: a program that leaves them out, or rounds other values in their place, can miss the bound.
Values may be sent and summed in bfloat16 or wider, within the bound.
No kernel may reach another device: no remote copies, remote signals or barrier semaphores. Data moves between devices by JAX's collectives and lax.ppermute only.
A program may use at most 448 MiB of HBM per device.

v0:
```python
import math

import jax
import jax.numpy as jnp
from jax import lax
from jax.sharding import PartitionSpec as P

BLOCK = 96


SHRINK = 0.01
NORM_EPS = 1e-05
HIGH = lax.Precision.HIGHEST


def gelu_exact(value):
    return jax.nn.gelu(value, approximate=False)


def gelu_grad(value, grad):
    return jax.vjp(gelu_exact, value)[1](grad)[0]


def phase_table(count_a, count_b, period):
    left = lax.broadcasted_iota(jnp.int32, (count_a, count_b), 0)
    right = lax.broadcasted_iota(jnp.int32, (count_a, count_b), 1)
    angle = (left * right % period).astype(jnp.float32) * (2.0 * math.pi / period)
    scale = 1.0 / math.sqrt(period)
    return (jnp.cos(angle) * scale, jnp.sin(angle) * scale)


def exact_mix(form, left, right):
    return jnp.einsum(form, left, right, precision=HIGH)


def block_mix(form, left, right):
    return jnp.einsum(form, left, right, preferred_element_type=jnp.float32)


def block_forward(spec_re, spec_im, filter_inner, inner_bias, filter_outer, outer_bias):
    form = "sykbi,bio->sykbo"
    first_re = (
        block_mix(form, spec_re, filter_inner[0])
        - block_mix(form, spec_im, filter_inner[1])
        + inner_bias[0]
    )
    first_im = (
        block_mix(form, spec_im, filter_inner[0])
        + block_mix(form, spec_re, filter_inner[1])
        + inner_bias[1]
    )
    mid_re = gelu_exact(first_re).astype(jnp.bfloat16)
    mid_im = gelu_exact(first_im).astype(jnp.bfloat16)
    second_re = (
        block_mix(form, mid_re, filter_outer[0])
        - block_mix(form, mid_im, filter_outer[1])
        + outer_bias[0]
    )
    second_im = (
        block_mix(form, mid_im, filter_outer[0])
        + block_mix(form, mid_re, filter_outer[1])
        + outer_bias[1]
    )
    return (
        first_re,
        first_im,
        mid_re,
        mid_im,
        jnp.tanh(second_re / SHRINK),
        jnp.tanh(second_im / SHRINK),
        second_re,
        second_im,
    )


def placed_at(vector, length, start):
    return lax.dynamic_update_slice_in_dim(jnp.zeros((length,), jnp.float32), vector, start, 0)


def per_device(
    patches,
    present,
    first_gain,
    first_shift,
    filter_inner,
    inner_bias,
    filter_outer,
    outer_bias,
    second_gain,
    second_shift,
    expand_weight,
    expand_bias,
    project_weight,
    project_bias,
    cotangent,
):
    patches = jnp.swapaxes(patches, 2, 3)
    cotangent = jnp.swapaxes(cotangent, 2, 3)
    snaps, rows_local, width, chans = patches.shape
    modes = width // 2
    full_rows = rows_local * lax.axis_size("sp")
    modes_local = modes // lax.axis_size("sp")
    model = chans * lax.axis_size("tp")
    groups = chans // BLOCK
    tokens = snaps * rows_local * width
    hidden_local = expand_bias.shape[0]
    hidden_all = hidden_local * lax.axis_size("tp")
    cos_w, sin_w = phase_table(width, modes, width)
    doubled = jnp.where(lax.broadcasted_iota(jnp.int32, (modes, 1), 0) == 0, 1.0, 2.0)
    inv_cos = cos_w.T * doubled
    inv_sin = sin_w.T * doubled
    cos_h, sin_h = phase_table(full_rows, full_rows, full_rows)
    field = patches.astype(jnp.float32)
    first_sums = lax.psum((jnp.sum(field, -1), jnp.sum(field * field, -1)), "tp")
    mean_one = first_sums[0][..., None] / model
    rstd_one = lax.rsqrt(first_sums[1][..., None] / model - mean_one * mean_one + NORM_EPS)
    normed_one = (field - mean_one) * rstd_one
    keep = present.astype(jnp.float32)[:, None, None, :]
    mixed = (normed_one * first_gain + first_shift) * keep
    lon_re = exact_mix("shwc,wk->shkc", mixed, cos_w)
    lon_im = -exact_mix("shwc,wk->shkc", mixed, sin_w)
    col_re, col_im = (
        lax.all_to_all(lon_re, "sp", split_axis=2, concat_axis=1, tiled=True),
        lax.all_to_all(lon_im, "sp", split_axis=2, concat_axis=1, tiled=True),
    )
    spec_re = exact_mix("shkc,yh->sykc", col_re, cos_h) + exact_mix("shkc,yh->sykc", col_im, sin_h)
    spec_im = exact_mix("shkc,yh->sykc", col_im, cos_h) - exact_mix("shkc,yh->sykc", col_re, sin_h)
    block_shape = (snaps, full_rows, modes_local, groups, BLOCK)
    spec_re_low = spec_re.astype(jnp.bfloat16).reshape(block_shape)
    spec_im_low = spec_im.astype(jnp.bfloat16).reshape(block_shape)
    kept = block_forward(
        spec_re_low, spec_im_low, filter_inner, inner_bias, filter_outer, outer_bias
    )
    bend_re, bend_im, second_re, second_im = (kept[4], kept[5], kept[6], kept[7])
    share_local = jnp.sum(1.0 - bend_re * bend_re) + jnp.sum(1.0 - bend_im * bend_im)
    mode_shape = (snaps, full_rows, modes_local, chans)
    shrunk_re = (second_re - SHRINK * bend_re).reshape(mode_shape)
    shrunk_im = (second_im - SHRINK * bend_im).reshape(mode_shape)
    back_re = exact_mix("sykc,yh->shkc", shrunk_re, cos_h) - exact_mix(
        "sykc,yh->shkc", shrunk_im, sin_h
    )
    back_im = exact_mix("sykc,yh->shkc", shrunk_im, cos_h) + exact_mix(
        "sykc,yh->shkc", shrunk_re, sin_h
    )
    row_re, row_im = (
        lax.all_to_all(back_re, "sp", split_axis=1, concat_axis=2, tiled=True),
        lax.all_to_all(back_im, "sp", split_axis=1, concat_axis=2, tiled=True),
    )
    spectral = exact_mix("shkc,kw->shwc", row_re, inv_cos) - exact_mix(
        "shkc,kw->shwc", row_im, inv_sin
    )
    section = field + mixed + spectral
    second_sums = lax.psum((jnp.sum(section, -1), jnp.sum(section * section, -1)), "tp")
    mean_two = second_sums[0][..., None] / model
    rstd_two = lax.rsqrt(second_sums[1][..., None] / model - mean_two * mean_two + NORM_EPS)
    normed_two = (section - mean_two) * rstd_two
    normal = (normed_two * second_gain + second_shift).astype(jnp.bfloat16)
    cot_field = cotangent.astype(jnp.float32)
    wide_in, wide_cot = (
        lax.all_gather(normal, "tp", axis=3, tiled=True),
        lax.all_gather(cotangent, "tp", axis=3, tiled=True),
    )
    wide_in = wide_in.reshape(tokens, model)
    wide_cot = wide_cot.reshape(tokens, model)
    hidden_pre = jnp.dot(wide_in, expand_weight, preferred_element_type=jnp.float32) + expand_bias
    hidden = gelu_exact(hidden_pre).astype(jnp.bfloat16)
    partial_out = jnp.dot(hidden, project_weight, preferred_element_type=jnp.float32)
    reduced = lax.psum_scatter(partial_out, "tp", scatter_dimension=1, tiled=True)
    hidden_grad = jnp.dot(wide_cot, project_weight.T, preferred_element_type=jnp.float32)
    pre_grad = gelu_grad(hidden_pre, hidden_grad).astype(jnp.bfloat16)
    project_grad = jnp.dot(hidden.T, wide_cot, preferred_element_type=jnp.float32)
    expand_grad = jnp.dot(wide_in.T, pre_grad, preferred_element_type=jnp.float32)
    bias_full = placed_at(
        jnp.sum(pre_grad.astype(jnp.float32), 0), hidden_all, lax.axis_index("tp") * hidden_local
    )
    normal_part = jnp.dot(pre_grad, expand_weight.T, preferred_element_type=jnp.float32)
    normal_flat = lax.psum_scatter(normal_part, "tp", scatter_dimension=1, tiled=True)
    result = section + reduced.reshape(snaps, rows_local, width, chans) + project_bias
    normal_grad = normal_flat.reshape(snaps, rows_local, width, chans)
    second_gain_local = jnp.sum(normal_grad * normed_two, (0, 1, 2))
    second_shift_local = jnp.sum(normal_grad, (0, 1, 2))
    scaled_two = normal_grad * second_gain
    back_two = lax.psum((jnp.sum(scaled_two, -1), jnp.sum(scaled_two * normed_two, -1)), "tp")
    section_grad = cot_field + rstd_two * (
        scaled_two - back_two[0][..., None] / model - normed_two * back_two[1][..., None] / model
    )
    freq_re = exact_mix("shwc,kw->shkc", section_grad, inv_cos)
    freq_im = -exact_mix("shwc,kw->shkc", section_grad, inv_sin)
    gcol_re, gcol_im = (
        lax.all_to_all(freq_re, "sp", split_axis=2, concat_axis=1, tiled=True),
        lax.all_to_all(freq_im, "sp", split_axis=2, concat_axis=1, tiled=True),
    )
    dz_re = (
        exact_mix("shkc,yh->sykc", gcol_re, cos_h) + exact_mix("shkc,yh->sykc", gcol_im, sin_h)
    ).reshape(block_shape)
    dz_im = (
        exact_mix("shkc,yh->sykc", gcol_im, cos_h) - exact_mix("shkc,yh->sykc", gcol_re, sin_h)
    ).reshape(block_shape)
    again = block_forward(
        spec_re_low, spec_im_low, filter_inner, inner_bias, filter_outer, outer_bias
    )
    first_re, first_im, mid_re, mid_im, bend_back_re, bend_back_im = (
        again[0],
        again[1],
        again[2],
        again[3],
        again[4],
        again[5],
    )
    grad_two_re = (dz_re * bend_back_re * bend_back_re).astype(jnp.bfloat16)
    grad_two_im = (dz_im * bend_back_im * bend_back_im).astype(jnp.bfloat16)
    weight_form = "sykbi,sykbo->bio"
    back_form = "sykbo,bio->sykbi"
    outer_grad = jnp.stack(
        [
            block_mix(weight_form, mid_re, grad_two_re)
            + block_mix(weight_form, mid_im, grad_two_im),
            block_mix(weight_form, mid_re, grad_two_im)
            - block_mix(weight_form, mid_im, grad_two_re),
        ]
    )
    outer_bias_local = jnp.stack(
        [
            jnp.sum(grad_two_re.astype(jnp.float32), (0, 1, 2)),
            jnp.sum(grad_two_im.astype(jnp.float32), (0, 1, 2)),
        ]
    )
    mid_grad_re = block_mix(back_form, grad_two_re, filter_outer[0]) + block_mix(
        back_form, grad_two_im, filter_outer[1]
    )
    mid_grad_im = block_mix(back_form, grad_two_im, filter_outer[0]) - block_mix(
        back_form, grad_two_re, filter_outer[1]
    )
    grad_one_re = gelu_grad(first_re, mid_grad_re).astype(jnp.bfloat16)
    grad_one_im = gelu_grad(first_im, mid_grad_im).astype(jnp.bfloat16)
    inner_grad = jnp.stack(
        [
            block_mix(weight_form, spec_re_low, grad_one_re)
            + block_mix(weight_form, spec_im_low, grad_one_im),
            block_mix(weight_form, spec_re_low, grad_one_im)
            - block_mix(weight_form, spec_im_low, grad_one_re),
        ]
    )
    inner_bias_local = jnp.stack(
        [
            jnp.sum(grad_one_re.astype(jnp.float32), (0, 1, 2)),
            jnp.sum(grad_one_im.astype(jnp.float32), (0, 1, 2)),
        ]
    )
    spec_grad_re = (
        block_mix(back_form, grad_one_re, filter_inner[0])
        + block_mix(back_form, grad_one_im, filter_inner[1])
    ).reshape(mode_shape)
    spec_grad_im = (
        block_mix(back_form, grad_one_im, filter_inner[0])
        - block_mix(back_form, grad_one_re, filter_inner[1])
    ).reshape(mode_shape)
    lat_re = exact_mix("sykc,yh->shkc", spec_grad_re, cos_h) - exact_mix(
        "sykc,yh->shkc", spec_grad_im, sin_h
    )
    lat_im = exact_mix("sykc,yh->shkc", spec_grad_re, sin_h) + exact_mix(
        "sykc,yh->shkc", spec_grad_im, cos_h
    )
    grow_re, grow_im = (
        lax.all_to_all(lat_re, "sp", split_axis=1, concat_axis=2, tiled=True),
        lax.all_to_all(lat_im, "sp", split_axis=1, concat_axis=2, tiled=True),
    )
    mixed_grad = (
        section_grad
        + exact_mix("shkc,wk->shwc", grow_re, cos_w)
        - exact_mix("shkc,wk->shwc", grow_im, sin_w)
    )
    masked_grad = mixed_grad * keep
    first_gain_local = jnp.sum(masked_grad * normed_one, (0, 1, 2))
    first_shift_local = jnp.sum(masked_grad, (0, 1, 2))
    scaled_one = masked_grad * first_gain
    back_one = lax.psum((jnp.sum(scaled_one, -1), jnp.sum(scaled_one * normed_one, -1)), "tp")
    patches_grad = section_grad + rstd_one * (
        scaled_one - back_one[0][..., None] / model - normed_one * back_one[1][..., None] / model
    )
    summed = (
        lax.psum_scatter(inner_grad, "sp", scatter_dimension=2, tiled=True),
        lax.psum_scatter(inner_bias_local, "sp", scatter_dimension=2, tiled=True),
        lax.psum_scatter(outer_grad, "sp", scatter_dimension=2, tiled=True),
        lax.psum_scatter(outer_bias_local, "sp", scatter_dimension=2, tiled=True),
        lax.psum_scatter(expand_grad, "sp", scatter_dimension=0, tiled=True),
        lax.psum_scatter(project_grad, "sp", scatter_dimension=1, tiled=True),
    )
    spectral_sums = (summed[0], summed[1], summed[2], summed[3])
    expand_sum, project_sum = (summed[4], summed[5])
    offset = lax.axis_index("tp") * chans
    stacked = jnp.stack(
        [
            placed_at(first_gain_local, model, offset),
            placed_at(first_shift_local, model, offset),
            placed_at(second_gain_local, model, offset),
            placed_at(second_shift_local, model, offset),
            placed_at(jnp.sum(cot_field, (0, 1, 2)), model, offset),
        ]
    )
    small = lax.psum((stacked, bias_full, share_local), ("sp", "tp"))
    share = small[2] / (snaps * full_rows * modes * model * 2)
    return (
        jnp.swapaxes(result, 2, 3),
        jnp.swapaxes(patches_grad, 2, 3),
        small[0][0],
        small[0][1],
        spectral_sums[0],
        spectral_sums[1],
        spectral_sums[2],
        spectral_sums[3],
        small[0][2],
        small[0][3],
        expand_sum,
        small[1],
        project_sum,
        small[0][4],
        share,
    )


def solution(mesh):
    return jax.shard_map(
        per_device,
        mesh=mesh,
        in_specs=(
            P(None, "sp", "tp", None),
            P(None, "tp"),
            P("tp"),
            P("tp"),
            P(None, "tp", None, None),
            P(None, "tp", None),
            P(None, "tp", None, None),
            P(None, "tp", None),
            P("tp"),
            P("tp"),
            P(None, "tp"),
            P("tp"),
            P("tp", None),
            P("tp"),
            P(None, "sp", "tp", None),
        ),
        out_specs=(
            P(None, "sp", "tp", None),
            P(None, "sp", "tp", None),
            P(),
            P(),
            P(None, "tp", "sp", None),
            P(None, "tp", "sp"),
            P(None, "tp", "sp", None),
            P(None, "tp", "sp"),
            P(),
            P(),
            P("sp", "tp"),
            P(),
            P("tp", "sp"),
            P(),
            P(),
        ),
        check_vma=False,
    )
```

profile of v0, /device:TPU:2, one launch (start us, length us, event | category | flops | bytes accessed | tf_op | source)
XLA Modules:
  0.0 2866.0 jit_solution(3225307633060310745)
XLA Ops:
  13.3 30.9 %all-reduce.25.cloned.1.call-done = (f32[4,12,256]{2,1,0:T(8,128)}, f32[4,12,256]{2,1,0:T(8,128)}) async-done(((f32[4,12,256]{2,1,0:T(8,128)}, f32[4,12,256]{2,1,0:T(8,128)}), (f32[4,12,256]{2,1,0:T(8,128)}, f32[4,12,256]{2,1,0:T(8,128)})) %all-reduce.25.cloned.1.call-update) | async-done | bytes 98320 | tf_op jit(solution)/shard_map/psum | solution.py:114
  45.1 12.3 negate_bitcast_fusion.1
  71.0 12.0 fusion.144
  90.1 118.2 %all-to-all-done.1 = f32[4,12,128,192]{3,0,1,2:T(4,128)} async-done(((f32[4,12,128,192]{3,0,1,2:T(4,128)}), f32[4,12,128,192]{3,0,1,2:T(4,128)}, u32[]{:S(2)}, u32[]{:S(2)}) %all-to-all-start.1) | async-done | bytes 4718624 | tf_op jit(solution)/shard_map/all_to_all | solution.py:124
  220.9 10.2 fusion.84
  231.1 10.7 fusion.86
  241.8 108.9 %all-to-all-done = f32[4,12,128,192]{3,0,1,2:T(4,128)} async-done(((f32[4,12,128,192]{3,0,1,2:T(4,128)}), f32[4,12,128,192]{3,0,1,2:T(4,128)}, u32[]{:S(2)}, u32[]{:S(2)}) %all-to-all-start) | async-done | bytes 4718624 | tf_op jit(solution)/shard_map/all_to_all | solution.py:123
  361.0 10.3 fusion.103
  387.3 10.0 fusion.102
  403.4 18.5 fusion.51
  422.0 16.6 fusion.49
  456.8 18.0 fusion.260
  487.7 17.3 add_bitcast_fusion.3
  516.6 14.8 fusion.262
  531.4 12.6 subtract_bitcast_fusion.3
  550.6 103.2 %all-to-all-done.3 = f32[4,96,16,192]{3,2,0,1:T(8,128)} async-done(((f32[4,96,16,192]{3,2,0,1:T(8,128)}), f32[4,96,16,192]{3,2,0,1:T(8,128)}, u32[]{:S(2)}, u32[]{:S(2)}) %all-to-all-start.3) | async-done | bytes 4718624 | tf_op jit(solution)/shard_map/all_to_all | solution.py:147
  665.2 130.6 %all-to-all-done.2 = f32[4,96,16,192]{3,2,0,1:T(8,128)} async-done(((f32[4,96,16,192]{3,2,0,1:T(8,128)}), f32[4,96,16,192]{3,2,0,1:T(8,128)}, u32[]{:S(2)}, u32[]{:S(2)}) %all-to-all-start.2) | async-done | bytes 4718624 | tf_op jit(solution)/shard_map/all_to_all | solution.py:146
  799.6 11.4 fusion.224
  811.2 19.0 fusion.480
  831.0 28.6 all-reduce.23.cloned.1.call-done
  861.2 8.0 add_convert_fusion.1
  869.7 111.6 %all-gather.5.cloned.1.call-done = bf16[4,12,256,768]{2,3,1,0:T(8,128)(2,1)} async-done(((bf16[4,12,256,192]{2,3,1,0:T(8,128)(2,1)}), bf16[4,12,256,768]{2,3,1,0:T(8,128)(2,1)}) %all-gather.5.cloned.1.call-update) | async-done | bytes 18874384 | tf_op jit(solution)/shard_map/all_gather | solution.py:161
  981.4 25.2 copy.270
  1006.6 96.7 %all-gather.3.cloned.1.call-done = bf16[4,12,256,768]{2,3,1,0:T(8,128)(2,1)} async-done(((bf16[4,12,256,192]{2,3,1,0:T(8,128)(2,1)}), bf16[4,12,256,768]{2,3,1,0:T(8,128)(2,1)}) %all-gather.3.cloned.1.call-update) | async-done | bytes 18874384 | tf_op jit(solution)/shard_map/all_gather | solution.py:160
  1103.3 24.6 copy.268
  1127.9 26.4 fusion.486
  1154.3 103.6 %convert_reduce_fusion = (f32[768]{0:T(1024)}, bf16[12288,768]{1,0:T(8,128)(2,1)}, f32[12288,768]{1,0:T(8,128)}) fusion(f32[12288,768]{1,0:T(8,128)} %fusion.486, f32[768]{0:T(1024)S(1)} %copy-done.47, bf16[12288,768]{1,0:T(8,128)(2,1)} %bitcast.639, bf16[768,768]{1,0:T(8,128)(2,1)S(1)} %copy-done), kind=kOutput, calls=%fused_computation.2 | convolution fusion | flops 15203302400 | bytes 114432000 | tf_op jit(solution)/shard_map/dot_general | solution.py:169
  1258.0 35.2 %fusion.488 = f32[12288,768]{0,1:T(8,128)} fusion(bf16[12288,768]{1,0:T(8,128)(2,1)} %get-tuple-element.112, bf16[768,768]{1,0:T(8,128)(2,1)S(1)} %copy-done.61), kind=kOutput, calls=%fused_computation.507 | convolution fusion | flops 14495514624 | bytes 57802752 | tf_op jit(solution)/shard_map/dot_general | solution.py:176
  1293.2 44.3 %multiply_convert_fusion = bf16[12288,768]{1,0:T(8,128)(2,1)} fusion(f32[12288,768]{1,0:T(8,128)} %get-tuple-element.113, f32[12288,768]{1,0:T(8,128)} %fusion.486, f32[768]{0:T(1024)S(1)} %copy-done.47), kind=kLoop, calls=%fused_computation.4 | loop fusion | flops 37748736 | bytes 94374912 | tf_op jit(solution)/shard_map/convert_element_type | solution.py:166
  1337.5 26.4 fusion.487
  1364.0 190.9 %reduce-scatter.9.cloned.1.call-done = f32[12288,192]{0,1:T(8,128)} async-done(((f32[12288,768]{0,1:T(8,128)}), f32[12288,192]{0,1:T(8,128)}) %reduce-scatter.9.cloned.1.call-update) | async-done | bytes 9437200 | tf_op jit(solution)/shard_map/reduce_scatter | solution.py:177
  1561.1 11.7 reshape.124
  1572.8 17.7 multiply_reduce_fusion
  1590.5 228.6 %reduce-scatter.7.cloned.1.call-done = f32[12288,192]{0,1:T(8,128)} async-done(((f32[12288,768]{0,1:T(8,128)}), f32[12288,192]{0,1:T(8,128)}) %reduce-scatter.7.cloned.1.call-update) | async-done | bytes 9437200 | tf_op jit(solution)/shard_map/reduce_scatter | solution.py:168
  1819.1 10.9 reshape.122
  1830.0 23.4 all-reduce.21.cloned.1.call-done
  1854.3 24.5 convert_add_fusion
  1882.6 10.5 negate_bitcast_fusion
  1906.3 12.4 convolution_bitcast_fusion
  1926.0 117.7 %all-to-all-done.5 = f32[4,12,128,192]{3,0,1,2:T(4,128)} async-done(((f32[4,12,128,192]{3,0,1,2:T(4,128)}), f32[4,12,128,192]{3,0,1,2:T(4,128)}, u32[]{:S(2)}, u32[]{:S(2)}) %all-to-all-start.5) | async-done | bytes 4718624 | tf_op jit(solution)/shard_map/all_to_all | solution.py:191
  2056.2 10.3 fusion.76
  2066.4 10.4 fusion.78
  2076.8 109.1 %all-to-all-done.4 = f32[4,12,128,192]{3,0,1,2:T(4,128)} async-done(((f32[4,12,128,192]{3,0,1,2:T(4,128)}), f32[4,12,128,192]{3,0,1,2:T(4,128)}, u32[]{:S(2)}, u32[]{:S(2)}) %all-to-all-start.4) | async-done | bytes 4718624 | tf_op jit(solution)/shard_map/all_to_all | solution.py:190
  2194.1 10.9 add_bitcast_fusion.2
  2205.0 10.5 subtract_bitcast_fusion.2
  2242.4 11.5 convert_reduce_fusion.2
  2261.6 8.9 convert_reduce_fusion.5
  2271.5 10.1 convert_reduce_fusion.4
  2311.4 15.2 fusion.258
  2326.7 12.6 subtract_bitcast_fusion
  2350.7 14.8 fusion.288
  2365.6 12.6 add_bitcast_fusion
  2384.8 103.2 %all-to-all-done.6 = f32[4,96,16,192]{3,2,0,1:T(8,128)} async-done(((f32[4,96,16,192]{3,2,0,1:T(8,128)}), f32[4,96,16,192]{3,2,0,1:T(8,128)}, u32[]{:S(2)}, u32[]{:S(2)}) %all-to-all-start.6) | async-done | bytes 4718624 | tf_op jit(solution)/shard_map/all_to_all | solution.py:265
  2492.8 8.7 copy.305
  2501.5 8.7 copy.307
  2532.6 102.8 %all-to-all-done.7 = f32[4,96,16,192]{3,2,0,1:T(8,128)} async-done(((f32[4,96,16,192]{3,2,0,1:T(8,128)}), f32[4,96,16,192]{3,2,0,1:T(8,128)}, u32[]{:S(2)}, u32[]{:S(2)}) %all-to-all-start.7) | async-done | bytes 4718624 | tf_op jit(solution)/shard_map/all_to_all | solution.py:266
  2642.0 15.4 fusion.226
  2657.5 22.8 fusion.24
  2680.3 21.7 fusion.490
  2702.2 21.5 fusion.489
  2727.2 19.9 all-reduce.5
  2751.4 39.8 %all-reduce.4 = (f32[5,768]{1,0:T(8,128)S(1)}, f32[3072]{0:T(1024)}, f32[]{:T(128)}) all-reduce(f32[5,768]{1,0:T(8,128)S(1)} %stack.62, f32[3072]{0:T(1024)S(1)} %dynamic_update_slice.28, f32[]{:T(128)S(6)} %add.331), channel_id=1, replica_groups=mesh['sp'=8,'tp'=4] {'sp','tp'}, use_global_device_ids=true, to_apply=%region_23.24 | all-reduce | flops 6913 | bytes 55304 | tf_op jit(solution)/shard_map/psum | solution.py:301
  2793.3 13.7 fusion.23
  2807.0 50.9 %reduce-scatter.11.cloned.1.call-done = f32[96,768]{1,0:T(8,128)} async-done(((f32[768,768]{1,0:T(8,128)}), f32[96,768]{1,0:T(8,128)}) %reduce-scatter.11.cloned.1.call-update) | async-done | bytes 294928 | tf_op jit(solution)/shard_map/reduce_scatter | solution.py:286
  (309 shorter events, 316.2 us)
Async XLA Ops:
  7.2 1147.1 %copy-start = (bf16[768,768]{1,0:T(8,128)(2,1)S(1)}, bf16[768,768]{1,0:T(8,128)(2,1)}, u32[]{:S(2)}) copy-start(bf16[768,768]{1,0:T(8,128)(2,1)} %param.27) | copy-start | bytes 3538948
  7.2 37.0 %all-reduce.25.cloned.1.call-start = ((), (), s32[]{:S(2)}) async-start(), calls=%async_computation.22 | async-start | bytes 262144 | tf_op jit(solution)/shard_map/psum | solution.py:114
  13.3 57.6 %copy-start.35 = (f32[4,192]{1,0:T(4,128)}, f32[4,192]{1,0:T(4,128)S(1)}, u32[]{:S(2)}) copy-start(f32[4,192]{1,0:T(4,128)S(1)} %convert_element_type.122) | copy-start | bytes 9220
  45.1 25.8 copy-start.21
  45.1 25.8 copy-start.24
  64.6 143.7 %all-to-all-start.1 = ((f32[4,12,128,192]{3,0,1,2:T(4,128)}), f32[4,12,128,192]{3,0,1,2:T(4,128)}, u32[]{:S(2)}, u32[]{:S(2)}) async-start(f32[4,12,128,192]{3,0,1,2:T(4,128)} %copy.241), calls=%async_computation.1 | async-start | bytes 12582912 | tf_op jit(solution)/shard_map/all_to_all | solution.py:124
  90.1 123.2 %copy-start.52 = (f32[2,2,96]{2,1,0:T(2,128)S(1)}, f32[2,2,96]{2,1,0:T(2,128)}, u32[]{:S(2)}) copy-start(f32[2,2,96]{2,1,0:T(2,128)} %param.20) | copy-start | bytes 4612
  90.1 123.2 %copy-start.53 = (f32[2,2,96]{2,1,0:T(2,128)S(1)}, f32[2,2,96]{2,1,0:T(2,128)}, u32[]{:S(2)}) copy-start(f32[2,2,96]{2,1,0:T(2,128)} %param.22) | copy-start | bytes 4612
  208.3 142.3 %all-to-all-start = ((f32[4,12,128,192]{3,0,1,2:T(4,128)}), f32[4,12,128,192]{3,0,1,2:T(4,128)}, u32[]{:S(2)}, u32[]{:S(2)}) async-start(f32[4,12,128,192]{3,0,1,2:T(4,128)} %copy.236), calls=%async_computation | async-start | bytes 12582912 | tf_op jit(solution)/shard_map/all_to_all | solution.py:123
  371.3 16.0 slice-start.11
  397.3 24.6 slice-start.23
  403.4 18.6 copy-start.5
  403.4 18.6 slice-start.24
  422.0 21.3 copy-start.6
  422.0 16.6 copy-start.31
  449.6 25.1 slice-start.17
  456.7 18.0 slice-start.18
  456.7 18.0 copy-start.9
  511.7 19.8 slice-start.5
  511.7 142.1 %all-to-all-start.3 = ((f32[4,96,16,192]{3,2,0,1:T(8,128)}), f32[4,96,16,192]{3,2,0,1:T(8,128)}, u32[]{:S(2)}, u32[]{:S(2)}) async-start(f32[4,96,16,192]{3,2,0,1:T(8,128)} %copy.264), calls=%async_computation.3 | async-start | bytes 12582912 | tf_op jit(solution)/shard_map/all_to_all | solution.py:147
  653.8 142.0 %all-to-all-start.2 = ((f32[4,96,16,192]{3,2,0,1:T(8,128)}), f32[4,96,16,192]{3,2,0,1:T(8,128)}, u32[]{:S(2)}, u32[]{:S(2)}) async-start(f32[4,96,16,192]{3,2,0,1:T(8,128)} %copy.258), calls=%async_computation.2 | async-start | bytes 12582912 | tf_op jit(solution)/shard_map/all_to_all | solution.py:146
  658.6 201.1 %all-reduce.23.cloned.1.call-start = ((), (), s32[]{:S(2)}) async-start(), calls=%async_computation.21 | async-start | bytes 262144 | tf_op jit(solution)/shard_map/psum | solution.py:153
  658.6 152.4 %copy-start.43 = (f32[128]{0:T(128)}, f32[128]{0:T(128)S(1)}, u32[]{:S(2)}) copy-start(f32[128]{0:T(128)S(1)} %fusion.378) | copy-start | bytes 1540
  795.8 15.3 slice-start.3
  795.8 15.3 slice-start.13
  811.2 50.0 %copy-start.38 = (f32[192]{0:T(256)S(1)}, f32[192]{0:T(256)}, u32[]{:S(2)}) copy-start(f32[192]{0:T(256)} %param.23) | copy-start | bytes 2308
  811.2 50.0 %copy-start.59 = (f32[192]{0:T(256)S(1)}, f32[192]{0:T(256)}, u32[]{:S(2)}) copy-start(f32[192]{0:T(256)} %param.24) | copy-start | bytes 2308
  830.3 151.1 %all-gather.5.cloned.1.call-start = ((), (), s32[]{:S(2)}) async-start(), calls=%async_computation.14 | async-start | bytes 23592960 | tf_op jit(solution)/shard_map/all_gather | solution.py:161
  831.0 272.3 %all-gather.3.cloned.1.call-start = ((), (), s32[]{:S(2)}) async-start(), calls=%async_computation.12 | async-start | bytes 23592960 | tf_op jit(solution)/shard_map/all_gather | solution.py:160
  869.3 685.6 %reduce-scatter.9.cloned.1.call-start = ((), (), s32[]{:S(2)}) async-start(), calls=%async_computation.15 | async-start | bytes 47185920 | tf_op jit(solution)/shard_map/reduce_scatter | solution.py:177
  1006.6 121.3 %copy-start.60 = (bf16[768,768]{1,0:T(8,128)(2,1)S(1)}, bf16[768,768]{1,0:T(8,128)(2,1)}, u32[]{:S(2)}) copy-start(bf16[768,768]{1,0:T(8,128)(2,1)} %param.25) | copy-start | bytes 3538948
  1127.9 26.4 copy-start.47
  1154.3 103.6 %copy-start.61 = (bf16[768,768]{1,0:T(8,128)(2,1)S(1)}, bf16[768,768]{1,0:T(8,128)(2,1)}, u32[]{:S(2)}) copy-start(bf16[768,768]{1,0:T(8,128)(2,1)} %param.25) | copy-start | bytes 3538948
  1293.2 525.9 %reduce-scatter.7.cloned.1.call-start = ((), (), s32[]{:S(2)}) async-start(), calls=%async_computation.13 | async-start | bytes 47185920 | tf_op jit(solution)/shard_map/reduce_scatter | solution.py:168
  1363.9 191.0 %copy-start.39 = (f32[192]{0:T(256)S(1)}, f32[192]{0:T(256)}, u32[]{:S(2)}) copy-start(f32[192]{0:T(256)} %param.23) | copy-start | bytes 2308
  1364.0 489.5 %all-reduce.21.cloned.1.call-start = ((), (), s32[]{:S(2)}) async-start(), calls=%async_computation.20 | async-start | bytes 262144 | tf_op jit(solution)/shard_map/psum | solution.py:183
  1590.5 263.8 %copy-start.56 = (f32[192]{0:T(256)S(1)}, f32[192]{0:T(256)}, u32[]{:S(2)}) copy-start(f32[192]{0:T(256)} %param.28) | copy-start | bytes 2308
  1854.3 28.3 copy-start.44
  1900.4 143.3 %all-to-all-start.5 = ((f32[4,12,128,192]{3,0,1,2:T(4,128)}), f32[4,12,128,192]{3,0,1,2:T(4,128)}, u32[]{:S(2)}, u32[]{:S(2)}) async-start(f32[4,12,128,192]{3,0,1,2:T(4,128)} %copy.277), calls=%async_computation.7 | async-start | bytes 12582912 | tf_op jit(solution)/shard_map/all_to_all | solution.py:191
  2043.7 142.2 %all-to-all-start.4 = ((f32[4,12,128,192]{3,0,1,2:T(4,128)}), f32[4,12,128,192]{3,0,1,2:T(4,128)}, u32[]{:S(2)}, u32[]{:S(2)}) async-start(f32[4,12,128,192]{3,0,1,2:T(4,128)} %copy.272), calls=%async_computation.6 | async-start | bytes 12582912 | tf_op jit(solution)/shard_map/all_to_all | solution.py:190
  2254.0 17.5 copy-start.11
  2345.8 19.7 slice-start.7
  2345.8 142.2 %all-to-all-start.6 = ((f32[4,96,16,192]{3,2,0,1:T(8,128)}), f32[4,96,16,192]{3,2,0,1:T(8,128)}, u32[]{:S(2)}, u32[]{:S(2)}) async-start(f32[4,96,16,192]{3,2,0,1:T(8,128)} %copy.294), calls=%async_computation.8 | async-start | bytes 12582912 | tf_op jit(solution)/shard_map/all_to_all | solution.py:265
  2488.0 147.4 %all-to-all-start.7 = ((f32[4,96,16,192]{3,2,0,1:T(8,128)}), f32[4,96,16,192]{3,2,0,1:T(8,128)}, u32[]{:S(2)}, u32[]{:S(2)}) async-start(f32[4,96,16,192]{3,2,0,1:T(8,128)} %copy.300), calls=%async_computation.9 | async-start | bytes 12582912 | tf_op jit(solution)/shard_map/all_to_all | solution.py:266
  2492.8 255.6 %all-reduce.17.cloned.1.call-start = ((), (), s32[]{:S(2)}) async-start(), calls=%async_computation.18 | async-start | bytes 786432
  2526.0 266.4 %all-reduce.19.cloned.1.call-start = ((), (), s32[]{:S(2)}) async-start(), calls=%async_computation.19 | async-start | bytes 262144 | tf_op jit(solution)/shard_map/psum | solution.py:277
  2635.4 22.0 slice-start
  2635.4 22.0 slice-start.1
  2642.0 15.5 slice-start.2
  2642.0 15.5 copy-start.23
  2642.0 15.5 copy-start.26
  2642.0 15.5 copy-start.37
  2642.0 15.5 copy-start.42
  2680.3 126.7 %reduce-scatter.13.cloned.1.call-start = ((), (), s32[]{:S(2)}) async-start(), calls=%async_computation.17 | async-start | bytes 2654208 | tf_op jit(solution)/shard_map/reduce_scatter | solution.py:287
  2702.0 21.6 copy-start.62
  2702.0 22.9 copy-start.50
  2702.1 23.2 copy-start.51
  2702.1 23.4 copy-start.48
  2702.1 23.6 copy-start.49
  2702.1 25.0 copy-start.45
  2702.1 25.0 copy-start.46
  2702.1 25.0 copy-start.57
  2702.1 25.0 copy-start.58
  2702.1 155.8 %reduce-scatter.11.cloned.1.call-start = ((), (), s32[]{:S(2)}) async-start(), calls=%async_computation.16 | async-start | bytes 2654208 | tf_op jit(solution)/shard_map/reduce_scatter | solution.py:286
  (43 other events, 337.2 us)
Sparse Core Ops, SparseCore 0:
  12.8 31.4 all-reduce.24
  830.4 29.2 all-reduce.22
  861.2 120.0 all-gather.4
  983.4 119.9 all-gather.2
  1293.3 261.5 reduce-scatter.8
  1557.5 261.5 reduce-scatter.6
  1822.1 31.3 all-reduce.20
  2526.2 147.3 all-reduce.16
  2680.4 29.1 all-reduce.18
  2714.0 70.9 reduce-scatter.12
  2789.4 68.4 reduce-scatter.10
where the time goes:
time: 2880 us; the launch traced here: 2870 us
  waiting for transfers between devices  1660 us (58%)
  matrix products  672 us (23%)
  local copies, waits for them, and re-layouts  282 us (10%)
  other arithmetic  135 us (5%)
  blocking collectives  59.7 us (2%)
  starting transfers between devices  42.4 us (1%)
    dot_general x24, matrix products, exact_mix(): return jnp.einsum(form, left, right, precision=HIGH)  317 us
    reduce_scatter x1, waiting for transfers between devices, per_device(): lax.psum_scatter(partial_out, 'tp', scatter_dimension=1, tiled=True)  229 us
    reduce_scatter x1, waiting for transfers between devices, per_device(): lax.psum_scatter(normal_part, 'tp', scatter_dimension=1, tiled=True)  191 us
    all_to_all x1, waiting for transfers between devices, per_device(): lax.all_to_all(back_re, 'sp', split_axis=1, concat_axis=2, tiled=True)  131 us
    dot_general x24, matrix products, block_mix(): return jnp.einsum(form, left, right, preferred_element_type=jnp.float32)  120 us
    all_to_all x1, waiting for transfers between devices, per_device(): lax.all_to_all(lon_im, 'sp', split_axis=2, concat_axis=1, tiled=True)  118 us
    all_to_all x1, waiting for transfers between devices, per_device(): lax.all_to_all(freq_im, 'sp', split_axis=2, concat_axis=1, tiled=True)  118 us
    all_gather x1, waiting for transfers between devices, per_device(): lax.all_gather(cotangent, 'tp', axis=3, tiled=True)  112 us
  transfers between devices with their start and end apart: 19, of which 16 were waited for; matrix products, arithmetic and copies ran while one was open for 16% of the time, Pallas kernels for 0%

commit v1 on v0

v1 whole, which is shorter than its diff:
```python
import functools
import math

import jax
import jax.numpy as jnp
import numpy as np
from jax import lax
from jax.experimental import pallas as pl
from jax.experimental.pallas import tpu as pltpu
from jax.sharding import Mesh, PartitionSpec as P

BLOCK = 96
SHRINK = 0.01
NORM_EPS = 1e-05
BF = jnp.bfloat16
F32 = jnp.float32
NN = (((1,), (0,)), ((), ()))
NT = (((1,), (1,)), ((), ()))
TN = (((0,), (0,)), ((), ()))
ERF_T = 0.3275911
ERF_POLY = (0.254829592, -0.284496736, 1.421413741, -1.453152027, 1.061405429)


def dot(left, right, dims=NN):
    return lax.dot_general(left, right, dims, preferred_element_type=F32)


def gelu_pair(value):
    root = jnp.abs(value) * (1.0 / math.sqrt(2.0))
    t = 1.0 / (1.0 + ERF_T * root)
    bell = jnp.exp(-0.5 * value * value)
    poly = 0.5 * ERF_POLY[4]
    for coef in ERF_POLY[3::-1]:
        poly = poly * t + 0.5 * coef
    tail = poly * t * bell
    phi = jnp.where(value >= 0, 1.0 - tail, tail)
    return value * phi, phi + value * bell * (1.0 / math.sqrt(2.0 * math.pi))


def split(value):
    high = value.astype(BF)
    return high, (value - high.astype(F32)).astype(BF)


def np_split(table):
    high = table.astype(np.float32).astype(jnp.bfloat16)
    low = (table - high.astype(np.float64)).astype(np.float32).astype(jnp.bfloat16)
    return jnp.asarray(high), jnp.asarray(low)


def lon_tables(width, modes):
    angle = 2.0 * np.pi * (np.outer(np.arange(modes), np.arange(width)) % width) / width
    scale = 1.0 / math.sqrt(width)
    cos, sin = np.cos(angle) * scale, np.sin(angle) * scale
    doubled = np.where(np.arange(modes) == 0, 1.0, 2.0)[:, None]
    plain = np.concatenate([cos, -sin], 0)
    weighted = np.concatenate([cos * doubled, -sin * doubled], 0)
    return plain, weighted


def lat_table(rows):
    angle = 2.0 * np.pi * (np.outer(np.arange(rows), np.arange(rows)) % rows) / rows
    scale = 1.0 / math.sqrt(rows)
    cos, sin = np.cos(angle) * scale, np.sin(angle) * scale
    return np.block([[cos, sin], [-sin, cos]])


def fold_lanes(value):
    total = value[:, :128]
    for at in range(128, value.shape[1], 128):
        total = total + value[:, at : at + 128]
    return total


def collect(place, pieces, field):
    per = pieces[0].shape[0]
    for k, piece in enumerate(pieces):
        field[pl.ds(place[k] * per, per)] = piece[...].astype(F32)


def plane_forward(parts, table, lat_hi, lat_lo, lons, spectra):
    rows, modes = lat_hi.shape[0] // 2, spectra.shape[1]
    feats = spectra.shape[0] // (2 * rows)
    table_hi, table_lo = table
    total = dot(parts[0], table_lo)
    if len(parts) > 1:
        total = total + dot(parts[1], table_hi)
    total = total + dot(parts[0], table_hi)
    for c in range(2):
        lons[c] = total[:, c * modes : (c + 1) * modes]
    for f in range(0, feats, 2):
        pair = []
        for g in (f, f + 1):
            pair.append(jnp.concatenate([lons[c, pl.ds(g, rows, stride=feats), :] for c in range(2)], axis=0))
        high, low = split(jnp.concatenate(pair, axis=1))
        out = dot(lat_hi, high) + (dot(lat_lo, high) + dot(lat_hi, low))
        for i, g in enumerate((f, f + 1)):
            spectra[pl.ds(g, 2 * rows, stride=feats), :] = out[:, i * modes : (i + 1) * modes]


def plane_inverse(table, lat_hi, lat_lo, lons, spectra):
    rows, modes = lat_hi.shape[0] // 2, spectra.shape[1]
    feats = spectra.shape[0] // (2 * rows)
    table_hi, table_lo = table
    for f in range(0, feats, 2):
        pair = [spectra[pl.ds(g, 2 * rows, stride=feats), :] for g in (f, f + 1)]
        high, low = split(jnp.concatenate(pair, axis=1))
        out = dot(lat_hi, high) + (dot(lat_lo, high) + dot(lat_hi, low))
        for i, g in enumerate((f, f + 1)):
            for c in range(2):
                lons[c, pl.ds(g, rows, stride=feats), :] = out[c * rows : (c + 1) * rows, i * modes : (i + 1) * modes]
    high, low = split(jnp.concatenate([lons[0], lons[1]], axis=1))
    return dot(high, table_hi) + (dot(high, table_lo) + dot(low, table_hi))


def spectrum_kernel(n, place, *refs):
    pieces, (mean, rstd, scale, shift, hi, lo, lat_hi, lat_lo, spec, field, lons, spectra) = refs[:n], refs[n:]
    collect(place, pieces, field)
    mixed = (field[...] - mean[...]) * rstd[...] * scale[...] + shift[...]
    rows, feats, width = mixed.shape
    parts = split(mixed.reshape(rows * feats, width))
    plane_forward(parts, (hi[...], lo[...]), lat_hi[...], lat_lo[...], lons, spectra)
    spec[...] = spectra[...].reshape(spec.shape).astype(BF)


def spectrum_back_kernel(sgrad, hi, lo, lat_hi, lat_lo, freq, lons, spectra):
    value = sgrad[...]
    rows, feats, width = value.shape
    if feats % 16:
        value = value.astype(F32).reshape(rows * feats, width).astype(BF)
    else:
        value = value.reshape(rows * feats, width)
    plane_forward((value,), (hi[...], lo[...]), lat_hi[...], lat_lo[...], lons, spectra)
    freq[...] = spectra[...].reshape(freq.shape)


def two_modes(ref, ky):
    return jnp.concatenate([jnp.concatenate([ref[0, k], ref[1, k]], axis=0) for k in (ky, ky + 1)], axis=1)


def put_modes(ref, ky, value):
    feats, modes = ref.shape[2], ref.shape[3]
    for i in range(2):
        for c in range(2):
            ref[c, ky + i] = value[c * feats : (c + 1) * feats, i * modes : (i + 1) * modes]


def filter_kernel(spec, w1, bias1, w2, bias2, kept, mid, slope, bend, share):
    @pl.when(pl.program_id(0) == 0)
    def _():
        share[...] = jnp.zeros_like(share)

    for ky in range(0, spec.shape[1], 2):
        act, deriv = gelu_pair(dot(w1[...], two_modes(spec, ky)) + bias1[...])
        act = act.astype(BF)
        put_modes(mid, ky, act)
        put_modes(slope, ky, deriv)
        second = dot(w2[...], act) + bias2[...]
        bent = jnp.tanh(second * (1.0 / SHRINK))
        square = bent * bent
        put_modes(bend, ky, square)
        put_modes(kept, ky, second - SHRINK * bent)
        share[...] += jnp.sum((1.0 - square).reshape(-1, 8, square.shape[1]), axis=0)


def filter_back_kernel(
    freq, spec, mid, slope, bend, w1, w2, sgrad, inner, outer, inner_bias, outer_bias
):
    @pl.when(pl.program_id(0) == 0)
    def _():
        for ref in (inner, outer, inner_bias, outer_bias):
            ref[...] = jnp.zeros_like(ref)

    for ky in range(0, spec.shape[1], 2):
        two = (two_modes(freq, ky) * two_modes(bend, ky)).astype(BF)
        outer[...] += dot(two_modes(mid, ky), two, NT)
        outer_bias[...] += fold_lanes(two.astype(F32))
        one = (dot(w2[...], two, TN) * two_modes(slope, ky)).astype(BF)
        inner[...] += dot(two_modes(spec, ky), one, NT)
        inner_bias[...] += fold_lanes(one.astype(F32))
        put_modes(sgrad, ky, dot(w1[...], one, TN))


def section_kernel(n, place, *refs):
    pieces, (mean, rstd, scale, shift, kept, hi, lo, lat_hi, lat_lo, section, field, lons, spectra) = refs[:n], refs[n:]
    spectra[...] = kept[...].reshape(spectra.shape)
    collect(place, pieces, field)
    value = field[...]
    mixed = (value - mean[...]) * rstd[...] * scale[...] + shift[...]
    spectral = plane_inverse((hi[...], lo[...]), lat_hi[...], lat_lo[...], lons, spectra)
    section[...] = (value + mixed + spectral.reshape(value.shape)).astype(BF)


def last_kernel(n, place, *refs):
    pieces = refs[:n]
    mean, rstd, scale, sgrad, freq, hi, lo, lat_hi, lat_lo, out, one, two, gain_sum, shift_sum, field, lons, spectra = refs[n:]
    spectra[...] = freq[...].reshape(spectra.shape)
    collect(place, pieces, field)
    normed = (field[...] - mean[...]) * rstd[...]
    grad = sgrad[...].astype(F32)
    mixed = grad + plane_inverse((hi[...], lo[...]), lat_hi[...], lat_lo[...], lons, spectra).reshape(grad.shape)
    gain_sum[...] = fold_lanes(jnp.sum(mixed * normed, axis=0))
    shift_sum[...] = fold_lanes(jnp.sum(mixed, axis=0))
    scaled = mixed * scale[...]
    out[...] = (grad + rstd[...] * scaled).astype(BF)

    @pl.when(pl.program_id(0) == 0)
    def _():
        one[...] = jnp.zeros_like(one)
        two[...] = jnp.zeros_like(two)

    one[...] += jnp.sum(scaled, axis=1, keepdims=True)
    two[...] += jnp.sum(scaled * normed, axis=1, keepdims=True)


def column_norm(value):
    mean = jnp.mean(value, axis=0, keepdims=True)
    centered = value - mean
    var = jnp.mean(centered * centered, axis=0, keepdims=True)
    rstd = lax.rsqrt(var + NORM_EPS)
    return centered * rstd, rstd


def feed_kernel(
    n, quarter, chunk, place, *refs
):
    cots = refs[:n]
    (section, we_t, wp, we, bias, gain, shift,
     normal, hidden, pre, cot, sgrad, bias_sum, gain_sum, shift_sum, cot_sum) = refs[n:]

    @pl.when(pl.program_id(0) == 0)
    def _():
        for ref in (bias_sum, gain_sum, shift_sum, cot_sum):
            ref[...] = jnp.zeros_like(ref)

    for k, piece in enumerate(cots):
        cot[pl.ds(place[k] * quarter, quarter), :] = piece[0]
    normed, rstd = column_norm(section[...].astype(F32).reshape(normal.shape))
    value = (normed * gain[...] + shift[...]).astype(BF)
    normal[...] = value
    wide = cot[...]
    part = we.shape[2]
    total = None
    for start in range(0, hidden.shape[0], chunk):
        rows = slice(start, start + chunk)
        before = dot(we_t[rows], value) + jnp.concatenate([bias[rows]] * (value.shape[1] // 128), axis=1)
        act, slope = gelu_pair(before)
        hidden[rows] = act.astype(BF)
        grad = (dot(wp[rows], wide) * slope).astype(BF)
        pre[rows] = grad
        bias_sum[rows] += fold_lanes(grad.astype(F32))
        t, at = start // part, start % part
        term = dot(we[t, :, at : at + chunk], grad)
        total = term if total is None else total + term
    gain_sum[...] += fold_lanes(total * normed)
    shift_sum[...] += fold_lanes(total)
    wide = wide.astype(F32)
    cot_sum[...] += fold_lanes(wide)
    scaled = total * gain[...]
    one = jnp.mean(scaled, axis=0, keepdims=True)
    two = jnp.mean(scaled * normed, axis=0, keepdims=True)
    grad = wide + rstd * (scaled - one - normed * two)
    sgrad[...] = grad.reshape(sgrad.shape).astype(BF)


def widen_kernel(slot, p0, p1, p2, p3, out):
    for k, piece in enumerate((p0, p1, p2, p3)):

        @pl.when(pl.program_id(0) == k)
        def _(piece=piece):
            out[0, 0] = piece[...].astype(F32)


def finish_kernel(n, feats, snap, part, *refs):
    pieces, (patches, mean, rstd, one, two, out) = refs[:n], refs[n:]
    normed = (patches[0].astype(F32) - mean[0]) * rstd[0]
    fix = rstd[0] * (one[0] + normed * two[0]) * (1.0 / feats)
    for k, piece in enumerate(pieces):

        @pl.when(pl.program_id(0) == k)
        def _(piece=piece):
            out[0] = piece[...].astype(F32) - fix


def whole(shape):
    return pl.BlockSpec(shape, lambda *_: (0,) * len(shape), pipeline_mode=pl.Buffered(1))


def fixed(shape):
    return pl.BlockSpec(shape, lambda *_: (0,) * len(shape))


def run(name, kernel, grid, ins, specs, outs, out_specs, scratch, mib, scalars=()):
    grid_spec = pltpu.PrefetchScalarGridSpec(
        num_scalar_prefetch=len(scalars), grid=grid, in_specs=specs, out_specs=out_specs, scratch_shapes=scratch
    )
    call = pl.pallas_call(
        kernel,
        grid_spec=grid_spec,
        out_shape=outs,
        compiler_params=pltpu.CompilerParams(vmem_limit_bytes=mib << 20),
        name=name,
    )
    return call(*scalars, *ins)


def complex_weight(pair):
    real, imag = pair[0].T, pair[1].T
    return jnp.concatenate([jnp.concatenate([real, -imag], 1), jnp.concatenate([imag, real], 1)], 0)


def weight_pair(full):
    full = full.reshape(2, BLOCK, 2, BLOCK)
    return jnp.stack([full[0, :, 0] + full[1, :, 1], full[0, :, 1] - full[1, :, 0]])


def per_device(
    sizes, patches, present, first_gain, first_shift, filter_inner, inner_bias, filter_outer, outer_bias,
    second_gain, second_shift, expand_weight, expand_bias, project_weight, project_bias, cotangent,
):
    planes, blocks_local, cut, tp = sizes
    inner = blocks_local * cut
    ranks = inner * tp
    owners = planes * inner
    snaps, per, quarter, width = patches.shape
    feats = quarter * tp
    mine = quarter // inner
    modes = width // 2
    rows = per * ranks
    toks = per * width
    hidden_local = expand_bias.shape[0]
    hiddens = hidden_local * tp
    z, y, j, t = (lax.axis_index(name) for name in ("z", "y", "j", "t"))
    r = y * cut + j
    me = z * inner + r
    every, sp = ("z", "y", "j", "t"), ("z", "y", "j")
    shape = jax.ShapeDtypeStruct

    def to_plane(array):
        array = array.reshape(snaps, per, inner, mine, width)
        out = []
        for k in range(owners):
            there = me ^ k
            piece = lax.dynamic_slice(
                array, (there // inner, 0, there % inner, 0, 0), (1, per, 1, mine, width)
            ).reshape(per, mine, width)
            out.append(lax.ppermute(piece, sp, [(a, a ^ k) for a in range(owners)]) if k else piece)
        return out

    pieces = to_plane(patches)
    origin = jnp.stack([me ^ k for k in range(owners)]).astype(jnp.int32)

    def route(k, back):
        pairs = [
            ((zz * inner + rr) * tp + tt, (((tt + k) % tp) * inner + rr) * tp + zz)
            for zz in range(planes)
            for rr in range(inner)
            for tt in range(tp)
        ]
        return [(b, a) for a, b in pairs] if back else pairs

    place = jnp.stack([(z - k) % tp for k in range(tp)]).astype(jnp.int32)
    slot = jnp.stack([(t + k) % tp for k in range(tp)]).astype(jnp.int32)
    late, pieces = lax.optimization_barrier((cotangent, pieces))
    cots = [
        lax.ppermute(lax.dynamic_index_in_dim(late, (t + k) % tp, 0, False), every, route(k, False)) for k in range(tp)
    ]

    field = patches.astype(F32)
    mean = jnp.mean(field, 2)
    square = jnp.sum(jnp.square(field - mean[:, :, None]), 2)
    gathered = lax.all_gather(jnp.stack([mean, square]), "t")
    mean = jnp.mean(gathered[:, 0], 0)
    square = jnp.sum(gathered[:, 1] + quarter * jnp.square(gathered[:, 0] - mean), 0)
    stats = jnp.stack([mean, lax.rsqrt(square / feats + NORM_EPS)], 2)
    sent = jnp.broadcast_to(stats[:, None], (snaps, inner, per, 2, width)).reshape(owners, per, 2, width)
    plane_stats = lax.all_to_all(sent, sp, 0, 0, tiled=True).reshape(rows, 2, 1, width)
    mean_one, rstd_one = plane_stats[:, 0], plane_stats[:, 1]

    def lanes(vector, width=width):
        return jnp.broadcast_to(vector[:, None], (vector.shape[0], width))

    def own_features(vector):
        return lax.dynamic_slice_in_dim(vector, r * mine, mine)

    keep = own_features(lax.dynamic_index_in_dim(present, z, 0, False).astype(F32))
    scale1, shift1 = lanes(own_features(first_gain) * keep), lanes(own_features(first_shift) * keep)

    def own_block(array):
        return lax.dynamic_index_in_dim(array, y, 1, False)

    w1, w2 = complex_weight(own_block(filter_inner)), complex_weight(own_block(filter_outer))
    bias1 = lanes(own_block(inner_bias).reshape(-1), 2 * modes)
    bias2 = lanes(own_block(outer_bias).reshape(-1), 2 * modes)
    plain, weighted = lon_tables(width, modes)
    lat = lat_table(rows)
    plain_t, weighted_t, plain_n, weighted_n = (np_split(a) for a in (plain.T, weighted.T, plain, weighted))
    lat_f, lat_b = np_split(lat), np_split(lat.T)

    some = 16 if mine % 16 == 0 else mine
    grid = (mine // some,)
    piece_specs = [pl.BlockSpec((per, some, width), lambda g, *_: (0, g, 0))] * owners
    stat_spec, feat_spec = whole((rows, 1, width)), pl.BlockSpec((some, width), lambda g, *_: (g, 0))
    lon_f, lon_b = [whole((width, 2 * modes))] * 2, [whole((2 * modes, width))] * 2
    lat_specs = [whole((2 * rows, 2 * rows))] * 2
    image_spec = pl.BlockSpec((rows, some, width), lambda g, *_: (0, g, 0))
    modes_spec = pl.BlockSpec((2, rows, some, modes), lambda g, *_: (0, 0, g, 0))
    scratch = [
        pltpu.VMEM((rows, some, width), F32),
        pltpu.VMEM((2, rows * some, modes), F32),
        pltpu.VMEM((2 * rows * some, modes), F32),
    ]
    mine_modes = (2, rows, mine, modes)
    spec = run(
        "spectrum", functools.partial(spectrum_kernel, owners), grid,
        (*pieces, mean_one, rstd_one, scale1, shift1, *plain_t, *lat_f),
        [*piece_specs, stat_spec, stat_spec, feat_spec, feat_spec, *lon_f, *lat_specs],
        shape(mine_modes, BF), modes_spec, scratch, 48, (origin,),
    )

    def to_blocks(array):
        return lax.all_to_all(array, "j", 1, 2, tiled=True) if cut > 1 else array

    def to_features(array):
        return lax.all_to_all(array, "j", 2, 1, tiled=True) if cut > 1 else array

    spec = to_blocks(spec)
    lats = rows // cut
    step = 8
    block_modes = (2, lats, BLOCK, modes)
    block_spec = pl.BlockSpec((2, step, BLOCK, modes), lambda g: (0, g, 0, 0))
    square_spec, lane_spec = whole((2 * BLOCK, 2 * BLOCK)), whole((2 * BLOCK, 2 * modes))
    kept, mid, slope, bend, share = run(
        "filter", filter_kernel, (lats // step,), (spec, w1, bias1, w2, bias2),
        [block_spec, square_spec, lane_spec, square_spec, lane_spec],
        (shape(block_modes, F32), shape(block_modes, BF), shape(block_modes, F32), shape(block_modes, F32),
         shape((8, 2 * modes), F32)),
        (block_spec, block_spec, block_spec, block_spec, fixed((8, 2 * modes))), [], 48,
    )
    section = run(
        "section", functools.partial(section_kernel, owners), grid,
        (*pieces, mean_one, rstd_one, scale1, shift1, to_features(kept), *weighted_n, *lat_b),
        [*piece_specs, stat_spec, stat_spec, feat_spec, feat_spec, modes_spec, *lon_b, *lat_specs],
        shape((rows, mine, width), BF), image_spec, scratch, 56, (origin,),
    )

    def exchange(array):
        return lax.all_to_all(array.reshape(ranks, per, mine, width), ("t", "y", "j"), 0, 0, tiled=True)

    section = exchange(section)

    small = lax.all_gather(jnp.stack([second_gain, second_shift, project_bias]), "t", axis=1, tiled=True)
    bias_all = lax.all_gather(expand_bias, "t", tiled=True)
    we = lax.all_gather(expand_weight, "t")
    wp = lax.all_gather(project_weight, "t", tiled=True)
    we_t = jnp.swapaxes(we, 1, 2).reshape(hiddens, feats)
    gain2, shift2 = lanes(small[0]), lanes(small[1])
    tok_spec = pl.BlockSpec((feats, width), lambda h, *_: (0, h))
    hid_spec = pl.BlockSpec((hiddens, width), lambda h, *_: (0, h))
    cot_specs = [pl.BlockSpec((1, quarter, width), lambda h, *_: (h, 0, 0))] * tp
    line_spec = pl.BlockSpec((ranks, 1, mine, width), lambda h, *_: (0, h, 0, 0))
    normal, hidden, pre, cot, sgrad, bias_sum, gain_sum, shift_sum, cot_sum = run(
        "feed", functools.partial(feed_kernel, tp, quarter, min(512, hidden_local // 2)), (per,),
        (*cots, section, we_t, wp, we, lanes(bias_all, 128), gain2, shift2),
        [*cot_specs, line_spec, whole((hiddens, feats)), whole((hiddens, feats)), whole((tp, feats, hidden_local)),
         whole((hiddens, 128)), whole((feats, width)), whole((feats, width))],
        (shape((feats, toks), BF), shape((hiddens, toks), BF), shape((hiddens, toks), BF), shape((feats, toks), BF),
         shape((ranks, per, mine, width), BF), shape((hiddens, 128), F32), *[shape((feats, 128), F32)] * 3),
        (tok_spec, hid_spec, hid_spec, tok_spec, line_spec, fixed((hiddens, 128)), *[fixed((feats, 128))] * 3),
        [], 60, (place,),
    )
    sgrad = exchange(sgrad).reshape(rows, mine, width)

    lines = jnp.moveaxis(section, 1, 2).reshape(feats, toks).astype(F32)
    result = dot(wp, hidden, TN) + lines + small[2][:, None]
    result = result.astype(BF).reshape(tp, quarter, toks)
    result = [
        lax.ppermute(lax.dynamic_index_in_dim(result, place[k], 0, False), every, route(k, True)) for k in range(tp)
    ]
    project_grad = dot(hidden, cot, NT)
    expand_grad = dot(normal, pre, NT)

    freq = run(
        "spectrum_back", spectrum_back_kernel, grid, (sgrad, *weighted_t, *lat_f),
        [image_spec, *lon_f, *lat_specs], shape(mine_modes, F32), modes_spec, scratch[1:], 48,
    )
    freq, inner_grad, outer_grad, inner_bias_grad, outer_bias_grad = run(
        "filter_back", filter_back_kernel, (lats // step,), (to_blocks(freq), spec, mid, slope, bend, w1, w2),
        [*[block_spec] * 5, square_spec, square_spec],
        (shape(block_modes, F32), *[shape((2 * BLOCK, 2 * BLOCK), F32)] * 2, *[shape((2 * BLOCK, 128), F32)] * 2),
        (block_spec, *[fixed((2 * BLOCK, 2 * BLOCK))] * 2, *[fixed((2 * BLOCK, 128))] * 2), [], 48,
    )
    grads, one, two, first_gain_sum, first_shift_sum = run(
        "last", functools.partial(last_kernel, owners), grid,
        (*pieces, mean_one, rstd_one, scale1, sgrad, to_features(freq), *plain_n, *lat_b),
        [*piece_specs, stat_spec, stat_spec, feat_spec, image_spec, modes_spec, *lon_b, *lat_specs],
        (shape((rows, mine, width), BF), *[shape((rows, 1, width), F32)] * 2, *[shape((mine, 128), F32)] * 2),
        (image_spec, *[fixed((rows, 1, width))] * 2, *[pl.BlockSpec((some, 128), lambda g, *_: (g, 0))] * 2),
        scratch, 56, (origin,),
    )
    grads = grads.reshape(owners, per, mine, width)
    outs = []
    for k in range(owners):
        piece = lax.dynamic_index_in_dim(grads, me ^ k, 0, False)
        outs.append(lax.ppermute(piece, sp, [(a, a ^ k) for a in range(owners)]) if k else piece)
    sums = jnp.stack([one.reshape(owners, per, width), two.reshape(owners, per, width)], 1)
    sums = lax.all_to_all(sums, sp, 0, 0, tiled=True).reshape(planes, inner, 2, per, 1, width)
    sums = lax.psum(jnp.sum(sums, 1), "t")

    line_specs = [
        pl.BlockSpec((quarter, width), lambda i, h, s, k=k: (0, jnp.where(i == k, h, jnp.where(i < k, 0, per - 1))))
        for k in range(tp)
    ]
    result = run(
        "widen", widen_kernel, (tp, per), result, line_specs, shape((snaps, per, quarter, width), F32),
        pl.BlockSpec((1, 1, quarter, width), lambda i, h, s: (s[i], h, 0, 0)), [], 32, (slot,),
    )
    one_spec = pl.BlockSpec((1, per, 1, width), lambda i, s, b: (s[i], 0, 0, 0))
    patch_spec = pl.BlockSpec((1, per, mine, width), lambda i, s, b: (s[i], 0, b[i], 0))
    patches_grad = run(
        "finish", functools.partial(finish_kernel, owners, feats), (owners,),
        (*outs, patches, stats[:, :, 0, None], stats[:, :, 1, None], sums[:, 0], sums[:, 1]),
        [*[fixed((per, mine, width))] * owners, patch_spec, *[one_spec] * 4],
        shape((snaps, per, quarter, width), F32), patch_spec, [], 48, (origin // inner, origin % inner),
    )

    def own(array, dim):
        array = lax.psum_scatter(array, "t", scatter_dimension=dim[0], tiled=True)
        return lax.psum_scatter(array, sp, scatter_dimension=dim[1], tiled=True)

    project_sum = own(project_grad, (0, 1))
    expand_sum = own(expand_grad, (1, 0))

    def with_bias(full, bias):
        bias = jnp.sum(bias, 1).reshape(2, BLOCK)
        return jnp.concatenate([weight_pair(full), bias[:, :, None]], 2)

    both = jnp.stack([with_bias(inner_grad, inner_bias_grad), with_bias(outer_grad, outer_bias_grad)])
    both = jnp.moveaxis(both, 2, 0)[:, :, :, None]
    both = lax.dynamic_update_slice(
        jnp.zeros((BLOCK, 2, 2, blocks_local, BLOCK + 1), F32), both, (0, 0, 0, y, 0)
    )
    both = lax.psum_scatter(both, sp, scatter_dimension=0, tiled=True)
    both = jnp.moveaxis(both, 0, 3)
    early = jnp.concatenate(
        [jnp.sum(gain_sum, 1), jnp.sum(shift_sum, 1), jnp.sum(cot_sum, 1), jnp.sum(bias_sum, 1), jnp.sum(share)[None]]
    )
    early = lax.psum(early, every)
    last = jnp.stack([jnp.sum(first_gain_sum, 1) * keep, jnp.sum(first_shift_sum, 1) * keep])
    last = lax.psum(
        lax.dynamic_update_slice(jnp.zeros((2, feats), F32), last, (0, t * quarter + r * mine)), every
    )
    return (
        result, patches_grad, last[0], last[1], both[0, ..., :BLOCK], both[0, ..., BLOCK],
        both[1, ..., :BLOCK], both[1, ..., BLOCK],
        early[:feats], early[feats : 2 * feats], expand_sum, early[3 * feats : 3 * feats + hiddens],
        project_sum, early[2 * feats : 3 * feats], early[-1] / (snaps * rows * modes * feats * 2),
    )


def solution(mesh):
    tp = mesh.shape["tp"]
    planes = tp
    inner = mesh.shape["sp"] // planes
    blocks_local = 2
    cut = inner // blocks_local
    mesh = Mesh(mesh.devices.reshape(planes, blocks_local, cut, tp), ("z", "y", "j", "t"))
    sp = ("z", "y", "j")
    image = P(None, sp, "t", None)
    return jax.shard_map(
        functools.partial(per_device, (planes, blocks_local, cut, tp)),
        mesh=mesh,
        in_specs=(
            image, P(None, "t"), P("t"), P("t"),
            P(None, "t", None, None), P(None, "t", None), P(None, "t", None, None), P(None, "t", None),
            P("t"), P("t"), P(None, "t"), P("t"), P("t", None), P("t"), image,
        ),
        out_specs=(
            image, image, P(), P(),
            P(None, "t", sp, None), P(None, "t", sp), P(None, "t", sp, None), P(None, "t", sp),
            P(), P(), P(sp, "t"), P(), P("t", sp), P(), P(),
        ),
        check_vma=False,
    )
```

time: 2880 us -> 1150 us (0.40)
  the two profiles are of different devices: /device:TPU:2 before, /device:TPU:12 now
where the time goes in v1:
time: 1150 us; the launch traced here: 1140 us
  waiting for transfers between devices  329 us (29%)
  blocking collectives  300 us (26%)
  Pallas kernels  238 us (21%)
  local copies, waits for them, and re-layouts  113 us (10%)
  matrix products  62.8 us (5%)
  starting transfers between devices  47 us (4%)
  other arithmetic  32.5 us (3%)
  between operations  18 us (2%)
    pallas_call x9, Pallas kernels, run(): return call(*scalars, *ins)  238 us
    ppermute x4, waiting for transfers between devices, per_device(): lax.ppermute(lax.dynamic_index_in_dim(result, place[k], 0, False), every,...  179 us
    all_to_all x1, blocking collectives, exchange(): lax.all_to_all(array.reshape(ranks, per, mine, width), ('t', 'y', 'j'), 0...  107 us
    all_gather x1, blocking collectives, per_device(): lax.all_gather(jnp.stack([second_gain, second_shift, project_bias]), 't',...  93.7 us
    ppermute x7, waiting for transfers between devices, per_device(): lax.ppermute(piece, sp, [(a, a ^ k) for a in range(owners)])  89.5 us
    psum x1, blocking collectives, per_device(): lax.psum(lax.dynamic_update_slice(jnp.zeros((2, feats), F32), last, (0, t...  84.4 us
    dot_general x3, matrix products, dot(): return lax.dot_general(left, right, dims, preferred_element_type=F32)  62.8 us
    unnamed x111, local copies, waits for them, and re-layouts  43.2 us
  transfers between devices with their start and end apart: 33, of which 11 were waited for; matrix products, arithmetic and copies ran while one was open for 15% of the time, Pallas kernels for 13%

profile of v1, /device:TPU:12, one launch (start us, length us, event | category | flops | bytes accessed | tf_op | source)
XLA Modules:
  0.0 1140.6 jit_solution(1127788485132760265)
XLA Ops:
  8.3 4.4 dynamic-slice_bitcast_fusion.16
  13.2 3.0 collective-permute-start.2
  16.2 2.6 collective-permute-start.3
  19.1 4.0 convert_reduce_fusion
  23.1 4.2 fusion.1
  27.4 9.0 all-gather
  38.2 6.5 all-to-all-start
  51.2 1.5 maximum_maximum_fusion.w1
  54.1 1.5 collective-permute-start.5
  57.4 1.4 copy.183
  59.8 1.5 maximum_maximum_fusion.1.w2
  62.6 37.5 %all-to-all-done = f32[8,12,2,256]{3,2,1,0:T(2,128)} async-done(((f32[8,12,2,256]{3,2,1,0:T(2,128)}), f32[8,12,2,256]{3,2,1,0:T(2,128)}, u32[]{:S(2)}, u32[]{:S(2)}) %all-to-all-start) | async-done | bytes 196640 | tf_op jit(solution)/shard_map/all_to_all | solution.py:377
  101.4 11.5 %collective-permute-done.5.refs_6_ = bf16[12,96,256]{2,1,0:T(8,128)(2,1)} collective-permute-done((bf16[12,96,256]{2,1,0:T(8,128)(2,1)}, bf16[12,96,256]{2,1,0:T(8,128)(2,1)}, u32[]{:S(2)}, u32[]{:S(2)}) %collective-permute-start.5) | collective-permute-done | bytes 589856 | tf_op jit(solution)/shard_map/ppermute | solution.py:347
  112.9 10.6 collective-permute-done.6.refs_7_
  128.7 22.3 %spectrum.1.spec = bf16[2,96,96,128]{3,2,1,0:T(8,128)(2,1)} custom-call(s32[8]{0:T(128)S(1)} %stack.130.place, bf16[12,96,256]{2,1,0:T(8,128)(2,1)S(1)} %get-tuple-element.49.refs_0_, bf16[12,96,256]{2,1,0:T(8,128)(2,1)S(1)} %collective-permute-done.refs_1_, bf16[12,96,256]{2,1,0:T(8,128)(2,1)S(1)} %collective-permute-done.1.refs_2_, ...), custom_call_target="tpu_custom_call" | custom-call | tf_op jit(solution)/shard_map/spectrum/pallas_call | solution.py:304
  151.3 17.3 %filter.1 = (f32[2,96,96,128]{3,2,1,0:T(8,128)}, bf16[2,96,96,128]{3,2,1,0:T(8,128)(2,1)S(1)}, f32[2,96,96,128]{3,2,1,0:T(8,128)}, f32[2,96,96,128]{3,2,1,0:T(8,128)}, f32[8,256]{1,0:T(8,128)S(1)}) custom-call(bf16[2,96,96,128]{3,2,1,0:T(8,128)(2,1)} %spectrum.1.spec, bf16[192,192]{1,0:T(8,128)(2,1)S(1)} %copy-done.12, ...), custom_call_target="tpu_custom_call" | custom-call | tf_op jit(solution)/shard_map/filter/pallas_call | solution.py:304
  168.6 2.3 copy-done.7
  170.9 17.4 %section.1 = bf16[96,96,256]{2,1,0:T(8,128)(2,1)} custom-call(s32[8]{0:T(128)} %copy-done.26, bf16[12,96,256]{2,1,0:T(8,128)(2,1)} %copy-done.1, bf16[12,96,256]{2,1,0:T(8,128)(2,1)} %copy-done.2, bf16[12,96,256]{2,1,0:T(8,128)(2,1)} %copy-done.3, bf16[12,96,256]{2,1,0:T(8,128)(2,1)} %copy-done.4, bf16[12,96,256]{2,1,0:T(8,128)(2,1)} %copy-done.5, ...), custom_call_target="tpu_custom_call" | custom-call | tf_op jit(solution)/shard_map/section/pallas_call | solution.py:304
  188.3 5.7 all-to-all-start.1
  194.0 4.6 dynamic-slice_bitcast_fusion.4
  198.6 1.9 collective-permute-start.7
  200.7 3.7 collective-permute-start.9
  205.1 93.7 %all-gather.3 = f32[4,192,3]{1,2,0:T(4,128)S(1)} all-gather(f32[1,192,3]{1,2,0:T(4,128)S(1)} %maximum_bitcast_fusion.2), channel_id=1, replica_groups=mesh['z'=4,'y'=2,'j'=1,'t'=4] {'t'}, dimensions={0}, use_global_device_ids=true | all-gather | bytes 11520 | tf_op jit(solution)/shard_map/all_gather | solution.py:452
  300.9 6.1 all-gather.2
  309.0 6.6 copy.146
  318.1 2.4 broadcast_in_dim.73.refs_8_
  320.4 86.3 %feed.1 = (bf16[768,3072]{1,0:T(8,128)(2,1)}, bf16[3072,3072]{1,0:T(8,128)(2,1)}, bf16[3072,3072]{1,0:T(8,128)(2,1)}, bf16[768,3072]{1,0:T(8,128)(2,1)}, bf16[8,...) custom-call(s32[4]{0:T(128)} %pad_add_fusion.1.place, ...), custom_call_target="tpu_custom_call" | custom-call | tf_op jit(solution)/shard_map/feed/pallas_call | solution.py:304
  406.7 21.0 %fusion.19 = f32[3072,768]{1,0:T(8,128)} fusion(bf16[3072,3072]{1,0:T(8,128)(2,1)} %get-tuple-element.58, bf16[768,3072]{1,0:T(8,128)(2,1)} %get-tuple-element.80), kind=kOutput, calls=%fused_computation.106 | convolution fusion | flops 14495514624 | bytes 33030144 | tf_op jit(solution)/shard_map/dot_general | solution.py:25
  428.0 21.2 %fusion.18 = f32[768,3072]{1,0:T(8,128)} fusion(bf16[768,3072]{1,0:T(8,128)(2,1)} %get-tuple-element.78, bf16[3072,3072]{1,0:T(8,128)(2,1)} %get-tuple-element.79), kind=kOutput, calls=%fused_computation.105 | convolution fusion | flops 14495514624 | bytes 33030144 | tf_op jit(solution)/shard_map/dot_general | solution.py:25
  449.3 106.9 %all_to_all.20 = bf16[8,12,96,256]{3,2,1,0:T(8,128)(2,1)S(1)} all-to-all(bf16[8,12,96,256]{3,2,1,0:T(8,128)(2,1)} %get-tuple-element.59), channel_id=1, replica_groups=mesh['z'=4,'y'=2,'j'=1,'t'=4] {'t','y','j'}, dimensions={0} | all-to-all | bytes 9437184 | tf_op jit(solution)/shard_map/all_to_all | solution.py:448
  556.2 17.2 %spectrum_back.1.freq = f32[2,96,96,128]{3,2,1,0:T(8,128)} custom-call(bf16[96,96,256]{2,1,0:T(8,128)(2,1)S(1)} %bitcast.217, bf16[256,256]{1,0:T(8,128)(2,1)S(1)} %copy-done.22, bf16[256,256]{1,0:T(8,128)(2,1)S(1)} %copy-done.23, bf16[192,192]{1,0:T(8,128)(2,1)S(1)} %copy-done.17, bf16[192,192]{1,0:T(8,128)(2,1)S(1)} %copy-done.19), custom_call_target="tpu_custom_call" | custom-call | tf_op jit(solution)/shard_map/spectrum_back/pallas_call | solution.py:304
  573.4 22.3 %filter_back.1 = (f32[2,96,96,128]{3,2,1,0:T(8,128)}, f32[192,192]{1,0:T(8,128)S(1)}, f32[192,192]{1,0:T(8,128)S(1)}, f32[192,128]{1,0:T(8,128)S(1)}, f32[192,128]{1,0:T(8,128)S(1)}) custom-call(f32[2,96,96,128]{3,2,1,0:T(8,128)} %spectrum_back.1.freq, bf16[2,96,96,128]{3,2,1,0:T(8,128)(2,1)S(1)} %bitcast.216, bf16[2,96,96,128]{3,2,1,0:T(8,128)(2,1)} %copy-done.7, ...), custom_call_target="tpu_custom_call" | custom-call | tf_op jit(solution)/shard_map/filter_back/pallas_call | solution.py:304
  596.7 22.4 %last.1 = (bf16[96,96,256]{2,1,0:T(8,128)(2,1)}, f32[96,1,256]{2,1,0:T(1,128)}, f32[96,1,256]{2,1,0:T(1,128)}, f32[96,128]{1,0:T(8,128)}, f32[96,128]{1,0:T(8,128)}) custom-call(s32[8]{0:T(128)} %copy-done.26, bf16[12,96,256]{2,1,0:T(8,128)(2,1)} %copy-done.1, bf16[12,96,256]{2,1,0:T(8,128)(2,1)} %copy-done.2, bf16[12,96,256]{2,1,0:T(8,128)(2,1)} %copy-done.3, ...), custom_call_target="tpu_custom_call" | custom-call | tf_op jit(solution)/shard_map/last/pallas_call | solution.py:304
  619.2 1.8 pad_maximum_fusion
  621.0 5.1 all-to-all-start.3
  626.8 8.1 dynamic_update_slice.7
  636.7 3.1 copy.167
  640.1 3.7 convert_bitcast_fusion
  643.8 10.1 copy.148
  653.9 18.1 %copy.194 = f32[96,8,12,256]{3,1,2,0:T(8,128)} copy(f32[96,8,12,256]{3,2,1,0:T(8,128)} %bitcast.220) | data formatting | bytes 18874368
  672.0 20.6 %fusion.3 = bf16[768,3072]{1,0:T(8,128)(2,1)S(1)} fusion(f32[768,3072]{1,0:T(8,128)} %bitcast.226, bf16[3072,3072]{1,0:T(8,128)(2,1)} %get-tuple-element.58, bf16[3072,768]{1,0:T(8,128)(2,1)} %all-gather.7.cloned.1.call-done.refs_6_, f32[768]{0:T(1024)S(1)} %copy-done.42), kind=kOutput, calls=%fused_computation.6 | convolution fusion | flops 14502592512 | bytes 37751808 | tf_op jit(solution)/shard_map/dot_general | solution.py:25
  692.6 2.3 dynamic-slice_bitcast_fusion
  694.9 1.9 collective-permute-start.11
  697.4 4.0 collective-permute-start.13
  701.8 1.5 copy.150.refs_9_
  703.2 1.5 copy.151.refs_10_
  710.7 2.5 reduce_sum.141
  718.4 1.9 constant_dynamic-update-slice_fusion
  720.3 4.5 collective-permute-done.11.p0
  724.8 25.3 %collective-permute-done.12.p1 = bf16[192,3072]{1,0:T(8,128)(2,1)S(1)} collective-permute-done((bf16[192,3072]{1,0:T(8,128)(2,1)}, bf16[192,3072]{1,0:T(8,128)(2,1)S(1)}, u32[]{:S(2)}, u32[]{:S(2)}) %collective-permute-start.12) | collective-permute-done | bytes 1179680 | tf_op jit(solution)/shard_map/ppermute | solution.py:478
  750.1 149.5 %collective-permute-done.13.p2 = bf16[192,3072]{1,0:T(8,128)(2,1)S(1)} collective-permute-done((bf16[192,3072]{1,0:T(8,128)(2,1)}, bf16[192,3072]{1,0:T(8,128)(2,1)S(1)}, u32[]{:S(2)}, u32[]{:S(2)}) %collective-permute-start.13) | collective-permute-done | bytes 1179680 | tf_op jit(solution)/shard_map/ppermute | solution.py:478
  899.6 21.8 %widen.1 = f32[4,12,192,256]{3,2,1,0:T(8,128)} custom-call(s32[4]{0:T(128)S(1)} %pad_add_fusion.slot, bf16[192,3072]{1,0:T(8,128)(2,1)S(1)} %collective-permute-done.11.p0, bf16[192,3072]{1,0:T(8,128)(2,1)S(1)} %collective-permute-done.12.p1, bf16[192,3072]{1,0:T(8,128)(2,1)S(1)} %collective-permute-done.13.p2, bf16[192,3072]{1,0:T(8,128)(2,1)} %collective-permute-done.14.p3), custom_call_target="tpu_custom_call" | custom-call | tf_op jit(solution)/shard_map/widen/pallas_call | solution.py:304
  923.3 4.4 dynamic-slice_bitcast_fusion.8
  928.2 1.5 collective-permute-start.16
  930.0 84.4 %all-reduce.1 = (f32[2,768]{1,0:T(2,128)S(1)}, f32[5377]{0:T(1024)S(1)}) all-reduce(f32[2,768]{1,0:T(2,128)S(1)} %dynamic_update_slice.6, f32[5377]{0:T(1024)S(1)} %copy-done.38), channel_id=1, replica_groups=mesh['z'=4,'y'=2,'j'=1,'t'=4] {'z','y','j','t'}, use_global_device_ids=true, to_apply=%region_8.9 | all-reduce | flops 6913 | bytes 55304 | tf_op jit(solution)/shard_map/psum | solution.py:550
  1015.6 1.9 collective-permute-start.18
  1017.4 1.7 collective-permute-start.19
  1023.5 1.5 collective-permute-start.21
  1030.7 8.9 collective-permute-done.17.refs_3_
  1039.6 42.5 %collective-permute-done.18.refs_4_ = bf16[12,96,256]{2,1,0:T(8,128)(2,1)S(1)} collective-permute-done((bf16[12,96,256]{2,1,0:T(8,128)(2,1)}, bf16[12,96,256]{2,1,0:T(8,128)(2,1)S(1)}, u32[]{:S(2)}, u32[]{:S(2)}) %collective-permute-start.18) | collective-permute-done | bytes 589856 | tf_op jit(solution)/shard_map/ppermute | solution.py:505
  1082.1 12.6 %collective-permute-done.19.refs_5_ = bf16[12,96,256]{2,1,0:T(8,128)(2,1)S(1)} collective-permute-done((bf16[12,96,256]{2,1,0:T(8,128)(2,1)}, bf16[12,96,256]{2,1,0:T(8,128)(2,1)S(1)}, u32[]{:S(2)}, u32[]{:S(2)}) %collective-permute-start.19) | collective-permute-done | bytes 589856 | tf_op jit(solution)/shard_map/ppermute | solution.py:505
  1094.7 13.9 %collective-permute-done.20.refs_6_ = bf16[12,96,256]{2,1,0:T(8,128)(2,1)} collective-permute-done((bf16[12,96,256]{2,1,0:T(8,128)(2,1)}, bf16[12,96,256]{2,1,0:T(8,128)(2,1)}, u32[]{:S(2)}, u32[]{:S(2)}) %collective-permute-start.20) | collective-permute-done | bytes 589856 | tf_op jit(solution)/shard_map/ppermute | solution.py:505
  1108.6 11.6 %collective-permute-done.21.refs_7_ = bf16[12,96,256]{2,1,0:T(8,128)(2,1)} collective-permute-done((bf16[12,96,256]{2,1,0:T(8,128)(2,1)}, bf16[12,96,256]{2,1,0:T(8,128)(2,1)}, u32[]{:S(2)}, u32[]{:S(2)}) %collective-permute-start.21) | collective-permute-done | bytes 589856 | tf_op jit(solution)/shard_map/ppermute | solution.py:505
  1121.9 10.5 finish.1
  (229 shorter events, 59.4 us)
Async XLA Ops:
  7.2 301.8 %all-gather.9.cloned.1.call-start = ((), (), s32[]{:S(2)}) async-start(), calls=%async_computation.13 | async-start | bytes 5898240 | tf_op jit(solution)/shard_map/all_gather | solution.py:454
  7.9 307.8 %all-gather.7.cloned.1.call-start = ((), (), s32[]{:S(2)}) async-start(), calls=%async_computation.8 | async-start | bytes 5898240 | tf_op jit(solution)/shard_map/all_gather | solution.py:455
  12.7 112.4 %copy-start.1 = (bf16[12,96,256]{2,1,0:T(8,128)(2,1)}, bf16[12,96,256]{2,1,0:T(8,128)(2,1)S(1)}, u32[]{:S(2)}) copy-start(bf16[12,96,256]{2,1,0:T(8,128)(2,1)S(1)} %get-tuple-element.49.refs_0_) | copy-start | bytes 1769476
  12.7 41.4 %collective-permute-start = (bf16[12,96,256]{2,1,0:T(8,128)(2,1)}, bf16[12,96,256]{2,1,0:T(8,128)(2,1)S(1)}, u32[]{:S(2)}, u32[]{:S(2)}) collective-permute-start(bf16[12,96,256]{2,1,0:T(8,128)(2,1)} %get-tuple-element.172), channel_id=1, source_target_pairs={{0,4},{4,0},{8,12},{12,8},{16,20},{20,16},{24,28},{28,24},{1,5},{5... | collective-permute-start | bytes 1769480 | tf_op jit(solution)/shard_map/ppermute | solution.py:347
  13.2 42.4 %collective-permute-start.1 = (bf16[12,96,256]{2,1,0:T(8,128)(2,1)}, bf16[12,96,256]{2,1,0:T(8,128)(2,1)S(1)}, u32[]{:S(2)}, u32[]{:S(2)}) collective-permute-start(bf16[12,96,256]{2,1,0:T(8,128)(2,1)} %get-tuple-element.171), channel_id=1, source_target_pairs={{0,8},{4,12},{8,0},{12,4},{16,24},{20,28},{24,16},{28,20},{1,9},{5... | collective-permute-start | bytes 1769480 | tf_op jit(solution)/shard_map/ppermute | solution.py:347
  13.2 88.2 %collective-permute-start.2 = (bf16[12,96,256]{2,1,0:T(8,128)(2,1)}, bf16[12,96,256]{2,1,0:T(8,128)(2,1)S(1)}, u32[]{:S(2)}, u32[]{:S(2)}) collective-permute-start(bf16[12,96,256]{2,1,0:T(8,128)(2,1)} %get-tuple-element.170), channel_id=1, source_target_pairs={{0,12},{4,8},{8,4},{12,0},{16,28},{20,24},{24,20},{28,16},{1,13},{... | collective-permute-start | bytes 1769480 | tf_op jit(solution)/shard_map/ppermute | solution.py:347
  16.2 85.2 %collective-permute-start.3 = (bf16[12,96,256]{2,1,0:T(8,128)(2,1)}, bf16[12,96,256]{2,1,0:T(8,128)(2,1)S(1)}, u32[]{:S(2)}, u32[]{:S(2)}) collective-permute-start(bf16[12,96,256]{2,1,0:T(8,128)(2,1)} %get-tuple-element.169), channel_id=1, source_target_pairs={{0,16},{4,20},{8,24},{12,28},{16,0},{20,4},{24,8},{28,12},{1,17},{... | collective-permute-start | bytes 1769480 | tf_op jit(solution)/shard_map/ppermute | solution.py:347
  18.8 82.7 %collective-permute-start.4 = (bf16[12,96,256]{2,1,0:T(8,128)(2,1)}, bf16[12,96,256]{2,1,0:T(8,128)(2,1)S(1)}, u32[]{:S(2)}, u32[]{:S(2)}) collective-permute-start(bf16[12,96,256]{2,1,0:T(8,128)(2,1)} %get-tuple-element.168), channel_id=1, source_target_pairs={{0,20},{4,16},{8,28},{12,24},{16,4},{20,0},{24,12},{28,8},{1,21},{... | collective-permute-start | bytes 1769480 | tf_op jit(solution)/shard_map/ppermute | solution.py:347
  23.1 33.0 %copy-start.45 = (f32[192]{0:T(256)S(1)}, f32[192]{0:T(256)}, u32[]{:S(2)}) copy-start(f32[192]{0:T(256)} %param.30) | copy-start | bytes 2308
  23.1 35.7 %copy-start.44 = (f32[2,2,96]{2,1,0:T(2,128)S(1)}, f32[2,2,96]{2,1,0:T(2,128)}, u32[]{:S(2)}) copy-start(f32[2,2,96]{2,1,0:T(2,128)} %param.32) | copy-start | bytes 4612
  38.2 61.9 %all-to-all-start = ((f32[8,12,2,256]{3,2,1,0:T(2,128)}), f32[8,12,2,256]{3,2,1,0:T(2,128)}, u32[]{:S(2)}, u32[]{:S(2)}) async-start(f32[8,12,2,256]{3,2,1,0:T(2,128)} %bitcast.230), calls=%async_computation | async-start | bytes 393216 | tf_op jit(solution)/shard_map/all_to_all | solution.py:377
  54.1 96.9 %copy-start.2 = (bf16[12,96,256]{2,1,0:T(8,128)(2,1)}, bf16[12,96,256]{2,1,0:T(8,128)(2,1)S(1)}, u32[]{:S(2)}) copy-start(bf16[12,96,256]{2,1,0:T(8,128)(2,1)S(1)} %collective-permute-done.refs_1_) | copy-start | bytes 1769476
  54.1 58.8 %collective-permute-start.5 = (bf16[12,96,256]{2,1,0:T(8,128)(2,1)}, bf16[12,96,256]{2,1,0:T(8,128)(2,1)}, u32[]{:S(2)}, u32[]{:S(2)}) collective-permute-start(bf16[12,96,256]{2,1,0:T(8,128)(2,1)} %get-tuple-element.167), channel_id=1, source_target_pairs={{0,24},{4,28},{8,16},{12,20},{16,8},{20,12},{24,0},{28,4},{1,25},{... | collective-permute-start | bytes 1769480 | tf_op jit(solution)/shard_map/ppermute | solution.py:347
  55.6 95.4 %copy-start.3 = (bf16[12,96,256]{2,1,0:T(8,128)(2,1)}, bf16[12,96,256]{2,1,0:T(8,128)(2,1)S(1)}, u32[]{:S(2)}) copy-start(bf16[12,96,256]{2,1,0:T(8,128)(2,1)S(1)} %collective-permute-done.1.refs_2_) | copy-start | bytes 1769476
  55.6 68.0 %collective-permute-start.6 = (bf16[12,96,256]{2,1,0:T(8,128)(2,1)}, bf16[12,96,256]{2,1,0:T(8,128)(2,1)}, u32[]{:S(2)}, u32[]{:S(2)}) collective-permute-start(bf16[12,96,256]{2,1,0:T(8,128)(2,1)} %get-tuple-element.166), channel_id=1, source_target_pairs={{0,28},{4,24},{8,20},{12,16},{16,12},{20,8},{24,4},{28,0},{1,29},{... | collective-permute-start | bytes 1769480 | tf_op jit(solution)/shard_map/ppermute | solution.py:347
  57.4 93.6 %copy-start.39 = (f32[96]{0:T(128)}, f32[96]{0:T(128)S(1)}, u32[]{:S(2)}) copy-start(f32[96]{0:T(128)S(1)} %get-tuple-element.149) | copy-start | bytes 1156
  59.8 91.2 %copy-start.26 = (s32[8]{0:T(128)}, s32[8]{0:T(128)S(1)}, u32[]{:S(2)}) copy-start(s32[8]{0:T(128)S(1)} %stack.130.place) | copy-start | bytes 100
  101.4 49.7 %copy-start.9 = (f32[96,1,256]{2,1,0:T(1,128)}, f32[96,1,256]{2,1,0:T(1,128)S(1)}, u32[]{:S(2)}) copy-start(f32[96,1,256]{2,1,0:T(1,128)S(1)} %get-tuple-element.185.refs_9_) | copy-start | bytes 294916
  101.4 49.7 %copy-start.10 = (f32[96,1,256]{2,1,0:T(1,128)}, f32[96,1,256]{2,1,0:T(1,128)S(1)}, u32[]{:S(2)}) copy-start(f32[96,1,256]{2,1,0:T(1,128)S(1)} %get-tuple-element.186.refs_8_) | copy-start | bytes 294916
  101.4 49.6 %copy-start.4 = (bf16[12,96,256]{2,1,0:T(8,128)(2,1)}, bf16[12,96,256]{2,1,0:T(8,128)(2,1)S(1)}, u32[]{:S(2)}) copy-start(bf16[12,96,256]{2,1,0:T(8,128)(2,1)S(1)} %collective-permute-done.2.refs_3_) | copy-start | bytes 1769476
  101.4 49.6 %copy-start.5 = (bf16[12,96,256]{2,1,0:T(8,128)(2,1)}, bf16[12,96,256]{2,1,0:T(8,128)(2,1)S(1)}, u32[]{:S(2)}) copy-start(bf16[12,96,256]{2,1,0:T(8,128)(2,1)S(1)} %collective-permute-done.3.refs_4_) | copy-start | bytes 1769476
  101.4 49.6 %copy-start.6 = (bf16[12,96,256]{2,1,0:T(8,128)(2,1)}, bf16[12,96,256]{2,1,0:T(8,128)(2,1)S(1)}, u32[]{:S(2)}) copy-start(bf16[12,96,256]{2,1,0:T(8,128)(2,1)S(1)} %collective-permute-done.4.refs_5_) | copy-start | bytes 1769476
  124.3 26.8 %copy-start.8 = (f32[96,256]{1,0:T(8,128)}, f32[96,256]{1,0:T(8,128)S(1)}, u32[]{:S(2)}) copy-start(f32[96,256]{1,0:T(8,128)S(1)} %broadcast_in_dim.33.refs_10_) | copy-start | bytes 294916
  125.1 26.0 %copy-start.11 = (f32[96,256]{1,0:T(8,128)}, f32[96,256]{1,0:T(8,128)S(1)}, u32[]{:S(2)}) copy-start(f32[96,256]{1,0:T(8,128)S(1)} %broadcast_in_dim.68.refs_11_) | copy-start | bytes 294916
  128.7 22.6 %copy-start.12 = (bf16[192,192]{1,0:T(8,128)(2,1)S(1)}, bf16[192,192]{1,0:T(8,128)(2,1)}, u32[]{:S(2)}) copy-start(bf16[192,192]{1,0:T(8,128)(2,1)} %maximum_maximum_fusion.w1) | copy-start | bytes 221188
  128.7 22.6 %copy-start.14 = (bf16[192,192]{1,0:T(8,128)(2,1)S(1)}, bf16[192,192]{1,0:T(8,128)(2,1)}, u32[]{:S(2)}) copy-start(bf16[192,192]{1,0:T(8,128)(2,1)} %maximum_maximum_fusion.1.w2) | copy-start | bytes 221188
  188.3 127.4 %all-to-all-start.1 = ((bf16[8,12,96,256]{3,2,1,0:T(8,128)(2,1)}), bf16[8,12,96,256]{3,2,1,0:T(8,128)(2,1)}, u32[]{:S(2)}, u32[]{:S(2)}) async-start(bf16[8,12,96,256]{3,2,1,0:T(8,128)(2,1)} %bitcast.223), calls=%async_computation.1 | async-start | bytes 9437184 | tf_op jit(solution)/shard_map/all_to_all | solution.py:448
  194.0 442.7 %reduce-scatter.12.cloned.1.call-start = ((), (), s32[]{:S(2)}) async-start(), calls=%async_computation.12 | async-start | bytes 11796480 | tf_op jit(solution)/shard_map/reduce_scatter | solution.py:528
  194.0 106.8 %copy-start.41 = (f32[768]{0:T(1024)S(1)}, f32[768]{0:T(1024)}, u32[]{:S(2)}) copy-start(f32[768]{0:T(1024)} %param.38) | copy-start | bytes 9220
  198.6 117.0 %collective-permute-start.10 = (bf16[12,192,256]{2,1,0:T(8,128)(2,1)}, bf16[12,192,256]{2,1,0:T(8,128)(2,1)S(1)}, u32[]{:S(2)}, u32[]{:S(2)}) collective-permute-start(bf16[12,192,256]{2,1,0:T(8,128)(2,1)} %get-tuple-element.162), channel_id=1, source_target_pairs={{0,24},{1,0},{2,8},{3,16},{4,28},{5,4},{6,12},{7,20},{8,25},{9,1},... | collective-permute-start | bytes 3538952 | tf_op jit(solution)/shard_map/ppermute | solution.py:366
  198.6 117.0 %collective-permute-start.7 = (bf16[12,192,256]{2,1,0:T(8,128)(2,1)}, bf16[12,192,256]{2,1,0:T(8,128)(2,1)S(1)}, u32[]{:S(2)}, u32[]{:S(2)}) collective-permute-start(bf16[12,192,256]{2,1,0:T(8,128)(2,1)} %get-tuple-element.165), channel_id=1, source_target_pairs={{0,0},{1,8},{2,16},{3,24},{4,4},{5,12},{6,20},{7,28},{8,1},{9,9},{... | collective-permute-start | bytes 3538952 | tf_op jit(solution)/shard_map/ppermute | solution.py:366
  200.5 115.1 %collective-permute-start.8 = (bf16[12,192,256]{2,1,0:T(8,128)(2,1)}, bf16[12,192,256]{2,1,0:T(8,128)(2,1)S(1)}, u32[]{:S(2)}, u32[]{:S(2)}) collective-permute-start(bf16[12,192,256]{2,1,0:T(8,128)(2,1)} %get-tuple-element.164), channel_id=1, source_target_pairs={{0,8},{1,16},{2,24},{3,0},{4,12},{5,20},{6,28},{7,4},{8,9},{9,17},... | collective-permute-start | bytes 3538952 | tf_op jit(solution)/shard_map/ppermute | solution.py:366
  200.7 115.0 %collective-permute-start.9 = (bf16[12,192,256]{2,1,0:T(8,128)(2,1)}, bf16[12,192,256]{2,1,0:T(8,128)(2,1)}, u32[]{:S(2)}, u32[]{:S(2)}) collective-permute-start(bf16[12,192,256]{2,1,0:T(8,128)(2,1)} %get-tuple-element.163), channel_id=1, source_target_pairs={{0,16},{1,24},{2,0},{3,8},{4,20},{5,28},{6,4},{7,12},{8,17},{9,25}... | collective-permute-start | bytes 3538952 | tf_op jit(solution)/shard_map/ppermute | solution.py:366
  427.7 244.2 %reduce-scatter.8.cloned.1.call-start = ((), (), s32[]{:S(2)}) async-start(), calls=%async_computation.10 | async-start | bytes 11796480 | tf_op jit(solution)/shard_map/reduce_scatter | solution.py:528
  449.2 106.9 %copy-start.17 = (bf16[192,192]{1,0:T(8,128)(2,1)S(1)}, bf16[192,192]{1,0:T(8,128)(2,1)}, u32[]{:S(2)}) copy-start(bf16[192,192]{1,0:T(8,128)(2,1)} %constant.307.clone.refs_14_.lat_hi) | copy-start | bytes 221188
  449.2 106.9 %copy-start.19 = (bf16[192,192]{1,0:T(8,128)(2,1)S(1)}, bf16[192,192]{1,0:T(8,128)(2,1)}, u32[]{:S(2)}) copy-start(bf16[192,192]{1,0:T(8,128)(2,1)} %constant.308.clone.refs_15_.lat_lo) | copy-start | bytes 221188
  449.2 106.9 %copy-start.22 = (bf16[256,256]{1,0:T(8,128)(2,1)S(1)}, bf16[256,256]{1,0:T(8,128)(2,1)}, u32[]{:S(2)}) copy-start(bf16[256,256]{1,0:T(8,128)(2,1)} %constant.301.clone.hi) | copy-start | bytes 393220
  449.2 106.9 %copy-start.23 = (bf16[256,256]{1,0:T(8,128)(2,1)S(1)}, bf16[256,256]{1,0:T(8,128)(2,1)}, u32[]{:S(2)}) copy-start(bf16[256,256]{1,0:T(8,128)(2,1)} %constant.302.clone.lo) | copy-start | bytes 393220
  449.3 124.1 %slice-start = ((s8[4718592]{0:T(1024)(128)(4,1)}), s8[4194304]{0:T(1024)(128)(4,1)S(1)}, s32[]{:S(2)}) async-start(s8[4718592]{0:T(1024)(128)(4,1)} %bitcast.215), calls=%async_computation.16 | async-start | bytes 8388608
  556.1 17.2 %copy-start = (bf16[8,12,96,256]{3,2,1,0:T(8,128)(2,1)}, bf16[8,12,96,256]{3,2,1,0:T(8,128)(2,1)S(1)}, u32[]{:S(2)}) copy-start(bf16[8,12,96,256]{3,2,1,0:T(8,128)(2,1)S(1)} %all_to_all.20) | copy-start | bytes 14155780
  556.1 17.2 %slice-start.1 = ((s8[4718592]{0:T(1024)(128)(4,1)}), s8[524288]{0:T(1024)(128)(4,1)S(1)}, s32[]{:S(2)}) async-start(s8[4718592]{0:T(1024)(128)(4,1)} %bitcast.215), calls=%async_computation.17 | async-start | bytes 1048576
  556.2 17.2 %copy-start.13 = (bf16[192,192]{1,0:T(8,128)(2,1)S(1)}, bf16[192,192]{1,0:T(8,128)(2,1)}, u32[]{:S(2)}) copy-start(bf16[192,192]{1,0:T(8,128)(2,1)} %maximum_maximum_fusion.w1) | copy-start | bytes 221188
  556.2 17.2 %copy-start.15 = (bf16[192,192]{1,0:T(8,128)(2,1)S(1)}, bf16[192,192]{1,0:T(8,128)(2,1)}, u32[]{:S(2)}) copy-start(bf16[192,192]{1,0:T(8,128)(2,1)} %maximum_maximum_fusion.1.w2) | copy-start | bytes 221188
  621.0 14.8 %all-to-all-start.3 = ((f32[8,2,12,256]{3,1,2,0:T(2,128)}), f32[8,2,12,256]{3,1,2,0:T(2,128)S(1)}, u32[]{:S(2)}, u32[]{:S(2)}) async-start(f32[8,2,12,256]{3,1,2,0:T(2,128)} %pad_maximum_fusion), calls=%async_computation.3 | async-start | bytes 393216 | tf_op jit(solution)/shard_map/all_to_all | solution.py:507
  626.1 395.7 %all-reduce.7.cloned.1.call-start = ((), (), s32[]{:S(2)}) async-start(), calls=%async_computation.15 | async-start | bytes 786432
  635.7 394.2 %all-reduce.5.cloned.1.call-start = ((), (), s32[]{:S(2)}) async-start(), calls=%async_computation.9 | async-start | bytes 196608 | tf_op jit(solution)/shard_map/psum | solution.py:508
  636.6 495.8 %reduce-scatter.14.cloned.1.call-start = ((), (), s32[]{:S(2)}) async-start(), calls=%async_computation.14 | async-start | bytes 2654208
  639.8 492.6 %reduce-scatter.10.cloned.1.call-start = ((), (), s32[]{:S(2)}) async-start(), calls=%async_computation.11 | async-start | bytes 2654208 | tf_op jit(solution)/shard_map/reduce_scatter | solution.py:529
  653.9 18.1 %copy-start.42 = (f32[768]{0:T(1024)S(1)}, f32[768]{0:T(1024)}, u32[]{:S(2)}) copy-start(f32[768]{0:T(1024)} %get-tuple-element.141) | copy-start | bytes 9220
  692.6 12.1 %copy-start.46 = (u32[32]{0:T(128)S(1)}, u32[32]{0:T(128)}, u32[]{:S(2)}) copy-start(u32[32]{0:T(128)} %constant.319) | copy-start | bytes 388
  692.6 13.4 %copy-start.27 = (s32[8]{0:T(128)S(1)}, s32[8]{0:T(128)}, u32[]{:S(2)}) copy-start(s32[8]{0:T(128)} %copy-done.26) | copy-start | bytes 100
  694.9 29.9 %collective-permute-start.11 = (bf16[192,3072]{1,0:T(8,128)(2,1)}, bf16[192,3072]{1,0:T(8,128)(2,1)S(1)}, u32[]{:S(2)}, u32[]{:S(2)}) collective-permute-start(bf16[192,3072]{1,0:T(8,128)(2,1)} %get-tuple-element.161), channel_id=1, source_target_pairs={{0,0},{8,1},{16,2},{24,3},{4,4},{12,5},{20,6},{28,7},{1,8},{9,9},{... | collective-permute-start | bytes 3538952 | tf_op jit(solution)/shard_map/ppermute | solution.py:478
  696.8 53.3 %collective-permute-start.12 = (bf16[192,3072]{1,0:T(8,128)(2,1)}, bf16[192,3072]{1,0:T(8,128)(2,1)S(1)}, u32[]{:S(2)}, u32[]{:S(2)}) collective-permute-start(bf16[192,3072]{1,0:T(8,128)(2,1)} %get-tuple-element.160), channel_id=1, source_target_pairs={{8,0},{16,1},{24,2},{0,3},{12,4},{20,5},{28,6},{4,7},{9,8},{17,9},... | collective-permute-start | bytes 3538952 | tf_op jit(solution)/shard_map/ppermute | solution.py:478
  697.4 202.2 %collective-permute-start.13 = (bf16[192,3072]{1,0:T(8,128)(2,1)}, bf16[192,3072]{1,0:T(8,128)(2,1)S(1)}, u32[]{:S(2)}, u32[]{:S(2)}) collective-permute-start(bf16[192,3072]{1,0:T(8,128)(2,1)} %get-tuple-element.159), channel_id=1, source_target_pairs={{16,0},{24,1},{0,2},{8,3},{20,4},{28,5},{4,6},{12,7},{17,8},{25,9}... | collective-permute-start | bytes 3538952 | tf_op jit(solution)/shard_map/ppermute | solution.py:478
  701.3 198.2 %collective-permute-start.14 = (bf16[192,3072]{1,0:T(8,128)(2,1)}, bf16[192,3072]{1,0:T(8,128)(2,1)}, u32[]{:S(2)}, u32[]{:S(2)}) collective-permute-start(bf16[192,3072]{1,0:T(8,128)(2,1)} %get-tuple-element.158), channel_id=1, source_target_pairs={{24,0},{0,1},{8,2},{16,3},{28,4},{4,5},{12,6},{20,7},{25,8},{1,9},... | collective-permute-start | bytes 3538952 | tf_op jit(solution)/shard_map/ppermute | solution.py:478
  923.3 197.0 %copy-start.28 = (s32[8]{0:T(128)S(1)}, s32[8]{0:T(128)}, u32[]{:S(2)}) copy-start(s32[8]{0:T(128)} %get-tuple-element.204.part) | copy-start | bytes 100
  923.3 197.0 %copy-start.29 = (s32[8]{0:T(128)S(1)}, s32[8]{0:T(128)}, u32[]{:S(2)}) copy-start(s32[8]{0:T(128)} %get-tuple-element.205.snap) | copy-start | bytes 100
  927.7 94.9 %collective-permute-start.15 = (bf16[12,96,256]{2,1,0:T(8,128)(2,1)}, bf16[12,96,256]{2,1,0:T(8,128)(2,1)S(1)}, u32[]{:S(2)}, u32[]{:S(2)}) collective-permute-start(bf16[12,96,256]{2,1,0:T(8,128)(2,1)} %get-tuple-element.156), channel_id=1, source_target_pairs={{0,4},{4,0},{8,12},{12,8},{16,20},{20,16},{24,28},{28,24},{1,5},{5... | collective-permute-start | bytes 1769480 | tf_op jit(solution)/shard_map/ppermute | solution.py:505
  928.2 95.3 %collective-permute-start.16 = (bf16[12,96,256]{2,1,0:T(8,128)(2,1)}, bf16[12,96,256]{2,1,0:T(8,128)(2,1)S(1)}, u32[]{:S(2)}, u32[]{:S(2)}) collective-permute-start(bf16[12,96,256]{2,1,0:T(8,128)(2,1)} %get-tuple-element.155), channel_id=1, source_target_pairs={{0,8},{4,12},{8,0},{12,4},{16,24},{20,28},{24,16},{28,20},{1,9},{5... | collective-permute-start | bytes 1769480 | tf_op jit(solution)/shard_map/ppermute | solution.py:505
  1015.6 24.1 %collective-permute-start.17 = (bf16[12,96,256]{2,1,0:T(8,128)(2,1)}, bf16[12,96,256]{2,1,0:T(8,128)(2,1)S(1)}, u32[]{:S(2)}, u32[]{:S(2)}) collective-permute-start(bf16[12,96,256]{2,1,0:T(8,128)(2,1)} %get-tuple-element.154), channel_id=1, source_target_pairs={{0,12},{4,8},{8,4},{12,0},{16,28},{20,24},{24,20},{28,16},{1,13},{... | collective-permute-start | bytes 1769480 | tf_op jit(solution)/shard_map/ppermute | solution.py:505
  1015.6 66.5 %collective-permute-start.18 = (bf16[12,96,256]{2,1,0:T(8,128)(2,1)}, bf16[12,96,256]{2,1,0:T(8,128)(2,1)S(1)}, u32[]{:S(2)}, u32[]{:S(2)}) collective-permute-start(bf16[12,96,256]{2,1,0:T(8,128)(2,1)} %get-tuple-element.153), channel_id=1, source_target_pairs={{0,16},{4,20},{8,24},{12,28},{16,0},{20,4},{24,8},{28,12},{1,17},{... | collective-permute-start | bytes 1769480 | tf_op jit(solution)/shard_map/ppermute | solution.py:505
  1017.4 77.3 %collective-permute-start.19 = (bf16[12,96,256]{2,1,0:T(8,128)(2,1)}, bf16[12,96,256]{2,1,0:T(8,128)(2,1)S(1)}, u32[]{:S(2)}, u32[]{:S(2)}) collective-permute-start(bf16[12,96,256]{2,1,0:T(8,128)(2,1)} %get-tuple-element.152), channel_id=1, source_target_pairs={{0,20},{4,16},{8,28},{12,24},{16,4},{20,0},{24,12},{28,8},{1,21},{... | collective-permute-start | bytes 1769480 | tf_op jit(solution)/shard_map/ppermute | solution.py:505
  1022.6 86.0 %collective-permute-start.20 = (bf16[12,96,256]{2,1,0:T(8,128)(2,1)}, bf16[12,96,256]{2,1,0:T(8,128)(2,1)}, u32[]{:S(2)}, u32[]{:S(2)}) collective-permute-start(bf16[12,96,256]{2,1,0:T(8,128)(2,1)} %get-tuple-element.151), channel_id=1, source_target_pairs={{0,24},{4,28},{8,16},{12,20},{16,8},{20,12},{24,0},{28,4},{1,25},{... | collective-permute-start | bytes 1769480 | tf_op jit(solution)/shard_map/ppermute | solution.py:505
  1023.5 96.8 %collective-permute-start.21 = (bf16[12,96,256]{2,1,0:T(8,128)(2,1)}, bf16[12,96,256]{2,1,0:T(8,128)(2,1)}, u32[]{:S(2)}, u32[]{:S(2)}) collective-permute-start(bf16[12,96,256]{2,1,0:T(8,128)(2,1)} %get-tuple-element.150), channel_id=1, source_target_pairs={{0,28},{4,24},{8,20},{12,16},{16,12},{20,8},{24,4},{28,0},{1,29},{... | collective-permute-start | bytes 1769480 | tf_op jit(solution)/shard_map/ppermute | solution.py:505
  (18 other events, 51.0 us)
Sparse Core Ops, SparseCore 0:
  9.6 40.6 all-gather.8
  51.8 37.4 all-gather.6
  427.9 128.4 reduce-scatter.11
  558.8 76.5 reduce-scatter.7
  638.6 170.6 all-reduce.6
  811.6 31.1 all-reduce.4
  846.8 77.7 reduce-scatter.13
  928.6 71.1 reduce-scatter.9

commit v2 on v1

--- a/solution.py
+++ b/solution.py
@@ -14,6 +14,7 @@
 NORM_EPS = 1e-05
 BF = jnp.bfloat16
 F32 = jnp.float32
+FLOPS, BYTES = 1_000_000_000, 3_400_000
 NN = (((1,), (0,)), ((), ()))
 NT = (((1,), (1,)), ((), ()))
 TN = (((0,), (0,)), ((), ()))
@@ -123,8 +124,14 @@
     spec[...] = spectra[...].reshape(spec.shape).astype(BF)
 
 
-def spectrum_back_kernel(sgrad, hi, lo, lat_hi, lat_lo, freq, lons, spectra):
-    value = sgrad[...]
+def join_lines(parts):
+    value = jnp.concatenate([part[...] for part in parts], axis=1)
+    return value.reshape(value.shape[0] * value.shape[1], *value.shape[2:])
+
+
+def spectrum_back_kernel(n, *refs):
+    parts, (hi, lo, lat_hi, lat_lo, freq, lons, spectra) = refs[:n], refs[n:]
+    value = join_lines(parts)
     rows, feats, width = value.shape
     if feats % 16:
         value = value.astype(F32).reshape(rows * feats, width).astype(BF)
@@ -182,22 +189,29 @@
 
 
 def section_kernel(n, place, *refs):
-    pieces, (mean, rstd, scale, shift, kept, hi, lo, lat_hi, lat_lo, section, field, lons, spectra) = refs[:n], refs[n:]
+    pieces, (mean, rstd, scale, shift, kept, hi, lo, lat_hi, lat_lo), rest = refs[:n], refs[n : n + 9], refs[n + 9 :]
+    outs, (field, lons, spectra) = rest[:-3], rest[-3:]
     spectra[...] = kept[...].reshape(spectra.shape)
     collect(place, pieces, field)
     value = field[...]
     mixed = (value - mean[...]) * rstd[...] * scale[...] + shift[...]
     spectral = plane_inverse((hi[...], lo[...]), lat_hi[...], lat_lo[...], lons, spectra)
-    section[...] = (value + mixed + spectral.reshape(value.shape)).astype(BF)
-
-
-def last_kernel(n, place, *refs):
-    pieces = refs[:n]
-    mean, rstd, scale, sgrad, freq, hi, lo, lat_hi, lat_lo, out, one, two, gain_sum, shift_sum, field, lons, spectra = refs[n:]
+    section = (value + mixed + spectral.reshape(value.shape)).astype(BF)
+    per = pieces[0].shape[0]
+    section = section.reshape(value.shape[0] // per, per, *value.shape[1:])
+    at = 0
+    for out in outs:
+        out[...] = section[:, at : at + out.shape[1]]
+        at += out.shape[1]
+
+
+def last_kernel(n, m, place, *refs):
+    pieces, sgrad = refs[:n], refs[n : n + m]
+    mean, rstd, scale, freq, hi, lo, lat_hi, lat_lo, out, one, two, gain_sum, shift_sum, field, lons, spectra = refs[n + m :]
     spectra[...] = freq[...].reshape(spectra.shape)
     collect(place, pieces, field)
     normed = (field[...] - mean[...]) * rstd[...]
-    grad = sgrad[...].astype(F32)
+    grad = join_lines(sgrad).astype(F32)
     mixed = grad + plane_inverse((hi[...], lo[...]), lat_hi[...], lat_lo[...], lons, spectra).reshape(grad.shape)
     gain_sum[...] = fold_lanes(jnp.sum(mixed * normed, axis=0))
     shift_sum[...] = fold_lanes(jnp.sum(mixed, axis=0))
@@ -225,8 +239,8 @@
     n, quarter, chunk, place, *refs
 ):
     cots = refs[:n]
-    (section, we_t, wp, we, bias, gain, shift,
-     normal, hidden, pre, cot, sgrad, bias_sum, gain_sum, shift_sum, cot_sum) = refs[n:]
+    section, we_t, wp, we, bias, gain, shift = refs[n : n + 7]
+    normal, hidden, pre, cot, sgrad, bias_sum, gain_sum, shift_sum, cot_sum = refs[-9:]
 
     @pl.when(pl.program_id(0) == 0)
     def _():
@@ -263,6 +277,27 @@
     sgrad[...] = grad.reshape(sgrad.shape).astype(BF)
 
 
+def result_kernel(quarter, n, place, hidden, wp_t, bias, *refs):
+    sections, outs, field = refs[:n], refs[n:-1], refs[-1]
+    value = dot(wp_t[...], hidden[...]) + jnp.concatenate([bias[...]] * (hidden.shape[1] // 128), axis=1)
+    at = 0
+    for section in sections:
+
+        @pl.when((pl.program_id(0) >= at) & (pl.program_id(0) < at + section.shape[1]))
+        def _(section=section, at=at):
+            line = section[:, pl.program_id(0) - at].astype(F32)
+            field[...] = value + line.reshape(value.shape)
+
+        at += section.shape[1]
+    for k, out in enumerate(outs):
+        out[...] = field[pl.ds(place[k] * quarter, quarter), :].astype(BF)
+
+
+def weight_kernel(place, normal, pre, cot, hidden, expand, project):
+    expand[0] = dot(normal[...], pre[...], NT)
+    project[0] = dot(cot[...], hidden[...], NT)
+
+
 def widen_kernel(slot, p0, p1, p2, p3, out):
     for k, piece in enumerate((p0, p1, p2, p3)):
 
@@ -271,15 +306,9 @@
             out[0, 0] = piece[...].astype(F32)
 
 
-def finish_kernel(n, feats, snap, part, *refs):
-    pieces, (patches, mean, rstd, one, two, out) = refs[:n], refs[n:]
+def finish_kernel(feats, grads, patches, mean, rstd, one, two, out):
     normed = (patches[0].astype(F32) - mean[0]) * rstd[0]
-    fix = rstd[0] * (one[0] + normed * two[0]) * (1.0 / feats)
-    for k, piece in enumerate(pieces):
-
-        @pl.when(pl.program_id(0) == k)
-        def _(piece=piece):
-            out[0] = piece[...].astype(F32) - fix
+    out[0] = grads[0].astype(F32) - rstd[0] * (one[0] + normed * two[0]) * (1.0 / feats)
 
 
 def whole(shape):
@@ -290,7 +319,7 @@
     return pl.BlockSpec(shape, lambda *_: (0,) * len(shape))
 
 
-def run(name, kernel, grid, ins, specs, outs, out_specs, scratch, mib, scalars=()):
+def run(name, kernel, grid, ins, specs, outs, out_specs, scratch, mib, micros, scalars=(), aliases=None):
     grid_spec = pltpu.PrefetchScalarGridSpec(
         num_scalar_prefetch=len(scalars), grid=grid, in_specs=specs, out_specs=out_specs, scratch_shapes=scratch
     )
@@ -299,6 +328,8 @@
         grid_spec=grid_spec,
         out_shape=outs,
         compiler_params=pltpu.CompilerParams(vmem_limit_bytes=mib << 20),
+        input_output_aliases=aliases or {},
+        cost_estimate=pl.CostEstimate(flops=int(micros * FLOPS), bytes_accessed=int(micros * BYTES), transcendentals=0),
         name=name,
     )
     return call(*scalars, *ins)
@@ -361,15 +392,30 @@
 
     place = jnp.stack([(z - k) % tp for k in range(tp)]).astype(jnp.int32)
     slot = jnp.stack([(t + k) % tp for k in range(tp)]).astype(jnp.int32)
+    parts = [per // 2, per - per // 2]
     late, pieces = lax.optimization_barrier((cotangent, pieces))
-    cots = [
-        lax.ppermute(lax.dynamic_index_in_dim(late, (t + k) % tp, 0, False), every, route(k, False)) for k in range(tp)
-    ]
+
+    def cot_part(array, start, n):
+        array = lax.slice_in_dim(array, start, start + n, axis=1)
+        return [
+            lax.ppermute(lax.dynamic_index_in_dim(array, (t + k) % tp, 0, False), every, route(k, False))
+            for k in range(tp)
+        ]
+
+    cots = [cot_part(late, 0, parts[0])]
 
     field = patches.astype(F32)
     mean = jnp.mean(field, 2)
     square = jnp.sum(jnp.square(field - mean[:, :, None]), 2)
-    gathered = lax.all_gather(jnp.stack([mean, square]), "t")
+    moments = (2, snaps, per, width)
+    count = math.prod(moments)
+    packed = jnp.concatenate(
+        [jnp.stack([mean, square]).reshape(-1), second_gain, second_shift, project_bias, expand_bias]
+    )
+    packed = lax.all_gather(packed, "t")
+    gathered = packed[:, :count].reshape(tp, *moments)
+    small = [packed[:, count + i * quarter : count + (i + 1) * quarter].reshape(-1) for i in range(3)]
+    bias_all = packed[:, count + 3 * quarter :].reshape(-1)
     mean = jnp.mean(gathered[:, 0], 0)
     square = jnp.sum(gathered[:, 1] + quarter * jnp.square(gathered[:, 0] - mean), 0)
     stats = jnp.stack([mean, lax.rsqrt(square / feats + NORM_EPS)], 2)
@@ -396,6 +442,11 @@
     lat = lat_table(rows)
     plain_t, weighted_t, plain_n, weighted_n = (np_split(a) for a in (plain.T, weighted.T, plain, weighted))
     lat_f, lat_b = np_split(lat), np_split(lat.T)
+
+    we = lax.all_gather(expand_weight, "t")
+    wp = lax.all_gather(project_weight, "t", tiled=True)
+    we_t, wp_t = jnp.swapaxes(we, 1, 2).reshape(hiddens, feats), wp.T
+    gain2, shift2, bias_lanes = lanes(small[0]), lanes(small[1]), lanes(bias_all, 128)
 
     some = 16 if mine % 16 == 0 else mine
     grid = (mine // some,)
@@ -415,7 +466,7 @@
         "spectrum", functools.partial(spectrum_kernel, owners), grid,
         (*pieces, mean_one, rstd_one, scale1, shift1, *plain_t, *lat_f),
         [*piece_specs, stat_spec, stat_spec, feat_spec, feat_spec, *lon_f, *lat_specs],
-        shape(mine_modes, BF), modes_spec, scratch, 48, (origin,),
+        shape(mine_modes, BF), modes_spec, scratch, 48, 22, (origin,),
     )
 
     def to_blocks(array):
@@ -435,124 +486,174 @@
         [block_spec, square_spec, lane_spec, square_spec, lane_spec],
         (shape(block_modes, F32), shape(block_modes, BF), shape(block_modes, F32), shape(block_modes, F32),
          shape((8, 2 * modes), F32)),
-        (block_spec, block_spec, block_spec, block_spec, fixed((8, 2 * modes))), [], 48,
-    )
-    section = run(
+        (block_spec, block_spec, block_spec, block_spec, fixed((8, 2 * modes))), [], 48, 17,
+    )
+    kept, late, cots[0] = lax.optimization_barrier((kept, late, cots[0]))
+    cots.append(cot_part(late, parts[0], parts[1]))
+    part_specs = [pl.BlockSpec((ranks, n, some, width), lambda g, *_: (0, 0, g, 0)) for n in parts]
+    sections = run(
         "section", functools.partial(section_kernel, owners), grid,
         (*pieces, mean_one, rstd_one, scale1, shift1, to_features(kept), *weighted_n, *lat_b),
         [*piece_specs, stat_spec, stat_spec, feat_spec, feat_spec, modes_spec, *lon_b, *lat_specs],
-        shape((rows, mine, width), BF), image_spec, scratch, 56, (origin,),
+        [shape((ranks, n, mine, width), BF) for n in parts], part_specs, scratch, 56, 17, (origin,),
     )
 
     def exchange(array):
-        return lax.all_to_all(array.reshape(ranks, per, mine, width), ("t", "y", "j"), 0, 0, tiled=True)
-
-    section = exchange(section)
-
-    small = lax.all_gather(jnp.stack([second_gain, second_shift, project_bias]), "t", axis=1, tiled=True)
-    bias_all = lax.all_gather(expand_bias, "t", tiled=True)
-    we = lax.all_gather(expand_weight, "t")
-    wp = lax.all_gather(project_weight, "t", tiled=True)
-    we_t = jnp.swapaxes(we, 1, 2).reshape(hiddens, feats)
-    gain2, shift2 = lanes(small[0]), lanes(small[1])
-    tok_spec = pl.BlockSpec((feats, width), lambda h, *_: (0, h))
-    hid_spec = pl.BlockSpec((hiddens, width), lambda h, *_: (0, h))
-    cot_specs = [pl.BlockSpec((1, quarter, width), lambda h, *_: (h, 0, 0))] * tp
-    line_spec = pl.BlockSpec((ranks, 1, mine, width), lambda h, *_: (0, h, 0, 0))
-    normal, hidden, pre, cot, sgrad, bias_sum, gain_sum, shift_sum, cot_sum = run(
-        "feed", functools.partial(feed_kernel, tp, quarter, min(512, hidden_local // 2)), (per,),
-        (*cots, section, we_t, wp, we, lanes(bias_all, 128), gain2, shift2),
-        [*cot_specs, line_spec, whole((hiddens, feats)), whole((hiddens, feats)), whole((tp, feats, hidden_local)),
-         whole((hiddens, 128)), whole((feats, width)), whole((feats, width))],
-        (shape((feats, toks), BF), shape((hiddens, toks), BF), shape((hiddens, toks), BF), shape((feats, toks), BF),
-         shape((ranks, per, mine, width), BF), shape((hiddens, 128), F32), *[shape((feats, 128), F32)] * 3),
-        (tok_spec, hid_spec, hid_spec, tok_spec, line_spec, fixed((hiddens, 128)), *[fixed((feats, 128))] * 3),
-        [], 60, (place,),
-    )
-    sgrad = exchange(sgrad).reshape(rows, mine, width)
-
-    lines = jnp.moveaxis(section, 1, 2).reshape(feats, toks).astype(F32)
-    result = dot(wp, hidden, TN) + lines + small[2][:, None]
-    result = result.astype(BF).reshape(tp, quarter, toks)
-    result = [
-        lax.ppermute(lax.dynamic_index_in_dim(result, place[k], 0, False), every, route(k, True)) for k in range(tp)
-    ]
-    project_grad = dot(hidden, cot, NT)
-    expand_grad = dot(normal, pre, NT)
+        return lax.all_to_all(array, ("t", "y", "j"), 0, 0, tiled=True)
+
+    outs = (
+        shape((feats, toks), BF), shape((hiddens, toks), BF), shape((hiddens, toks), BF), shape((feats, toks), BF),
+    )
+    sum_shapes = [shape((hiddens, 128), F32), *[shape((feats, 128), F32)] * 3]
+    sgrads, sums, done, start = [], [], (), 0
+    received = []
+    for n, section, part_cots in zip(parts, sections, cots):
+        section = exchange(section)
+        tok_spec = pl.BlockSpec((feats, width), lambda h, *_, start=start: (0, h + start))
+        hid_spec = pl.BlockSpec((hiddens, width), lambda h, *_, start=start: (0, h + start))
+        cot_specs = [pl.BlockSpec((1, quarter, width), lambda h, *_: (h, 0, 0))] * tp
+        line_spec = pl.BlockSpec((ranks, 1, mine, width), lambda h, *_: (0, h, 0, 0))
+        any_spec = pl.BlockSpec(memory_space=pl.ANY)
+        *done, sgrad, s0, s1, s2, s3 = run(
+            "feed", functools.partial(feed_kernel, tp, quarter, min(512, hidden_local // 2)), (n,),
+            (*part_cots, section, we_t, wp, we, bias_lanes, gain2, shift2, *done),
+            [*cot_specs, line_spec, whole((hiddens, feats)), whole((hiddens, feats)),
+             whole((tp, feats, hidden_local)), whole((hiddens, 128)), whole((feats, width)), whole((feats, width)),
+             *[any_spec] * len(done)],
+            (*outs, shape((ranks, n, mine, width), BF), *sum_shapes),
+            (tok_spec, hid_spec, hid_spec, tok_spec, line_spec, fixed((hiddens, 128)), *[fixed((feats, 128))] * 3),
+            [], 60, 43, (place,), {8 + tp + i: i for i in range(len(done))},
+        )
+        sgrads.append(exchange(sgrad))
+        sums.append((s0, s1, s2, s3))
+        received.append(section)
+        start += n
+    normal, hidden, pre, cot = done
+    bias_sum, gain_sum, shift_sum, cot_sum = (a + b for a, b in zip(*sums))
+
+    piece_out = pl.BlockSpec((quarter, width), lambda h, *_: (0, h))
+    result = run(
+        "result", functools.partial(result_kernel, quarter, len(parts)), (per,),
+        (hidden, wp_t, lanes(small[2], 128), *received),
+        [pl.BlockSpec((hiddens, width), lambda h, *_: (0, h)), whole((feats, hiddens)), whole((feats, 128)),
+         *[pl.BlockSpec((ranks, n, mine, width), lambda *_: (0, 0, 0, 0), pipeline_mode=pl.Buffered(1)) for n in parts]],
+        [shape((quarter, toks), BF)] * tp, [piece_out] * tp, [pltpu.VMEM((feats, width), F32)], 48, 22, (place,),
+    )
+    result = [lax.ppermute(result[k], every, route(k, True)) for k in range(tp)]
 
     freq = run(
-        "spectrum_back", spectrum_back_kernel, grid, (sgrad, *weighted_t, *lat_f),
-        [image_spec, *lon_f, *lat_specs], shape(mine_modes, F32), modes_spec, scratch[1:], 48,
+        "spectrum_back", functools.partial(spectrum_back_kernel, len(parts)), grid, (*sgrads, *weighted_t, *lat_f),
+        [*part_specs, *lon_f, *lat_specs], shape(mine_modes, F32), modes_spec, scratch[1:], 48, 17,
     )
     freq, inner_grad, outer_grad, inner_bias_grad, outer_bias_grad = run(
         "filter_back", filter_back_kernel, (lats // step,), (to_blocks(freq), spec, mid, slope, bend, w1, w2),
         [*[block_spec] * 5, square_spec, square_spec],
         (shape(block_modes, F32), *[shape((2 * BLOCK, 2 * BLOCK), F32)] * 2, *[shape((2 * BLOCK, 128), F32)] * 2),
-        (block_spec, *[fixed((2 * BLOCK, 2 * BLOCK))] * 2, *[fixed((2 * BLOCK, 128))] * 2), [], 48,
+        (block_spec, *[fixed((2 * BLOCK, 2 * BLOCK))] * 2, *[fixed((2 * BLOCK, 128))] * 2), [], 48, 24,
     )
     grads, one, two, first_gain_sum, first_shift_sum = run(
-        "last", functools.partial(last_kernel, owners), grid,
-        (*pieces, mean_one, rstd_one, scale1, sgrad, to_features(freq), *plain_n, *lat_b),
-        [*piece_specs, stat_spec, stat_spec, feat_spec, image_spec, modes_spec, *lon_b, *lat_specs],
+        "last", functools.partial(last_kernel, owners, len(parts)), grid,
+        (*pieces, *sgrads, mean_one, rstd_one, scale1, to_features(freq), *plain_n, *lat_b),
+        [*piece_specs, *part_specs, stat_spec, stat_spec, feat_spec, modes_spec, *lon_b, *lat_specs],
         (shape((rows, mine, width), BF), *[shape((rows, 1, width), F32)] * 2, *[shape((mine, 128), F32)] * 2),
         (image_spec, *[fixed((rows, 1, width))] * 2, *[pl.BlockSpec((some, 128), lambda g, *_: (g, 0))] * 2),
-        scratch, 56, (origin,),
-    )
-    grads = grads.reshape(owners, per, mine, width)
-    outs = []
-    for k in range(owners):
-        piece = lax.dynamic_index_in_dim(grads, me ^ k, 0, False)
-        outs.append(lax.ppermute(piece, sp, [(a, a ^ k) for a in range(owners)]) if k else piece)
-    sums = jnp.stack([one.reshape(owners, per, width), two.reshape(owners, per, width)], 1)
-    sums = lax.all_to_all(sums, sp, 0, 0, tiled=True).reshape(planes, inner, 2, per, 1, width)
-    sums = lax.psum(jnp.sum(sums, 1), "t")
-
+        scratch, 56, 22, (origin,),
+    )
+    _, normal, hidden, pre, cot = lax.optimization_barrier((first_gain_sum, normal, hidden, pre, cot))
+    def with_bias(full, bias):
+        bias = jnp.sum(bias, 1).reshape(2, BLOCK)
+        return jnp.concatenate([weight_pair(full), bias[:, :, None]], 2)
+
+    filters = jnp.stack([with_bias(inner_grad, inner_bias_grad), with_bias(outer_grad, outer_bias_grad)])
+    filters = jnp.moveaxis(filters, 2, 0).reshape(owners, -1)
+    early = jnp.concatenate(
+        [jnp.sum(gain_sum, 1), jnp.sum(shift_sum, 1), jnp.sum(cot_sum, 1), jnp.sum(bias_sum, 1), jnp.sum(share)[None]]
+    )
+    line = per * width
+    feature_sums = jnp.stack([jnp.sum(first_gain_sum, 1) * keep, jnp.sum(first_shift_sum, 1) * keep]).reshape(-1)
+    tail = jnp.concatenate(
+        [one.reshape(owners, line), two.reshape(owners, line), filters,
+         jnp.broadcast_to(jnp.concatenate([feature_sums, early]), (owners, 2 * mine + early.shape[0]))], 1
+    )
+    tail = lax.all_to_all(tail, sp, 0, 0, tiled=True)
+    tail, grads = lax.optimization_barrier((tail, grads))
+    grads = lax.all_to_all(grads.reshape(owners, per, mine, width), sp, 0, 0, tiled=True)
+    cuts = [2 * line, 2 * line + filters.shape[1], 2 * line + filters.shape[1] + 2 * mine]
+    lines, filters, feature_sums, early = jnp.split(tail, cuts, axis=1)
+    lines = jnp.sum(lines.reshape(planes, inner, -1), 1).reshape(-1)
+    filters = jnp.sum(filters.reshape(planes, blocks_local, cut, BLOCK // owners, 2, 2, BLOCK + 1), (0, 2))
+    filters = jnp.transpose(filters, (2, 3, 0, 1, 4))
+    feature_sums = jnp.sum(feature_sums.reshape(planes, inner, 2, mine), 0).swapaxes(0, 1).reshape(-1)
+    tail = lax.all_gather(jnp.concatenate([lines, feature_sums, jnp.sum(early, 0)]), "t")
+    cuts = [planes * 2 * line, planes * 2 * line + 2 * quarter]
+    lines, last, early = jnp.split(tail, cuts, axis=1)
+    fixes = jnp.sum(lines, 0).reshape(planes, 2, per, 1, width)
+    last = last.reshape(tp, 2, quarter).swapaxes(0, 1).reshape(2, feats)
+    early = jnp.sum(early, 0)
+
+    order = jnp.stack([t ^ k for k in range(tp)]).astype(jnp.int32)
+    half = hidden_local // 2
+    hid_rows = pl.BlockSpec((half, toks), lambda k, i, o: (o[k] * 2 + i, 0))
+    out_cols = pl.BlockSpec((1, feats, half), lambda k, i, o: (k, 0, i))
+    expand_grad, project_grad = run(
+        "weights", weight_kernel, (tp, 2), (normal, pre, cot, hidden),
+        [whole((feats, toks)), hid_rows, whole((feats, toks)), hid_rows],
+        [shape((tp, feats, hidden_local), F32)] * 2, [out_cols] * 2, [], 60, 44, (order,),
+    )
+
+    expand_grad, *result = lax.optimization_barrier((expand_grad, *result))
     line_specs = [
         pl.BlockSpec((quarter, width), lambda i, h, s, k=k: (0, jnp.where(i == k, h, jnp.where(i < k, 0, per - 1))))
         for k in range(tp)
     ]
     result = run(
         "widen", widen_kernel, (tp, per), result, line_specs, shape((snaps, per, quarter, width), F32),
-        pl.BlockSpec((1, 1, quarter, width), lambda i, h, s: (s[i], h, 0, 0)), [], 32, (slot,),
-    )
-    one_spec = pl.BlockSpec((1, per, 1, width), lambda i, s, b: (s[i], 0, 0, 0))
-    patch_spec = pl.BlockSpec((1, per, mine, width), lambda i, s, b: (s[i], 0, b[i], 0))
+        pl.BlockSpec((1, 1, quarter, width), lambda i, h, s: (s[i], h, 0, 0)), [], 32, 22, (slot,),
+    )
+    one_spec = pl.BlockSpec((1, per, 1, width), lambda i: (i // inner, 0, 0, 0))
+    patch_spec = pl.BlockSpec((1, per, mine, width), lambda i: (i // inner, 0, i % inner, 0))
     patches_grad = run(
-        "finish", functools.partial(finish_kernel, owners, feats), (owners,),
-        (*outs, patches, stats[:, :, 0, None], stats[:, :, 1, None], sums[:, 0], sums[:, 1]),
-        [*[fixed((per, mine, width))] * owners, patch_spec, *[one_spec] * 4],
-        shape((snaps, per, quarter, width), F32), patch_spec, [], 48, (origin // inner, origin % inner),
-    )
-
-    def own(array, dim):
-        array = lax.psum_scatter(array, "t", scatter_dimension=dim[0], tiled=True)
-        return lax.psum_scatter(array, sp, scatter_dimension=dim[1], tiled=True)
-
-    project_sum = own(project_grad, (0, 1))
-    expand_sum = own(expand_grad, (1, 0))
-
-    def with_bias(full, bias):
-        bias = jnp.sum(bias, 1).reshape(2, BLOCK)
-        return jnp.concatenate([weight_pair(full), bias[:, :, None]], 2)
-
-    both = jnp.stack([with_bias(inner_grad, inner_bias_grad), with_bias(outer_grad, outer_bias_grad)])
-    both = jnp.moveaxis(both, 2, 0)[:, :, :, None]
-    both = lax.dynamic_update_slice(
-        jnp.zeros((BLOCK, 2, 2, blocks_local, BLOCK + 1), F32), both, (0, 0, 0, y, 0)
-    )
-    both = lax.psum_scatter(both, sp, scatter_dimension=0, tiled=True)
-    both = jnp.moveaxis(both, 0, 3)
-    early = jnp.concatenate(
-        [jnp.sum(gain_sum, 1), jnp.sum(shift_sum, 1), jnp.sum(cot_sum, 1), jnp.sum(bias_sum, 1), jnp.sum(share)[None]]
-    )
-    early = lax.psum(early, every)
-    last = jnp.stack([jnp.sum(first_gain_sum, 1) * keep, jnp.sum(first_shift_sum, 1) * keep])
-    last = lax.psum(
-        lax.dynamic_update_slice(jnp.zeros((2, feats), F32), last, (0, t * quarter + r * mine)), every
-    )
+        "finish", functools.partial(finish_kernel, feats), (owners,),
+        (grads, patches, stats[:, :, 0, None], stats[:, :, 1, None], fixes[:, 0], fixes[:, 1]),
+        [pl.BlockSpec((1, per, mine, width), lambda i: (i, 0, 0, 0)), patch_spec, *[one_spec] * 4],
+        shape((snaps, per, quarter, width), F32), patch_spec, [], 48, 11,
+    )
+
+    def trade(theirs, axes, bit, size):
+        return lax.ppermute(theirs.astype(BF), axes, [(a, a ^ bit) for a in range(size)]).astype(F32)
+
+    def trade_rows(array, bit):
+        side = (me // bit) % 2
+        array = array.reshape(2, array.shape[0] // 2, *array.shape[1:])
+        theirs = lax.dynamic_index_in_dim(array, 1 - side, 0, False)
+        return lax.dynamic_index_in_dim(array, side, 0, False) + trade(theirs, sp, bit, owners)
+
+    bits = [1 << i for i in range(owners.bit_length() - 1)]
+
+    def total_of(blocks, rows_first):
+        blocks = [block.reshape(owners, feats // owners, hidden_local) for block in blocks]
+        near = [blocks[k] + trade(blocks[k + 1], "t", 1, tp) for k in range(0, tp, 2)]
+        if rows_first:
+            near = [n.reshape(owners // 2, 2, feats // owners, hidden_local).swapaxes(0, 1).reshape(n.shape) for n in near]
+            near = trade_rows(jnp.concatenate(near, 2), bits[0])
+            near = [near[..., i * hidden_local : (i + 1) * hidden_local] for i in range(tp // 2)]
+        step = 1
+        while len(near) > 1:
+            near = [near[i] + trade(near[i + 1], "t", 2 * step, tp) for i in range(0, len(near), 2)]
+            step *= 2
+        total = near[0]
+        if not rows_first:
+            total = total.reshape(owners // 2, 2, feats // owners, hidden_local).swapaxes(0, 1)
+            total = trade_rows(total.reshape(owners, feats // owners, hidden_local), bits[0])
+        for bit in bits[:0:-1]:
+            total = trade_rows(total, bit)
+        return total[0]
+
+    expand_sum = total_of([expand_grad[k] for k in range(tp)], False)
+    project_sum = total_of([project_grad[k] for k in range(tp)], True).T
     return (
-        result, patches_grad, last[0], last[1], both[0, ..., :BLOCK], both[0, ..., BLOCK],
-        both[1, ..., :BLOCK], both[1, ..., BLOCK],
+        result, patches_grad, last[0], last[1], filters[0, ..., :BLOCK], filters[0, ..., BLOCK],
+        filters[1, ..., :BLOCK], filters[1, ..., BLOCK],
         early[:feats], early[feats : 2 * feats], expand_sum, early[3 * feats : 3 * feats + hiddens],
         project_sum, early[2 * feats : 3 * feats], early[-1] / (snaps * rows * modes * feats * 2),
     )

time: 1150 us -> 794 us (0.69)
  the two profiles are of different devices: /device:TPU:12 before, /device:TPU:2 now
where the time goes in v2:
time: 794 us; the launch traced here: 783 us
  Pallas kernels  325 us (41%)
  starting transfers between devices  208 us (26%)
  waiting for transfers between devices  115 us (14%)
  local copies, waits for them, and re-layouts  78 us (10%)
  other arithmetic  38 us (5%)
  between operations  19.4 us (2%)
    pallas_call x12, Pallas kernels, run(): return call(*scalars, *ins)  325 us
    ppermute x12, starting transfers between devices, trade(): lax.ppermute(theirs.astype(BF), axes, [(a, a ^ bit) for a in range(size)])  68 us
    ppermute x8, starting transfers between devices, cot_part(): lax.ppermute(lax.dynamic_index_in_dim(array, (t + k) % tp, 0, False), eve...  48.9 us
    unnamed x6, waiting for transfers between devices  39.2 us
    ppermute x12, waiting for transfers between devices, trade(): lax.ppermute(theirs.astype(BF), axes, [(a, a ^ bit) for a in range(size)])  36.6 us
    all_to_all x1, waiting for transfers between devices, per_device(): lax.all_to_all(sent, sp, 0, 0, tiled=True).reshape(rows, 2, 1, width)  35.2 us
    ppermute x4, starting transfers between devices, per_device(): result = [lax.ppermute(result[k], every, route(k, True)) for k in range(tp)]  30 us
    all_to_all x4, starting transfers between devices, exchange(): return lax.all_to_all(array, ('t', 'y', 'j'), 0, 0, tiled=True)  19.3 us
  transfers between devices with their start and end apart: 42, of which 10 were waited for; matrix products, arithmetic and copies ran while one was open for 12% of the time, Pallas kernels for 40%

profile of v2, /device:TPU:2, one launch (start us, length us, event | category | flops | bytes accessed | tf_op | source)
XLA Modules:
  0.0 782.8 jit_solution(4059612223483449462)
XLA Ops:
  7.2 3.4 convert_reduce_fusion
  11.0 1.9 fusion.1
  17.2 4.4 dynamic-slice_bitcast_fusion.8
  25.2 2.6 collective-permute-start.3
  29.1 2.4 copy.193
  33.2 15.6 %all-reduce.5.cloned.1.call-done = f32[103680]{0:T(1024)} async-done(((f32[103680]{0:T(1024)}), f32[103680]{0:T(1024)}) %all-reduce.5.cloned.1.call-update) | async-done | bytes 414736
  51.0 2.1 reshape.317
  56.7 5.9 all-to-all-start
  62.6 3.9 collective-permute-start.5
  73.4 35.2 %all-to-all-done = f32[8,12,2,256]{3,2,1,0:T(2,128)} async-done(((f32[8,12,2,256]{3,2,1,0:T(2,128)}), f32[8,12,2,256]{3,2,1,0:T(2,128)}, u32[]{:S(2)}, u32[]{:S(2)}) %all-to-all-start) | async-done | bytes 196640 | tf_op jit(solution)/shard_map/all_to_all | solution.py:423
  109.9 2.1 slice-done.3
  112.3 30.8 %collective-permute-start.7 = (bf16[6,192,256]{2,1,0:T(8,128)(2,1)S(1)}, bf16[6,192,256]{2,1,0:T(8,128)(2,1)S(1)}, u32[]{:S(2)}, u32[]{:S(2)}) collective-permute-start(bf16[6,192,256]{2,1,0:T(8,128)(2,1)S(1)} %get-tuple-element.206), channel_id=1, source_target_pairs={{0,0},{1,8},{2,16},{3,24},{4,4},{5,12},{6,20},{7,28},{8,1},{9,9},{... | collective-permute-start | bytes 1769480 | tf_op jit(solution)/shard_map/ppermute | solution.py:401
  143.1 2.6 collective-permute-start.9
  145.7 2.4 collective-permute-start.10
  148.4 22.3 %spectrum.1.spec = bf16[2,96,96,128]{3,2,1,0:T(8,128)(2,1)} custom-call(s32[8]{0:T(128)S(1)} %stack.130.place, bf16[12,96,256]{2,1,0:T(8,128)(2,1)S(1)} %get-tuple-element.82.refs_0_, bf16[12,96,256]{2,1,0:T(8,128)(2,1)S(1)} %collective-permute-done.refs_1_, bf16[12,96,256]{2,1,0:T(8,128)(2,1)S(1)} %collective-permute-done.1.refs_2_, ...), custom_call_target="tpu_custom_call" | custom-call | flops 22000001024 | bytes 74800000 | tf_op jit(solution)/shard_map/spectrum/pallas_call | solution.py:335
  170.9 17.2 %filter.1 = (f32[2,96,96,128]{3,2,1,0:T(8,128)}, bf16[2,96,96,128]{3,2,1,0:T(8,128)(2,1)S(1)}, f32[2,96,96,128]{3,2,1,0:T(8,128)}, f32[2,96,96,128]{3,2,1,0:T(8,128)}, f32[8,256]{1,0:T(8,128)S(1)}) custom-call(bf16[2,96,96,128]{3,2,1,0:T(8,128)(2,1)} %spectrum.1.spec, bf16[192,192]{1,0:T(8,128)(2,1)S(1)} %maximum_maximum_fusion.w1, ...), custom_call_target="tpu_custom_call" | custom-call | flops 16999999488 | bytes 57800000 | tf_op jit(solution)/shard_map/filter/pallas_call | solution.py:335
  188.1 2.1 copy-done.25
  191.4 17.5 %section.1 = (bf16[8,6,96,256]{3,2,1,0:T(8,128)(2,1)}, bf16[8,6,96,256]{3,2,1,0:T(8,128)(2,1)}) custom-call(s32[8]{0:T(128)} %copy-done.10, bf16[12,96,256]{2,1,0:T(8,128)(2,1)} %copy-done.1, bf16[12,96,256]{2,1,0:T(8,128)(2,1)} %copy-done.12, bf16[12,96,256]{2,1,0:T(8,128)(2,1)} %copy-done.13, bf16[12,96,256]{2,1,0:T(8,128)(2,1)} %copy-done.14, ...), custom_call_target="tpu_custom_call" | custom-call | flops 16999999488 | bytes 57800000 | tf_op jit(solution)/shard_map/section/pallas_call | solution.py:335
  208.9 4.5 all-to-all-start.1
  218.0 1.7 slice-done.4
  220.9 2.0 collective-permute-start.11
  223.0 7.3 collective-permute-start.12
  230.2 3.7 collective-permute-start.14
  234.0 6.6 copy.192
  240.6 6.6 copy.194.refs_6_
  247.2 4.2 all-to-all-done.1.refs_4_.refs_0_
  252.8 5.8 all-to-all-start.3
  262.5 47.9 %feed.2 = (bf16[768,3072]{1,0:T(8,128)(2,1)}, bf16[3072,3072]{1,0:T(8,128)(2,1)}, bf16[3072,3072]{1,0:T(8,128)(2,1)}, bf16[768,3072]{1,0:T(8,128)(2,1)}, bf16[8,...) custom-call(s32[4]{0:T(128)} %pad_add_fusion.2.place, ...), custom_call_target="tpu_custom_call" | custom-call | flops 43000000512 | bytes 146200000 | tf_op jit(solution)/shard_map/feed/pallas_call | solution.py:335
  310.3 4.4 all-to-all-start.2
  314.8 47.8 %feed.3 = (bf16[768,3072]{1,0:T(8,128)(2,1)}, bf16[3072,3072]{1,0:T(8,128)(2,1)}, bf16[3072,3072]{1,0:T(8,128)(2,1)}, bf16[768,3072]{1,0:T(8,128)(2,1)}, bf16[8,...) custom-call(s32[4]{0:T(128)} %pad_add_fusion.2.place, ...), custom_call_target="tpu_custom_call", output_to_operand_aliasing={{0}: (12, {}), {1}: (13, {}), {2}: (14, {}), {3}: (15, {})} | custom-call | flops 43000000512 | bytes 146200000 | tf_op jit(solution)/shard_map/feed/pallas_call | solution.py:335
  362.6 4.5 all-to-all-start.4
  367.4 24.2 %result.1 = (bf16[192,3072]{1,0:T(8,128)(2,1)}, bf16[192,3072]{1,0:T(8,128)(2,1)}, bf16[192,3072]{1,0:T(8,128)(2,1)}, bf16[192,3072]{1,0:T(8,128)(2,1)}) custom-call(s32[4]{0:T(128)S(1)} %copy-done.11, bf16[3072,3072]{1,0:T(8,128)(2,1)} %get-tuple-element.118.hidden, bf16[768,3072]{1,0:T(8,128)(2,1)} %bitcast.232, f32[768,128]{1,0:T(8,128)S(1)} %broadcast_in_dim.82.bias, ...), custom_call_target="tpu_custom_call" | custom-call | flops 22000001024 | bytes 74800000 | tf_op jit(solution)/shard_map/result/pallas_call | solution.py:335
  391.5 2.0 collective-permute-start.15
  393.6 17.9 %collective-permute-start.16 = (bf16[192,3072]{1,0:T(8,128)(2,1)}, bf16[192,3072]{1,0:T(8,128)(2,1)}, u32[]{:S(2)}, u32[]{:S(2)}) collective-permute-start(bf16[192,3072]{1,0:T(8,128)(2,1)} %get-tuple-element.121), channel_id=1, source_target_pairs={{8,0},{16,1},{24,2},{0,3},{12,4},{20,5},{28,6},{4,7},{9,8},{17,9},... | collective-permute-start | bytes 3538952 | tf_op jit(solution)/shard_map/ppermute | solution.py:542
  411.5 3.3 collective-permute-start.17
  414.8 6.7 collective-permute-start.18
  422.8 18.1 %spectrum_back.1.freq = f32[2,96,96,128]{3,2,1,0:T(8,128)} custom-call(bf16[8,6,96,256]{3,2,1,0:T(8,128)(2,1)S(1)} %all-to-all-done.2.refs_0_.refs_8_, bf16[8,6,96,256]{3,2,1,0:T(8,128)(2,1)} %all-to-all-done.4.refs_1_.refs_9_, bf16[256,256]{1,0:T(8,128)(2,1)S(1)} %copy-done.16, bf16[256,256]{1,0:T(8,128)(2,1)S(1)} %copy-done.17, ...), custom_call_target="tpu_custom_call" | custom-call | flops 16999999488 | bytes 57800000 | tf_op jit(solution)/shard_map/spectrum_back/pallas_call | solution.py:335
  440.9 2.3 copy-done.24
  443.3 21.9 %filter_back.1 = (f32[2,96,96,128]{3,2,1,0:T(8,128)}, f32[192,192]{1,0:T(8,128)S(1)}, f32[192,192]{1,0:T(8,128)S(1)}, f32[192,128]{1,0:T(8,128)S(1)}, f32[192,128]{1,0:T(8,128)S(1)}) custom-call(f32[2,96,96,128]{3,2,1,0:T(8,128)} %spectrum_back.1.freq, bf16[2,96,96,128]{3,2,1,0:T(8,128)(2,1)S(1)} %copy-done.24, bf16[2,96,96,128]{3,2,1,0:T(8,128)(2,1)} %copy-done.25, ...), custom_call_target="tpu_custom_call" | custom-call | flops 24000000000 | bytes 81600000 | tf_op jit(solution)/shard_map/filter_back/pallas_call | solution.py:335
  465.1 22.3 %last.1 = (bf16[96,96,256]{2,1,0:T(8,128)(2,1)}, f32[96,1,256]{2,1,0:T(1,128)}, f32[96,1,256]{2,1,0:T(1,128)}, f32[96,128]{1,0:T(8,128)}, f32[96,128]{1,0:T(8,128)}) custom-call(s32[8]{0:T(128)} %copy-done.10, bf16[12,96,256]{2,1,0:T(8,128)(2,1)} %copy-done.1, bf16[12,96,256]{2,1,0:T(8,128)(2,1)} %copy-done.12, bf16[12,96,256]{2,1,0:T(8,128)(2,1)} %copy-done.13, ...), custom_call_target="tpu_custom_call" | custom-call | flops 22000001024 | bytes 74800000 | tf_op jit(solution)/shard_map/last/pallas_call | solution.py:335
  495.2 4.1 all-to-all-start.5
  499.3 47.5 %weights.1 = (f32[4,768,768]{2,1,0:T(8,128)}, f32[4,768,768]{2,1,0:T(8,128)}) custom-call(s32[4]{0:T(128)} %pad_add_fusion.1.place, bf16[768,3072]{1,0:T(8,128)(2,1)} %get-tuple-element.115.normal, bf16[3072,3072]{1,0:T(8,128)(2,1)} %get-tuple-element.116.pre, bf16[768,3072]{1,0:T(8,128)(2,1)} %get-tuple-element.117.cot, ...), custom_call_target="tpu_custom_call" | custom-call | flops 44000002048 | bytes 149600000 | tf_op jit(solution)/shard_map/weights/pallas_call | solution.py:335
  546.9 4.3 convert.11
  552.8 48.1 %collective-permute-start.20 = (bf16[8,96,768]{2,1,0:T(8,128)(2,1)}, bf16[8,96,768]{2,1,0:T(8,128)(2,1)}, u32[]{:S(2)}, u32[]{:S(2)}) collective-permute-start(bf16[8,96,768]{2,1,0:T(8,128)(2,1)} %bitcast.90), channel_id=1, source_target_pairs={{0,1},{1,0},{2,3},{3,2},{4,5},{5,4},{6,7},{7,6},{8,9},{9,8},{10,11... | collective-permute-start | bytes 3538952 | tf_op jit(solution)/shard_map/ppermute | solution.py:623
  604.5 18.7 %all-to-all-start.6 = ((bf16[8,12,96,256]{3,2,1,0:T(8,128)(2,1)}), bf16[8,12,96,256]{3,2,1,0:T(8,128)(2,1)}, u32[]{:S(2)}, u32[]{:S(2)}) async-start(bf16[8,12,96,256]{3,2,1,0:T(8,128)(2,1)} %bitcast.233), calls=%async_computation.6 | async-start | bytes 9437184 | tf_op jit(solution)/shard_map/all_to_all | solution.py:580
  623.3 27.5 %widen.1 = f32[4,12,192,256]{3,2,1,0:T(8,128)} custom-call(s32[4]{0:T(128)S(1)} %pad_add_fusion.slot, bf16[192,3072]{1,0:T(8,128)(2,1)} %collective-permute-done.15.p0, bf16[192,3072]{1,0:T(8,128)(2,1)} %collective-permute-done.16.p1, bf16[192,3072]{1,0:T(8,128)(2,1)} %collective-permute-done.17.p2, bf16[192,3072]{1,0:T(8,128)(2,1)} %collective-permute-done.18.p3), custom_call_target="tpu_custom_call" | custom-call | flops 22000001024 | bytes 74800000 | tf_op jit(solution)/shard_map/widen/pallas_call | solution.py:335
  650.8 4.1 fusion.21
  654.9 4.8 fusion.20
  662.8 2.7 add_convert_fusion
  665.5 1.8 convert_add_fusion.1
  671.3 2.0 collective-permute-start.27
  676.0 22.8 %all-reduce.7.cloned.1.call-done = f32[121348]{0:T(1024)} async-done(((f32[121348]{0:T(1024)}), f32[121348]{0:T(1024)}) %all-reduce.7.cloned.1.call-update) | async-done | bytes 485408
  703.7 2.8 convert_add_fusion.2
  706.6 1.7 collective-permute-start.22
  708.3 8.3 %collective-permute-done.27 = bf16[4,96,1536]{2,1,0:T(8,128)(2,1)} collective-permute-done((bf16[4,96,1536]{2,1,0:T(8,128)(2,1)}, bf16[4,96,1536]{2,1,0:T(8,128)(2,1)}, u32[]{:S(2)}, u32[]{:S(2)}) %collective-permute-start.27) | collective-permute-done | bytes 1179680 | tf_op jit(solution)/shard_map/ppermute | solution.py:623
  719.0 10.1 %collective-permute-done.22 = bf16[4,96,768]{2,1,0:T(8,128)(2,1)S(1)} collective-permute-done((bf16[4,96,768]{2,1,0:T(8,128)(2,1)S(1)}, bf16[4,96,768]{2,1,0:T(8,128)(2,1)S(1)}, u32[]{:S(2)}, u32[]{:S(2)}) %collective-permute-start.22) | collective-permute-done | bytes 589856 | tf_op jit(solution)/shard_map/ppermute | solution.py:623
  729.3 1.7 collective-permute-start.23
  730.9 2.7 collective-permute-done.28
  733.8 1.6 collective-permute-start.29
  735.5 4.7 collective-permute-done.23
  740.2 11.5 %collective-permute-start.24 = (bf16[1,96,768]{2,1,0:T(8,128)(2,1)S(1)}, bf16[1,96,768]{2,1,0:T(8,128)(2,1)S(1)}, u32[]{:S(2)}, u32[]{:S(2)}) collective-permute-start(bf16[1,96,768]{2,1,0:T(8,128)(2,1)S(1)} %dynamic-slice_convert_fusion.3), channel_id=1, source_target_pairs={{0,8},{4,12},{8,0},{12,4},{16,24},{20,28},{24,16},{28,20},{1,9},{5... | collective-permute-start | bytes 442376 | tf_op jit(solution)/shard_map/ppermute | solution.py:623
  751.7 6.4 collective-permute-done.29
  759.1 4.4 collective-permute-done.30
  764.2 10.4 %finish.1 = f32[4,12,192,256]{3,2,1,0:T(8,128)} custom-call(bf16[8,12,96,256]{3,2,1,0:T(8,128)(2,1)} %all-to-all-done.6.grads, bf16[4,12,192,256]{3,2,1,0:T(8,128)(2,1)} %patches.1, f32[4,12,1,256]{3,2,1,0:T(1,128)S(1)} %copy.207.mean, f32[4,12,1,256]{3,2,1,0:T(1,128)S(1)} %copy.208.rstd, f32[4,12,1,256]{3,2,1,0:T(1,128)S(1)} %get-tuple-element.221.one, ...), custom_call_target="tpu_custom_call" | custom-call | flops 11000000512 | bytes 37400000 | tf_op jit(solution)/shard_map/finish/pallas_call | solution.py:335
  (328 shorter events, 68.6 us)
Async XLA Ops:
  7.2 41.7 %all-reduce.5.cloned.1.call-start = ((), (), s32[]{:S(2)}) async-start(), calls=%async_computation.9 | async-start | bytes 835584
  16.1 217.9 %all-gather.8.cloned.1.call-start = ((), (), s32[]{:S(2)}) async-start(), calls=%async_computation.8 | async-start | bytes 5898240 | tf_op jit(solution)/shard_map/all_gather | solution.py:446
  16.9 223.7 %all-gather.6.cloned.1.call-start = ((), (), s32[]{:S(2)}) async-start(), calls=%async_computation.7 | async-start | bytes 5898240 | tf_op jit(solution)/shard_map/all_gather | solution.py:447
  21.6 126.6 %copy-start.1 = (bf16[12,96,256]{2,1,0:T(8,128)(2,1)}, bf16[12,96,256]{2,1,0:T(8,128)(2,1)S(1)}, u32[]{:S(2)}) copy-start(bf16[12,96,256]{2,1,0:T(8,128)(2,1)S(1)} %get-tuple-element.82.refs_0_) | copy-start | bytes 1769476
  21.6 40.9 %collective-permute-start = (bf16[12,96,256]{2,1,0:T(8,128)(2,1)}, bf16[12,96,256]{2,1,0:T(8,128)(2,1)S(1)}, u32[]{:S(2)}, u32[]{:S(2)}) collective-permute-start(bf16[12,96,256]{2,1,0:T(8,128)(2,1)} %get-tuple-element.197), channel_id=1, source_target_pairs={{0,4},{4,0},{8,12},{12,8},{16,20},{20,16},{24,28},{28,24},{1,5},{5... | collective-permute-start | bytes 1769480 | tf_op jit(solution)/shard_map/ppermute | solution.py:378
  23.2 43.2 %collective-permute-start.1 = (bf16[12,96,256]{2,1,0:T(8,128)(2,1)}, bf16[12,96,256]{2,1,0:T(8,128)(2,1)S(1)}, u32[]{:S(2)}, u32[]{:S(2)}) collective-permute-start(bf16[12,96,256]{2,1,0:T(8,128)(2,1)} %get-tuple-element.196), channel_id=1, source_target_pairs={{0,8},{4,12},{8,0},{12,4},{16,24},{20,28},{24,16},{28,20},{1,9},{5... | collective-permute-start | bytes 1769480 | tf_op jit(solution)/shard_map/ppermute | solution.py:378
  24.8 85.0 %collective-permute-start.2 = (bf16[12,96,256]{2,1,0:T(8,128)(2,1)}, bf16[12,96,256]{2,1,0:T(8,128)(2,1)S(1)}, u32[]{:S(2)}, u32[]{:S(2)}) collective-permute-start(bf16[12,96,256]{2,1,0:T(8,128)(2,1)} %get-tuple-element.195), channel_id=1, source_target_pairs={{0,12},{4,8},{8,4},{12,0},{16,28},{20,24},{24,20},{28,16},{1,13},{... | collective-permute-start | bytes 1769480 | tf_op jit(solution)/shard_map/ppermute | solution.py:378
  25.2 84.6 %collective-permute-start.3 = (bf16[12,96,256]{2,1,0:T(8,128)(2,1)}, bf16[12,96,256]{2,1,0:T(8,128)(2,1)S(1)}, u32[]{:S(2)}, u32[]{:S(2)}) collective-permute-start(bf16[12,96,256]{2,1,0:T(8,128)(2,1)} %get-tuple-element.194), channel_id=1, source_target_pairs={{0,16},{4,20},{8,24},{12,28},{16,0},{20,4},{24,8},{28,12},{1,17},{... | collective-permute-start | bytes 1769480 | tf_op jit(solution)/shard_map/ppermute | solution.py:378
  27.8 82.1 %collective-permute-start.4 = (bf16[12,96,256]{2,1,0:T(8,128)(2,1)}, bf16[12,96,256]{2,1,0:T(8,128)(2,1)}, u32[]{:S(2)}, u32[]{:S(2)}) collective-permute-start(bf16[12,96,256]{2,1,0:T(8,128)(2,1)} %get-tuple-element.193), channel_id=1, source_target_pairs={{0,20},{4,16},{8,28},{12,24},{16,4},{20,0},{24,12},{28,8},{1,21},{... | collective-permute-start | bytes 1769480 | tf_op jit(solution)/shard_map/ppermute | solution.py:378
  33.2 137.7 %copy-start.4 = (bf16[192,192]{1,0:T(8,128)(2,1)}, bf16[192,192]{1,0:T(8,128)(2,1)S(1)}, u32[]{:S(2)}) copy-start(bf16[192,192]{1,0:T(8,128)(2,1)S(1)} %maximum_maximum_fusion.w1) | copy-start | bytes 221188
  56.7 51.9 %all-to-all-start = ((f32[8,12,2,256]{3,2,1,0:T(2,128)}), f32[8,12,2,256]{3,2,1,0:T(2,128)}, u32[]{:S(2)}, u32[]{:S(2)}) async-start(f32[8,12,2,256]{3,2,1,0:T(2,128)} %bitcast.244), calls=%async_computation | async-start | bytes 393216 | tf_op jit(solution)/shard_map/all_to_all | solution.py:423
  62.6 85.7 %copy-start.12 = (bf16[12,96,256]{2,1,0:T(8,128)(2,1)}, bf16[12,96,256]{2,1,0:T(8,128)(2,1)S(1)}, u32[]{:S(2)}) copy-start(bf16[12,96,256]{2,1,0:T(8,128)(2,1)S(1)} %collective-permute-done.refs_1_) | copy-start | bytes 1769476
  62.6 47.3 %collective-permute-start.5 = (bf16[12,96,256]{2,1,0:T(8,128)(2,1)}, bf16[12,96,256]{2,1,0:T(8,128)(2,1)}, u32[]{:S(2)}, u32[]{:S(2)}) collective-permute-start(bf16[12,96,256]{2,1,0:T(8,128)(2,1)} %get-tuple-element.192), channel_id=1, source_target_pairs={{0,24},{4,28},{8,16},{12,20},{16,8},{20,12},{24,0},{28,4},{1,25},{... | collective-permute-start | bytes 1769480 | tf_op jit(solution)/shard_map/ppermute | solution.py:378
  66.5 81.8 %copy-start.13 = (bf16[12,96,256]{2,1,0:T(8,128)(2,1)}, bf16[12,96,256]{2,1,0:T(8,128)(2,1)S(1)}, u32[]{:S(2)}) copy-start(bf16[12,96,256]{2,1,0:T(8,128)(2,1)S(1)} %collective-permute-done.1.refs_2_) | copy-start | bytes 1769476
  66.5 43.4 %collective-permute-start.6 = (bf16[12,96,256]{2,1,0:T(8,128)(2,1)}, bf16[12,96,256]{2,1,0:T(8,128)(2,1)}, u32[]{:S(2)}, u32[]{:S(2)}) collective-permute-start(bf16[12,96,256]{2,1,0:T(8,128)(2,1)} %get-tuple-element.191), channel_id=1, source_target_pairs={{0,28},{4,24},{8,20},{12,16},{16,12},{20,8},{24,4},{28,0},{1,29},{... | collective-permute-start | bytes 1769480 | tf_op jit(solution)/shard_map/ppermute | solution.py:378
  69.3 40.6 %copy-start.48 = (f32[96]{0:T(128)}, f32[96]{0:T(128)S(1)}, u32[]{:S(2)}) copy-start(f32[96]{0:T(128)S(1)} %get-tuple-element.182) | copy-start | bytes 1156
  71.7 76.6 %copy-start.10 = (s32[8]{0:T(128)}, s32[8]{0:T(128)S(1)}, u32[]{:S(2)}) copy-start(s32[8]{0:T(128)S(1)} %stack.130.place) | copy-start | bytes 100
  72.6 98.3 %copy-start.8 = (bf16[192,192]{1,0:T(8,128)(2,1)}, bf16[192,192]{1,0:T(8,128)(2,1)S(1)}, u32[]{:S(2)}) copy-start(bf16[192,192]{1,0:T(8,128)(2,1)S(1)} %maximum_maximum_fusion.1.w2) | copy-start | bytes 221188
  109.8 38.5 %copy-start.6 = (f32[96,1,256]{2,1,0:T(1,128)}, f32[96,1,256]{2,1,0:T(1,128)S(1)}, u32[]{:S(2)}) copy-start(f32[96,1,256]{2,1,0:T(1,128)S(1)} %get-tuple-element.218.refs_9_.refs_11_) | copy-start | bytes 294916
  109.8 38.5 %copy-start.7 = (f32[96,1,256]{2,1,0:T(1,128)}, f32[96,1,256]{2,1,0:T(1,128)S(1)}, u32[]{:S(2)}) copy-start(f32[96,1,256]{2,1,0:T(1,128)S(1)} %get-tuple-element.219.refs_8_.refs_10_) | copy-start | bytes 294916
  109.8 38.5 %copy-start.14 = (bf16[12,96,256]{2,1,0:T(8,128)(2,1)}, bf16[12,96,256]{2,1,0:T(8,128)(2,1)S(1)}, u32[]{:S(2)}) copy-start(bf16[12,96,256]{2,1,0:T(8,128)(2,1)S(1)} %collective-permute-done.2.refs_3_) | copy-start | bytes 1769476
  109.9 38.5 %copy-start.15 = (bf16[12,96,256]{2,1,0:T(8,128)(2,1)}, bf16[12,96,256]{2,1,0:T(8,128)(2,1)S(1)}, u32[]{:S(2)}) copy-start(bf16[12,96,256]{2,1,0:T(8,128)(2,1)S(1)} %collective-permute-done.3.refs_4_) | copy-start | bytes 1769476
  112.3 78.0 %collective-permute-start.7 = (bf16[6,192,256]{2,1,0:T(8,128)(2,1)S(1)}, bf16[6,192,256]{2,1,0:T(8,128)(2,1)S(1)}, u32[]{:S(2)}, u32[]{:S(2)}) collective-permute-start(bf16[6,192,256]{2,1,0:T(8,128)(2,1)S(1)} %get-tuple-element.206), channel_id=1, source_target_pairs={{0,0},{1,8},{2,16},{3,24},{4,4},{5,12},{6,20},{7,28},{8,1},{9,9},{... | collective-permute-start | bytes 1769480 | tf_op jit(solution)/shard_map/ppermute | solution.py:401
  143.0 47.3 %collective-permute-start.8 = (bf16[6,192,256]{2,1,0:T(8,128)(2,1)S(1)}, bf16[6,192,256]{2,1,0:T(8,128)(2,1)S(1)}, u32[]{:S(2)}, u32[]{:S(2)}) collective-permute-start(bf16[6,192,256]{2,1,0:T(8,128)(2,1)S(1)} %get-tuple-element.205), channel_id=1, source_target_pairs={{0,8},{1,16},{2,24},{3,0},{4,12},{5,20},{6,28},{7,4},{8,9},{9,17},... | collective-permute-start | bytes 1769480 | tf_op jit(solution)/shard_map/ppermute | solution.py:401
  143.1 47.2 %collective-permute-start.9 = (bf16[6,192,256]{2,1,0:T(8,128)(2,1)S(1)}, bf16[6,192,256]{2,1,0:T(8,128)(2,1)S(1)}, u32[]{:S(2)}, u32[]{:S(2)}) collective-permute-start(bf16[6,192,256]{2,1,0:T(8,128)(2,1)S(1)} %get-tuple-element.204), channel_id=1, source_target_pairs={{0,16},{1,24},{2,0},{3,8},{4,20},{5,28},{6,4},{7,12},{8,17},{9,25}... | collective-permute-start | bytes 1769480 | tf_op jit(solution)/shard_map/ppermute | solution.py:401
  145.7 44.6 %collective-permute-start.10 = (bf16[6,192,256]{2,1,0:T(8,128)(2,1)S(1)}, bf16[6,192,256]{2,1,0:T(8,128)(2,1)S(1)}, u32[]{:S(2)}, u32[]{:S(2)}) collective-permute-start(bf16[6,192,256]{2,1,0:T(8,128)(2,1)S(1)} %get-tuple-element.203), channel_id=1, source_target_pairs={{0,24},{1,0},{2,8},{3,16},{4,28},{5,4},{6,12},{7,20},{8,25},{9,1},... | collective-permute-start | bytes 1769480 | tf_op jit(solution)/shard_map/ppermute | solution.py:401
  208.9 42.5 %all-to-all-start.1 = ((bf16[8,6,96,256]{3,2,1,0:T(8,128)(2,1)}), bf16[8,6,96,256]{3,2,1,0:T(8,128)(2,1)S(1)}, u32[]{:S(2)}, u32[]{:S(2)}) async-start(bf16[8,6,96,256]{3,2,1,0:T(8,128)(2,1)} %get-tuple-element.97), calls=%async_computation.1 | async-start | bytes 4718592 | tf_op jit(solution)/shard_map/all_to_all | solution.py:502
  220.9 93.9 %collective-permute-start.11 = (bf16[6,192,256]{2,1,0:T(8,128)(2,1)}, bf16[6,192,256]{2,1,0:T(8,128)(2,1)}, u32[]{:S(2)}, u32[]{:S(2)}) collective-permute-start(bf16[6,192,256]{2,1,0:T(8,128)(2,1)} %get-tuple-element.202), channel_id=1, source_target_pairs={{0,0},{1,8},{2,16},{3,24},{4,4},{5,12},{6,20},{7,28},{8,1},{9,9},{... | collective-permute-start | bytes 1769480 | tf_op jit(solution)/shard_map/ppermute | solution.py:401
  223.0 91.8 %collective-permute-start.12 = (bf16[6,192,256]{2,1,0:T(8,128)(2,1)}, bf16[6,192,256]{2,1,0:T(8,128)(2,1)}, u32[]{:S(2)}, u32[]{:S(2)}) collective-permute-start(bf16[6,192,256]{2,1,0:T(8,128)(2,1)} %get-tuple-element.201), channel_id=1, source_target_pairs={{0,8},{1,16},{2,24},{3,0},{4,12},{5,20},{6,28},{7,4},{8,9},{9,17},... | collective-permute-start | bytes 1769480 | tf_op jit(solution)/shard_map/ppermute | solution.py:401
  230.2 84.6 %collective-permute-start.13 = (bf16[6,192,256]{2,1,0:T(8,128)(2,1)}, bf16[6,192,256]{2,1,0:T(8,128)(2,1)}, u32[]{:S(2)}, u32[]{:S(2)}) collective-permute-start(bf16[6,192,256]{2,1,0:T(8,128)(2,1)} %get-tuple-element.200), channel_id=1, source_target_pairs={{0,16},{1,24},{2,0},{3,8},{4,20},{5,28},{6,4},{7,12},{8,17},{9,25}... | collective-permute-start | bytes 1769480 | tf_op jit(solution)/shard_map/ppermute | solution.py:401
  230.2 84.6 %collective-permute-start.14 = (bf16[6,192,256]{2,1,0:T(8,128)(2,1)S(1)}, bf16[6,192,256]{2,1,0:T(8,128)(2,1)}, u32[]{:S(2)}, u32[]{:S(2)}) collective-permute-start(bf16[6,192,256]{2,1,0:T(8,128)(2,1)S(1)} %get-tuple-element.199), channel_id=1, source_target_pairs={{0,24},{1,0},{2,8},{3,16},{4,28},{5,4},{6,12},{7,20},{8,25},{9,1},... | collective-permute-start | bytes 1769480 | tf_op jit(solution)/shard_map/ppermute | solution.py:401
  252.8 57.5 %all-to-all-start.3 = ((bf16[8,6,96,256]{3,2,1,0:T(8,128)(2,1)}), bf16[8,6,96,256]{3,2,1,0:T(8,128)(2,1)}, u32[]{:S(2)}, u32[]{:S(2)}) async-start(bf16[8,6,96,256]{3,2,1,0:T(8,128)(2,1)} %get-tuple-element.100), calls=%async_computation.3 | async-start | bytes 4718592 | tf_op jit(solution)/shard_map/all_to_all | solution.py:502
  310.3 52.3 %all-to-all-start.2 = ((bf16[8,6,96,256]{3,2,1,0:T(8,128)(2,1)}), bf16[8,6,96,256]{3,2,1,0:T(8,128)(2,1)S(1)}, u32[]{:S(2)}, u32[]{:S(2)}) async-start(bf16[8,6,96,256]{3,2,1,0:T(8,128)(2,1)} %get-tuple-element.98), calls=%async_computation.2 | async-start | bytes 4718592 | tf_op jit(solution)/shard_map/all_to_all | solution.py:502
  362.6 60.1 %copy-start = (bf16[8,6,96,256]{3,2,1,0:T(8,128)(2,1)}, bf16[8,6,96,256]{3,2,1,0:T(8,128)(2,1)S(1)}, u32[]{:S(2)}) copy-start(bf16[8,6,96,256]{3,2,1,0:T(8,128)(2,1)S(1)} %all-to-all-done.2.refs_0_.refs_8_) | copy-start | bytes 7077892
  362.6 60.0 %all-to-all-start.4 = ((bf16[8,6,96,256]{3,2,1,0:T(8,128)(2,1)}), bf16[8,6,96,256]{3,2,1,0:T(8,128)(2,1)}, u32[]{:S(2)}, u32[]{:S(2)}) async-start(bf16[8,6,96,256]{3,2,1,0:T(8,128)(2,1)} %get-tuple-element.105), calls=%async_computation.4 | async-start | bytes 4718592 | tf_op jit(solution)/shard_map/all_to_all | solution.py:502
  367.3 54.2 %copy-start.41 = (f32[768,128]{1,0:T(8,128)S(1)}, f32[768,128]{1,0:T(8,128)}, u32[]{:S(2)}) copy-start(f32[768,128]{1,0:T(8,128)} %get-tuple-element.135) | copy-start | bytes 1179652
  367.3 54.2 %copy-start.44 = (f32[768,128]{1,0:T(8,128)S(1)}, f32[768,128]{1,0:T(8,128)}, u32[]{:S(2)}) copy-start(f32[768,128]{1,0:T(8,128)} %get-tuple-element.136) | copy-start | bytes 1179652
  367.3 54.4 %copy-start.40 = (f32[768,128]{1,0:T(8,128)S(1)}, f32[768,128]{1,0:T(8,128)}, u32[]{:S(2)}) copy-start(f32[768,128]{1,0:T(8,128)} %get-tuple-element.137) | copy-start | bytes 1179652
  367.3 54.4 %copy-start.43 = (f32[768,128]{1,0:T(8,128)S(1)}, f32[768,128]{1,0:T(8,128)}, u32[]{:S(2)}) copy-start(f32[768,128]{1,0:T(8,128)} %get-tuple-element.138) | copy-start | bytes 1179652
  367.3 54.6 %copy-start.39 = (f32[768,128]{1,0:T(8,128)S(1)}, f32[768,128]{1,0:T(8,128)}, u32[]{:S(2)}) copy-start(f32[768,128]{1,0:T(8,128)} %get-tuple-element.139) | copy-start | bytes 1179652
  367.3 54.6 %copy-start.42 = (f32[768,128]{1,0:T(8,128)S(1)}, f32[768,128]{1,0:T(8,128)}, u32[]{:S(2)}) copy-start(f32[768,128]{1,0:T(8,128)} %get-tuple-element.140) | copy-start | bytes 1179652
  367.4 54.8 %copy-start.36 = (f32[3072,128]{1,0:T(8,128)S(1)}, f32[3072,128]{1,0:T(8,128)}, u32[]{:S(2)}) copy-start(f32[3072,128]{1,0:T(8,128)} %get-tuple-element.142) | copy-start | bytes 4718596
  391.5 155.3 %collective-permute-start.15 = (bf16[192,3072]{1,0:T(8,128)(2,1)}, bf16[192,3072]{1,0:T(8,128)(2,1)}, u32[]{:S(2)}, u32[]{:S(2)}) collective-permute-start(bf16[192,3072]{1,0:T(8,128)(2,1)} %get-tuple-element.120), channel_id=1, source_target_pairs={{0,0},{8,1},{16,2},{24,3},{4,4},{12,5},{20,6},{28,7},{1,8},{9,9},{... | collective-permute-start | bytes 3538952 | tf_op jit(solution)/shard_map/ppermute | solution.py:542
  393.6 153.3 %collective-permute-start.16 = (bf16[192,3072]{1,0:T(8,128)(2,1)}, bf16[192,3072]{1,0:T(8,128)(2,1)}, u32[]{:S(2)}, u32[]{:S(2)}) collective-permute-start(bf16[192,3072]{1,0:T(8,128)(2,1)} %get-tuple-element.121), channel_id=1, source_target_pairs={{8,0},{16,1},{24,2},{0,3},{12,4},{20,5},{28,6},{4,7},{9,8},{17,9},... | collective-permute-start | bytes 3538952 | tf_op jit(solution)/shard_map/ppermute | solution.py:542
  411.5 135.3 %collective-permute-start.17 = (bf16[192,3072]{1,0:T(8,128)(2,1)}, bf16[192,3072]{1,0:T(8,128)(2,1)}, u32[]{:S(2)}, u32[]{:S(2)}) collective-permute-start(bf16[192,3072]{1,0:T(8,128)(2,1)} %get-tuple-element.122), channel_id=1, source_target_pairs={{16,0},{24,1},{0,2},{8,3},{20,4},{28,5},{4,6},{12,7},{17,8},{25,9}... | collective-permute-start | bytes 3538952 | tf_op jit(solution)/shard_map/ppermute | solution.py:542
  414.8 132.1 %collective-permute-start.18 = (bf16[192,3072]{1,0:T(8,128)(2,1)}, bf16[192,3072]{1,0:T(8,128)(2,1)}, u32[]{:S(2)}, u32[]{:S(2)}) collective-permute-start(bf16[192,3072]{1,0:T(8,128)(2,1)} %get-tuple-element.123), channel_id=1, source_target_pairs={{24,0},{0,1},{8,2},{16,3},{28,4},{4,5},{12,6},{20,7},{25,8},{1,9},... | collective-permute-start | bytes 3538952 | tf_op jit(solution)/shard_map/ppermute | solution.py:542
  495.2 109.0 %all-to-all-start.5 = ((f32[8,1,16369]{2,1,0:T(1,128)}), f32[8,1,16369]{2,1,0:T(1,128)S(1)}, u32[]{:S(2)}, u32[]{:S(2)}) async-start(f32[8,1,16369]{2,1,0:T(1,128)} %all_to_all.31), calls=%async_computation.5 | async-start | bytes 1048576 | tf_op jit(solution)/shard_map/all_to_all | solution.py:578
  546.9 54.0 %slice-start = ((s8[9437184]{0:T(1024)(128)(4,1)}), s8[4194304]{0:T(1024)(128)(4,1)S(1)}, s32[]{:S(2)}) async-start(s8[9437184]{0:T(1024)(128)(4,1)} %bitcast.215), calls=%async_computation.11 | async-start | bytes 8388608
  546.9 54.0 %slice-start.1 = ((s8[9437184]{0:T(1024)(128)(4,1)}), s8[4194304]{0:T(1024)(128)(4,1)S(1)}, s32[]{:S(2)}) async-start(s8[9437184]{0:T(1024)(128)(4,1)} %bitcast.215), calls=%async_computation.12 | async-start | bytes 8388608
  546.9 54.0 %slice-start.2 = ((s8[9437184]{0:T(1024)(128)(4,1)}), s8[1048576]{0:T(1024)(128)(4,1)S(1)}, s32[]{:S(2)}) async-start(s8[9437184]{0:T(1024)(128)(4,1)} %bitcast.215), calls=%async_computation.13 | async-start | bytes 2097152
  552.8 110.0 %collective-permute-start.20 = (bf16[8,96,768]{2,1,0:T(8,128)(2,1)}, bf16[8,96,768]{2,1,0:T(8,128)(2,1)}, u32[]{:S(2)}, u32[]{:S(2)}) collective-permute-start(bf16[8,96,768]{2,1,0:T(8,128)(2,1)} %bitcast.90), channel_id=1, source_target_pairs={{0,1},{1,0},{2,3},{3,2},{4,5},{5,4},{6,7},{7,6},{8,9},{9,8},{10,11... | collective-permute-start | bytes 3538952 | tf_op jit(solution)/shard_map/ppermute | solution.py:623
  600.9 102.8 %collective-permute-start.19 = (bf16[8,96,768]{2,1,0:T(8,128)(2,1)}, bf16[8,96,768]{2,1,0:T(8,128)(2,1)}, u32[]{:S(2)}, u32[]{:S(2)}) collective-permute-start(bf16[8,96,768]{2,1,0:T(8,128)(2,1)} %bitcast.88), channel_id=1, source_target_pairs={{0,1},{1,0},{2,3},{3,2},{4,5},{5,4},{6,7},{7,6},{8,9},{9,8},{10,11... | collective-permute-start | bytes 3538952 | tf_op jit(solution)/shard_map/ppermute | solution.py:623
  603.0 62.5 %collective-permute-start.25 = (bf16[8,96,768]{2,1,0:T(8,128)(2,1)}, bf16[8,96,768]{2,1,0:T(8,128)(2,1)}, u32[]{:S(2)}, u32[]{:S(2)}) collective-permute-start(bf16[8,96,768]{2,1,0:T(8,128)(2,1)} %bitcast.99), channel_id=1, source_target_pairs={{0,1},{1,0},{2,3},{3,2},{4,5},{5,4},{6,7},{7,6},{8,9},{9,8},{10,11... | collective-permute-start | bytes 3538952 | tf_op jit(solution)/shard_map/ppermute | solution.py:623
  604.2 63.0 %collective-permute-start.26 = (bf16[8,96,768]{2,1,0:T(8,128)(2,1)}, bf16[8,96,768]{2,1,0:T(8,128)(2,1)}, u32[]{:S(2)}, u32[]{:S(2)}) collective-permute-start(bf16[8,96,768]{2,1,0:T(8,128)(2,1)} %bitcast.103), channel_id=1, source_target_pairs={{0,1},{1,0},{2,3},{3,2},{4,5},{5,4},{6,7},{7,6},{8,9},{9,8},{10,11... | collective-permute-start | bytes 3538952 | tf_op jit(solution)/shard_map/ppermute | solution.py:623
  604.5 159.7 %all-to-all-start.6 = ((bf16[8,12,96,256]{3,2,1,0:T(8,128)(2,1)}), bf16[8,12,96,256]{3,2,1,0:T(8,128)(2,1)}, u32[]{:S(2)}, u32[]{:S(2)}) async-start(bf16[8,12,96,256]{3,2,1,0:T(8,128)(2,1)} %bitcast.233), calls=%async_computation.6 | async-start | bytes 9437184 | tf_op jit(solution)/shard_map/all_to_all | solution.py:580
  623.2 75.6 %all-reduce.7.cloned.1.call-start = ((), (), s32[]{:S(2)}) async-start(), calls=%async_computation.10 | async-start | bytes 974848
  665.5 38.2 %collective-permute-start.21 = (bf16[8,96,768]{2,1,0:T(8,128)(2,1)}, bf16[8,96,768]{2,1,0:T(8,128)(2,1)}, u32[]{:S(2)}, u32[]{:S(2)}) collective-permute-start(bf16[8,96,768]{2,1,0:T(8,128)(2,1)} %add_convert_fusion), channel_id=1, source_target_pairs={{0,2},{1,3},{2,0},{3,1},{4,6},{5,7},{6,4},{7,5},{8,10},{9,11},{10,... | collective-permute-start | bytes 3538952 | tf_op jit(solution)/shard_map/ppermute | solution.py:623
  671.3 45.3 %collective-permute-start.27 = (bf16[4,96,1536]{2,1,0:T(8,128)(2,1)}, bf16[4,96,1536]{2,1,0:T(8,128)(2,1)}, u32[]{:S(2)}, u32[]{:S(2)}) collective-permute-start(bf16[4,96,1536]{2,1,0:T(8,128)(2,1)} %fusion.7), channel_id=1, source_target_pairs={{0,4},{4,0},{8,12},{12,8},{16,20},{20,16},{24,28},{28,24},{1,5},{5... | collective-permute-start | bytes 3538952 | tf_op jit(solution)/shard_map/ppermute | solution.py:623
  706.6 22.5 %collective-permute-start.22 = (bf16[4,96,768]{2,1,0:T(8,128)(2,1)S(1)}, bf16[4,96,768]{2,1,0:T(8,128)(2,1)S(1)}, u32[]{:S(2)}, u32[]{:S(2)}) collective-permute-start(bf16[4,96,768]{2,1,0:T(8,128)(2,1)S(1)} %fusion.8), channel_id=1, source_target_pairs={{0,4},{4,0},{8,12},{12,8},{16,20},{20,16},{24,28},{28,24},{1,5},{5... | collective-permute-start | bytes 1769480 | tf_op jit(solution)/shard_map/ppermute | solution.py:623
  718.3 15.3 %collective-permute-start.28 = (bf16[4,96,768]{2,1,0:T(8,128)(2,1)S(1)}, bf16[4,96,768]{2,1,0:T(8,128)(2,1)S(1)}, u32[]{:S(2)}, u32[]{:S(2)}) collective-permute-start(bf16[4,96,768]{2,1,0:T(8,128)(2,1)S(1)} %slice.249), channel_id=1, source_target_pairs={{0,2},{1,3},{2,0},{3,1},{4,6},{5,7},{6,4},{7,5},{8,10},{9,11},{10,... | collective-permute-start | bytes 1769480 | tf_op jit(solution)/shard_map/ppermute | solution.py:623
  729.3 10.8 %collective-permute-start.23 = (bf16[2,96,768]{2,1,0:T(8,128)(2,1)S(1)}, bf16[2,96,768]{2,1,0:T(8,128)(2,1)S(1)}, u32[]{:S(2)}, u32[]{:S(2)}) collective-permute-start(bf16[2,96,768]{2,1,0:T(8,128)(2,1)S(1)} %fusion.9), channel_id=1, source_target_pairs={{0,16},{4,20},{8,24},{12,28},{16,0},{20,4},{24,8},{28,12},{1,17},{... | collective-permute-start | bytes 884744 | tf_op jit(solution)/shard_map/ppermute | solution.py:623
  733.8 24.3 %collective-permute-start.29 = (bf16[2,96,768]{2,1,0:T(8,128)(2,1)S(1)}, bf16[2,96,768]{2,1,0:T(8,128)(2,1)S(1)}, u32[]{:S(2)}, u32[]{:S(2)}) collective-permute-start(bf16[2,96,768]{2,1,0:T(8,128)(2,1)S(1)} %fusion.10), channel_id=1, source_target_pairs={{0,16},{4,20},{8,24},{12,28},{16,0},{20,4},{24,8},{28,12},{1,17},{... | collective-permute-start | bytes 884744 | tf_op jit(solution)/shard_map/ppermute | solution.py:623
  740.2 18.1 %collective-permute-start.24 = (bf16[1,96,768]{2,1,0:T(8,128)(2,1)S(1)}, bf16[1,96,768]{2,1,0:T(8,128)(2,1)S(1)}, u32[]{:S(2)}, u32[]{:S(2)}) collective-permute-start(bf16[1,96,768]{2,1,0:T(8,128)(2,1)S(1)} %dynamic-slice_convert_fusion.3), channel_id=1, source_target_pairs={{0,8},{4,12},{8,0},{12,4},{16,24},{20,28},{24,16},{28,20},{1,9},{5... | collective-permute-start | bytes 442376 | tf_op jit(solution)/shard_map/ppermute | solution.py:623
  758.3 5.2 collective-permute-start.30
  (45 other events, 502.2 us)
Sparse Core Ops, SparseCore 0:
  16.2 32.5 all-reduce.4
  50.5 37.5 all-gather.7
  89.7 43.7 all-gather.5
  662.4 36.4 all-reduce.6

commit v3 on v2

v3 whole, which is shorter than its diff:
```python
import functools
import math

import jax
import jax.numpy as jnp
import numpy as np
from jax import lax
from jax.experimental import pallas as pl
from jax.experimental.pallas import tpu as pltpu
from jax.sharding import Mesh, PartitionSpec as P

BLOCK = 96
SHRINK = 0.01
NORM_EPS = 1e-05
BF = jnp.bfloat16
F32 = jnp.float32
FLOPS, BYTES = 1_000_000_000, 3_400_000
NN = (((1,), (0,)), ((), ()))
NT = (((1,), (1,)), ((), ()))
TN = (((0,), (0,)), ((), ()))
ERF_T = 0.3275911
ERF_POLY = (0.254829592, -0.284496736, 1.421413741, -1.453152027, 1.061405429)


def dot(left, right, dims=NN):
    return lax.dot_general(left, right, dims, preferred_element_type=F32)


def gelu_pair(value):
    root = jnp.abs(value) * (1.0 / math.sqrt(2.0))
    t = 1.0 / (1.0 + ERF_T * root)
    bell = jnp.exp(-0.5 * value * value)
    poly = 0.5 * ERF_POLY[4]
    for coef in ERF_POLY[3::-1]:
        poly = poly * t + 0.5 * coef
    tail = poly * t * bell
    phi = jnp.where(value >= 0, 1.0 - tail, tail)
    return value * phi, phi + value * bell * (1.0 / math.sqrt(2.0 * math.pi))


def split(value):
    high = value.astype(BF)
    return high, (value - high.astype(F32)).astype(BF)


def np_split(table):
    high = table.astype(np.float32).astype(jnp.bfloat16)
    low = (table - high.astype(np.float64)).astype(np.float32).astype(jnp.bfloat16)
    return jnp.asarray(high), jnp.asarray(low)


def lon_tables(width, modes):
    angle = 2.0 * np.pi * (np.outer(np.arange(modes), np.arange(width)) % width) / width
    scale = 1.0 / math.sqrt(width)
    cos, sin = np.cos(angle) * scale, np.sin(angle) * scale
    doubled = np.where(np.arange(modes) == 0, 1.0, 2.0)[:, None]
    plain = np.concatenate([cos, -sin], 0)
    weighted = np.concatenate([cos * doubled, -sin * doubled], 0)
    return plain, weighted


def swapped(index):
    return index % 2 * 2 + index // 2


def swap_planes(array):
    return array.reshape(2, 2, -1, *array.shape[1:]).swapaxes(0, 1).reshape(array.shape)


def lat_table(rows):
    angle = 2.0 * np.pi * (np.outer(np.arange(rows), np.arange(rows)) % rows) / rows
    scale = 1.0 / math.sqrt(rows)
    cos, sin = swap_planes((np.cos(angle) * scale).T).T, swap_planes((np.sin(angle) * scale).T).T
    return np.block([[cos, sin], [-sin, cos]])


def fold_lanes(value):
    total = value[:, :128]
    for at in range(128, value.shape[1], 128):
        total = total + value[:, at : at + 128]
    return total


def collect(pieces):
    value = pieces[...].astype(F32)
    value = value.reshape(4, value.shape[0] // 4 * value.shape[1], *value.shape[2:])
    return jnp.concatenate([value[swapped(i)] for i in range(4)], axis=0)


def lat_product(lat, high, low):
    size = lat.shape[1]
    both = dot(lat, high)
    return both[:size] + (both[size:] + dot(lat[:size], low))


def plane_forward(parts, table, lat, lons, spectra):
    rows, modes = lat.shape[1] // 2, spectra.shape[1]
    feats = spectra.shape[0] // (2 * rows)
    table_hi, table_lo = table
    total = dot(parts[0], table_lo)
    if len(parts) > 1:
        total = total + dot(parts[1], table_hi)
    total = total + dot(parts[0], table_hi)
    for c in range(2):
        lons[c] = total[:, c * modes : (c + 1) * modes]
    for f in range(0, feats, 2):
        pair = []
        for g in (f, f + 1):
            pair.append(jnp.concatenate([lons[c, pl.ds(g, rows, stride=feats), :] for c in range(2)], axis=0))
        high, low = split(jnp.concatenate(pair, axis=1))
        out = lat_product(lat, high, low)
        for i, g in enumerate((f, f + 1)):
            spectra[pl.ds(g, 2 * rows, stride=feats), :] = out[:, i * modes : (i + 1) * modes]


def plane_inverse(table, lat, lons, spectra):
    rows, modes = lat.shape[1] // 2, spectra.shape[1]
    feats = spectra.shape[0] // (2 * rows)
    table_hi, table_lo = table
    for f in range(0, feats, 2):
        pair = [spectra[pl.ds(g, 2 * rows, stride=feats), :] for g in (f, f + 1)]
        high, low = split(jnp.concatenate(pair, axis=1))
        out = lat_product(lat, high, low)
        for i, g in enumerate((f, f + 1)):
            for c in range(2):
                lons[c, pl.ds(g, rows, stride=feats), :] = out[c * rows : (c + 1) * rows, i * modes : (i + 1) * modes]
    high, low = split(jnp.concatenate([lons[0], lons[1]], axis=1))
    return dot(high, table_hi) + (dot(high, table_lo) + dot(low, table_hi))


def spectrum_kernel(pieces, mean, rstd, scale, shift, hi, lo, lat, spec, lons, spectra):
    mixed = (collect(pieces) - mean[...]) * rstd[...] * scale[...] + shift[...]
    rows, feats, width = mixed.shape
    parts = split(mixed.reshape(rows * feats, width))
    plane_forward(parts, (hi[...], lo[...]), lat[...], lons, spectra)
    spec[...] = spectra[...].reshape(spec.shape).astype(BF)


def join_lines(parts):
    value = jnp.concatenate([part[...] for part in parts], axis=1)
    return value.reshape(value.shape[0] * value.shape[1], *value.shape[2:])


def spectrum_back_kernel(n, *refs):
    parts, (hi, lo, lat, freq, lons, spectra) = refs[:n], refs[n:]
    value = join_lines(parts)
    rows, feats, width = value.shape
    if feats % 16:
        value = value.astype(F32).reshape(rows * feats, width).astype(BF)
    else:
        value = value.reshape(rows * feats, width)
    plane_forward((value,), (hi[...], lo[...]), lat[...], lons, spectra)
    freq[...] = spectra[...].reshape(freq.shape)


def two_modes(ref, ky):
    return jnp.concatenate([jnp.concatenate([ref[0, k], ref[1, k]], axis=0) for k in (ky, ky + 1)], axis=1)


def put_modes(ref, ky, value):
    feats, modes = ref.shape[2], ref.shape[3]
    for i in range(2):
        for c in range(2):
            ref[c, ky + i] = value[c * feats : (c + 1) * feats, i * modes : (i + 1) * modes]


def filter_kernel(spec, w1, bias1, w2, bias2, kept, mid, slope, bend, share):
    @pl.when(pl.program_id(0) == 0)
    def _():
        share[...] = jnp.zeros_like(share)

    for ky in range(0, spec.shape[1], 2):
        act, deriv = gelu_pair(dot(w1[...], two_modes(spec, ky)) + bias1[...])
        act = act.astype(BF)
        put_modes(mid, ky, act)
        put_modes(slope, ky, deriv)
        second = dot(w2[...], act) + bias2[...]
        bent = jnp.tanh(second * (1.0 / SHRINK))
        square = bent * bent
        put_modes(bend, ky, square)
        put_modes(kept, ky, second - SHRINK * bent)
        share[...] += jnp.sum((1.0 - square).reshape(-1, 8, square.shape[1]), axis=0)


def filter_back_kernel(
    freq, spec, mid, slope, bend, w1, w2, sgrad, inner, outer, inner_bias, outer_bias
):
    @pl.when(pl.program_id(0) == 0)
    def _():
        for ref in (inner, outer, inner_bias, outer_bias):
            ref[...] = jnp.zeros_like(ref)

    for ky in range(0, spec.shape[1], 2):
        two = (two_modes(freq, ky) * two_modes(bend, ky)).astype(BF)
        outer[...] += dot(two_modes(mid, ky), two, NT)
        outer_bias[...] += fold_lanes(two.astype(F32))
        one = (dot(w2[...], two, TN) * two_modes(slope, ky)).astype(BF)
        inner[...] += dot(two_modes(spec, ky), one, NT)
        inner_bias[...] += fold_lanes(one.astype(F32))
        put_modes(sgrad, ky, dot(w1[...], one, TN))


def section_kernel(pieces, mean, rstd, scale, shift, kept, hi, lo, lat, *refs):
    outs, (lons, spectra) = refs[:-2], refs[-2:]
    spectra[...] = kept[...].reshape(spectra.shape)
    value = collect(pieces)
    mixed = (value - mean[...]) * rstd[...] * scale[...] + shift[...]
    spectral = plane_inverse((hi[...], lo[...]), lat[...], lons, spectra)
    section = (value + mixed + spectral.reshape(value.shape)).astype(BF)
    section = section.reshape(pieces.shape[0], pieces.shape[1], *value.shape[1:])
    at = 0
    for out in outs:
        out[...] = section[:, at : at + out.shape[1]]
        at += out.shape[1]


def last_kernel(n, pieces, *refs):
    sgrad, (mean, rstd, scale, freq, hi, lo, lat, out, sums, gain_sum, shift_sum, lons, spectra) = refs[:n], refs[n:]
    spectra[...] = freq[...].reshape(spectra.shape)
    normed = (collect(pieces) - mean[...]) * rstd[...]
    grad = join_lines(sgrad).astype(F32)
    mixed = grad + plane_inverse((hi[...], lo[...]), lat[...], lons, spectra).reshape(grad.shape)
    gain_sum[...] = fold_lanes(jnp.sum(mixed * normed, axis=0))
    shift_sum[...] = fold_lanes(jnp.sum(mixed, axis=0))
    scaled = mixed * scale[...]
    value = (grad + rstd[...] * scaled).astype(BF)
    block = value.shape[0] // 4
    for i in range(4):
        out[i * block : (i + 1) * block] = value[swapped(i) * block : (swapped(i) + 1) * block]

    @pl.when(pl.program_id(0) == 0)
    def _():
        sums[...] = jnp.zeros_like(sums)

    for c, term in enumerate((scaled, scaled * normed)):
        term = jnp.sum(term, axis=1)
        for i in range(4):
            sums[i * block : (i + 1) * block, c] += term[swapped(i) * block : (swapped(i) + 1) * block]


def column_norm(value):
    mean = jnp.mean(value, axis=0, keepdims=True)
    centered = value - mean
    var = jnp.mean(centered * centered, axis=0, keepdims=True)
    rstd = lax.rsqrt(var + NORM_EPS)
    return centered * rstd, rstd


def feed_kernel(
    n, quarter, chunk, place, *refs
):
    cots = refs[:n]
    section, we_t, wp, we, bias, gain, shift = refs[n : n + 7]
    normal, hidden, pre, cot, sgrad, bias_sum, gain_sum, shift_sum, cot_sum = refs[-9:]

    @pl.when(pl.program_id(0) == 0)
    def _():
        for ref in (bias_sum, gain_sum, shift_sum, cot_sum):
            ref[...] = jnp.zeros_like(ref)

    for k, piece in enumerate(cots):
        cot[pl.ds(place[k] * quarter, quarter), :] = piece[0]
    normed, rstd = column_norm(section[...].astype(F32).reshape(normal.shape))
    value = (normed * gain[...] + shift[...]).astype(BF)
    normal[...] = value
    wide = cot[...]
    part = we.shape[2]
    total = None
    for start in range(0, hidden.shape[0], chunk):
        rows = slice(start, start + chunk)
        before = dot(we_t[rows], value) + jnp.concatenate([bias[rows]] * (value.shape[1] // 128), axis=1)
        act, slope = gelu_pair(before)
        hidden[rows] = act.astype(BF)
        grad = (dot(wp[rows], wide) * slope).astype(BF)
        pre[rows] = grad
        bias_sum[rows] += fold_lanes(grad.astype(F32))
        t, at = start // part, start % part
        term = dot(we[t, :, at : at + chunk], grad)
        total = term if total is None else total + term
    gain_sum[...] += fold_lanes(total * normed)
    shift_sum[...] += fold_lanes(total)
    wide = wide.astype(F32)
    cot_sum[...] += fold_lanes(wide)
    scaled = total * gain[...]
    one = jnp.mean(scaled, axis=0, keepdims=True)
    two = jnp.mean(scaled * normed, axis=0, keepdims=True)
    grad = wide + rstd * (scaled - one - normed * two)
    sgrad[...] = grad.reshape(sgrad.shape).astype(BF)


def result_kernel(quarter, place, hidden, wp_t, bias, section, *refs):
    outs, field = refs[-5:-1], refs[-1]
    value = dot(wp_t[...], hidden[...]) + jnp.concatenate([bias[...]] * (hidden.shape[1] // 128), axis=1)
    field[...] = value + section[...].astype(F32).reshape(value.shape)
    for k, out in enumerate(outs):
        out[...] = field[pl.ds(place[k] * quarter, quarter), :].astype(BF)


def weight_sent_kernel(order, normal, pre, cot, hidden, out):
    out[0, 0] = dot(normal[...], pre[...], NT).astype(BF)
    out[0, 1] = dot(cot[...], hidden[...], NT).astype(BF)


def weight_kept_kernel(order, side, normal, pre, cot, hidden, came, expand_mine, expand_sent, project_mine, project_sent):
    expand = dot(normal[...], pre[...], NT) + came[0, 0].astype(F32)
    project = dot(cot[...], hidden[...], NT) + came[0, 1].astype(F32)

    @pl.when(pl.program_id(0) == 0)
    def _():
        expand_mine[...] = expand

    @pl.when(pl.program_id(0) == 1)
    def _():
        expand_sent[...] = expand.astype(BF)

    blocks = project_mine.shape[1]
    project = project.reshape(blocks, 2, project.shape[0] // (2 * blocks), project.shape[1])
    odd = side[0] == 1
    project_mine[0] = jnp.where(odd, project[:, 1], project[:, 0])
    project_sent[0] = jnp.where(odd, project[:, 0], project[:, 1]).astype(BF)


def widen_kernel(layout, slot, *refs):
    pieces, out = refs[:-1], refs[-1]
    width = out.shape[3]
    for piece, (k, start, n) in zip(pieces, layout):

        @pl.when(pl.program_id(0) == k)
        def _(piece=piece, start=start, n=n):
            for i in range(n):
                out[0, start + i] = piece[:, i * width : (i + 1) * width].astype(F32)


def finish_kernel(feats, grads, patches, mean, rstd, one, two, out):
    normed = (patches[0].astype(F32) - mean[0]) * rstd[0]
    out[0] = grads[0].astype(F32) - rstd[0] * (one[0] + normed * two[0]) * (1.0 / feats)


def whole(shape):
    return pl.BlockSpec(shape, lambda *_: (0,) * len(shape), pipeline_mode=pl.Buffered(1))


def fixed(shape):
    return pl.BlockSpec(shape, lambda *_: (0,) * len(shape))


def run(name, kernel, grid, ins, specs, outs, out_specs, scratch, mib, micros, scalars=(), aliases=None):
    grid_spec = pltpu.PrefetchScalarGridSpec(
        num_scalar_prefetch=len(scalars), grid=grid, in_specs=specs, out_specs=out_specs, scratch_shapes=scratch
    )
    call = pl.pallas_call(
        kernel,
        grid_spec=grid_spec,
        out_shape=outs,
        compiler_params=pltpu.CompilerParams(vmem_limit_bytes=mib << 20),
        input_output_aliases=aliases or {},
        cost_estimate=pl.CostEstimate(flops=int(micros * FLOPS), bytes_accessed=int(micros * BYTES), transcendentals=0),
        name=name,
    )
    return call(*scalars, *ins)


def complex_weight(pair):
    real, imag = pair[0].T, pair[1].T
    return jnp.concatenate([jnp.concatenate([real, -imag], 1), jnp.concatenate([imag, real], 1)], 0)


def weight_pair(full):
    full = full.reshape(2, BLOCK, 2, BLOCK)
    return jnp.stack([full[0, :, 0] + full[1, :, 1], full[0, :, 1] - full[1, :, 0]])


def per_device(
    sizes, patches, present, first_gain, first_shift, filter_inner, inner_bias, filter_outer, outer_bias,
    second_gain, second_shift, expand_weight, expand_bias, project_weight, project_bias, cotangent,
):
    planes, blocks_local, cut, tp = sizes
    inner = blocks_local * cut
    ranks = inner * tp
    owners = planes * inner
    snaps, per, quarter, width = patches.shape
    feats = quarter * tp
    mine = quarter // inner
    modes = width // 2
    rows = per * ranks
    toks = per * width
    hidden_local = expand_bias.shape[0]
    hiddens = hidden_local * tp
    z, y, j, t = (lax.axis_index(name) for name in ("z", "y", "j", "t"))
    r = y * cut + j
    me = z * inner + r
    every, sp = ("z", "y", "j", "t"), ("z", "y", "j")
    shape = jax.ShapeDtypeStruct

    pieces = patches.reshape(snaps, per, inner, mine, width).swapaxes(1, 2).reshape(owners, per, mine, width)
    pieces = lax.all_to_all(pieces, sp, 0, 0, tiled=True)

    def route(k, back):
        pairs = [
            ((zz * inner + rr) * tp + tt, (((swapped(tt) + k) % tp) * inner + rr) * tp + swapped(zz))
            for zz in range(planes)
            for rr in range(inner)
            for tt in range(tp)
        ]
        return [(b, a) for a, b in pairs] if back else pairs

    place = jnp.stack([swapped((z - k) % tp) for k in range(tp)]).astype(jnp.int32)
    slot = jnp.stack([(swapped(t) + k) % tp for k in range(tp)]).astype(jnp.int32)
    field = patches.astype(F32)
    mean = jnp.mean(field, 2)
    square = jnp.sum(jnp.square(field - mean[:, :, None]), 2)
    gathered = lax.all_gather(jnp.stack([mean, square]), "t")
    packed = lax.all_gather(jnp.concatenate([second_gain, second_shift, project_bias, expand_bias]), "t")
    small = [packed[:, i * quarter : (i + 1) * quarter].reshape(-1) for i in range(3)]
    bias_all = packed[:, 3 * quarter :].reshape(-1)
    mean = jnp.mean(gathered[:, 0], 0)
    square = jnp.sum(gathered[:, 1] + quarter * jnp.square(gathered[:, 0] - mean), 0)
    stats = jnp.stack([mean, lax.rsqrt(square / feats + NORM_EPS)], 2)
    plane_stats = []
    for k in range(owners):
        piece = lax.dynamic_index_in_dim(stats, (me ^ k) // inner, 0, False)
        plane_stats.append(lax.ppermute(piece, sp, [(a, a ^ k) for a in range(owners)]) if k else piece)
    plane_stats = jnp.stack(plane_stats)
    bit = 1
    while bit < owners:
        turned = plane_stats.reshape(-1, 2, bit, per, 2, width)
        plane_stats = jnp.where((me // bit) % 2 == 1, turned[:, ::-1], turned).reshape(owners, per, 2, width)
        bit *= 2
    plane_stats = swap_planes(plane_stats.reshape(rows, 2, 1, width))

    def lanes(vector, width=width):
        return jnp.broadcast_to(vector[:, None], (vector.shape[0], width))

    def own_features(vector):
        return lax.dynamic_slice_in_dim(vector, r * mine, mine)

    keep = own_features(lax.dynamic_index_in_dim(present, z, 0, False).astype(F32))
    scale1, shift1 = lanes(own_features(first_gain) * keep), lanes(own_features(first_shift) * keep)

    def own_block(array):
        return lax.dynamic_index_in_dim(array, y, 1, False)

    w1, w2 = complex_weight(own_block(filter_inner)), complex_weight(own_block(filter_outer))
    bias1 = lanes(own_block(inner_bias).reshape(-1), 2 * modes)
    bias2 = lanes(own_block(outer_bias).reshape(-1), 2 * modes)
    plain, weighted = lon_tables(width, modes)
    lat = lat_table(rows)
    plain_t, weighted_t, plain_n, weighted_n = (np_split(a) for a in (plain.T, weighted.T, plain, weighted))
    lat_f, lat_b = (jnp.concatenate(np_split(a)) for a in (lat, lat.T))

    we = lax.all_gather(expand_weight, "t")
    wp = lax.all_gather(project_weight, "t", tiled=True)
    we_t, wp_t = jnp.swapaxes(we, 1, 2).reshape(hiddens, feats), wp.T
    parts = [per // 2, per - per // 2]
    gain2, shift2, bias_lanes = lanes(small[0]), lanes(small[1]), lanes(bias_all, 128)
    cotangents = [
        [lax.dynamic_slice(cotangent, (slot[k], at, 0, 0), (1, n, quarter, width))[0] for k in range(tp)]
        for at, n in zip((0, parts[0]), parts)
    ]
    plane_stats, we, wp, we_t, wp_t, gain2, shift2, bias_lanes = lax.optimization_barrier(
        (plane_stats, we, wp, we_t, wp_t, gain2, shift2, bias_lanes)
    )
    mean_one, rstd_one = plane_stats[:, 0], plane_stats[:, 1]
    late, pieces = lax.optimization_barrier((cotangents, pieces))
    cots = [[lax.ppermute(piece, every, route(k, False)) for k, piece in enumerate(late[0])]]

    some = 16 if mine % 16 == 0 else mine
    grid = (mine // some,)
    piece_spec = pl.BlockSpec((owners, per, some, width), lambda g, *_: (0, 0, g, 0))
    stat_spec, feat_spec = whole((rows, 1, width)), pl.BlockSpec((some, width), lambda g, *_: (g, 0))
    lon_f, lon_b = [whole((width, 2 * modes))] * 2, [whole((2 * modes, width))] * 2
    lat_specs = [whole((4 * rows, 2 * rows))]
    image_spec = pl.BlockSpec((rows, some, width), lambda g, *_: (0, g, 0))
    modes_spec = pl.BlockSpec((2, rows, some, modes), lambda g, *_: (0, 0, g, 0))
    scratch = [
        pltpu.VMEM((2, rows * some, modes), F32),
        pltpu.VMEM((2 * rows * some, modes), F32),
    ]
    mine_modes = (2, rows, mine, modes)
    spec = run(
        "spectrum", spectrum_kernel, grid,
        (pieces, mean_one, rstd_one, scale1, shift1, *plain_t, lat_f),
        [piece_spec, stat_spec, stat_spec, feat_spec, feat_spec, *lon_f, *lat_specs],
        shape(mine_modes, BF), modes_spec, scratch, 48, 22,
    )

    def to_blocks(array):
        return lax.all_to_all(array, "j", 1, 2, tiled=True) if cut > 1 else array

    def to_features(array):
        return lax.all_to_all(array, "j", 2, 1, tiled=True) if cut > 1 else array

    spec = to_blocks(spec)
    lats = rows // cut
    step = 8
    block_modes = (2, lats, BLOCK, modes)
    block_spec = pl.BlockSpec((2, step, BLOCK, modes), lambda g: (0, g, 0, 0))
    square_spec, lane_spec = whole((2 * BLOCK, 2 * BLOCK)), whole((2 * BLOCK, 2 * modes))
    kept, mid, slope, bend, share = run(
        "filter", filter_kernel, (lats // step,), (spec, w1, bias1, w2, bias2),
        [block_spec, square_spec, lane_spec, square_spec, lane_spec],
        (shape(block_modes, F32), shape(block_modes, BF), shape(block_modes, F32), shape(block_modes, F32),
         shape((8, 2 * modes), F32)),
        (block_spec, block_spec, block_spec, block_spec, fixed((8, 2 * modes))), [], 48, 17,
    )
    kept, late, cots[0] = lax.optimization_barrier((kept, late, cots[0]))
    part_specs = [pl.BlockSpec((ranks, n, some, width), lambda g, *_: (0, 0, g, 0)) for n in parts]
    sections = run(
        "section", section_kernel, grid,
        (pieces, mean_one, rstd_one, scale1, shift1, to_features(kept), *weighted_n, lat_b),
        [piece_spec, stat_spec, stat_spec, feat_spec, feat_spec, modes_spec, *lon_b, *lat_specs],
        [shape((ranks, n, mine, width), BF) for n in parts], part_specs, scratch, 56, 17,
    )

    def exchange(array):
        return lax.all_to_all(array, ("t", "y", "j"), 0, 0, tiled=True)

    outs = (
        shape((feats, toks), BF), shape((hiddens, toks), BF), shape((hiddens, toks), BF), shape((feats, toks), BF),
    )
    sum_shapes = [shape((hiddens, 128), F32), *[shape((feats, 128), F32)] * 3]
    sgrads, sums, done, start = [], [], (), 0
    received, results = [], []
    early_rounds, late_rounds = (0, 2), (1, 3)
    for n, section in zip(parts, sections):
        section = exchange(section)
        if not received:
            section, late = lax.optimization_barrier((section, late))
            cots.append([lax.ppermute(piece, every, route(k, False)) for k, piece in enumerate(late[1])])
        tok_spec = pl.BlockSpec((feats, width), lambda h, *_, start=start: (0, h + start))
        hid_spec = pl.BlockSpec((hiddens, width), lambda h, *_, start=start: (0, h + start))
        cot_specs = [pl.BlockSpec((1, quarter, width), lambda h, *_: (h, 0, 0))] * tp
        line_spec = pl.BlockSpec((ranks, 1, mine, width), lambda h, *_: (0, h, 0, 0))
        any_spec = pl.BlockSpec(memory_space=pl.ANY)
        *done, sgrad, s0, s1, s2, s3 = run(
            "feed", functools.partial(feed_kernel, tp, quarter, min(512, hidden_local // 2)), (n,),
            (*cots[len(received)], section, we_t, wp, we, bias_lanes, gain2, shift2, *done),
            [*cot_specs, line_spec, whole((hiddens, feats)), whole((hiddens, feats)),
             whole((tp, feats, hidden_local)), whole((hiddens, 128)), whole((feats, width)), whole((feats, width)),
             *[any_spec] * len(done)],
            (*outs, shape((ranks, n, mine, width), BF), *sum_shapes),
            (tok_spec, hid_spec, hid_spec, tok_spec, line_spec, fixed((hiddens, 128)), *[fixed((feats, 128))] * 3),
            [], 60, 0.01 if start else 43, (place,), {8 + tp + i: i for i in range(len(done))},
        )
        if start:
            sgrad, done, results, sgrads = lax.optimization_barrier((sgrad, done, results, sgrads))
            third = hidden_local // 3
            resident = whole((feats, toks))
            hid_rows = pl.BlockSpec((third, toks), lambda k, i, o, *_: (o[k] * 3 + i, 0))
            both_cols = pl.BlockSpec((1, 2, feats, third), lambda k, i, *_: (k, 0, 0, i))
            normal, hidden, pre, cot = done
            products = (normal, pre, cot, hidden)
            product_specs = [resident, hid_rows, resident, hid_rows]
            sent = run(
                "weights_sent", weight_sent_kernel, (tp // 2, 3), products, product_specs,
                shape((tp // 2, 2, feats, hidden_local), BF), both_cols, [], 60, 0.01,
                (jnp.stack([t ^ k for k in range(1, tp, 2)]).astype(jnp.int32),),
            )
            came = lax.ppermute(sent, "t", [(a, a ^ 1) for a in range(tp)])
        part_out = shape((quarter, n * width), BF)
        rows_out = run(
            "result", functools.partial(result_kernel, quarter), (n,), (done[1], wp_t, lanes(small[2], 128), section),
            [hid_spec, whole((feats, hiddens)), whole((feats, 128)), line_spec],
            [part_out] * tp, [pl.BlockSpec((quarter, width), lambda h, *_: (0, h))] * tp,
            [pltpu.VMEM((feats, width), F32)], 48, 0.01 if start else 43, (place,),
        )
        sgrad = exchange(sgrad)
        if start:
            side = (me % 2).astype(jnp.int32).reshape(1)
            half_rows = owners // 2
            strip = feats // owners
            mine_cols = pl.BlockSpec((feats, third), lambda k, i, *_: (0, jnp.where(k == 0, i, 2)))
            sent_cols = pl.BlockSpec((feats, third), lambda k, i, *_: (0, jnp.where(k == 0, 0, i)))
            row_cols = pl.BlockSpec((1, half_rows, strip, third), lambda k, i, *_: (k, 0, 0, i))
            row_shape = (tp // 2, half_rows, strip, hidden_local)
            kept_products = run(
                "weights_kept", weight_kept_kernel, (tp // 2, 3), (*products, came), [*product_specs, both_cols],
                (shape((feats, hidden_local), F32), shape((feats, hidden_local), BF), shape(row_shape, F32),
                 shape(row_shape, BF)),
                (mine_cols, sent_cols, row_cols, row_cols), [], 60, 0.01,
                (jnp.stack([t ^ k for k in range(0, tp, 2)]).astype(jnp.int32), side),
            )
            sgrad, kept_products = lax.optimization_barrier((sgrad, kept_products))
        else:
            rows_out, done = lax.optimization_barrier((rows_out, done))
        results += [
            lax.ppermute(rows_out[k], every, route(k, True)) for k in (early_rounds if start else range(tp))
        ]
        sgrads.append(sgrad)
        sums.append((s0, s1, s2, s3))
        received.append(section)
        start += n
    bias_sum, gain_sum, shift_sum, cot_sum = (a + b for a, b in zip(*sums))

    def trade(theirs, axes, bit, size):
        return lax.ppermute(theirs, axes, [(a, a ^ bit) for a in range(size)])

    def halves(array, bit):
        other = 1 - (me // bit) % 2
        return lax.dynamic_index_in_dim(array, 1 - other, 0, False), lax.dynamic_index_in_dim(array, other, 0, False)

    expand_mine, expand_sent, project_mine, project_sent = kept_products
    first_came = [trade(expand_sent, "t", 2, tp), trade(project_sent, sp, 1, owners)]

    freq = run(
        "spectrum_back", functools.partial(spectrum_back_kernel, len(parts)), grid, (*sgrads, *weighted_t, lat_f),
        [*part_specs, *lon_f, *lat_specs], shape(mine_modes, F32), modes_spec, scratch, 48, 0.01,
    )
    freq, results, first_came, rows_out = lax.optimization_barrier((freq, results, first_came, rows_out))
    results += [lax.ppermute(rows_out[k], every, route(k, True)) for k in late_rounds]
    expand = expand_mine + first_came[0].astype(F32)
    project = project_mine + first_came[1].astype(F32)
    expand, theirs = halves(expand.reshape(half_rows, 2, strip, hidden_local).swapaxes(0, 1), 1)
    second_came = [trade(theirs.astype(BF), sp, 1, owners), trade(project[1].astype(BF), "t", 2, tp)]
    freq, inner_grad, outer_grad, inner_bias_grad, outer_bias_grad = run(
        "filter_back", filter_back_kernel, (lats // step,), (to_blocks(freq), spec, mid, slope, bend, w1, w2),
        [*[block_spec] * 5, square_spec, square_spec],
        (shape(block_modes, F32), *[shape((2 * BLOCK, 2 * BLOCK), F32)] * 2, *[shape((2 * BLOCK, 128), F32)] * 2),
        (block_spec, *[fixed((2 * BLOCK, 2 * BLOCK))] * 2, *[fixed((2 * BLOCK, 128))] * 2), [], 48, 0.01,
    )
    freq, second_came = lax.optimization_barrier((freq, second_came))
    expand = expand + second_came[0].astype(F32)
    project = project[0] + second_came[1].astype(F32)
    weights = jnp.stack([expand, project], 1)
    bit = 2
    while bit < inner:
        weights = weights.reshape(-1, 2, *weights.shape[1:])
        weights, theirs = halves(weights.swapaxes(0, 1), bit)
        weights = weights + trade(theirs.astype(BF), sp, bit, owners).astype(F32)
        bit *= 2
    weights = [lax.dynamic_index_in_dim(weights, z, 0, False)] + [
        trade(lax.dynamic_index_in_dim(weights, z ^ k, 0, False).astype(BF), "z", k, planes) for k in range(1, planes)
    ]
    grads, lines, first_gain_sum, first_shift_sum = run(
        "last", functools.partial(last_kernel, len(parts)), grid,
        (pieces, *sgrads, mean_one, rstd_one, scale1, to_features(freq), *plain_n, lat_b),
        [piece_spec, *part_specs, stat_spec, stat_spec, feat_spec, modes_spec, *lon_b, *lat_specs],
        (shape((rows, mine, width), BF), shape((rows, 2, width), F32), *[shape((mine, 128), F32)] * 2),
        (image_spec, fixed((rows, 2, width)), *[pl.BlockSpec((some, 128), lambda g, *_: (g, 0))] * 2),
        scratch, 56, 0.01,
    )
    def with_bias(full, bias):
        bias = jnp.sum(bias, 1).reshape(2, BLOCK)
        return jnp.concatenate([weight_pair(full), bias[:, :, None]], 2)

    filters = jnp.stack([with_bias(inner_grad, inner_bias_grad), with_bias(outer_grad, outer_bias_grad)])
    filters = jnp.moveaxis(filters, 2, 0).reshape(owners, -1)
    early = jnp.concatenate(
        [jnp.sum(gain_sum, 1), jnp.sum(shift_sum, 1), jnp.sum(cot_sum, 1), jnp.sum(bias_sum, 1), jnp.sum(share)[None]]
    )
    grads, lines, results, weights = lax.optimization_barrier((grads, lines, results, weights))
    expand_sum, project_sum = weights[0] + sum(piece.astype(F32) for piece in weights[1:])
    project_sum = project_sum.T
    line = per * width
    feature_sums = jnp.stack([jnp.sum(first_gain_sum, 1) * keep, jnp.sum(first_shift_sum, 1) * keep]).reshape(-1)
    tail = jnp.concatenate(
        [lines.reshape(owners, 2 * line), filters,
         jnp.broadcast_to(jnp.concatenate([feature_sums, early]), (owners, 2 * mine + early.shape[0]))], 1
    )
    tail = lax.all_to_all(tail, sp, 0, 0, tiled=True)
    tail, grads = lax.optimization_barrier((tail, grads))
    grads = lax.all_to_all(grads.reshape(owners, per, mine, width), sp, 0, 0, tiled=True)
    cuts = [2 * line, 2 * line + filters.shape[1], 2 * line + filters.shape[1] + 2 * mine]
    lines, filters, feature_sums, early = jnp.split(tail, cuts, axis=1)
    lines = jnp.sum(lines.reshape(planes, inner, -1), 1).reshape(-1)
    filters = jnp.sum(filters.reshape(planes, blocks_local, cut, BLOCK // owners, 2, 2, BLOCK + 1), (0, 2))
    filters = jnp.transpose(filters, (2, 3, 0, 1, 4))
    feature_sums = jnp.sum(feature_sums.reshape(planes, inner, 2, mine), 0).swapaxes(0, 1)
    spread = lax.dynamic_update_slice(
        jnp.zeros((2, tp, quarter), F32), feature_sums.reshape(2, 1, quarter), (0, t, 0)
    ).reshape(-1)
    tail = jnp.concatenate([lines, spread, jnp.sum(early, 0)])
    bit = 1
    while bit < tp:
        tail = tail + trade(tail, "t", bit, tp)
        bit *= 2
    cuts = [planes * 2 * line, planes * 2 * line + 2 * feats]
    lines, last, early = jnp.split(tail, cuts)
    fixes = lines.reshape(planes, per, 2, 1, width)
    last = last.reshape(2, feats)

    layout = [(k, 0, parts[0]) for k in range(tp)] + [(k, parts[0], parts[1]) for k in (*early_rounds, *late_rounds)]
    result = run(
        "widen", functools.partial(widen_kernel, layout), (tp,), results, [whole((quarter, n * width)) for _, _, n in layout],
        shape((snaps, per, quarter, width), F32),
        pl.BlockSpec((1, per, quarter, width), lambda i, s: (s[i], 0, 0, 0)), [], 32, 8, (slot,),
    )
    one_spec = pl.BlockSpec((1, per, 1, width), lambda i: (i // inner, 0, 0, 0))
    patch_spec = pl.BlockSpec((1, per, mine, width), lambda i: (i // inner, 0, i % inner, 0))
    patches_grad = run(
        "finish", functools.partial(finish_kernel, feats), (owners,),
        (grads, patches, stats[:, :, 0, None], stats[:, :, 1, None], fixes[:, :, 0], fixes[:, :, 1]),
        [pl.BlockSpec((1, per, mine, width), lambda i: (i, 0, 0, 0)), patch_spec, *[one_spec] * 4],
        shape((snaps, per, quarter, width), F32), patch_spec, [], 48, 11,
    )

    return (
        result, patches_grad, last[0], last[1], filters[0, ..., :BLOCK], filters[0, ..., BLOCK],
        filters[1, ..., :BLOCK], filters[1, ..., BLOCK],
        early[:feats], early[feats : 2 * feats], expand_sum, early[3 * feats : 3 * feats + hiddens],
        project_sum, early[2 * feats : 3 * feats], early[-1] / (snaps * rows * modes * feats * 2),
    )


def solution(mesh):
    tp = mesh.shape["tp"]
    planes = tp
    inner = mesh.shape["sp"] // planes
    blocks_local = 2
    cut = inner // blocks_local
    mesh = Mesh(mesh.devices.reshape(planes, blocks_local, cut, tp), ("z", "y", "j", "t"))
    sp = ("z", "y", "j")
    image = P(None, sp, "t", None)
    return jax.shard_map(
        functools.partial(per_device, (planes, blocks_local, cut, tp)),
        mesh=mesh,
        in_specs=(
            image, P(None, "t"), P("t"), P("t"),
            P(None, "t", None, None), P(None, "t", None), P(None, "t", None, None), P(None, "t", None),
            P("t"), P("t"), P(None, "t"), P("t"), P("t", None), P("t"), image,
        ),
        out_specs=(
            image, image, P(), P(),
            P(None, "t", sp, None), P(None, "t", sp), P(None, "t", sp, None), P(None, "t", sp),
            P(), P(), P(sp, "t"), P(), P("t", sp), P(), P(),
        ),
        check_vma=False,
    )
```

time: 794 us -> 760 us (0.957)
  starting transfers between devices: 208 us -> 111 us
  waiting for transfers between devices: 115 us -> 190 us
  blocking collectives: 0 us -> 38.1 us
  Pallas kernels: 325 us -> 297 us
  local copies, waits for them, and re-layouts: 78 us -> 60.9 us
    ppermute x31 -> x33, starting transfers between devices: 160 us -> 69.8 us  [the longest x8 17.1 us: per_device(): lax.ppermute(piece, every, route(k, False))]
    all_to_all x1, waiting for transfers between devices: 0.01 us -> 85.7 us  [per_device(): lax.all_to_all(grads.reshape(owners, per, mine, width), sp, 0, 0, tiled=T...]
    ppermute x31 -> x33, waiting for transfers between devices: 36.6 us -> 80.9 us  [the longest x7 55.1 us: per_device(): lax.ppermute(piece, sp, [(a, a ^ k) for a in range(owners)])]
    unnamed x6 -> x2, waiting for transfers between devices: 39.2 us -> 0.7 us
    all_to_all x2 -> x1, waiting for transfers between devices: 35.2 us -> 0.01 us  [per_device(): pieces = lax.all_to_all(pieces, sp, 0, 0, tiled=True)]
    pallas_call x12 -> x14, Pallas kernels: 325 us -> 297 us  [run(): return call(*scalars, *ins)]
    all_to_all x4, waiting for transfers between devices: 4.2 us -> 23.1 us  [exchange(): return lax.all_to_all(array, ('t', 'y', 'j'), 0, 0, tiled=True)]
    all_to_all x0 -> x1, blocking collectives: none -> 18.2 us  [per_device(): tail = lax.all_to_all(tail, sp, 0, 0, tiled=True)]
  transfers between devices with their start and end apart: 42 -> 41, of which waited for: 10 -> 9; matrix products, arithmetic and copies ran while one was open for 12% -> 10% of each run, Pallas kernels for 40% -> 33%
where the time goes in v3:
time: 760 us; the launch traced here: 749 us
  Pallas kernels  297 us (39%)
  waiting for transfers between devices  190 us (25%)
  starting transfers between devices  111 us (15%)
  local copies, waits for them, and re-layouts  60.9 us (8%)
  blocking collectives  38.1 us (5%)
  other arithmetic  32.9 us (4%)
  between operations  18.8 us (2%)
    pallas_call x14, Pallas kernels, run(): return call(*scalars, *ins)  297 us
    all_to_all x1, waiting for transfers between devices, per_device(): lax.all_to_all(grads.reshape(owners, per, mine, width), sp, 0, 0, tiled=T...  85.7 us
    ppermute x7, waiting for transfers between devices, per_device(): lax.ppermute(piece, sp, [(a, a ^ k) for a in range(owners)])  55.1 us
    all_to_all x4, starting transfers between devices, exchange(): return lax.all_to_all(array, ('t', 'y', 'j'), 0, 0, tiled=True)  29.8 us
    all_to_all x4, waiting for transfers between devices, exchange(): return lax.all_to_all(array, ('t', 'y', 'j'), 0, 0, tiled=True)  23.1 us
    ppermute x8, waiting for transfers between devices, per_device(): lax.ppermute(rows_out[k], every, route(k, True))  22.9 us
    all_to_all x1, blocking collectives, per_device(): tail = lax.all_to_all(tail, sp, 0, 0, tiled=True)  18.2 us
    unnamed x162, local copies, waits for them, and re-layouts  18.1 us
  transfers between devices with their start and end apart: 41, of which 9 were waited for; matrix products, arithmetic and copies ran while one was open for 10% of the time, Pallas kernels for 33%

profile of v3, /device:TPU:2, one launch (start us, length us, event | category | flops | bytes accessed | tf_op | source)
XLA Modules:
  0.0 749.0 jit_solution(7701028934371509465)
XLA Ops:
  7.9 2.8 fusion.38
  10.7 2.6 pad_maximum_fusion
  13.3 6.0 all-to-all-start
  20.9 3.3 convert_reduce_fusion
  24.3 4.2 fusion.1
  28.7 8.8 %all-gather = f32[8,4,12,256]{3,1,2,0:T(4,128)S(1)} all-gather(f32[2,4,12,256]{3,1,2,0:T(4,128)S(1)} %copy.272), channel_id=2, replica_groups=mesh['z'=4,'y'=2,'j'=1,'t'=4] {'t'}, dimensions={0}, use_global_device_ids=true | all-gather | bytes 491520 | tf_op jit(solution)/shard_map/all_gather | solution.py:412
  38.0 1.9 collective-permute-start
  40.0 1.5 collective-permute-start.1
  41.8 2.8 collective-permute-start.3
  47.8 11.1 %all-reduce = f32[5376]{0:T(1024)S(1)} all-reduce(f32[5376]{0:T(1024)S(1)} %dynamic-update-slice), channel_id=4, replica_groups=mesh['z'=4,'y'=2,'j'=1,'t'=4] {'t'}, use_global_device_ids=true, to_apply=%add | all-reduce | flops 5376 | bytes 43008
  60.4 4.7 dynamic-slice_bitcast_fusion
  65.4 3.3 collective-permute-start.5
  68.7 29.2 %collective-permute-done.1 = f32[12,2,256]{2,1,0:T(2,128)S(1)} collective-permute-done((f32[12,2,256]{2,1,0:T(2,128)S(1)}, f32[12,2,256]{2,1,0:T(2,128)S(1)}, u32[]{:S(2)}, u32[]{:S(2)}) %collective-permute-start.1) | collective-permute-done | bytes 24608 | tf_op jit(solution)/shard_map/ppermute | solution.py:422
  97.9 3.7 collective-permute-start.6
  102.4 24.7 %collective-permute-done.3 = f32[12,2,256]{2,1,0:T(2,128)S(1)} collective-permute-done((f32[12,2,256]{2,1,0:T(2,128)S(1)}, f32[12,2,256]{2,1,0:T(2,128)S(1)}, u32[]{:S(2)}, u32[]{:S(2)}) %collective-permute-start.3) | collective-permute-done | bytes 24608 | tf_op jit(solution)/shard_map/ppermute | solution.py:422
  129.8 6.6 copy.295
  138.6 1.6 broadcast_in_dim.73.refs_8_
  140.4 2.9 collective-permute-start.7
  143.4 3.5 collective-permute-start.9
  147.4 19.6 %spectrum.1.spec = bf16[2,96,96,128]{3,2,1,0:T(8,128)(2,1)S(1)} custom-call(bf16[8,12,96,256]{3,2,1,0:T(8,128)(2,1)} %all-to-all-done.pieces, f32[96,1,256]{2,1,0:T(1,128)S(1)} %get-tuple-element.363.mean.refs_2_, f32[96,1,256]{2,1,0:T(1,128)S(1)} %get-tuple-element.362.rstd.refs_3_, f32[96,256]{1,0:T(8,128)S(1)} %broadcast_in_dim.74.scale.refs_4_, ...), custom_call_target="tpu_custom_call" | custom-call | flops 22000001024 | bytes 74800000 | tf_op jit(solution)/shard_map/spectrum/pallas_call | solution.py:360
  167.0 2.1 copy-done.2
  169.3 17.3 %filter.1 = (f32[2,96,96,128]{3,2,1,0:T(8,128)}, bf16[2,96,96,128]{3,2,1,0:T(8,128)(2,1)S(1)}, f32[2,96,96,128]{3,2,1,0:T(8,128)}, f32[2,96,96,128]{3,2,1,0:T(8,128)}, f32[8,256]{1,0:T(8,128)S(1)}) custom-call(bf16[2,96,96,128]{3,2,1,0:T(8,128)(2,1)} %copy-done.2, bf16[192,192]{1,0:T(8,128)(2,1)S(1)} %maximum_maximum_fusion.w1, ...), custom_call_target="tpu_custom_call" | custom-call | flops 16999999488 | bytes 57800000 | tf_op jit(solution)/shard_map/filter/pallas_call | solution.py:360
  186.6 2.1 copy-done.3
  190.8 16.2 %section.1 = (bf16[8,6,96,256]{3,2,1,0:T(8,128)(2,1)}, bf16[8,6,96,256]{3,2,1,0:T(8,128)(2,1)}) custom-call(bf16[8,12,96,256]{3,2,1,0:T(8,128)(2,1)} %all-to-all-done.pieces, f32[96,1,256]{2,1,0:T(1,128)} %copy-done.12, f32[96,1,256]{2,1,0:T(1,128)} %copy-done.11, f32[96,256]{1,0:T(8,128)} %copy-done.6, f32[96,256]{1,0:T(8,128)} %copy-done.17, ...), custom_call_target="tpu_custom_call" | custom-call | flops 16999999488 | bytes 57800000 | tf_op jit(solution)/shard_map/section/pallas_call | solution.py:360
  207.0 8.8 %all-to-all-start.1 = ((bf16[8,6,96,256]{3,2,1,0:T(8,128)(2,1)}), bf16[8,6,96,256]{3,2,1,0:T(8,128)(2,1)S(1)}, u32[]{:S(2)}, u32[]{:S(2)}) async-start(bf16[8,6,96,256]{3,2,1,0:T(8,128)(2,1)} %get-tuple-element.157), calls=%async_computation.1 | async-start | bytes 4718592 | tf_op jit(solution)/shard_map/all_to_all | solution.py:516
  216.5 6.6 copy.299.refs_6_
  223.1 20.2 %all-to-all-done.1.refs_4_.section = bf16[8,6,96,256]{3,2,1,0:T(8,128)(2,1)S(1)} async-done(((bf16[8,6,96,256]{3,2,1,0:T(8,128)(2,1)}), bf16[8,6,96,256]{3,2,1,0:T(8,128)(2,1)S(1)}, u32[]{:S(2)}, u32[]{:S(2)}) %all-to-all-start.1) | async-done | bytes 2359328 | tf_op jit(solution)/shard_map/all_to_all | solution.py:516
  244.7 5.0 all-to-all-start.2
  249.7 2.9 collective-permute-start.11
  254.1 5.6 collective-permute-start.13
  260.1 48.0 %feed.2 = (bf16[768,3072]{1,0:T(8,128)(2,1)}, bf16[3072,3072]{1,0:T(8,128)(2,1)}, bf16[3072,3072]{1,0:T(8,128)(2,1)}, bf16[768,3072]{1,0:T(8,128)(2,1)}, bf16[8,...) custom-call(s32[4]{0:T(128)} %pad_add_fusion.1.place, ...), custom_call_target="tpu_custom_call" | custom-call | flops 43000000512 | bytes 146200000 | tf_op jit(solution)/shard_map/feed/pallas_call | solution.py:360
  309.5 4.8 all-to-all-start.3
  314.5 1.7 copy-done.5
  316.2 13.0 %result.2 = (bf16[192,1536]{1,0:T(8,128)(2,1)}, bf16[192,1536]{1,0:T(8,128)(2,1)}, bf16[192,1536]{1,0:T(8,128)(2,1)}, bf16[192,1536]{1,0:T(8,128)(2,1)S(1)}) custom-call(s32[4]{0:T(128)S(1)} %copy-done.18, bf16[3072,3072]{1,0:T(8,128)(2,1)} %get-tuple-element.188.hidden.refs_12_, bf16[768,3072]{1,0:T(8,128)(2,1)} %bitcast.222, ...), custom_call_target="tpu_custom_call" | custom-call | flops 43000000512 | bytes 146200000 | tf_op jit(solution)/shard_map/result/pallas_call | solution.py:360
  329.2 2.7 collective-permute-start.15
  334.0 2.6 collective-permute-start.18
  337.2 47.8 %feed.3 = (bf16[768,3072]{1,0:T(8,128)(2,1)}, bf16[3072,3072]{1,0:T(8,128)(2,1)}, bf16[3072,3072]{1,0:T(8,128)(2,1)}, bf16[768,3072]{1,0:T(8,128)(2,1)}, bf16[8,...) custom-call(s32[4]{0:T(128)} %pad_add_fusion.1.place, ...), custom_call_target="tpu_custom_call", output_to_operand_aliasing={{0}: (12, {}), {1}: (13, {}), {2}: (14, {}), {3}: (15, {})} | custom-call | flops 10000000 | bytes 34000 | tf_op jit(solution)/shard_map/feed/pallas_call | solution.py:360
  385.0 7.2 collective-permute-done.15.refs_0_
  392.3 22.3 %weights_sent.1 = bf16[2,2,768,768]{3,2,1,0:T(8,128)(2,1)} custom-call(s32[2]{0:T(128)} %pad_add_fusion.3.order, bf16[768,3072]{1,0:T(8,128)(2,1)} %get-tuple-element.203.normal, bf16[3072,3072]{1,0:T(8,128)(2,1)} %get-tuple-element.204.pre, bf16[768,3072]{1,0:T(8,128)(2,1)} %get-tuple-element.205.cot, bf16[3072,3072]{1,0:T(8,128)(2,1)} %get-tuple-element.206.hidden), custom_call_target="tpu_custom_call" | custom-call | flops 10000000 | bytes 34000 | tf_op jit(solution)/shard_map/weights_sent/pallas_call | solution.py:360
  414.6 12.5 %collective-permute-start.19 = (bf16[2,2,768,768]{3,2,1,0:T(8,128)(2,1)}, bf16[2,2,768,768]{3,2,1,0:T(8,128)(2,1)}, u32[]{:S(2)}, u32[]{:S(2)}) collective-permute-start(bf16[2,2,768,768]{3,2,1,0:T(8,128)(2,1)} %weights_sent.1), channel_id=1, source_target_pairs={{0,1},{1,0},{2,3},{3,2},{4,5},{5,4},{6,7},{7,6},{8,9},{9,8},{10,11... | collective-permute-start | bytes 14155784 | tf_op jit(solution)/shard_map/ppermute | solution.py:559
  427.0 11.2 %all-to-all-start.4 = ((bf16[8,6,96,256]{3,2,1,0:T(8,128)(2,1)}), bf16[8,6,96,256]{3,2,1,0:T(8,128)(2,1)}, u32[]{:S(2)}, u32[]{:S(2)}) async-start(bf16[8,6,96,256]{3,2,1,0:T(8,128)(2,1)} %get-tuple-element.202), calls=%async_computation.4 | async-start | bytes 4718592 | tf_op jit(solution)/shard_map/all_to_all | solution.py:516
  438.8 24.5 %weights_kept.1 = (f32[768,768]{1,0:T(8,128)}, bf16[768,768]{1,0:T(8,128)(2,1)}, f32[2,4,96,768]{3,2,1,0:T(8,128)}, bf16[2,4,96,768]{3,2,1,0:T(8,128)(2,1)}) custom-call(s32[2]{0:T(128)} %pad_add_fusion.2.order, s32[1]{0:T(128)} %bitcast.65.side, bf16[768,3072]{1,0:T(8,128)(2,1)} %get-tuple-element.203.normal, bf16[3072,3072]{1,0:T(8,128)(2,1)} %get-tuple-element.204.pre, ...), custom_call_target="tpu_custom_call" | custom-call | flops 10000000 | bytes 34000 | tf_op jit(solution)/shard_map/weights_kept/pallas_call | solution.py:360
  463.3 2.9 all-to-all-done.4.refs_1_
  469.0 13.4 %result.3 = (bf16[192,1536]{1,0:T(8,128)(2,1)S(1)}, bf16[192,1536]{1,0:T(8,128)(2,1)}, bf16[192,1536]{1,0:T(8,128)(2,1)S(1)}, bf16[192,1536]{1,0:T(8,128)(2,1)}) custom-call(s32[4]{0:T(128)S(1)} %copy-done.19, bf16[3072,3072]{1,0:T(8,128)(2,1)} %get-tuple-element.206.hidden, bf16[768,3072]{1,0:T(8,128)(2,1)} %bitcast.223, ...), custom_call_target="tpu_custom_call" | custom-call | flops 10000000 | bytes 34000 | tf_op jit(solution)/shard_map/result/pallas_call | solution.py:360
  482.4 2.3 collective-permute-start.20
  486.5 17.4 %spectrum_back.1.freq = f32[2,96,96,128]{3,2,1,0:T(8,128)} custom-call(bf16[8,6,96,256]{3,2,1,0:T(8,128)(2,1)} %all-to-all-done.3.refs_0_, bf16[8,6,96,256]{3,2,1,0:T(8,128)(2,1)} %all-to-all-done.4.refs_1_, bf16[256,256]{1,0:T(8,128)(2,1)S(1)} %copy-done.15, bf16[256,256]{1,0:T(8,128)(2,1)S(1)} %copy-done.16, bf16[384,192]{1,0:T(8,128)(2,1)S(1)} %copy-done.14), custom_call_target="tpu_custom_call" | custom-call | flops 10000000 | bytes 34000 | tf_op jit(solution)/shard_map/spectrum_back/pallas_call | solution.py:360
  503.9 15.7 %collective-permute-done.20.refs_4_ = bf16[192,1536]{1,0:T(8,128)(2,1)S(1)} collective-permute-done((bf16[192,1536]{1,0:T(8,128)(2,1)S(1)}, bf16[192,1536]{1,0:T(8,128)(2,1)S(1)}, u32[]{:S(2)}, u32[]{:S(2)}) %collective-permute-start.20) | collective-permute-done | bytes 589856 | tf_op jit(solution)/shard_map/ppermute | solution.py:587
  519.7 1.7 convert_add_fusion.1
  526.2 6.4 collective-permute-start.27
  532.7 21.9 %filter_back.1 = (f32[2,96,96,128]{3,2,1,0:T(8,128)}, f32[192,192]{1,0:T(8,128)S(1)}, f32[192,192]{1,0:T(8,128)S(1)}, f32[192,128]{1,0:T(8,128)S(1)}, f32[192,128]{1,0:T(8,128)S(1)}) custom-call(f32[2,96,96,128]{3,2,1,0:T(8,128)} %spectrum_back.1.freq, bf16[2,96,96,128]{3,2,1,0:T(8,128)(2,1)S(1)} %bitcast.215, bf16[2,96,96,128]{3,2,1,0:T(8,128)(2,1)} %copy-done.3, ...), custom_call_target="tpu_custom_call" | custom-call | flops 10000000 | bytes 34000 | tf_op jit(solution)/shard_map/filter_back/pallas_call | solution.py:360
  557.2 1.7 fusion.3
  559.4 1.6 fusion.4
  562.0 2.3 collective-permute-start.29
  564.3 2.0 collective-permute-start.30
  566.3 20.9 %last.1 = (bf16[96,96,256]{2,1,0:T(8,128)(2,1)}, f32[96,2,256]{2,1,0:T(2,128)}, f32[96,128]{1,0:T(8,128)}, f32[96,128]{1,0:T(8,128)}) custom-call(bf16[8,12,96,256]{3,2,1,0:T(8,128)(2,1)} %all-to-all-done.pieces, bf16[8,6,96,256]{3,2,1,0:T(8,128)(2,1)} %all-to-all-done.3.refs_0_, bf16[8,6,96,256]{3,2,1,0:T(8,128)(2,1)} %all-to-all-done.4.refs_1_, ...), custom_call_target="tpu_custom_call" | custom-call | flops 10000000 | bytes 34000 | tf_op jit(solution)/shard_map/last/pallas_call | solution.py:360
  592.1 2.0 concatenate.57
  594.2 1.9 fusion.10
  599.6 18.2 %all_to_all.42 = f32[8,1,16369]{2,1,0:T(1,128)S(1)} all-to-all(f32[8,1,16369]{2,1,0:T(1,128)S(1)} %all_to_all.31), channel_id=1, replica_groups=mesh['z'=4,'y'=2,'j'=1,'t'=4] {'z','y','j'}, dimensions={0} | all-to-all | bytes 1047616 | tf_op jit(solution)/shard_map/all_to_all | solution.py:660
  618.9 5.0 all-to-all-start.6
  624.2 1.6 add_add_fusion
  627.8 4.5 widen.1
  639.1 2.8 collective-permute-done.32
  644.5 85.7 %all-to-all-done.6.grads = bf16[8,12,96,256]{3,2,1,0:T(8,128)(2,1)} async-done(((bf16[8,12,96,256]{3,2,1,0:T(8,128)(2,1)}), bf16[8,12,96,256]{3,2,1,0:T(8,128)(2,1)}, u32[]{:S(2)}, u32[]{:S(2)}) %all-to-all-start.6) | async-done | bytes 4718624 | tf_op jit(solution)/shard_map/all_to_all | solution.py:662
  730.1 10.4 %finish.1 = f32[4,12,192,256]{3,2,1,0:T(8,128)} custom-call(bf16[8,12,96,256]{3,2,1,0:T(8,128)(2,1)} %all-to-all-done.6.grads, bf16[4,12,192,256]{3,2,1,0:T(8,128)(2,1)} %patches.1, f32[4,12,1,256]{3,2,1,0:T(1,128)S(1)} %copy.314.mean, f32[4,12,1,256]{3,2,1,0:T(1,128)S(1)} %copy.315.rstd, f32[4,12,1,256]{3,2,1,0:T(1,128)S(1)} %get-tuple-element.370.one, ...), custom_call_target="tpu_custom_call" | custom-call | flops 11000000512 | bytes 37400000 | tf_op jit(solution)/shard_map/finish/pallas_call | solution.py:360
  (341 shorter events, 57.8 us)
Async XLA Ops:
  7.2 122.6 %all-gather.8.cloned.1.call-start = ((), (), s32[]{:S(2)}) async-start(), calls=%async_computation.8 | async-start | bytes 5898240 | tf_op jit(solution)/shard_map/all_gather | solution.py:451
  13.3 127.1 %all-to-all-start = ((bf16[8,12,96,256]{3,2,1,0:T(8,128)(2,1)}), bf16[8,12,96,256]{3,2,1,0:T(8,128)(2,1)}, u32[]{:S(2)}, u32[]{:S(2)}) async-start(bf16[8,12,96,256]{3,2,1,0:T(8,128)(2,1)} %bitcast.221), calls=%async_computation | async-start | bytes 9437184 | tf_op jit(solution)/shard_map/all_to_all | solution.py:396
  19.3 117.2 %all-gather.6.cloned.1.call-start = ((), (), s32[]{:S(2)}) async-start(), calls=%async_computation.7 | async-start | bytes 5898240 | tf_op jit(solution)/shard_map/all_gather | solution.py:452
  28.5 30.5 %copy-start.56 = (bf16[2,2,96,96]{3,2,1,0:T(8,128)(2,1)S(1)}, bf16[2,2,96,96]{3,2,1,0:T(8,128)(2,1)}, u32[]{:S(2)}) copy-start(bf16[2,2,96,96]{3,2,1,0:T(8,128)(2,1)} %param.33) | copy-start | bytes 221188
  28.5 30.4 %copy-start.57 = (bf16[2,2,96,96]{3,2,1,0:T(8,128)(2,1)S(1)}, bf16[2,2,96,96]{3,2,1,0:T(8,128)(2,1)}, u32[]{:S(2)}) copy-start(bf16[2,2,96,96]{3,2,1,0:T(8,128)(2,1)} %param.31) | copy-start | bytes 221188
  28.6 30.8 %copy-start.66 = (f32[192]{0:T(256)S(1)}, f32[192]{0:T(256)}, u32[]{:S(2)}) copy-start(f32[192]{0:T(256)} %param.30) | copy-start | bytes 2308
  28.6 31.6 %copy-start.67 = (f32[192]{0:T(256)S(1)}, f32[192]{0:T(256)}, u32[]{:S(2)}) copy-start(f32[192]{0:T(256)} %param.29) | copy-start | bytes 2308
  37.8 27.2 %copy-start.44 = (f32[4,12,1,256]{3,0,1,2:T(4,128)}, f32[4,12,1,256]{3,0,1,2:T(4,128)S(1)}, u32[]{:S(2)}) copy-start(f32[4,12,1,256]{3,0,1,2:T(4,128)S(1)} %get-tuple-element.394) | copy-start | bytes 147460
  37.8 27.2 %copy-start.46 = (f32[4,12,1,256]{3,0,1,2:T(4,128)}, f32[4,12,1,256]{3,0,1,2:T(4,128)S(1)}, u32[]{:S(2)}) copy-start(f32[4,12,1,256]{3,0,1,2:T(4,128)S(1)} %get-tuple-element.395) | copy-start | bytes 147460
  38.0 27.3 %collective-permute-start = (f32[12,2,256]{2,1,0:T(2,128)S(1)}, f32[12,2,256]{2,1,0:T(2,128)S(1)}, u32[]{:S(2)}, u32[]{:S(2)}) collective-permute-start(f32[12,2,256]{2,1,0:T(2,128)S(1)} %bitcast.264), channel_id=1, source_target_pairs={{0,4},{4,0},{8,12},{12,8},{16,20},{20,16},{24,28},{28,24},{1,5},{5... | collective-permute-start | bytes 73736 | tf_op jit(solution)/shard_map/ppermute | solution.py:422
  40.0 58.0 %collective-permute-start.1 = (f32[12,2,256]{2,1,0:T(2,128)S(1)}, f32[12,2,256]{2,1,0:T(2,128)S(1)}, u32[]{:S(2)}, u32[]{:S(2)}) collective-permute-start(f32[12,2,256]{2,1,0:T(2,128)S(1)} %bitcast.263), channel_id=1, source_target_pairs={{0,8},{4,12},{8,0},{12,4},{16,24},{20,28},{24,16},{28,20},{1,9},{5... | collective-permute-start | bytes 73736 | tf_op jit(solution)/shard_map/ppermute | solution.py:422
  41.5 60.8 %collective-permute-start.2 = (f32[12,2,256]{2,1,0:T(2,128)S(1)}, f32[12,2,256]{2,1,0:T(2,128)S(1)}, u32[]{:S(2)}, u32[]{:S(2)}) collective-permute-start(f32[12,2,256]{2,1,0:T(2,128)S(1)} %bitcast.257), channel_id=1, source_target_pairs={{0,12},{4,8},{8,4},{12,0},{16,28},{20,24},{24,20},{28,16},{1,13},{... | collective-permute-start | bytes 73736 | tf_op jit(solution)/shard_map/ppermute | solution.py:422
  41.8 85.3 %collective-permute-start.3 = (f32[12,2,256]{2,1,0:T(2,128)S(1)}, f32[12,2,256]{2,1,0:T(2,128)S(1)}, u32[]{:S(2)}, u32[]{:S(2)}) collective-permute-start(f32[12,2,256]{2,1,0:T(2,128)S(1)} %bitcast.259), channel_id=1, source_target_pairs={{0,16},{4,20},{8,24},{12,28},{16,0},{20,4},{24,8},{28,12},{1,17},{... | collective-permute-start | bytes 73736 | tf_op jit(solution)/shard_map/ppermute | solution.py:422
  44.7 83.6 %collective-permute-start.4 = (f32[12,2,256]{2,1,0:T(2,128)S(1)}, f32[12,2,256]{2,1,0:T(2,128)S(1)}, u32[]{:S(2)}, u32[]{:S(2)}) collective-permute-start(f32[12,2,256]{2,1,0:T(2,128)S(1)} %bitcast.261), channel_id=1, source_target_pairs={{0,20},{4,16},{8,28},{12,24},{16,4},{20,0},{24,12},{28,8},{1,21},{... | collective-permute-start | bytes 73736 | tf_op jit(solution)/shard_map/ppermute | solution.py:422
  60.3 41.7 %copy-start.64 = (f32[2,2,96]{2,1,0:T(2,128)S(1)}, f32[2,2,96]{2,1,0:T(2,128)}, u32[]{:S(2)}) copy-start(f32[2,2,96]{2,1,0:T(2,128)} %param.32) | copy-start | bytes 4612
  60.4 41.7 %copy-start.65 = (f32[2,2,96]{2,1,0:T(2,128)S(1)}, f32[2,2,96]{2,1,0:T(2,128)}, u32[]{:S(2)}) copy-start(f32[2,2,96]{2,1,0:T(2,128)} %param.34) | copy-start | bytes 4612
  65.2 104.1 %copy-start.7 = (bf16[192,192]{1,0:T(8,128)(2,1)}, bf16[192,192]{1,0:T(8,128)(2,1)S(1)}, u32[]{:S(2)}) copy-start(bf16[192,192]{1,0:T(8,128)(2,1)S(1)} %maximum_maximum_fusion.w1) | copy-start | bytes 221188
  65.4 63.0 %collective-permute-start.5 = (f32[12,2,256]{2,1,0:T(2,128)S(1)}, f32[12,2,256]{2,1,0:T(2,128)S(1)}, u32[]{:S(2)}, u32[]{:S(2)}) collective-permute-start(f32[12,2,256]{2,1,0:T(2,128)S(1)} %bitcast.266), channel_id=1, source_target_pairs={{0,24},{4,28},{8,16},{12,20},{16,8},{20,12},{24,0},{28,4},{1,25},{... | collective-permute-start | bytes 73736 | tf_op jit(solution)/shard_map/ppermute | solution.py:422
  97.9 30.4 %collective-permute-start.6 = (f32[12,2,256]{2,1,0:T(2,128)S(1)}, f32[12,2,256]{2,1,0:T(2,128)S(1)}, u32[]{:S(2)}, u32[]{:S(2)}) collective-permute-start(f32[12,2,256]{2,1,0:T(2,128)S(1)} %bitcast.265), channel_id=1, source_target_pairs={{0,28},{4,24},{8,20},{12,16},{16,12},{20,8},{24,4},{28,0},{1,29},{... | collective-permute-start | bytes 73736 | tf_op jit(solution)/shard_map/ppermute | solution.py:422
  101.8 67.5 %copy-start.9 = (bf16[192,192]{1,0:T(8,128)(2,1)}, bf16[192,192]{1,0:T(8,128)(2,1)S(1)}, u32[]{:S(2)}) copy-start(bf16[192,192]{1,0:T(8,128)(2,1)S(1)} %maximum_maximum_fusion.1.w2) | copy-start | bytes 221188
  140.4 26.5 %copy-start.11 = (f32[96,1,256]{2,1,0:T(1,128)}, f32[96,1,256]{2,1,0:T(1,128)S(1)}, u32[]{:S(2)}) copy-start(f32[96,1,256]{2,1,0:T(1,128)S(1)} %get-tuple-element.362.rstd.refs_3_) | copy-start | bytes 294916
  140.4 26.5 %copy-start.12 = (f32[96,1,256]{2,1,0:T(1,128)}, f32[96,1,256]{2,1,0:T(1,128)S(1)}, u32[]{:S(2)}) copy-start(f32[96,1,256]{2,1,0:T(1,128)S(1)} %get-tuple-element.363.mean.refs_2_) | copy-start | bytes 294916
  140.4 48.3 %collective-permute-start.7 = (bf16[6,192,256]{2,1,0:T(8,128)(2,1)S(1)}, bf16[6,192,256]{2,1,0:T(8,128)(2,1)S(1)}, u32[]{:S(2)}, u32[]{:S(2)}) collective-permute-start(bf16[6,192,256]{2,1,0:T(8,128)(2,1)S(1)} %get-tuple-element.148), channel_id=1, source_target_pairs={{0,0},{1,16},{2,8},{3,24},{4,4},{5,20},{6,12},{7,28},{8,2},{9,18},... | collective-permute-start | bytes 1769480 | tf_op jit(solution)/shard_map/ppermute | solution.py:465
  143.3 45.4 %collective-permute-start.8 = (bf16[6,192,256]{2,1,0:T(8,128)(2,1)S(1)}, bf16[6,192,256]{2,1,0:T(8,128)(2,1)S(1)}, u32[]{:S(2)}, u32[]{:S(2)}) collective-permute-start(bf16[6,192,256]{2,1,0:T(8,128)(2,1)S(1)} %get-tuple-element.149), channel_id=1, source_target_pairs={{0,8},{1,24},{2,16},{3,0},{4,12},{5,28},{6,20},{7,4},{8,10},{9,26}... | collective-permute-start | bytes 1769480 | tf_op jit(solution)/shard_map/ppermute | solution.py:465
  143.4 45.3 %collective-permute-start.9 = (bf16[6,192,256]{2,1,0:T(8,128)(2,1)S(1)}, bf16[6,192,256]{2,1,0:T(8,128)(2,1)S(1)}, u32[]{:S(2)}, u32[]{:S(2)}) collective-permute-start(bf16[6,192,256]{2,1,0:T(8,128)(2,1)S(1)} %get-tuple-element.150), channel_id=1, source_target_pairs={{0,16},{1,0},{2,24},{3,8},{4,20},{5,4},{6,28},{7,12},{8,18},{9,2},... | collective-permute-start | bytes 1769480 | tf_op jit(solution)/shard_map/ppermute | solution.py:465
  146.9 41.8 %collective-permute-start.10 = (bf16[6,192,256]{2,1,0:T(8,128)(2,1)S(1)}, bf16[6,192,256]{2,1,0:T(8,128)(2,1)S(1)}, u32[]{:S(2)}, u32[]{:S(2)}) collective-permute-start(bf16[6,192,256]{2,1,0:T(8,128)(2,1)S(1)} %get-tuple-element.151), channel_id=1, source_target_pairs={{0,24},{1,8},{2,0},{3,16},{4,28},{5,12},{6,4},{7,20},{8,26},{9,10}... | collective-permute-start | bytes 1769480 | tf_op jit(solution)/shard_map/ppermute | solution.py:465
  147.2 19.7 %copy-start.6 = (f32[96,256]{1,0:T(8,128)}, f32[96,256]{1,0:T(8,128)S(1)}, u32[]{:S(2)}) copy-start(f32[96,256]{1,0:T(8,128)S(1)} %broadcast_in_dim.74.scale.refs_4_) | copy-start | bytes 294916
  207.0 36.3 %all-to-all-start.1 = ((bf16[8,6,96,256]{3,2,1,0:T(8,128)(2,1)}), bf16[8,6,96,256]{3,2,1,0:T(8,128)(2,1)S(1)}, u32[]{:S(2)}, u32[]{:S(2)}) async-start(bf16[8,6,96,256]{3,2,1,0:T(8,128)(2,1)} %get-tuple-element.157), calls=%async_computation.1 | async-start | bytes 4718592 | tf_op jit(solution)/shard_map/all_to_all | solution.py:516
  244.7 63.4 %all-to-all-start.2 = ((bf16[8,6,96,256]{3,2,1,0:T(8,128)(2,1)}), bf16[8,6,96,256]{3,2,1,0:T(8,128)(2,1)S(1)}, u32[]{:S(2)}, u32[]{:S(2)}) async-start(bf16[8,6,96,256]{3,2,1,0:T(8,128)(2,1)} %get-tuple-element.166), calls=%async_computation.2 | async-start | bytes 4718592 | tf_op jit(solution)/shard_map/all_to_all | solution.py:516
  249.7 82.3 %collective-permute-start.11 = (bf16[6,192,256]{2,1,0:T(8,128)(2,1)}, bf16[6,192,256]{2,1,0:T(8,128)(2,1)S(1)}, u32[]{:S(2)}, u32[]{:S(2)}) collective-permute-start(bf16[6,192,256]{2,1,0:T(8,128)(2,1)} %get-tuple-element.162), channel_id=1, source_target_pairs={{0,0},{1,16},{2,8},{3,24},{4,4},{5,20},{6,12},{7,28},{8,2},{9,18},... | collective-permute-start | bytes 1769480 | tf_op jit(solution)/shard_map/ppermute | solution.py:529
  252.6 80.2 %collective-permute-start.12 = (bf16[6,192,256]{2,1,0:T(8,128)(2,1)}, bf16[6,192,256]{2,1,0:T(8,128)(2,1)S(1)}, u32[]{:S(2)}, u32[]{:S(2)}) collective-permute-start(bf16[6,192,256]{2,1,0:T(8,128)(2,1)} %get-tuple-element.163), channel_id=1, source_target_pairs={{0,8},{1,24},{2,16},{3,0},{4,12},{5,28},{6,20},{7,4},{8,10},{9,26}... | collective-permute-start | bytes 1769480 | tf_op jit(solution)/shard_map/ppermute | solution.py:529
  254.1 79.9 %collective-permute-start.13 = (bf16[6,192,256]{2,1,0:T(8,128)(2,1)}, bf16[6,192,256]{2,1,0:T(8,128)(2,1)}, u32[]{:S(2)}, u32[]{:S(2)}) collective-permute-start(bf16[6,192,256]{2,1,0:T(8,128)(2,1)} %get-tuple-element.164), channel_id=1, source_target_pairs={{0,16},{1,0},{2,24},{3,8},{4,20},{5,4},{6,28},{7,12},{8,18},{9,2},... | collective-permute-start | bytes 1769480 | tf_op jit(solution)/shard_map/ppermute | solution.py:529
  259.7 77.4 %collective-permute-start.14 = (bf16[6,192,256]{2,1,0:T(8,128)(2,1)}, bf16[6,192,256]{2,1,0:T(8,128)(2,1)}, u32[]{:S(2)}, u32[]{:S(2)}) collective-permute-start(bf16[6,192,256]{2,1,0:T(8,128)(2,1)} %get-tuple-element.165), channel_id=1, source_target_pairs={{0,24},{1,8},{2,0},{3,16},{4,28},{5,12},{6,4},{7,20},{8,26},{9,10}... | collective-permute-start | bytes 1769480 | tf_op jit(solution)/shard_map/ppermute | solution.py:529
  309.5 82.7 %all-to-all-start.3 = ((bf16[8,6,96,256]{3,2,1,0:T(8,128)(2,1)}), bf16[8,6,96,256]{3,2,1,0:T(8,128)(2,1)}, u32[]{:S(2)}, u32[]{:S(2)}) async-start(bf16[8,6,96,256]{3,2,1,0:T(8,128)(2,1)} %get-tuple-element.200), calls=%async_computation.3 | async-start | bytes 4718592 | tf_op jit(solution)/shard_map/all_to_all | solution.py:516
  329.2 63.0 %collective-permute-start.15 = (bf16[192,1536]{1,0:T(8,128)(2,1)}, bf16[192,1536]{1,0:T(8,128)(2,1)S(1)}, u32[]{:S(2)}, u32[]{:S(2)}) collective-permute-start(bf16[192,1536]{1,0:T(8,128)(2,1)} %get-tuple-element.196), channel_id=1, source_target_pairs={{0,0},{16,1},{8,2},{24,3},{4,4},{20,5},{12,6},{28,7},{2,8},{18,9},... | collective-permute-start | bytes 1769480 | tf_op jit(solution)/shard_map/ppermute | solution.py:587
  332.0 60.2 %collective-permute-start.16 = (bf16[192,1536]{1,0:T(8,128)(2,1)}, bf16[192,1536]{1,0:T(8,128)(2,1)S(1)}, u32[]{:S(2)}, u32[]{:S(2)}) collective-permute-start(bf16[192,1536]{1,0:T(8,128)(2,1)} %get-tuple-element.197), channel_id=1, source_target_pairs={{8,0},{24,1},{16,2},{0,3},{12,4},{28,5},{20,6},{4,7},{10,8},{26,9}... | collective-permute-start | bytes 1769480 | tf_op jit(solution)/shard_map/ppermute | solution.py:587
  332.8 59.4 %collective-permute-start.17 = (bf16[192,1536]{1,0:T(8,128)(2,1)}, bf16[192,1536]{1,0:T(8,128)(2,1)S(1)}, u32[]{:S(2)}, u32[]{:S(2)}) collective-permute-start(bf16[192,1536]{1,0:T(8,128)(2,1)} %get-tuple-element.198), channel_id=1, source_target_pairs={{16,0},{0,1},{24,2},{8,3},{20,4},{4,5},{28,6},{12,7},{18,8},{2,9},... | collective-permute-start | bytes 1769480 | tf_op jit(solution)/shard_map/ppermute | solution.py:587
  334.0 58.2 %collective-permute-start.18 = (bf16[192,1536]{1,0:T(8,128)(2,1)S(1)}, bf16[192,1536]{1,0:T(8,128)(2,1)S(1)}, u32[]{:S(2)}, u32[]{:S(2)}) collective-permute-start(bf16[192,1536]{1,0:T(8,128)(2,1)S(1)} %get-tuple-element.199), channel_id=1, source_target_pairs={{24,0},{8,1},{0,2},{16,3},{28,4},{12,5},{4,6},{20,7},{26,8},{10,9}... | collective-permute-start | bytes 1769480 | tf_op jit(solution)/shard_map/ppermute | solution.py:587
  392.2 22.3 %copy-start.20 = (bf16[192,1536]{1,0:T(8,128)(2,1)}, bf16[192,1536]{1,0:T(8,128)(2,1)S(1)}, u32[]{:S(2)}) copy-start(bf16[192,1536]{1,0:T(8,128)(2,1)S(1)} %collective-permute-done.16.refs_1_) | copy-start | bytes 1769476
  392.2 22.3 %copy-start.22 = (bf16[192,1536]{1,0:T(8,128)(2,1)}, bf16[192,1536]{1,0:T(8,128)(2,1)S(1)}, u32[]{:S(2)}) copy-start(bf16[192,1536]{1,0:T(8,128)(2,1)S(1)} %collective-permute-done.17.refs_2_) | copy-start | bytes 1769476
  392.2 22.3 %copy-start.24 = (bf16[192,1536]{1,0:T(8,128)(2,1)}, bf16[192,1536]{1,0:T(8,128)(2,1)S(1)}, u32[]{:S(2)}) copy-start(bf16[192,1536]{1,0:T(8,128)(2,1)S(1)} %collective-permute-done.18.refs_3_) | copy-start | bytes 1769476
  414.6 24.2 %collective-permute-start.19 = (bf16[2,2,768,768]{3,2,1,0:T(8,128)(2,1)}, bf16[2,2,768,768]{3,2,1,0:T(8,128)(2,1)}, u32[]{:S(2)}, u32[]{:S(2)}) collective-permute-start(bf16[2,2,768,768]{3,2,1,0:T(8,128)(2,1)} %weights_sent.1), channel_id=1, source_target_pairs={{0,1},{1,0},{2,3},{3,2},{4,5},{5,4},{6,7},{7,6},{8,9},{9,8},{10,11... | collective-permute-start | bytes 14155784 | tf_op jit(solution)/shard_map/ppermute | solution.py:559
  427.0 39.1 %all-to-all-start.4 = ((bf16[8,6,96,256]{3,2,1,0:T(8,128)(2,1)}), bf16[8,6,96,256]{3,2,1,0:T(8,128)(2,1)}, u32[]{:S(2)}, u32[]{:S(2)}) async-start(bf16[8,6,96,256]{3,2,1,0:T(8,128)(2,1)} %get-tuple-element.202), calls=%async_computation.4 | async-start | bytes 4718592 | tf_op jit(solution)/shard_map/all_to_all | solution.py:516
  438.8 30.2 %copy-start.1 = (bf16[8,6,96,256]{3,2,1,0:T(8,128)(2,1)S(1)}, bf16[8,6,96,256]{3,2,1,0:T(8,128)(2,1)}, u32[]{:S(2)}) copy-start(bf16[8,6,96,256]{3,2,1,0:T(8,128)(2,1)} %copy-done) | copy-start | bytes 7077892
  438.8 30.2 %copy-start.19 = (s32[4]{0:T(128)S(1)}, s32[4]{0:T(128)}, u32[]{:S(2)}) copy-start(s32[4]{0:T(128)} %pad_add_fusion.1.place) | copy-start | bytes 52
  466.2 53.5 %collective-permute-start.22 = (bf16[768,768]{1,0:T(8,128)(2,1)}, bf16[768,768]{1,0:T(8,128)(2,1)}, u32[]{:S(2)}, u32[]{:S(2)}) collective-permute-start(bf16[768,768]{1,0:T(8,128)(2,1)} %get-tuple-element.218), channel_id=1, source_target_pairs={{0,2},{1,3},{2,0},{3,1},{4,6},{5,7},{6,4},{7,5},{8,10},{9,11},{10,... | collective-permute-start | bytes 3538952 | tf_op jit(solution)/shard_map/ppermute | solution.py:596
  466.9 52.7 %collective-permute-start.23 = (bf16[2,4,96,768]{3,2,1,0:T(8,128)(2,1)}, bf16[2,4,96,768]{3,2,1,0:T(8,128)(2,1)}, u32[]{:S(2)}, u32[]{:S(2)}) collective-permute-start(bf16[2,4,96,768]{3,2,1,0:T(8,128)(2,1)} %get-tuple-element.219), channel_id=1, source_target_pairs={{0,4},{4,0},{8,12},{12,8},{16,20},{20,16},{24,28},{28,24},{1,5},{5... | collective-permute-start | bytes 3538952 | tf_op jit(solution)/shard_map/ppermute | solution.py:596
  482.4 37.2 %collective-permute-start.20 = (bf16[192,1536]{1,0:T(8,128)(2,1)S(1)}, bf16[192,1536]{1,0:T(8,128)(2,1)S(1)}, u32[]{:S(2)}, u32[]{:S(2)}) collective-permute-start(bf16[192,1536]{1,0:T(8,128)(2,1)S(1)} %get-tuple-element.216), channel_id=1, source_target_pairs={{0,0},{16,1},{8,2},{24,3},{4,4},{20,5},{12,6},{28,7},{2,8},{18,9},... | collective-permute-start | bytes 1769480 | tf_op jit(solution)/shard_map/ppermute | solution.py:587
  484.7 34.9 %collective-permute-start.21 = (bf16[192,1536]{1,0:T(8,128)(2,1)S(1)}, bf16[192,1536]{1,0:T(8,128)(2,1)S(1)}, u32[]{:S(2)}, u32[]{:S(2)}) collective-permute-start(bf16[192,1536]{1,0:T(8,128)(2,1)S(1)} %get-tuple-element.217), channel_id=1, source_target_pairs={{16,0},{0,1},{24,2},{8,3},{20,4},{4,5},{28,6},{12,7},{18,8},{2,9},... | collective-permute-start | bytes 1769480 | tf_op jit(solution)/shard_map/ppermute | solution.py:587
  486.5 33.1 %copy-start.39 = (f32[768,768]{1,0:T(8,128)S(1)}, f32[768,768]{1,0:T(8,128)}, u32[]{:S(2)}) copy-start(f32[768,768]{1,0:T(8,128)} %get-tuple-element.227) | copy-start | bytes 7077892
  522.3 34.9 %collective-permute-start.24 = (bf16[4,96,768]{2,1,0:T(8,128)(2,1)}, bf16[4,96,768]{2,1,0:T(8,128)(2,1)}, u32[]{:S(2)}, u32[]{:S(2)}) collective-permute-start(bf16[4,96,768]{2,1,0:T(8,128)(2,1)} %fusion.5), channel_id=1, source_target_pairs={{0,4},{4,0},{8,12},{12,8},{16,20},{20,16},{24,28},{28,24},{1,5},{5... | collective-permute-start | bytes 1769480 | tf_op jit(solution)/shard_map/ppermute | solution.py:596
  525.2 29.3 %copy-start.37 = (f32[2,4,96,768]{3,2,1,0:T(8,128)}, f32[2,4,96,768]{3,2,1,0:T(8,128)S(1)}, u32[]{:S(2)}) copy-start(f32[2,4,96,768]{3,2,1,0:T(8,128)S(1)} %convert_add_fusion) | copy-start | bytes 7077892
  526.2 31.0 %collective-permute-start.25 = (bf16[4,96,768]{2,1,0:T(8,128)(2,1)}, bf16[4,96,768]{2,1,0:T(8,128)(2,1)}, u32[]{:S(2)}, u32[]{:S(2)}) collective-permute-start(bf16[4,96,768]{2,1,0:T(8,128)(2,1)} %fusion.6), channel_id=1, source_target_pairs={{0,2},{1,3},{2,0},{3,1},{4,6},{5,7},{6,4},{7,5},{8,10},{9,11},{10,... | collective-permute-start | bytes 1769480 | tf_op jit(solution)/shard_map/ppermute | solution.py:596
  526.2 69.9 %collective-permute-start.26 = (bf16[192,1536]{1,0:T(8,128)(2,1)}, bf16[192,1536]{1,0:T(8,128)(2,1)S(1)}, u32[]{:S(2)}, u32[]{:S(2)}) collective-permute-start(bf16[192,1536]{1,0:T(8,128)(2,1)} %get-tuple-element.240), channel_id=1, source_target_pairs={{8,0},{24,1},{16,2},{0,3},{12,4},{28,5},{20,6},{4,7},{10,8},{26,9}... | collective-permute-start | bytes 1769480 | tf_op jit(solution)/shard_map/ppermute | solution.py:610
  526.2 69.9 %collective-permute-start.27 = (bf16[192,1536]{1,0:T(8,128)(2,1)}, bf16[192,1536]{1,0:T(8,128)(2,1)S(1)}, u32[]{:S(2)}, u32[]{:S(2)}) collective-permute-start(bf16[192,1536]{1,0:T(8,128)(2,1)} %get-tuple-element.241), channel_id=1, source_target_pairs={{24,0},{8,1},{0,2},{16,3},{28,4},{12,5},{4,6},{20,7},{26,8},{10,9}... | collective-permute-start | bytes 1769480 | tf_op jit(solution)/shard_map/ppermute | solution.py:610
  562.0 34.1 %collective-permute-start.28 = (bf16[2,96,768]{2,1,0:T(8,128)(2,1)}, bf16[2,96,768]{2,1,0:T(8,128)(2,1)}, u32[]{:S(2)}, u32[]{:S(2)}) collective-permute-start(bf16[2,96,768]{2,1,0:T(8,128)(2,1)} %get-tuple-element.348), channel_id=1, source_target_pairs={{0,8},{8,0},{16,24},{24,16},{1,9},{9,1},{17,25},{25,17},{2,10},{10... | collective-permute-start | bytes 884744 | tf_op jit(solution)/shard_map/ppermute | solution.py:596
  562.0 34.1 %collective-permute-start.29 = (bf16[2,96,768]{2,1,0:T(8,128)(2,1)}, bf16[2,96,768]{2,1,0:T(8,128)(2,1)}, u32[]{:S(2)}, u32[]{:S(2)}) collective-permute-start(bf16[2,96,768]{2,1,0:T(8,128)(2,1)} %get-tuple-element.349), channel_id=1, source_target_pairs={{0,16},{8,24},{16,0},{24,8},{1,17},{9,25},{17,1},{25,9},{2,18},{10... | collective-permute-start | bytes 884744 | tf_op jit(solution)/shard_map/ppermute | solution.py:596
  564.3 25.8 %copy-start.59 = (f32[96]{0:T(128)S(1)}, f32[96]{0:T(128)}, u32[]{:S(2)}) copy-start(f32[96]{0:T(128)} %copy-done.58) | copy-start | bytes 1156
  564.3 31.8 %collective-permute-start.30 = (bf16[2,96,768]{2,1,0:T(8,128)(2,1)}, bf16[2,96,768]{2,1,0:T(8,128)(2,1)}, u32[]{:S(2)}, u32[]{:S(2)}) collective-permute-start(bf16[2,96,768]{2,1,0:T(8,128)(2,1)} %get-tuple-element.347), channel_id=1, source_target_pairs={{0,24},{8,16},{16,8},{24,0},{1,25},{9,17},{17,9},{25,1},{2,26},{10... | collective-permute-start | bytes 884744 | tf_op jit(solution)/shard_map/ppermute | solution.py:596
  596.1 22.9 %copy-start.28 = (bf16[192,1536]{1,0:T(8,128)(2,1)}, bf16[192,1536]{1,0:T(8,128)(2,1)S(1)}, u32[]{:S(2)}) copy-start(bf16[192,1536]{1,0:T(8,128)(2,1)S(1)} %collective-permute-done.26.refs_6_) | copy-start | bytes 1769476
  596.1 22.9 %copy-start.30 = (bf16[192,1536]{1,0:T(8,128)(2,1)}, bf16[192,1536]{1,0:T(8,128)(2,1)S(1)}, u32[]{:S(2)}) copy-start(bf16[192,1536]{1,0:T(8,128)(2,1)S(1)} %collective-permute-done.27.refs_7_) | copy-start | bytes 1769476
  618.9 111.2 %all-to-all-start.6 = ((bf16[8,12,96,256]{3,2,1,0:T(8,128)(2,1)}), bf16[8,12,96,256]{3,2,1,0:T(8,128)(2,1)}, u32[]{:S(2)}, u32[]{:S(2)}) async-start(bf16[8,12,96,256]{3,2,1,0:T(8,128)(2,1)} %bitcast.226), calls=%async_computation.6 | async-start | bytes 9437184 | tf_op jit(solution)/shard_map/all_to_all | solution.py:662
  634.2 2.2 collective-permute-start.31
  636.3 5.6 collective-permute-start.32
  (52 other events, 385.9 us)
Sparse Core Ops, SparseCore 0:
  9.6 39.6 all-gather.7
  51.4 37.4 all-gather.5

commit v4 on v3

v4 whole, which is shorter than its diff:
```python
import functools
import math

import jax
import jax.numpy as jnp
import numpy as np
from jax import lax
from jax.experimental import pallas as pl
from jax.experimental.pallas import tpu as pltpu
from jax.sharding import Mesh, PartitionSpec as P

BLOCK = 96
SHRINK = 0.01
NORM_EPS = 1e-05
BF = jnp.bfloat16
F32 = jnp.float32
FLOPS, BYTES = 1_000_000_000, 3_400_000
NN = (((1,), (0,)), ((), ()))
NT = (((1,), (1,)), ((), ()))
TN = (((0,), (0,)), ((), ()))


def dot(left, right, dims=NN):
    return lax.dot_general(left, right, dims, preferred_element_type=F32)


def gelu_pair(value):
    phi = 0.5 * lax.erf(value * (1.0 / math.sqrt(2.0))) + 0.5
    bell = jnp.exp2(value * value * (-0.5 / math.log(2.0)))
    return value * phi, phi + value * bell * (1.0 / math.sqrt(2.0 * math.pi))


def split(value):
    high = value.astype(BF)
    return high, (value - high.astype(F32)).astype(BF)


def np_split(table):
    high = table.astype(np.float32).astype(jnp.bfloat16)
    low = (table - high.astype(np.float64)).astype(np.float32).astype(jnp.bfloat16)
    return jnp.asarray(high), jnp.asarray(low)


def lon_tables(width, modes):
    angle = 2.0 * np.pi * (np.outer(np.arange(modes), np.arange(width)) % width) / width
    scale = 1.0 / math.sqrt(width)
    cos, sin = np.cos(angle) * scale, np.sin(angle) * scale
    doubled = np.where(np.arange(modes) == 0, 1.0, 2.0)[:, None]
    plain = np.concatenate([cos, -sin], 0)
    weighted = np.concatenate([cos * doubled, -sin * doubled], 0)
    return plain, weighted


def swapped(index):
    return index % 2 * 2 + index // 2


class Rows:
    def __init__(self, per, inner, quarters):
        self.per, self.inner, self.quarters = per, inner, quarters
        self.even = per % 2 == 0
        self.sizes = [per // 2, per - per // 2]

    def block(self, t, part):
        return t % 2 * 2 + (t // 2 + part) % 2 if self.even else swapped(t)

    def quarter(self, block, part):
        return (block + part) % 2 * 2 + block // 2 if self.even else swapped(block)

    def start(self, block, part):
        return (block + part) % 2 * self.sizes[0] if self.even else part * self.sizes[0]

    def order(self):
        held = []
        for t in range(self.quarters):
            for r in range(self.inner):
                for part in range(2):
                    block = self.block(t, part)
                    held.append(((block * self.inner + r) * self.per + self.start(block, part), self.sizes[part]))
        return held


def in_order(array, order):
    return jnp.concatenate([array[at : at + n] for at, n in order], axis=0)


def out_of_order(array, order):
    at = 0
    for row, n in order:
        yield row, n, array[at : at + n]
        at += n


def lat_table(rows, order):
    angle = 2.0 * np.pi * (np.outer(np.arange(rows), np.arange(rows)) % rows) / rows
    scale = 1.0 / math.sqrt(rows)
    held = np.concatenate([np.arange(at, at + n) for at, n in order])
    cos, sin = np.cos(angle)[:, held] * scale, np.sin(angle)[:, held] * scale
    return np.block([[cos, sin], [-sin, cos]])


def fold_lanes(value):
    total = value[:, :128]
    for at in range(128, value.shape[1], 128):
        total = total + value[:, at : at + 128]
    return total


def collect(pieces, order):
    value = pieces[...].astype(F32)
    return in_order(value.reshape(value.shape[0] * value.shape[1], *value.shape[2:]), order)


def lat_product(lat, high, low=None):
    size = lat.shape[1]
    both = dot(lat, high)
    rest = both[size:] if low is None else both[size:] + dot(lat[:size], low)
    return both[:size] + rest


def plane_forward(parts, table, lat, lons, spectra):
    rows, modes = lat.shape[1] // 2, spectra.shape[1]
    feats = spectra.shape[0] // (2 * rows)
    table_hi, table_lo = table
    total = dot(parts[0], table_lo)
    if len(parts) > 1:
        total = total + dot(parts[1], table_hi)
    total = total + dot(parts[0], table_hi)
    for c in range(2):
        lons[c] = total[:, c * modes : (c + 1) * modes]
    for f in range(0, feats, 2):
        pair = []
        for g in (f, f + 1):
            pair.append(jnp.concatenate([lons[c, pl.ds(g, rows, stride=feats), :] for c in range(2)], axis=0))
        high, low = split(jnp.concatenate(pair, axis=1))
        out = lat_product(lat, high, low)
        for i, g in enumerate((f, f + 1)):
            spectra[pl.ds(g, 2 * rows, stride=feats), :] = out[:, i * modes : (i + 1) * modes]


def plane_inverse(table, lat, lons, spectra):
    rows, modes = lat.shape[1] // 2, spectra.shape[1]
    feats = spectra.shape[0] // (2 * rows)
    for f in range(0, feats, 2):
        pair = [spectra[pl.ds(g, 2 * rows, stride=feats), :] for g in (f, f + 1)]
        out = lat_product(lat, jnp.concatenate(pair, axis=1).astype(BF))
        for i, g in enumerate((f, f + 1)):
            for c in range(2):
                lons[c, pl.ds(g, rows, stride=feats), :] = out[c * rows : (c + 1) * rows, i * modes : (i + 1) * modes]
    table_hi, table_lo = table
    value = jnp.concatenate([lons[0], lons[1]], axis=1).astype(BF)
    return dot(value, table_hi) + dot(value, table_lo)


def spectrum_kernel(order, pieces, mean, rstd, scale, shift, hi, lo, lat, spec, lons, spectra):
    mixed = (collect(pieces, order) - mean[...]) * rstd[...] * scale[...] + shift[...]
    rows, feats, width = mixed.shape
    parts = split(mixed.reshape(rows * feats, width))
    plane_forward(parts, (hi[...], lo[...]), lat[...], lons, spectra)
    spec[...] = spectra[...].reshape(spec.shape).astype(BF)


def join_lines(parts):
    value = jnp.concatenate([part[...] for part in parts], axis=1)
    return value.reshape(value.shape[0] * value.shape[1], *value.shape[2:])


def spectrum_back_kernel(n, *refs):
    parts, (hi, lo, lat, freq, lons, spectra) = refs[:n], refs[n:]
    value = join_lines(parts)
    rows, feats, width = value.shape
    if feats % 16:
        value = value.astype(F32).reshape(rows * feats, width).astype(BF)
    else:
        value = value.reshape(rows * feats, width)
    plane_forward((value,), (hi[...], lo[...]), lat[...], lons, spectra)
    freq[...] = spectra[...].reshape(freq.shape).astype(BF)


def two_modes(ref, ky):
    return jnp.concatenate([jnp.concatenate([ref[0, k], ref[1, k]], axis=0) for k in (ky, ky + 1)], axis=1)


def put_modes(ref, ky, value):
    feats, modes = ref.shape[2], ref.shape[3]
    for i in range(2):
        for c in range(2):
            ref[c, ky + i] = value[c * feats : (c + 1) * feats, i * modes : (i + 1) * modes].astype(ref.dtype)


def filter_kernel(spec, w1, bias1, w2, bias2, kept, mid, slope, bend, share):
    @pl.when(pl.program_id(0) == 0)
    def _():
        share[...] = jnp.zeros_like(share)

    for ky in range(0, spec.shape[1], 2):
        act, deriv = gelu_pair(dot(w1[...], two_modes(spec, ky)) + bias1[...])
        act = act.astype(BF)
        put_modes(mid, ky, act)
        put_modes(slope, ky, deriv)
        second = dot(w2[...], act) + bias2[...]
        bent = jnp.tanh(second * (1.0 / SHRINK))
        square = bent * bent
        put_modes(bend, ky, square)
        put_modes(kept, ky, second - SHRINK * bent)
        share[...] += jnp.sum((1.0 - square).reshape(-1, 8, square.shape[1]), axis=0)


def filter_back_kernel(
    freq, spec, mid, slope, bend, w1, w2, sgrad, inner, outer, inner_bias, outer_bias
):
    @pl.when(pl.program_id(0) == 0)
    def _():
        for ref in (inner, outer, inner_bias, outer_bias):
            ref[...] = jnp.zeros_like(ref)

    for ky in range(0, spec.shape[1], 2):
        two = (two_modes(freq, ky).astype(F32) * two_modes(bend, ky).astype(F32)).astype(BF)
        outer[...] += dot(two_modes(mid, ky), two, NT)
        outer_bias[...] += fold_lanes(two.astype(F32))
        one = (dot(w2[...], two, TN) * two_modes(slope, ky).astype(F32)).astype(BF)
        inner[...] += dot(two_modes(spec, ky), one, NT)
        inner_bias[...] += fold_lanes(one.astype(F32))
        put_modes(sgrad, ky, dot(w1[...], one, TN))


def section_kernel(order, pieces, mean, rstd, scale, shift, kept, hi, lo, lat, *refs):
    outs, (lons, spectra) = refs[:-2], refs[-2:]
    spectra[...] = kept[...].astype(F32).reshape(spectra.shape)
    value = collect(pieces, order)
    mixed = (value - mean[...]) * rstd[...] * scale[...] + shift[...]
    spectral = plane_inverse((hi[...], lo[...]), lat[...], lons, spectra)
    section = (value + mixed + spectral.reshape(value.shape)).astype(BF)
    section = section.reshape(pieces.shape[0], pieces.shape[1], *value.shape[1:])
    at = 0
    for out in outs:
        out[...] = section[:, at : at + out.shape[1]]
        at += out.shape[1]


def last_kernel(order, n, pieces, *refs):
    sgrad, (mean, rstd, scale, freq, hi, lo, lat, out, sums, gain_sum, shift_sum, lons, spectra) = refs[:n], refs[n:]
    spectra[...] = freq[...].astype(F32).reshape(spectra.shape)
    normed = (collect(pieces, order) - mean[...]) * rstd[...]
    grad = join_lines(sgrad).astype(F32)
    mixed = grad + plane_inverse((hi[...], lo[...]), lat[...], lons, spectra).reshape(grad.shape)
    gain_sum[...] = fold_lanes(jnp.sum(mixed * normed, axis=0))
    shift_sum[...] = fold_lanes(jnp.sum(mixed, axis=0))
    scaled = mixed * scale[...]
    value = (grad + rstd[...] * scaled).astype(BF)
    for at, n, part in out_of_order(value, order):
        out[at : at + n] = part

    @pl.when(pl.program_id(0) == 0)
    def _():
        sums[...] = jnp.zeros_like(sums)

    for c, term in enumerate((scaled, scaled * normed)):
        term = jnp.sum(term, axis=1)
        for at, n, part in out_of_order(term, order):
            sums[at : at + n, c] += part


def column_norm(value):
    mean = jnp.mean(value, axis=0, keepdims=True)
    centered = value - mean
    var = jnp.mean(centered * centered, axis=0, keepdims=True)
    rstd = lax.rsqrt(var + NORM_EPS)
    return centered * rstd, rstd


def feed_kernel(
    n, quarter, chunk, place, *refs
):
    cots = refs[:n]
    section, we_t, wp, we, bias, gain, shift = refs[n : n + 7]
    normal, hidden, pre, cot, sgrad, gain_sum, shift_sum = refs[-7:]

    @pl.when(pl.program_id(0) == 0)
    def _():
        gain_sum[...] = jnp.zeros_like(gain_sum)
        shift_sum[...] = jnp.zeros_like(shift_sum)

    for k, piece in enumerate(cots):
        cot[pl.ds(place[k] * quarter, quarter), :] = piece[0]
    normed, rstd = column_norm(section[...].astype(F32).reshape(normal.shape))
    value = (normed * gain[...] + shift[...]).astype(BF)
    normal[...] = value
    wide = cot[...]

    def bend(start, before, grad):
        rows = slice(start, start + chunk)
        act, slope = gelu_pair(before + jnp.concatenate([bias[rows]] * (value.shape[1] // 128), axis=1))
        hidden[rows] = act.astype(BF)
        pre[rows] = (grad * slope).astype(BF)

    ready = None
    for start in range(0, hidden.shape[0], chunk):
        rows = slice(start, start + chunk)
        products = start, dot(we_t[rows], value), dot(wp[rows], wide)
        if ready:
            bend(*ready)
        ready = products
    bend(*ready)
    part = we.shape[2]
    total = sum(dot(we[t], pre[t * part : (t + 1) * part]) for t in range(we.shape[0]))
    gain_sum[...] += fold_lanes(total * normed)
    shift_sum[...] += fold_lanes(total)
    wide = wide.astype(F32)
    scaled = total * gain[...]
    one = jnp.mean(scaled, axis=0, keepdims=True)
    two = jnp.mean(scaled * normed, axis=0, keepdims=True)
    grad = wide + rstd * (scaled - one - normed * two)
    sgrad[...] = grad.reshape(sgrad.shape).astype(BF)


def result_kernel(quarter, parts, place, hidden, wp_t, bias, *refs):
    sections, outs, field = refs[: len(parts)], refs[len(parts) : -1], refs[-1]
    row = pl.program_id(0)
    value = dot(wp_t[...], hidden[...]) + jnp.concatenate([bias[...]] * (hidden.shape[1] // 128), axis=1)
    at = 0
    for i, (section, n) in enumerate(zip(sections, parts)):

        @pl.when((row >= at) & (row < at + n))
        def _(i=i, section=section, at=at):
            field[...] = value + section[:, row - at].astype(F32).reshape(value.shape)
            for k, out in enumerate(outs[i :: len(parts)]):
                out[...] = field[pl.ds(place[k] * quarter, quarter), :].astype(BF)

        at += n


def weight_kernel(order, normal, pre, cot, hidden, sent, kept, bias_sum, cot_sum):
    products = dot(normal[...], pre[...], NT), dot(cot[...], hidden[...], NT)
    bias_sum[...] = fold_lanes(pre[...].astype(F32))
    away = pl.program_id(0) < pl.num_programs(0) // 2

    @pl.when((pl.program_id(0) == 0) & (pl.program_id(1) == 0))
    def _():
        cot_sum[...] = fold_lanes(cot[...].astype(F32))

    @pl.when(away)
    def _():
        for kind in range(2):
            sent[0, kind] = products[kind].astype(BF)

    @pl.when(jnp.logical_not(away))
    def _():
        for kind in range(2):
            kept[0, kind] = products[kind]


def widen_kernel(parts, slot, starts, *refs):
    pieces, out = refs[:-1], refs[-1]
    width = out.shape[3]
    for i, piece in enumerate(pieces):
        k, part = divmod(i, len(parts))

        @pl.when(pl.program_id(0) == k)
        def _(piece=piece, part=part):
            for row in range(parts[part]):
                out[0, starts[part] + row] = piece[:, row * width : (row + 1) * width].astype(F32)


def finish_kernel(feats, grads, patches, mean, rstd, one, two, out):
    normed = (patches[0].astype(F32) - mean[0]) * rstd[0]
    out[0] = grads[0].astype(F32) - rstd[0] * (one[0] + normed * two[0]) * (1.0 / feats)


def whole(shape):
    return pl.BlockSpec(shape, lambda *_: (0,) * len(shape), pipeline_mode=pl.Buffered(1))


def fixed(shape):
    return pl.BlockSpec(shape, lambda *_: (0,) * len(shape))


def run(name, kernel, grid, ins, specs, outs, out_specs, scratch, mib, micros, scalars=(), aliases=None):
    grid_spec = pltpu.PrefetchScalarGridSpec(
        num_scalar_prefetch=len(scalars), grid=grid, in_specs=specs, out_specs=out_specs, scratch_shapes=scratch
    )
    call = pl.pallas_call(
        kernel,
        grid_spec=grid_spec,
        out_shape=outs,
        compiler_params=pltpu.CompilerParams(vmem_limit_bytes=mib << 20),
        input_output_aliases=aliases or {},
        cost_estimate=pl.CostEstimate(flops=int(micros * FLOPS), bytes_accessed=int(micros * BYTES), transcendentals=0),
        name=name,
    )
    return call(*scalars, *ins)


def complex_weight(pair):
    real, imag = pair[0].T, pair[1].T
    return jnp.concatenate([jnp.concatenate([real, -imag], 1), jnp.concatenate([imag, real], 1)], 0)


def weight_pair(full):
    full = full.reshape(2, BLOCK, 2, BLOCK)
    return jnp.stack([full[0, :, 0] + full[1, :, 1], full[0, :, 1] - full[1, :, 0]])


def per_device(
    sizes, patches, present, first_gain, first_shift, filter_inner, inner_bias, filter_outer, outer_bias,
    second_gain, second_shift, expand_weight, expand_bias, project_weight, project_bias, cotangent,
):
    planes, blocks_local, cut, tp = sizes
    inner = blocks_local * cut
    ranks = inner * tp
    owners = planes * inner
    snaps, per, quarter, width = patches.shape
    feats = quarter * tp
    mine = quarter // inner
    modes = width // 2
    rows = per * ranks
    toks = per * width
    hidden_local = expand_bias.shape[0]
    hiddens = hidden_local * tp
    z, y, j, t = (lax.axis_index(name) for name in ("z", "y", "j", "t"))
    r = y * cut + j
    me = z * inner + r
    every, sp = ("z", "y", "j", "t"), ("z", "y", "j")
    shape = jax.ShapeDtypeStruct

    pieces = patches.reshape(snaps, per, inner, mine, width).swapaxes(1, 2).reshape(owners, per, mine, width)
    pieces = lax.all_to_all(pieces, sp, 0, 0, tiled=True)

    held = Rows(per, inner, tp)
    order, parts = held.order(), held.sizes

    def route(k, part, back):
        pairs = [
            ((zz * inner + rr) * tp + tt, (((swapped(tt) + k) % tp) * inner + rr) * tp + held.quarter(zz, part))
            for zz in range(planes)
            for rr in range(inner)
            for tt in range(tp)
        ]
        return [(b, a) for a, b in pairs] if back else pairs

    place = jnp.stack([swapped((z - k) % tp) for k in range(tp)]).astype(jnp.int32)
    slot = jnp.stack([(swapped(t) + k) % tp for k in range(tp)]).astype(jnp.int32)
    field = patches.astype(F32)
    mean = jnp.mean(field, 2)
    square = jnp.sum(jnp.square(field - mean[:, :, None]), 2)
    gathered = lax.all_gather(jnp.stack([mean, square]), "t")
    packed = lax.all_gather(jnp.concatenate([second_gain, second_shift, project_bias, expand_bias]), "t")
    small = [packed[:, i * quarter : (i + 1) * quarter].reshape(-1) for i in range(3)]
    bias_all = packed[:, 3 * quarter :].reshape(-1)
    mean = jnp.mean(gathered[:, 0], 0)
    square = jnp.sum(gathered[:, 1] + quarter * jnp.square(gathered[:, 0] - mean), 0)
    stats = jnp.stack([mean, lax.rsqrt(square / feats + NORM_EPS)], 2)
    def lanes(vector, width=width):
        return jnp.broadcast_to(vector[:, None], (vector.shape[0], width))

    we = lax.all_gather(expand_weight, "t")
    wp = lax.all_gather(project_weight, "t", tiled=True)
    we_t, wp_t = jnp.swapaxes(we, 1, 2).reshape(hiddens, feats), wp.T
    gain2, shift2, bias_lanes = lanes(small[0]), lanes(small[1]), lanes(bias_all, 128)
    sent_stats, we, wp, we_t, wp_t, gain2, shift2, bias_lanes = lax.optimization_barrier(
        (stats, we, wp, we_t, wp_t, gain2, shift2, bias_lanes)
    )
    plane_stats = []
    for k in range(owners):
        piece = lax.dynamic_index_in_dim(sent_stats, (me ^ k) // inner, 0, False)
        plane_stats.append(lax.ppermute(piece, sp, [(a, a ^ k) for a in range(owners)]) if k else piece)
    plane_stats = jnp.stack(plane_stats)
    bit = 1
    while bit < owners:
        turned = plane_stats.reshape(-1, 2, bit, per, 2, width)
        plane_stats = jnp.where((me // bit) % 2 == 1, turned[:, ::-1], turned).reshape(owners, per, 2, width)
        bit *= 2
    plane_stats = in_order(plane_stats.reshape(rows, 2, 1, width), order)
    mean_one, rstd_one = plane_stats[:, 0], plane_stats[:, 1]

    def own_features(vector):
        return lax.dynamic_slice_in_dim(vector, r * mine, mine)

    keep = own_features(lax.dynamic_index_in_dim(present, z, 0, False).astype(F32))
    scale1, shift1 = lanes(own_features(first_gain) * keep), lanes(own_features(first_shift) * keep)

    def own_block(array):
        return lax.dynamic_index_in_dim(array, y, 1, False)

    w1, w2 = complex_weight(own_block(filter_inner)), complex_weight(own_block(filter_outer))
    bias1 = lanes(own_block(inner_bias).reshape(-1), 2 * modes)
    bias2 = lanes(own_block(outer_bias).reshape(-1), 2 * modes)
    plain, weighted = lon_tables(width, modes)
    lat = lat_table(rows, order)
    plain_t, weighted_t, plain_n, weighted_n = (np_split(a) for a in (plain.T, weighted.T, plain, weighted))
    lat_f, lat_b = (jnp.concatenate(np_split(a)) for a in (lat, lat.T))

    cotangents = [
        [lax.dynamic_slice(cotangent, (slot[k], held.start(z, part), 0, 0), (1, n, quarter, width))[0] for k in range(tp)]
        for part, n in enumerate(parts)
    ]
    late, pieces = lax.optimization_barrier((cotangents, pieces))
    cots = [[lax.ppermute(piece, every, route(k, 0, False)) for k, piece in enumerate(late[0])]]

    some = 16 if mine % 16 == 0 else mine
    grid = (mine // some,)
    piece_spec = pl.BlockSpec((owners, per, some, width), lambda g, *_: (0, 0, g, 0))
    stat_spec, feat_spec = whole((rows, 1, width)), pl.BlockSpec((some, width), lambda g, *_: (g, 0))
    lon_f, lon_b = [whole((width, 2 * modes))] * 2, [whole((2 * modes, width))] * 2
    lat_specs = [whole((4 * rows, 2 * rows))]
    image_spec = pl.BlockSpec((rows, some, width), lambda g, *_: (0, g, 0))
    modes_spec = pl.BlockSpec((2, rows, some, modes), lambda g, *_: (0, 0, g, 0))
    scratch = [
        pltpu.VMEM((2, rows * some, modes), F32),
        pltpu.VMEM((2 * rows * some, modes), F32),
    ]
    mine_modes = (2, rows, mine, modes)
    spec = run(
        "spectrum", functools.partial(spectrum_kernel, order), grid,
        (pieces, mean_one, rstd_one, scale1, shift1, *plain_t, lat_f),
        [piece_spec, stat_spec, stat_spec, feat_spec, feat_spec, *lon_f, *lat_specs],
        shape(mine_modes, BF), modes_spec, scratch, 48, 22,
    )

    def to_blocks(array):
        return lax.all_to_all(array, "j", 1, 2, tiled=True) if cut > 1 else array

    def to_features(array):
        return lax.all_to_all(array, "j", 2, 1, tiled=True) if cut > 1 else array

    spec = to_blocks(spec)
    lats = rows // cut
    step = 8
    block_modes = (2, lats, BLOCK, modes)
    block_spec = pl.BlockSpec((2, step, BLOCK, modes), lambda g: (0, g, 0, 0))
    square_spec, lane_spec = whole((2 * BLOCK, 2 * BLOCK)), whole((2 * BLOCK, 2 * modes))
    kept, mid, slope, bend, share = run(
        "filter", filter_kernel, (lats // step,), (spec, w1, bias1, w2, bias2),
        [block_spec, square_spec, lane_spec, square_spec, lane_spec],
        (*[shape(block_modes, BF)] * 4, shape((8, 2 * modes), F32)),
        (block_spec, block_spec, block_spec, block_spec, fixed((8, 2 * modes))), [], 48, 17,
    )
    kept, late, cots[0] = lax.optimization_barrier((kept, late, cots[0]))
    part_specs = [pl.BlockSpec((ranks, n, some, width), lambda g, *_: (0, 0, g, 0)) for n in parts]
    sections = run(
        "section", functools.partial(section_kernel, order), grid,
        (pieces, mean_one, rstd_one, scale1, shift1, to_features(kept), *weighted_n, lat_b),
        [piece_spec, stat_spec, stat_spec, feat_spec, feat_spec, modes_spec, *lon_b, *lat_specs],
        [shape((ranks, n, mine, width), BF) for n in parts], part_specs, scratch, 56, 17,
    )

    def exchange(array):
        return lax.all_to_all(array, ("t", "y", "j"), 0, 0, tiled=True)

    outs = (
        shape((feats, toks), BF), shape((hiddens, toks), BF), shape((hiddens, toks), BF), shape((feats, toks), BF),
    )
    sum_shapes = [shape((feats, 128), F32)] * 2
    sgrads, sums, done, start = [], [], (), 0
    received = []
    for n, section in zip(parts, sections):
        section = exchange(section)
        if not received:
            section, late = lax.optimization_barrier((section, late))
            cots.append([lax.ppermute(piece, every, route(k, 1, False)) for k, piece in enumerate(late[1])])
        tok_spec = pl.BlockSpec((feats, width), lambda h, *_, start=start: (0, h + start))
        hid_spec = pl.BlockSpec((hiddens, width), lambda h, *_, start=start: (0, h + start))
        cot_specs = [pl.BlockSpec((1, quarter, width), lambda h, *_: (h, 0, 0))] * tp
        line_spec = pl.BlockSpec((ranks, 1, mine, width), lambda h, *_: (0, h, 0, 0))
        any_spec = pl.BlockSpec(memory_space=pl.ANY)
        *done, sgrad, s0, s1 = run(
            "feed", functools.partial(feed_kernel, tp, quarter, min(256, hidden_local)), (n,),
            (*cots[len(received)], section, we_t, wp, we, bias_lanes, gain2, shift2, *done),
            [*cot_specs, line_spec, whole((hiddens, feats)), whole((hiddens, feats)),
             whole((tp, feats, hidden_local)), whole((hiddens, 128)), whole((feats, width)), whole((feats, width)),
             *[any_spec] * len(done)],
            (*outs, shape((ranks, n, mine, width), BF), *sum_shapes),
            (tok_spec, hid_spec, hid_spec, tok_spec, line_spec, *[fixed((feats, 128))] * 2),
            [], 60, 43, (place,), {8 + tp + i: i for i in range(len(done))},
        )
        if start:
            sgrad, done, sgrads = lax.optimization_barrier((sgrad, done, sgrads))
            rows_out = run(
                "result", functools.partial(result_kernel, quarter, parts), (per,),
                (done[1], wp_t, lanes(small[2], 128), *received, section),
                [pl.BlockSpec((hiddens, width), lambda h, *_: (0, h)), whole((feats, hiddens)), whole((feats, 128)),
                 *[whole((ranks, m, mine, width)) for m in parts]],
                [shape((quarter, m * width), BF) for _ in range(tp) for m in parts],
                [pl.BlockSpec((quarter, width), lambda h, *_, at=at, m=m: (0, jnp.clip(h - at, 0, m - 1)))
                 for _ in range(tp) for at, m in zip((0, parts[0]), parts)],
                [pltpu.VMEM((feats, width), F32)], 48, 0.01, (place,),
            )
            rows_out, done = lax.optimization_barrier((rows_out, done))
            results = [None] * (2 * tp)

            def send_results(rounds):
                for k in rounds:
                    for part in range(2):
                        results[2 * k + part] = lax.ppermute(rows_out[2 * k + part], every, route(k, part, True))

            send_results((0, 1))
        sgrad = exchange(sgrad)
        if start:
            third, half = hidden_local // 3, tp // 2
            resident = whole((feats, toks))
            hid_rows = pl.BlockSpec((third, toks), lambda k, i, o: (o[k] * 3 + i, 0))
            normal, hidden, pre, cot = done
            sent, kept_products, bias_sum, cot_sum = run(
                "weights", weight_kernel, (tp, 3), (normal, pre, cot, hidden), [resident, hid_rows, resident, hid_rows],
                [shape((half, 2, feats, hidden_local), BF), shape((half, 2, feats, hidden_local), F32),
                 shape((hiddens, 128), F32), shape((feats, 128), F32)],
                [pl.BlockSpec((1, 2, feats, third), lambda k, i, o: (jnp.minimum(k, half - 1), 0, 0, jnp.where(k < half, i, 2))),
                 pl.BlockSpec((1, 2, feats, third), lambda k, i, o: (jnp.maximum(k - half, 0), 0, 0, jnp.where(k < half, 0, i))),
                 pl.BlockSpec((third, 128), lambda k, i, o: (o[k] * 3 + i, 0)), fixed((feats, 128))],
                [], 60, 0.01,
                (jnp.stack([t ^ k for k in (*range(1, tp, 2), *range(0, tp, 2))]).astype(jnp.int32),),
            )
            sgrad, sent, results, rows_out = lax.optimization_barrier((sgrad, sent, results, rows_out))
            came = lax.ppermute(sent, "t", [(a, a ^ 1) for a in range(tp)])
            send_results((2, 3))
        sgrads.append(sgrad)
        sums.append((s0, s1))
        received.append(section)
        start += n
    gain_sum, shift_sum = (a + b for a, b in zip(*sums))

    def trade(theirs, axes, bit, size):
        return lax.ppermute(theirs, axes, [(a, a ^ bit) for a in range(size)])

    def halves(array, bit):
        other = 1 - (me // bit) % 2
        return lax.dynamic_index_in_dim(array, 1 - other, 0, False), lax.dynamic_index_in_dim(array, other, 0, False)


    freq = run(
        "spectrum_back", functools.partial(spectrum_back_kernel, len(parts)), grid, (*sgrads, *weighted_t, lat_f),
        [*part_specs, *lon_f, *lat_specs], shape(mine_modes, BF), modes_spec, scratch, 48, 0.01,
    )
    freq, came = lax.optimization_barrier((freq, came))
    weights = (kept_products + came.astype(F32)).reshape(half, 2, owners // 2, 2, feats // owners, hidden_local)
    weights, theirs = halves(jnp.moveaxis(weights, 3, 0), 1)
    came = trade(theirs.astype(BF), sp, 1, owners)
    freq, inner_grad, outer_grad, inner_bias_grad, outer_bias_grad = run(
        "filter_back", filter_back_kernel, (lats // step,), (to_blocks(freq), spec, mid, slope, bend, w1, w2),
        [*[block_spec] * 5, square_spec, square_spec],
        (shape(block_modes, BF), *[shape((2 * BLOCK, 2 * BLOCK), F32)] * 2, *[shape((2 * BLOCK, 128), F32)] * 2),
        (block_spec, *[fixed((2 * BLOCK, 2 * BLOCK))] * 2, *[fixed((2 * BLOCK, 128))] * 2), [], 48, 0.01,
    )
    freq, results = lax.optimization_barrier((freq, results))
    grads, lines, first_gain_sum, first_shift_sum = run(
        "last", functools.partial(last_kernel, order, len(parts)), grid,
        (pieces, *sgrads, mean_one, rstd_one, scale1, to_features(freq), *plain_n, lat_b),
        [piece_spec, *part_specs, stat_spec, stat_spec, feat_spec, modes_spec, *lon_b, *lat_specs],
        (shape((rows, mine, width), BF), shape((rows, 2, width), F32), *[shape((mine, 128), F32)] * 2),
        (image_spec, fixed((rows, 2, width)), *[pl.BlockSpec((some, 128), lambda g, *_: (g, 0))] * 2),
        scratch, 56, 0.01,
    )
    def with_bias(full, bias):
        bias = jnp.sum(bias, 1).reshape(2, BLOCK)
        return jnp.concatenate([weight_pair(full), bias[:, :, None]], 2)

    filters = jnp.stack([with_bias(inner_grad, inner_bias_grad), with_bias(outer_grad, outer_bias_grad)])
    filters = jnp.moveaxis(filters, 2, 0).reshape(owners, -1)
    early = jnp.concatenate(
        [jnp.sum(gain_sum, 1), jnp.sum(shift_sum, 1), jnp.sum(cot_sum, 1), jnp.sum(bias_sum, 1), jnp.sum(share)[None]]
    )
    grads, lines, results, came = lax.optimization_barrier((grads, lines, results, came))
    weights = weights + came.astype(F32)
    weights = jnp.moveaxis(weights[0] + trade(weights[1].astype(BF), "t", 2, tp).astype(F32), 1, 0)
    bit = 2
    while bit < inner:
        weights = weights.reshape(-1, 2, *weights.shape[1:])
        weights, theirs = halves(weights.swapaxes(0, 1), bit)
        weights = weights + trade(theirs.astype(BF), sp, bit, owners).astype(F32)
        bit *= 2
    expand_sum, project_sum = sum(
        trade(lax.dynamic_index_in_dim(weights, z ^ k, 0, False).astype(BF), "z", k, planes).astype(F32)
        for k in range(1, planes)
    ) + lax.dynamic_index_in_dim(weights, z, 0, False)
    project_sum = project_sum.T
    line = per * width
    feature_sums = jnp.stack([jnp.sum(first_gain_sum, 1) * keep, jnp.sum(first_shift_sum, 1) * keep]).reshape(-1)
    tail = jnp.concatenate(
        [lines.reshape(owners, 2 * line), filters,
         jnp.broadcast_to(jnp.concatenate([feature_sums, early]), (owners, 2 * mine + early.shape[0]))], 1
    )
    tail = lax.all_to_all(tail, sp, 0, 0, tiled=True)
    tail, grads = lax.optimization_barrier((tail, grads))
    grads = lax.all_to_all(grads.reshape(owners, per, mine, width), sp, 0, 0, tiled=True)
    cuts = [2 * line, 2 * line + filters.shape[1], 2 * line + filters.shape[1] + 2 * mine]
    lines, filters, feature_sums, early = jnp.split(tail, cuts, axis=1)
    lines = jnp.sum(lines.reshape(planes, inner, -1), 1).reshape(-1)
    filters = jnp.sum(filters.reshape(planes, blocks_local, cut, BLOCK // owners, 2, 2, BLOCK + 1), (0, 2))
    filters = jnp.transpose(filters, (2, 3, 0, 1, 4))
    feature_sums = jnp.sum(feature_sums.reshape(planes, inner, 2, mine), 0).swapaxes(0, 1)
    spread = lax.dynamic_update_slice(
        jnp.zeros((2, tp, quarter), F32), feature_sums.reshape(2, 1, quarter), (0, t, 0)
    ).reshape(-1)
    tail = jnp.concatenate([lines, spread, jnp.sum(early, 0)])
    bit = 1
    while bit < tp:
        tail = tail + trade(tail, "t", bit, tp)
        bit *= 2
    cuts = [planes * 2 * line, planes * 2 * line + 2 * feats]
    lines, last, early = jnp.split(tail, cuts)
    fixes = lines.reshape(planes, per, 2, 1, width)
    last = last.reshape(2, feats)

    starts = jnp.stack([jnp.asarray(held.start(z, part), jnp.int32) for part in range(2)])
    result = run(
        "widen", functools.partial(widen_kernel, parts), (tp,), results,
        [whole((quarter, n * width)) for _ in range(tp) for n in parts], shape((snaps, per, quarter, width), F32),
        pl.BlockSpec((1, per, quarter, width), lambda i, s, _: (s[i], 0, 0, 0)), [], 32, 8, (slot, starts),
    )
    one_spec = pl.BlockSpec((1, per, 1, width), lambda i: (i // inner, 0, 0, 0))
    patch_spec = pl.BlockSpec((1, per, mine, width), lambda i: (i // inner, 0, i % inner, 0))
    patches_grad = run(
        "finish", functools.partial(finish_kernel, feats), (owners,),
        (grads, patches, stats[:, :, 0, None], stats[:, :, 1, None], fixes[:, :, 0], fixes[:, :, 1]),
        [pl.BlockSpec((1, per, mine, width), lambda i: (i, 0, 0, 0)), patch_spec, *[one_spec] * 4],
        shape((snaps, per, quarter, width), F32), patch_spec, [], 48, 11,
    )

    return (
        result, patches_grad, last[0], last[1], filters[0, ..., :BLOCK], filters[0, ..., BLOCK],
        filters[1, ..., :BLOCK], filters[1, ..., BLOCK],
        early[:feats], early[feats : 2 * feats], expand_sum, early[3 * feats : 3 * feats + hiddens],
        project_sum, early[2 * feats : 3 * feats], early[-1] / (snaps * rows * modes * feats * 2),
    )


def solution(mesh):
    tp = mesh.shape["tp"]
    planes = tp
    inner = mesh.shape["sp"] // planes
    blocks_local = 2
    cut = inner // blocks_local
    mesh = Mesh(mesh.devices.reshape(planes, blocks_local, cut, tp), ("z", "y", "j", "t"))
    sp = ("z", "y", "j")
    image = P(None, sp, "t", None)
    return jax.shard_map(
        functools.partial(per_device, (planes, blocks_local, cut, tp)),
        mesh=mesh,
        in_specs=(
            image, P(None, "t"), P("t"), P("t"),
            P(None, "t", None, None), P(None, "t", None), P(None, "t", None, None), P(None, "t", None),
            P("t"), P("t"), P(None, "t"), P("t"), P("t", None), P("t"), image,
        ),
        out_specs=(
            image, image, P(), P(),
            P(None, "t", sp, None), P(None, "t", sp), P(None, "t", sp, None), P(None, "t", sp),
            P(), P(), P(sp, "t"), P(), P("t", sp), P(), P(),
        ),
        check_vma=False,
    )
```

time: 760 us -> 696 us (0.916)
  Pallas kernels: 297 us -> 254 us
  starting transfers between devices: 111 us -> 97.3 us
  waiting for transfers between devices: 190 us -> 180 us
    ppermute x9 -> x7, waiting for transfers between devices: 2.86 us -> 98.8 us  [trade(): return lax.ppermute(theirs, axes, [(a, a ^ bit) for a in range(size)])]
    all_to_all x1, waiting for transfers between devices: 85.7 us -> 0.01 us  [per_device(): lax.all_to_all(grads.reshape(owners, per, mine, width), sp, 0, 0, tiled=T...]
    pallas_call x14 -> x12, Pallas kernels: 297 us -> 254 us  [run(): return call(*scalars, *ins)]
    ppermute x7, waiting for transfers between devices: 55.1 us -> 26.3 us  [per_device(): lax.ppermute(piece, sp, [(a, a ^ k) for a in range(owners)])]
    all_gather x1, waiting for transfers between devices: 0.02 us -> 24.4 us  [per_device(): wp = lax.all_gather(project_weight, 't', tiled=True)]
    ppermute x16, waiting for transfers between devices: 22.9 us -> 1.84 us  [the longest x8 1.82 us: send_results(): lax.ppermute(rows_out[2 * k + part], every, route(k, part, True))]
    ppermute x1, starting transfers between devices: 12.5 us -> 0.01 us  [per_device(): came = lax.ppermute(sent, 't', [(a, a ^ 1) for a in range(tp)])]
    add x3 -> x4, other arithmetic: 4.84 us -> 15.6 us  [the longest x1 9.71 us: per_device(): kept_products + came.astype(F32)]
  transfers between devices with their start and end apart: 41 -> 39, of which waited for: 9 -> 10; matrix products, arithmetic and copies ran while one was open for 10% -> 12% of each run, Pallas kernels for 33% -> 34%
where the time goes in v4:
time: 696 us; the launch traced here: 685 us
  Pallas kernels  254 us (36%)
  waiting for transfers between devices  180 us (26%)
  starting transfers between devices  97.3 us (14%)
  local copies, waits for them, and re-layouts  60.4 us (9%)
  other arithmetic  37.4 us (5%)
  blocking collectives  37 us (5%)
  between operations  18.7 us (3%)
    pallas_call x12, Pallas kernels, run(): return call(*scalars, *ins)  254 us
    ppermute x7, waiting for transfers between devices, trade(): return lax.ppermute(theirs, axes, [(a, a ^ bit) for a in range(size)])  98.8 us
    all_to_all x4, starting transfers between devices, exchange(): return lax.all_to_all(array, ('t', 'y', 'j'), 0, 0, tiled=True)  28.7 us
    all_to_all x4, waiting for transfers between devices, exchange(): return lax.all_to_all(array, ('t', 'y', 'j'), 0, 0, tiled=True)  28.2 us
    ppermute x7, waiting for transfers between devices, per_device(): lax.ppermute(piece, sp, [(a, a ^ k) for a in range(owners)])  26.3 us
    all_gather x1, waiting for transfers between devices, per_device(): wp = lax.all_gather(project_weight, 't', tiled=True)  24.4 us
    ppermute x8, starting transfers between devices, send_results(): lax.ppermute(rows_out[2 * k + part], every, route(k, part, True))  22.9 us
    unnamed x117, local copies, waits for them, and re-layouts  20 us
  transfers between devices with their start and end apart: 39, of which 10 were waited for; matrix products, arithmetic and copies ran while one was open for 12% of the time, Pallas kernels for 34%

profile of v4, /device:TPU:2, one launch (start us, length us, event | category | flops | bytes accessed | tf_op | source)
XLA Modules:
  0.0 684.9 jit_solution(17784085119028063361)
XLA Ops:
  8.0 2.4 copy.267
  10.4 2.8 fusion.18
  13.1 2.6 pad_maximum_fusion
  15.7 5.8 all-to-all-start
  21.7 3.3 convert_reduce_fusion
  25.4 4.1 fusion.1
  31.3 11.5 %all-reduce = f32[5376]{0:T(1024)S(1)} all-reduce(f32[5376]{0:T(1024)S(1)} %dynamic-update-slice), channel_id=4, replica_groups=mesh['z'=4,'y'=2,'j'=1,'t'=4] {'t'}, use_global_device_ids=true, to_apply=%add | all-reduce | flops 5376 | bytes 43008
  45.0 6.1 all-gather
  52.1 3.9 dynamic-slice_bitcast_fusion
  56.0 7.0 %copy.268 = bf16[4,768,768]{2,1,0:T(8,128)(2,1)} copy(bf16[4,768,768]{1,2,0:T(8,128)(2,1)} %bitcast.192) | data formatting | bytes 9437184 | tf_op jit(solution)/shard_map/transpose | solution.py:458
  63.0 24.4 %all-gather.6.cloned.1.call-done = bf16[3072,768]{0,1:T(8,128)(2,1)} async-done(((bf16[768,768]{0,1:T(8,128)(2,1)}), bf16[3072,768]{0,1:T(8,128)(2,1)}) %all-gather.6.cloned.1.call-update) | async-done | bytes 4718608 | tf_op jit(solution)/shard_map/all_gather | solution.py:457
  89.6 1.6 broadcast_in_dim.70.refs_8_
  91.4 1.8 collective-permute-start
  93.2 1.6 collective-permute-start.1
  95.4 2.7 collective-permute-start.3
  99.6 3.4 collective-permute-start.5
  104.2 25.2 %collective-permute-done.3 = f32[12,2,256]{2,1,0:T(2,128)S(1)} collective-permute-done((f32[12,2,256]{2,1,0:T(2,128)S(1)}, f32[12,2,256]{2,1,0:T(2,128)S(1)}, u32[]{:S(2)}, u32[]{:S(2)}) %collective-permute-start.3) | collective-permute-done | bytes 24608 | tf_op jit(solution)/shard_map/ppermute | solution.py:466
  132.4 2.9 collective-permute-start.7
  135.4 3.6 collective-permute-start.9
  139.4 19.3 %spectrum.1.spec = bf16[2,96,96,128]{3,2,1,0:T(8,128)(2,1)S(1)} custom-call(bf16[8,12,96,256]{3,2,1,0:T(8,128)(2,1)} %all-to-all-done.pieces, f32[96,1,256]{2,1,0:T(1,128)S(1)} %get-tuple-element.353.mean.refs_2_, f32[96,1,256]{2,1,0:T(1,128)S(1)} %get-tuple-element.352.rstd.refs_3_, f32[96,256]{1,0:T(8,128)S(1)} %broadcast_in_dim.71.scale.refs_4_, ...), custom_call_target="tpu_custom_call" | custom-call | flops 22000001024 | bytes 74800000 | tf_op jit(solution)/shard_map/spectrum/pallas_call | solution.py:391
  158.8 2.2 copy-done.2
  161.1 14.3 %filter.1 = (bf16[2,96,96,128]{3,2,1,0:T(8,128)(2,1)S(1)}, bf16[2,96,96,128]{3,2,1,0:T(8,128)(2,1)}, bf16[2,96,96,128]{3,2,1,0:T(8,128)(2,1)}, bf16[2,96,96,128]{3,2,1,0:T(8,128)(2,1)}, f32[8,256]{1,0:T(8,128)S(1)}) custom-call(bf16[2,96,96,128]{3,2,1,0:T(8,128)(2,1)} %copy-done.2, bf16[192,192]{1,0:T(8,128)(2,1)S(1)} %maximum_maximum_fusion.w1, ...), custom_call_target="tpu_custom_call" | custom-call | flops 16999999488 | bytes 57800000 | tf_op jit(solution)/shard_map/filter/pallas_call | solution.py:391
  175.4 2.2 copy-done.18
  179.6 13.4 %section.1 = (bf16[8,6,96,256]{3,2,1,0:T(8,128)(2,1)}, bf16[8,6,96,256]{3,2,1,0:T(8,128)(2,1)}) custom-call(bf16[8,12,96,256]{3,2,1,0:T(8,128)(2,1)} %all-to-all-done.pieces, f32[96,1,256]{2,1,0:T(1,128)} %copy-done.5, f32[96,1,256]{2,1,0:T(1,128)} %copy-done.4, f32[96,256]{1,0:T(8,128)} %copy-done.3, f32[96,256]{1,0:T(8,128)} %copy-done.10, ...), custom_call_target="tpu_custom_call" | custom-call | flops 16999999488 | bytes 57800000 | tf_op jit(solution)/shard_map/section/pallas_call | solution.py:391
  193.0 12.2 %all-to-all-start.1 = ((bf16[8,6,96,256]{3,2,1,0:T(8,128)(2,1)}), bf16[8,6,96,256]{3,2,1,0:T(8,128)(2,1)S(1)}, u32[]{:S(2)}, u32[]{:S(2)}) async-start(bf16[8,6,96,256]{3,2,1,0:T(8,128)(2,1)} %get-tuple-element.152), calls=%async_computation.1 | async-start | bytes 4718592 | tf_op jit(solution)/shard_map/all_to_all | solution.py:548
  205.8 6.6 copy.288.refs_6_
  212.4 20.3 %all-to-all-done.1.refs_4_.refs_0_ = bf16[8,6,96,256]{3,2,1,0:T(8,128)(2,1)S(1)} async-done(((bf16[8,6,96,256]{3,2,1,0:T(8,128)(2,1)}), bf16[8,6,96,256]{3,2,1,0:T(8,128)(2,1)S(1)}, u32[]{:S(2)}, u32[]{:S(2)}) %all-to-all-start.1) | async-done | bytes 2359328 | tf_op jit(solution)/shard_map/all_to_all | solution.py:548
  232.7 5.7 all-to-all-start.2
  238.4 1.5 collective-permute-start.11
  239.9 3.1 collective-permute-start.12
  243.0 1.9 collective-permute-start.13
  246.4 35.5 %feed.2 = (bf16[768,3072]{1,0:T(8,128)(2,1)}, bf16[3072,3072]{1,0:T(8,128)(2,1)}, bf16[3072,3072]{1,0:T(8,128)(2,1)}, bf16[768,3072]{1,0:T(8,128)(2,1)}, bf16[8,...) custom-call(s32[4]{0:T(128)} %pad_add_fusion.2.place, bf16[6,192,256]{2,1,0:T(8,128)(2,1)} %copy-done.40, ...), custom_call_target="tpu_custom_call" | custom-call | flops 43000000512 | bytes 146200000 | tf_op jit(solution)/shard_map/feed/pallas_call | solution.py:391
  281.9 7.9 %all-to-all-done.2.refs_4_.refs_1_ = bf16[8,6,96,256]{3,2,1,0:T(8,128)(2,1)} async-done(((bf16[8,6,96,256]{3,2,1,0:T(8,128)(2,1)}), bf16[8,6,96,256]{3,2,1,0:T(8,128)(2,1)}, u32[]{:S(2)}, u32[]{:S(2)}) %all-to-all-start.2) | async-done | bytes 2359328 | tf_op jit(solution)/shard_map/all_to_all | solution.py:548
  289.9 6.5 all-to-all-start.3
  296.4 35.6 %feed.3 = (bf16[768,3072]{1,0:T(8,128)(2,1)}, bf16[3072,3072]{1,0:T(8,128)(2,1)}, bf16[3072,3072]{1,0:T(8,128)(2,1)}, bf16[768,3072]{1,0:T(8,128)(2,1)}, bf16[8,...) custom-call(s32[4]{0:T(128)} %pad_add_fusion.2.place, ...), custom_call_target="tpu_custom_call", output_to_operand_aliasing={{0}: (12, {}), {1}: (13, {}), {2}: (14, {}), {3}: (15, {})} | custom-call | flops 43000000512 | bytes 146200000 | tf_op jit(solution)/shard_map/feed/pallas_call | solution.py:391
  332.0 4.3 all-to-all-start.4
  336.6 24.8 %result.1 = (bf16[192,1536]{1,0:T(8,128)(2,1)}, bf16[192,1536]{1,0:T(8,128)(2,1)}, bf16[192,1536]{1,0:T(8,128)(2,1)}, bf16[192,1536]{1,0:T(8,128)(2,1)}, bf16[19...) custom-call(s32[4]{0:T(128)S(1)} %copy-done.11, ...), custom_call_target="tpu_custom_call" | custom-call | flops 10000000 | bytes 34000 | tf_op jit(solution)/shard_map/result/pallas_call | solution.py:391
  364.6 1.9 collective-permute-start.15
  366.6 4.2 collective-permute-start.16
  370.7 5.4 collective-permute-start.18
  376.7 41.6 %weights.1 = (bf16[2,2,768,768]{3,2,1,0:T(8,128)(2,1)}, f32[2,2,768,768]{3,2,1,0:T(8,128)}, f32[3072,128]{1,0:T(8,128)}, f32[768,128]{1,0:T(8,128)}) custom-call(s32[4]{0:T(128)} %pad_add_fusion.3.order, bf16[768,3072]{1,0:T(8,128)(2,1)} %get-tuple-element.198.normal, bf16[3072,3072]{1,0:T(8,128)(2,1)} %get-tuple-element.199.pre, ...), custom_call_target="tpu_custom_call" | custom-call | flops 10000000 | bytes 34000 | tf_op jit(solution)/shard_map/weights/pallas_call | solution.py:391
  418.4 1.8 collective-permute-done.18.refs_3_
  420.6 4.9 collective-permute-start.21
  425.5 6.1 collective-permute-start.23
  431.6 16.5 %spectrum_back.1.freq = bf16[2,96,96,128]{3,2,1,0:T(8,128)(2,1)} custom-call(bf16[8,6,96,256]{3,2,1,0:T(8,128)(2,1)S(1)} %all-to-all-done.3.refs_0_, bf16[8,6,96,256]{3,2,1,0:T(8,128)(2,1)} %all-to-all-done.4.refs_1_, bf16[256,256]{1,0:T(8,128)(2,1)S(1)} %copy-done.8, bf16[256,256]{1,0:T(8,128)(2,1)S(1)} %copy-done.9, bf16[384,192]{1,0:T(8,128)(2,1)S(1)} %copy-done.7), custom_call_target="tpu_custom_call" | custom-call | flops 10000000 | bytes 34000 | tf_op jit(solution)/shard_map/spectrum_back/pallas_call | solution.py:391
  448.2 9.7 %convert_add_fusion = f32[2,2,768,768]{3,2,1,0:T(8,128)} fusion(f32[2,2,768,768]{3,2,1,0:T(8,128)} %get-tuple-element.237, bf16[2,2,768,768]{3,2,1,0:T(8,128)(2,1)} %collective-permute-done.19), kind=kLoop, calls=%fused_computation.4 | loop fusion | flops 4718592 | bytes 23592960 | tf_op jit(solution)/shard_map/add | solution.py:635
  457.9 2.7 fusion.2
  460.6 1.5 collective-permute-start.24
  466.2 1.9 reduce_sum.164
  468.1 17.4 %filter_back.1 = (bf16[2,96,96,128]{3,2,1,0:T(8,128)(2,1)S(1)}, f32[192,192]{1,0:T(8,128)S(1)}, f32[192,192]{1,0:T(8,128)S(1)}, f32[192,128]{1,0:T(8,128)S(1)}, f32[192,128]{1,0:T(8,128)S(1)}) custom-call(bf16[2,96,96,128]{3,2,1,0:T(8,128)(2,1)} %spectrum_back.1.freq, bf16[2,96,96,128]{3,2,1,0:T(8,128)(2,1)} %copy-done.2, ...), custom_call_target="tpu_custom_call" | custom-call | flops 10000000 | bytes 34000 | tf_op jit(solution)/shard_map/filter_back/pallas_call | solution.py:391
  485.6 2.2 copy-done.1
  489.8 18.2 %last.1 = (bf16[96,96,256]{2,1,0:T(8,128)(2,1)}, f32[96,2,256]{2,1,0:T(2,128)}, f32[96,128]{1,0:T(8,128)}, f32[96,128]{1,0:T(8,128)}) custom-call(bf16[8,12,96,256]{3,2,1,0:T(8,128)(2,1)} %all-to-all-done.pieces, bf16[8,6,96,256]{3,2,1,0:T(8,128)(2,1)} %copy-done, bf16[8,6,96,256]{3,2,1,0:T(8,128)(2,1)} %all-to-all-done.4.refs_1_, f32[96,1,256]{2,1,0:T(1,128)} %copy-done.5, ...), custom_call_target="tpu_custom_call" | custom-call | flops 10000000 | bytes 34000 | tf_op jit(solution)/shard_map/last/pallas_call | solution.py:391
  512.3 19.3 %all_to_all.42 = f32[8,1,16369]{2,1,0:T(1,128)S(1)} all-to-all(f32[8,1,16369]{2,1,0:T(1,128)S(1)} %all_to_all.31), channel_id=1, replica_groups=mesh['z'=4,'y'=2,'j'=1,'t'=4] {'z','y','j'}, dimensions={0} | all-to-all | bytes 1047616 | tf_op jit(solution)/shard_map/all_to_all | solution.py:682
  531.9 5.0 all-to-all-start.6
  537.2 3.5 bitcast_add_fusion
  540.8 2.2 copy-done.19
  543.1 6.8 widen.1
  552.3 2.1 collective-permute-start.26
  556.5 15.6 %collective-permute-done.26 = f32[31489]{0:T(1024)S(1)} collective-permute-done((f32[31489]{0:T(1024)S(1)}, f32[31489]{0:T(1024)S(1)}, u32[]{:S(2)}, u32[]{:S(2)}) %collective-permute-start.26) | collective-permute-done | bytes 125988 | tf_op jit(solution)/shard_map/ppermute | solution.py:623
  572.2 2.3 fusion.3
  575.4 3.5 collective-permute-start.30
  582.3 42.4 %collective-permute-done.30 = bf16[2,96,768]{2,1,0:T(8,128)(2,1)S(1)} collective-permute-done((bf16[2,96,768]{2,1,0:T(8,128)(2,1)}, bf16[2,96,768]{2,1,0:T(8,128)(2,1)S(1)}, u32[]{:S(2)}, u32[]{:S(2)}) %collective-permute-start.30) | collective-permute-done | bytes 294944 | tf_op jit(solution)/shard_map/ppermute | solution.py:623
  624.7 40.6 %collective-permute-done.29 = bf16[2,96,768]{2,1,0:T(8,128)(2,1)S(1)} collective-permute-done((bf16[2,96,768]{2,1,0:T(8,128)(2,1)}, bf16[2,96,768]{2,1,0:T(8,128)(2,1)S(1)}, u32[]{:S(2)}, u32[]{:S(2)}) %collective-permute-start.29) | collective-permute-done | bytes 294944 | tf_op jit(solution)/shard_map/ppermute | solution.py:623
  666.3 10.4 %finish.1 = f32[4,12,192,256]{3,2,1,0:T(8,128)} custom-call(bf16[8,12,96,256]{3,2,1,0:T(8,128)(2,1)} %all-to-all-done.6.grads, bf16[4,12,192,256]{3,2,1,0:T(8,128)(2,1)} %patches.1, f32[4,12,1,256]{3,2,1,0:T(1,128)S(1)} %copy.301.mean, f32[4,12,1,256]{3,2,1,0:T(1,128)S(1)} %copy.302.rstd, f32[4,12,1,256]{3,2,1,0:T(1,128)S(1)} %get-tuple-element.360.one, ...), custom_call_target="tpu_custom_call" | custom-call | flops 11000000512 | bytes 37400000 | tf_op jit(solution)/shard_map/finish/pallas_call | solution.py:391
  (287 shorter events, 42.6 us)
Async XLA Ops:
  7.2 48.8 %all-gather.8.cloned.1.call-start = ((), (), s32[]{:S(2)}) async-start(), calls=%async_computation.8 | async-start | bytes 5898240 | tf_op jit(solution)/shard_map/all_gather | solution.py:456
  7.9 79.5 %all-gather.6.cloned.1.call-start = ((), (), s32[]{:S(2)}) async-start(), calls=%async_computation.7 | async-start | bytes 5898240 | tf_op jit(solution)/shard_map/all_gather | solution.py:457
  15.7 116.7 %all-to-all-start = ((bf16[8,12,96,256]{3,2,1,0:T(8,128)(2,1)}), bf16[8,12,96,256]{3,2,1,0:T(8,128)(2,1)}, u32[]{:S(2)}, u32[]{:S(2)}) async-start(bf16[8,12,96,256]{3,2,1,0:T(8,128)(2,1)} %bitcast.190), calls=%async_computation | async-start | bytes 9437184 | tf_op jit(solution)/shard_map/all_to_all | solution.py:427
  21.6 8.0 %copy-start.44 = (u32[32]{0:T(128)S(1)}, u32[32]{0:T(128)}, u32[]{:S(2)}) copy-start(u32[32]{0:T(128)} %constant.384) | copy-start | bytes 388
  21.6 9.3 %copy-start.32 = (f32[768]{0:T(1024)S(1)}, f32[768]{0:T(1024)}, u32[]{:S(2)}) copy-start(f32[768]{0:T(1024)} %param.38) | copy-start | bytes 9220
  21.6 9.3 %copy-start.33 = (f32[192]{0:T(256)S(1)}, f32[192]{0:T(256)}, u32[]{:S(2)}) copy-start(f32[192]{0:T(256)} %param.35) | copy-start | bytes 2308
  21.6 9.3 %copy-start.34 = (f32[192]{0:T(256)S(1)}, f32[192]{0:T(256)}, u32[]{:S(2)}) copy-start(f32[192]{0:T(256)} %param.36) | copy-start | bytes 2308
  21.6 9.3 %copy-start.35 = (f32[192]{0:T(256)S(1)}, f32[192]{0:T(256)}, u32[]{:S(2)}) copy-start(f32[192]{0:T(256)} %param.40) | copy-start | bytes 2308
  21.6 22.1 %copy-start.27 = (bf16[2,2,96,96]{3,2,1,0:T(8,128)(2,1)S(1)}, bf16[2,2,96,96]{3,2,1,0:T(8,128)(2,1)}, u32[]{:S(2)}) copy-start(bf16[2,2,96,96]{3,2,1,0:T(8,128)(2,1)} %param.33) | copy-start | bytes 221188
  21.6 22.1 %copy-start.28 = (bf16[2,2,96,96]{3,2,1,0:T(8,128)(2,1)S(1)}, bf16[2,2,96,96]{3,2,1,0:T(8,128)(2,1)}, u32[]{:S(2)}) copy-start(bf16[2,2,96,96]{3,2,1,0:T(8,128)(2,1)} %param.31) | copy-start | bytes 221188
  21.6 22.6 %copy-start.38 = (f32[192]{0:T(256)S(1)}, f32[192]{0:T(256)}, u32[]{:S(2)}) copy-start(f32[192]{0:T(256)} %param.30) | copy-start | bytes 2308
  25.0 26.4 %copy-start.39 = (f32[192]{0:T(256)S(1)}, f32[192]{0:T(256)}, u32[]{:S(2)}) copy-start(f32[192]{0:T(256)} %param.29) | copy-start | bytes 2308
  45.0 11.0 %copy-start.30 = (f32[96]{0:T(128)}, f32[96]{0:T(128)S(1)}, u32[]{:S(2)}) copy-start(f32[96]{0:T(128)S(1)} %get-tuple-element.326) | copy-start | bytes 1156
  56.0 47.9 %copy-start.36 = (f32[2,2,96]{2,1,0:T(2,128)S(1)}, f32[2,2,96]{2,1,0:T(2,128)}, u32[]{:S(2)}) copy-start(f32[2,2,96]{2,1,0:T(2,128)} %param.32) | copy-start | bytes 4612
  56.0 47.9 %copy-start.37 = (f32[2,2,96]{2,1,0:T(2,128)S(1)}, f32[2,2,96]{2,1,0:T(2,128)}, u32[]{:S(2)}) copy-start(f32[2,2,96]{2,1,0:T(2,128)} %param.34) | copy-start | bytes 4612
  63.0 76.3 %copy-start.6 = (bf16[384,192]{1,0:T(8,128)(2,1)S(1)}, bf16[384,192]{1,0:T(8,128)(2,1)}, u32[]{:S(2)}) copy-start(bf16[384,192]{1,0:T(8,128)(2,1)} %constant.380.lat.refs_4_) | copy-start | bytes 442372
  63.0 76.3 %copy-start.16 = (bf16[256,256]{1,0:T(8,128)(2,1)S(1)}, bf16[256,256]{1,0:T(8,128)(2,1)}, u32[]{:S(2)}) copy-start(bf16[256,256]{1,0:T(8,128)(2,1)} %constant.362.clone.hi) | copy-start | bytes 393220
  63.0 76.3 %copy-start.17 = (bf16[256,256]{1,0:T(8,128)(2,1)S(1)}, bf16[256,256]{1,0:T(8,128)(2,1)}, u32[]{:S(2)}) copy-start(bf16[256,256]{1,0:T(8,128)(2,1)} %constant.363.clone.lo) | copy-start | bytes 393220
  91.4 8.2 %collective-permute-start = (f32[12,2,256]{2,1,0:T(2,128)S(1)}, f32[12,2,256]{2,1,0:T(2,128)S(1)}, u32[]{:S(2)}, u32[]{:S(2)}) collective-permute-start(f32[12,2,256]{2,1,0:T(2,128)S(1)} %bitcast.253), channel_id=1, source_target_pairs={{0,4},{4,0},{8,12},{12,8},{16,20},{20,16},{24,28},{28,24},{1,5},{5... | collective-permute-start | bytes 73736 | tf_op jit(solution)/shard_map/ppermute | solution.py:466
  93.2 9.8 %collective-permute-start.1 = (f32[12,2,256]{2,1,0:T(2,128)S(1)}, f32[12,2,256]{2,1,0:T(2,128)S(1)}, u32[]{:S(2)}, u32[]{:S(2)}) collective-permute-start(f32[12,2,256]{2,1,0:T(2,128)S(1)} %bitcast.252), channel_id=1, source_target_pairs={{0,8},{4,12},{8,0},{12,4},{16,24},{20,28},{24,16},{28,20},{1,9},{5... | collective-permute-start | bytes 73736 | tf_op jit(solution)/shard_map/ppermute | solution.py:466
  95.0 9.2 %collective-permute-start.2 = (f32[12,2,256]{2,1,0:T(2,128)S(1)}, f32[12,2,256]{2,1,0:T(2,128)S(1)}, u32[]{:S(2)}, u32[]{:S(2)}) collective-permute-start(f32[12,2,256]{2,1,0:T(2,128)S(1)} %bitcast.243), channel_id=1, source_target_pairs={{0,12},{4,8},{8,4},{12,0},{16,28},{20,24},{24,20},{28,16},{1,13},{... | collective-permute-start | bytes 73736 | tf_op jit(solution)/shard_map/ppermute | solution.py:466
  95.4 34.0 %collective-permute-start.3 = (f32[12,2,256]{2,1,0:T(2,128)S(1)}, f32[12,2,256]{2,1,0:T(2,128)S(1)}, u32[]{:S(2)}, u32[]{:S(2)}) collective-permute-start(f32[12,2,256]{2,1,0:T(2,128)S(1)} %bitcast.245), channel_id=1, source_target_pairs={{0,16},{4,20},{8,24},{12,28},{16,0},{20,4},{24,8},{28,12},{1,17},{... | collective-permute-start | bytes 73736 | tf_op jit(solution)/shard_map/ppermute | solution.py:466
  98.1 32.5 %collective-permute-start.4 = (f32[12,2,256]{2,1,0:T(2,128)S(1)}, f32[12,2,256]{2,1,0:T(2,128)S(1)}, u32[]{:S(2)}, u32[]{:S(2)}) collective-permute-start(f32[12,2,256]{2,1,0:T(2,128)S(1)} %bitcast.247), channel_id=1, source_target_pairs={{0,20},{4,16},{8,28},{12,24},{16,4},{20,0},{24,12},{28,8},{1,21},{... | collective-permute-start | bytes 73736 | tf_op jit(solution)/shard_map/ppermute | solution.py:466
  99.6 31.0 %collective-permute-start.5 = (f32[12,2,256]{2,1,0:T(2,128)S(1)}, f32[12,2,256]{2,1,0:T(2,128)S(1)}, u32[]{:S(2)}, u32[]{:S(2)}) collective-permute-start(f32[12,2,256]{2,1,0:T(2,128)S(1)} %bitcast.249), channel_id=1, source_target_pairs={{0,24},{4,28},{8,16},{12,20},{16,8},{20,12},{24,0},{28,4},{1,25},{... | collective-permute-start | bytes 73736 | tf_op jit(solution)/shard_map/ppermute | solution.py:466
  103.0 27.6 %collective-permute-start.6 = (f32[12,2,256]{2,1,0:T(2,128)S(1)}, f32[12,2,256]{2,1,0:T(2,128)S(1)}, u32[]{:S(2)}, u32[]{:S(2)}) collective-permute-start(f32[12,2,256]{2,1,0:T(2,128)S(1)} %bitcast.242), channel_id=1, source_target_pairs={{0,28},{4,24},{8,20},{12,16},{16,12},{20,8},{24,4},{28,0},{1,29},{... | collective-permute-start | bytes 73736 | tf_op jit(solution)/shard_map/ppermute | solution.py:466
  132.4 26.3 %copy-start.4 = (f32[96,1,256]{2,1,0:T(1,128)}, f32[96,1,256]{2,1,0:T(1,128)S(1)}, u32[]{:S(2)}) copy-start(f32[96,1,256]{2,1,0:T(1,128)S(1)} %get-tuple-element.352.rstd.refs_3_) | copy-start | bytes 294916
  132.4 26.3 %copy-start.5 = (f32[96,1,256]{2,1,0:T(1,128)}, f32[96,1,256]{2,1,0:T(1,128)S(1)}, u32[]{:S(2)}) copy-start(f32[96,1,256]{2,1,0:T(1,128)S(1)} %get-tuple-element.353.mean.refs_2_) | copy-start | bytes 294916
  132.4 45.2 %collective-permute-start.7 = (bf16[6,192,256]{2,1,0:T(8,128)(2,1)}, bf16[6,192,256]{2,1,0:T(8,128)(2,1)S(1)}, u32[]{:S(2)}, u32[]{:S(2)}) collective-permute-start(bf16[6,192,256]{2,1,0:T(8,128)(2,1)} %get-tuple-element.143), channel_id=1, source_target_pairs={{0,0},{1,16},{2,8},{3,24},{4,4},{5,20},{6,12},{7,28},{8,2},{9,18},... | collective-permute-start | bytes 1769480 | tf_op jit(solution)/shard_map/ppermute | solution.py:498
  135.3 42.3 %collective-permute-start.8 = (bf16[6,192,256]{2,1,0:T(8,128)(2,1)}, bf16[6,192,256]{2,1,0:T(8,128)(2,1)S(1)}, u32[]{:S(2)}, u32[]{:S(2)}) collective-permute-start(bf16[6,192,256]{2,1,0:T(8,128)(2,1)} %get-tuple-element.144), channel_id=1, source_target_pairs={{0,8},{1,24},{2,16},{3,0},{4,12},{5,28},{6,20},{7,4},{8,10},{9,26}... | collective-permute-start | bytes 1769480 | tf_op jit(solution)/shard_map/ppermute | solution.py:498
  135.4 42.2 %collective-permute-start.9 = (bf16[6,192,256]{2,1,0:T(8,128)(2,1)S(1)}, bf16[6,192,256]{2,1,0:T(8,128)(2,1)S(1)}, u32[]{:S(2)}, u32[]{:S(2)}) collective-permute-start(bf16[6,192,256]{2,1,0:T(8,128)(2,1)S(1)} %get-tuple-element.145), channel_id=1, source_target_pairs={{0,16},{1,0},{2,24},{3,8},{4,20},{5,4},{6,28},{7,12},{8,18},{9,2},... | collective-permute-start | bytes 1769480 | tf_op jit(solution)/shard_map/ppermute | solution.py:498
  139.0 38.7 %collective-permute-start.10 = (bf16[6,192,256]{2,1,0:T(8,128)(2,1)S(1)}, bf16[6,192,256]{2,1,0:T(8,128)(2,1)S(1)}, u32[]{:S(2)}, u32[]{:S(2)}) collective-permute-start(bf16[6,192,256]{2,1,0:T(8,128)(2,1)S(1)} %get-tuple-element.146), channel_id=1, source_target_pairs={{0,24},{1,8},{2,0},{3,16},{4,28},{5,12},{6,4},{7,20},{8,26},{9,10}... | collective-permute-start | bytes 1769480 | tf_op jit(solution)/shard_map/ppermute | solution.py:498
  139.2 19.5 %copy-start.3 = (f32[96,256]{1,0:T(8,128)}, f32[96,256]{1,0:T(8,128)S(1)}, u32[]{:S(2)}) copy-start(f32[96,256]{1,0:T(8,128)S(1)} %broadcast_in_dim.71.scale.refs_4_) | copy-start | bytes 294916
  139.4 19.4 %copy-start.10 = (f32[96,256]{1,0:T(8,128)}, f32[96,256]{1,0:T(8,128)S(1)}, u32[]{:S(2)}) copy-start(f32[96,256]{1,0:T(8,128)S(1)} %broadcast_in_dim.72.shift) | copy-start | bytes 294916
  193.0 39.7 %all-to-all-start.1 = ((bf16[8,6,96,256]{3,2,1,0:T(8,128)(2,1)}), bf16[8,6,96,256]{3,2,1,0:T(8,128)(2,1)S(1)}, u32[]{:S(2)}, u32[]{:S(2)}) async-start(bf16[8,6,96,256]{3,2,1,0:T(8,128)(2,1)} %get-tuple-element.152), calls=%async_computation.1 | async-start | bytes 4718592 | tf_op jit(solution)/shard_map/all_to_all | solution.py:548
  232.7 13.7 %copy-start.20 = (bf16[8,6,96,256]{3,2,1,0:T(8,128)(2,1)}, bf16[8,6,96,256]{3,2,1,0:T(8,128)(2,1)S(1)}, u32[]{:S(2)}) copy-start(bf16[8,6,96,256]{3,2,1,0:T(8,128)(2,1)S(1)} %all-to-all-done.1.refs_4_.refs_0_) | copy-start | bytes 7077892
  232.7 57.2 %all-to-all-start.2 = ((bf16[8,6,96,256]{3,2,1,0:T(8,128)(2,1)}), bf16[8,6,96,256]{3,2,1,0:T(8,128)(2,1)}, u32[]{:S(2)}, u32[]{:S(2)}) async-start(bf16[8,6,96,256]{3,2,1,0:T(8,128)(2,1)} %get-tuple-element.161), calls=%async_computation.2 | async-start | bytes 4718592 | tf_op jit(solution)/shard_map/all_to_all | solution.py:548
  238.4 57.9 %collective-permute-start.11 = (bf16[6,192,256]{2,1,0:T(8,128)(2,1)}, bf16[6,192,256]{2,1,0:T(8,128)(2,1)}, u32[]{:S(2)}, u32[]{:S(2)}) collective-permute-start(bf16[6,192,256]{2,1,0:T(8,128)(2,1)} %get-tuple-element.157), channel_id=1, source_target_pairs={{0,2},{1,18},{2,10},{3,26},{4,6},{5,22},{6,14},{7,30},{8,0},{9,16}... | collective-permute-start | bytes 1769480 | tf_op jit(solution)/shard_map/ppermute | solution.py:560
  239.9 56.4 %collective-permute-start.12 = (bf16[6,192,256]{2,1,0:T(8,128)(2,1)}, bf16[6,192,256]{2,1,0:T(8,128)(2,1)}, u32[]{:S(2)}, u32[]{:S(2)}) collective-permute-start(bf16[6,192,256]{2,1,0:T(8,128)(2,1)} %get-tuple-element.158), channel_id=1, source_target_pairs={{0,10},{1,26},{2,18},{3,2},{4,14},{5,30},{6,22},{7,6},{8,8},{9,24}... | collective-permute-start | bytes 1769480 | tf_op jit(solution)/shard_map/ppermute | solution.py:560
  243.0 53.3 %collective-permute-start.13 = (bf16[6,192,256]{2,1,0:T(8,128)(2,1)}, bf16[6,192,256]{2,1,0:T(8,128)(2,1)}, u32[]{:S(2)}, u32[]{:S(2)}) collective-permute-start(bf16[6,192,256]{2,1,0:T(8,128)(2,1)} %get-tuple-element.159), channel_id=1, source_target_pairs={{0,18},{1,2},{2,26},{3,10},{4,22},{5,6},{6,30},{7,14},{8,16},{9,0}... | collective-permute-start | bytes 1769480 | tf_op jit(solution)/shard_map/ppermute | solution.py:560
  244.9 51.4 %collective-permute-start.14 = (bf16[6,192,256]{2,1,0:T(8,128)(2,1)S(1)}, bf16[6,192,256]{2,1,0:T(8,128)(2,1)}, u32[]{:S(2)}, u32[]{:S(2)}) collective-permute-start(bf16[6,192,256]{2,1,0:T(8,128)(2,1)S(1)} %get-tuple-element.160), channel_id=1, source_target_pairs={{0,26},{1,10},{2,2},{3,18},{4,30},{5,14},{6,6},{7,22},{8,24},{9,8}... | collective-permute-start | bytes 1769480 | tf_op jit(solution)/shard_map/ppermute | solution.py:560
  289.9 42.1 %all-to-all-start.3 = ((bf16[8,6,96,256]{3,2,1,0:T(8,128)(2,1)}), bf16[8,6,96,256]{3,2,1,0:T(8,128)(2,1)S(1)}, u32[]{:S(2)}, u32[]{:S(2)}) async-start(bf16[8,6,96,256]{3,2,1,0:T(8,128)(2,1)} %get-tuple-element.182), calls=%async_computation.3 | async-start | bytes 4718592 | tf_op jit(solution)/shard_map/all_to_all | solution.py:548
  332.0 99.6 %copy-start = (bf16[8,6,96,256]{3,2,1,0:T(8,128)(2,1)}, bf16[8,6,96,256]{3,2,1,0:T(8,128)(2,1)S(1)}, u32[]{:S(2)}) copy-start(bf16[8,6,96,256]{3,2,1,0:T(8,128)(2,1)S(1)} %all-to-all-done.3.refs_0_) | copy-start | bytes 7077892
  332.0 88.2 %all-to-all-start.4 = ((bf16[8,6,96,256]{3,2,1,0:T(8,128)(2,1)}), bf16[8,6,96,256]{3,2,1,0:T(8,128)(2,1)}, u32[]{:S(2)}, u32[]{:S(2)}) async-start(bf16[8,6,96,256]{3,2,1,0:T(8,128)(2,1)} %get-tuple-element.184), calls=%async_computation.4 | async-start | bytes 4718592 | tf_op jit(solution)/shard_map/all_to_all | solution.py:548
  364.6 53.7 %collective-permute-start.15 = (bf16[192,1536]{1,0:T(8,128)(2,1)}, bf16[192,1536]{1,0:T(8,128)(2,1)}, u32[]{:S(2)}, u32[]{:S(2)}) collective-permute-start(bf16[192,1536]{1,0:T(8,128)(2,1)} %get-tuple-element.203), channel_id=1, source_target_pairs={{0,0},{16,1},{8,2},{24,3},{4,4},{20,5},{12,6},{28,7},{2,8},{18,9},... | collective-permute-start | bytes 1769480 | tf_op jit(solution)/shard_map/ppermute | solution.py:594
  366.6 51.8 %collective-permute-start.16 = (bf16[192,1536]{1,0:T(8,128)(2,1)}, bf16[192,1536]{1,0:T(8,128)(2,1)}, u32[]{:S(2)}, u32[]{:S(2)}) collective-permute-start(bf16[192,1536]{1,0:T(8,128)(2,1)} %get-tuple-element.204), channel_id=1, source_target_pairs={{2,0},{18,1},{10,2},{26,3},{6,4},{22,5},{14,6},{30,7},{0,8},{16,9}... | collective-permute-start | bytes 1769480 | tf_op jit(solution)/shard_map/ppermute | solution.py:594
  370.7 47.7 %collective-permute-start.17 = (bf16[192,1536]{1,0:T(8,128)(2,1)}, bf16[192,1536]{1,0:T(8,128)(2,1)}, u32[]{:S(2)}, u32[]{:S(2)}) collective-permute-start(bf16[192,1536]{1,0:T(8,128)(2,1)} %get-tuple-element.205), channel_id=1, source_target_pairs={{8,0},{24,1},{16,2},{0,3},{12,4},{28,5},{20,6},{4,7},{10,8},{26,9}... | collective-permute-start | bytes 1769480 | tf_op jit(solution)/shard_map/ppermute | solution.py:594
  370.7 49.5 %collective-permute-start.18 = (bf16[192,1536]{1,0:T(8,128)(2,1)}, bf16[192,1536]{1,0:T(8,128)(2,1)}, u32[]{:S(2)}, u32[]{:S(2)}) collective-permute-start(bf16[192,1536]{1,0:T(8,128)(2,1)} %get-tuple-element.206), channel_id=1, source_target_pairs={{10,0},{26,1},{18,2},{2,3},{14,4},{30,5},{22,6},{6,7},{8,8},{24,9}... | collective-permute-start | bytes 1769480 | tf_op jit(solution)/shard_map/ppermute | solution.py:594
  376.7 54.9 %copy-start.7 = (bf16[384,192]{1,0:T(8,128)(2,1)S(1)}, bf16[384,192]{1,0:T(8,128)(2,1)}, u32[]{:S(2)}) copy-start(bf16[384,192]{1,0:T(8,128)(2,1)} %constant.380.lat.refs_4_) | copy-start | bytes 442372
  376.7 54.9 %copy-start.8 = (bf16[256,256]{1,0:T(8,128)(2,1)S(1)}, bf16[256,256]{1,0:T(8,128)(2,1)}, u32[]{:S(2)}) copy-start(bf16[256,256]{1,0:T(8,128)(2,1)} %constant.364.clone.refs_2_) | copy-start | bytes 393220
  376.7 54.9 %copy-start.9 = (bf16[256,256]{1,0:T(8,128)(2,1)S(1)}, bf16[256,256]{1,0:T(8,128)(2,1)}, u32[]{:S(2)}) copy-start(bf16[256,256]{1,0:T(8,128)(2,1)} %constant.365.clone.refs_3_) | copy-start | bytes 393220
  420.2 28.0 %collective-permute-start.19 = (bf16[2,2,768,768]{3,2,1,0:T(8,128)(2,1)}, bf16[2,2,768,768]{3,2,1,0:T(8,128)(2,1)}, u32[]{:S(2)}, u32[]{:S(2)}) collective-permute-start(bf16[2,2,768,768]{3,2,1,0:T(8,128)(2,1)} %get-tuple-element.212), channel_id=1, source_target_pairs={{0,1},{1,0},{2,3},{3,2},{4,5},{5,4},{6,7},{7,6},{8,9},{9,8},{10,11... | collective-permute-start | bytes 14155784 | tf_op jit(solution)/shard_map/ppermute | solution.py:614
  420.2 67.6 %collective-permute-start.20 = (bf16[192,1536]{1,0:T(8,128)(2,1)}, bf16[192,1536]{1,0:T(8,128)(2,1)}, u32[]{:S(2)}, u32[]{:S(2)}) collective-permute-start(bf16[192,1536]{1,0:T(8,128)(2,1)} %copy-done.15), channel_id=1, source_target_pairs={{16,0},{0,1},{24,2},{8,3},{20,4},{4,5},{28,6},{12,7},{18,8},{2,9},... | collective-permute-start | bytes 1769480 | tf_op jit(solution)/shard_map/ppermute | solution.py:594
  420.6 67.2 %collective-permute-start.21 = (bf16[192,1536]{1,0:T(8,128)(2,1)}, bf16[192,1536]{1,0:T(8,128)(2,1)}, u32[]{:S(2)}, u32[]{:S(2)}) collective-permute-start(bf16[192,1536]{1,0:T(8,128)(2,1)} %copy-done.14), channel_id=1, source_target_pairs={{18,0},{2,1},{26,2},{10,3},{22,4},{6,5},{30,6},{14,7},{16,8},{0,9}... | collective-permute-start | bytes 1769480 | tf_op jit(solution)/shard_map/ppermute | solution.py:594
  425.5 62.3 %collective-permute-start.22 = (bf16[192,1536]{1,0:T(8,128)(2,1)}, bf16[192,1536]{1,0:T(8,128)(2,1)}, u32[]{:S(2)}, u32[]{:S(2)}) collective-permute-start(bf16[192,1536]{1,0:T(8,128)(2,1)} %copy-done.13), channel_id=1, source_target_pairs={{24,0},{8,1},{0,2},{16,3},{28,4},{12,5},{4,6},{20,7},{26,8},{10,9}... | collective-permute-start | bytes 1769480 | tf_op jit(solution)/shard_map/ppermute | solution.py:594
  425.5 62.3 %collective-permute-start.23 = (bf16[192,1536]{1,0:T(8,128)(2,1)}, bf16[192,1536]{1,0:T(8,128)(2,1)}, u32[]{:S(2)}, u32[]{:S(2)}) collective-permute-start(bf16[192,1536]{1,0:T(8,128)(2,1)} %copy-done.12), channel_id=1, source_target_pairs={{26,0},{10,1},{2,2},{18,3},{30,4},{14,5},{6,6},{22,7},{24,8},{8,9}... | collective-permute-start | bytes 1769480 | tf_op jit(solution)/shard_map/ppermute | solution.py:594
  460.6 50.0 %collective-permute-start.24 = (bf16[2,2,4,96,768]{4,3,1,2,0:T(8,128)(2,1)S(1)}, bf16[2,2,4,96,768]{4,3,1,2,0:T(8,128)(2,1)}, u32[]{:S(2)}, u32[]{:S(2)}) collective-permute-start(bf16[2,2,4,96,768]{4,3,1,2,0:T(8,128)(2,1)S(1)} %fusion.2), channel_id=1, source_target_pairs={{0,4},{4,0},{8,12},{12,8},{16,20},{20,16},{24,28},{28,24},{1,5},{5... | collective-permute-start | bytes 7077896 | tf_op jit(solution)/shard_map/ppermute | solution.py:623
  489.8 20.0 %copy-start.31 = (f32[96]{0:T(128)S(1)}, f32[96]{0:T(128)}, u32[]{:S(2)}) copy-start(f32[96]{0:T(128)} %copy-done.30) | copy-start | bytes 1156
  531.9 134.4 %all-to-all-start.6 = ((bf16[8,12,96,256]{3,2,1,0:T(8,128)(2,1)}), bf16[8,12,96,256]{3,2,1,0:T(8,128)(2,1)}, u32[]{:S(2)}, u32[]{:S(2)}) async-start(bf16[8,12,96,256]{3,2,1,0:T(8,128)(2,1)} %bitcast.197), calls=%async_computation.6 | async-start | bytes 9437184 | tf_op jit(solution)/shard_map/all_to_all | solution.py:684
  543.1 29.1 %collective-permute-start.27 = (bf16[2,4,96,768]{3,2,0,1:T(8,128)(2,1)S(1)}, bf16[2,4,96,768]{3,2,0,1:T(8,128)(2,1)}, u32[]{:S(2)}, u32[]{:S(2)}) collective-permute-start(bf16[2,4,96,768]{3,2,0,1:T(8,128)(2,1)S(1)} %fusion.4), channel_id=1, source_target_pairs={{0,2},{1,3},{2,0},{3,1},{4,6},{5,7},{6,4},{7,5},{8,10},{9,11},{10,... | collective-permute-start | bytes 3538952 | tf_op jit(solution)/shard_map/ppermute | solution.py:623
  550.9 1.4 collective-permute-start.25
  552.3 19.8 %collective-permute-start.26 = (f32[31489]{0:T(1024)S(1)}, f32[31489]{0:T(1024)S(1)}, u32[]{:S(2)}, u32[]{:S(2)}) collective-permute-start(f32[31489]{0:T(1024)S(1)} %fusion.24), channel_id=1, source_target_pairs={{0,2},{1,3},{2,0},{3,1},{4,6},{5,7},{6,4},{7,5},{8,10},{9,11},{10,... | collective-permute-start | bytes 377876 | tf_op jit(solution)/shard_map/ppermute | solution.py:623
  575.4 49.3 %collective-permute-start.30 = (bf16[2,96,768]{2,1,0:T(8,128)(2,1)}, bf16[2,96,768]{2,1,0:T(8,128)(2,1)S(1)}, u32[]{:S(2)}, u32[]{:S(2)}) collective-permute-start(bf16[2,96,768]{2,1,0:T(8,128)(2,1)} %get-tuple-element.338), channel_id=1, source_target_pairs={{0,24},{8,16},{16,8},{24,0},{1,25},{9,17},{17,9},{25,1},{2,26},{10... | collective-permute-start | bytes 884744 | tf_op jit(solution)/shard_map/ppermute | solution.py:623
  578.9 86.4 %collective-permute-start.29 = (bf16[2,96,768]{2,1,0:T(8,128)(2,1)}, bf16[2,96,768]{2,1,0:T(8,128)(2,1)S(1)}, u32[]{:S(2)}, u32[]{:S(2)}) collective-permute-start(bf16[2,96,768]{2,1,0:T(8,128)(2,1)} %get-tuple-element.339), channel_id=1, source_target_pairs={{0,16},{8,24},{16,0},{24,8},{1,17},{9,25},{17,1},{25,9},{2,18},{10... | collective-permute-start | bytes 884744 | tf_op jit(solution)/shard_map/ppermute | solution.py:623
  578.9 86.4 %collective-permute-start.28 = (bf16[2,96,768]{2,1,0:T(8,128)(2,1)}, bf16[2,96,768]{2,1,0:T(8,128)(2,1)S(1)}, u32[]{:S(2)}, u32[]{:S(2)}) collective-permute-start(bf16[2,96,768]{2,1,0:T(8,128)(2,1)} %get-tuple-element.337), channel_id=1, source_target_pairs={{0,8},{8,0},{16,24},{24,16},{1,9},{9,1},{17,25},{25,17},{2,10},{10... | collective-permute-start | bytes 884744 | tf_op jit(solution)/shard_map/ppermute | solution.py:623
  (20 other events, 47.0 us)
Sparse Core Ops, SparseCore 0:
  9.6 38.0 all-gather.7
  49.8 37.5 all-gather.5

commit v5 on v4

--- a/solution.py
+++ b/solution.py
@@ -322,8 +322,8 @@
     for i, (section, n) in enumerate(zip(sections, parts)):
 
         @pl.when((row >= at) & (row < at + n))
-        def _(i=i, section=section, at=at):
-            field[...] = value + section[:, row - at].astype(F32).reshape(value.shape)
+        def _(i=i, section=section):
+            field[...] = value + section[...].astype(F32).reshape(value.shape)
             for k, out in enumerate(outs[i :: len(parts)]):
                 out[...] = field[pl.ds(place[k] * quarter, quarter), :].astype(BF)
 
@@ -348,6 +348,18 @@
     def _():
         for kind in range(2):
             kept[0, kind] = products[kind]
+
+
+def add_kernel(side, kept, came, mine, theirs):
+    blocks = mine.shape[2]
+    value = [
+        (kept[i, 0] + came[i, 0].astype(F32)).reshape(blocks, 2, -1, mine.shape[4]) for i in range(2)
+    ]
+    own, other = [[jnp.where(side[0] == bit, v[:, 1], v[:, 0]) for v in value] for bit in (1, 0)]
+    even = side[1] == 0
+    for i in range(2):
+        mine[i, 0] = jnp.where(even, value[0][:, i], own[i])
+        theirs[i, 0] = jnp.where(even, value[1][:, i], other[i]).astype(BF)
 
 
 def widen_kernel(parts, slot, starts, *refs):
@@ -362,9 +374,15 @@
                 out[0, starts[part] + row] = piece[:, row * width : (row + 1) * width].astype(F32)
 
 
-def finish_kernel(feats, grads, patches, mean, rstd, one, two, out):
+def finish_kernel(feats, patches, mean, rstd, one, two, *refs):
+    grads, out = refs[:-1], refs[-1]
     normed = (patches[0].astype(F32) - mean[0]) * rstd[0]
-    out[0] = grads[0].astype(F32) - rstd[0] * (one[0] + normed * two[0]) * (1.0 / feats)
+    fix = rstd[0] * (one[0] + normed * two[0]) * (1.0 / feats)
+    at = 0
+    for grad in grads:
+        here = slice(at, at + grad.shape[2])
+        out[0, :, here] = grad[0].astype(F32) - fix[:, here]
+        at += grad.shape[2]
 
 
 def whole(shape):
@@ -383,7 +401,7 @@
         kernel,
         grid_spec=grid_spec,
         out_shape=outs,
-        compiler_params=pltpu.CompilerParams(vmem_limit_bytes=mib << 20),
+        compiler_params=pltpu.CompilerParams(vmem_limit_bytes=max(mib, 62) << 20),
         input_output_aliases=aliases or {},
         cost_estimate=pl.CostEstimate(flops=int(micros * FLOPS), bytes_accessed=int(micros * BYTES), transcendentals=0),
         name=name,
@@ -464,12 +482,12 @@
     for k in range(owners):
         piece = lax.dynamic_index_in_dim(sent_stats, (me ^ k) // inner, 0, False)
         plane_stats.append(lax.ppermute(piece, sp, [(a, a ^ k) for a in range(owners)]) if k else piece)
-    plane_stats = jnp.stack(plane_stats)
     bit = 1
     while bit < owners:
-        turned = plane_stats.reshape(-1, 2, bit, per, 2, width)
-        plane_stats = jnp.where((me // bit) % 2 == 1, turned[:, ::-1], turned).reshape(owners, per, 2, width)
+        turn = (me // bit) % 2 == 1
+        plane_stats = [jnp.where(turn, plane_stats[k ^ bit], plane_stats[k]) for k in range(owners)]
         bit *= 2
+    plane_stats = jnp.stack(plane_stats)
     plane_stats = in_order(plane_stats.reshape(rows, 2, 1, width), order)
     mean_one, rstd_one = plane_stats[:, 0], plane_stats[:, 1]
 
@@ -579,7 +597,8 @@
                 "result", functools.partial(result_kernel, quarter, parts), (per,),
                 (done[1], wp_t, lanes(small[2], 128), *received, section),
                 [pl.BlockSpec((hiddens, width), lambda h, *_: (0, h)), whole((feats, hiddens)), whole((feats, 128)),
-                 *[whole((ranks, m, mine, width)) for m in parts]],
+                 *[pl.BlockSpec((ranks, 1, mine, width), lambda h, *_, at=at, m=m: (0, jnp.clip(h - at, 0, m - 1), 0, 0))
+                   for at, m in zip((0, parts[0]), parts)]],
                 [shape((quarter, m * width), BF) for _ in range(tp) for m in parts],
                 [pl.BlockSpec((quarter, width), lambda h, *_, at=at, m=m: (0, jnp.clip(h - at, 0, m - 1)))
                  for _ in range(tp) for at, m in zip((0, parts[0]), parts)],
@@ -632,9 +651,24 @@
         [*part_specs, *lon_f, *lat_specs], shape(mine_modes, BF), modes_spec, scratch, 48, 0.01,
     )
     freq, came = lax.optimization_barrier((freq, came))
-    weights = (kept_products + came.astype(F32)).reshape(half, 2, owners // 2, 2, feats // owners, hidden_local)
-    weights, theirs = halves(jnp.moveaxis(weights, 3, 0), 1)
-    came = trade(theirs.astype(BF), sp, 1, owners)
+    side = jnp.stack([me % 2, t % 2]).astype(jnp.int32)
+    strip = feats // owners
+    third = hidden_local // 3
+    halves_shape = (2, 2, owners // 2, strip, hidden_local)
+    halves_block = pl.BlockSpec((2, 1, owners // 2, strip, third), lambda kind, i, _: (0, kind, 0, 0, i))
+    weights, theirs = run(
+        "add", add_kernel, (2, 3), (kept_products, came),
+        [pl.BlockSpec((half, 1, feats, third), lambda kind, i, _: (0, kind, 0, i))] * 2,
+        (shape(halves_shape, F32), shape(halves_shape, BF)), (halves_block, halves_block), [], 48, 0.01, (side,),
+    )
+    steps_first = [
+        (rank, rank ^ 2 if rank % 2 == 0 else rank ^ tp) for rank in range(planes * inner * tp)
+    ]
+    steps_second = [(rank, rank ^ tp if rank % 2 == 0 else rank ^ 2) for rank in range(planes * inner * tp)]
+    own_half = jnp.where(t % 2 == 0, me % 2, 0)
+    sent_half = jnp.where(t % 2 == 0, 1 - me % 2, 1)
+    freq, theirs, weights = lax.optimization_barrier((freq, theirs, weights))
+    came = lax.ppermute(theirs, every, steps_first)
     freq, inner_grad, outer_grad, inner_bias_grad, outer_bias_grad = run(
         "filter_back", filter_back_kernel, (lats // step,), (to_blocks(freq), spec, mid, slope, bend, w1, w2),
         [*[block_spec] * 5, square_spec, square_spec],
@@ -642,14 +676,34 @@
         (block_spec, *[fixed((2 * BLOCK, 2 * BLOCK))] * 2, *[fixed((2 * BLOCK, 128))] * 2), [], 48, 0.01,
     )
     freq, results = lax.optimization_barrier((freq, results))
-    grads, lines, first_gain_sum, first_shift_sum = run(
-        "last", functools.partial(last_kernel, order, len(parts)), grid,
-        (pieces, *sgrads, mean_one, rstd_one, scale1, to_features(freq), *plain_n, lat_b),
-        [piece_spec, *part_specs, stat_spec, stat_spec, feat_spec, modes_spec, *lon_b, *lat_specs],
-        (shape((rows, mine, width), BF), shape((rows, 2, width), F32), *[shape((mine, 128), F32)] * 2),
-        (image_spec, fixed((rows, 2, width)), *[pl.BlockSpec((some, 128), lambda g, *_: (g, 0))] * 2),
-        scratch, 56, 0.01,
-    )
+    cuts = [grid[0] // 2, grid[0] - grid[0] // 2] if grid[0] > 1 else [1]
+    grads, lines, first_sums, at = [], [], [], 0
+    freq = to_features(freq)
+    for i, n in enumerate(cuts):
+        here = lambda g, at=at: g + at
+        image_part = pl.BlockSpec((rows, some, width), lambda g: (0, g, 0))
+        grad, line_sums, *sums_here = run(
+            "last", functools.partial(last_kernel, order, len(parts)), (n,),
+            (pieces, *sgrads, mean_one, rstd_one, scale1, freq, *plain_n, lat_b),
+            [pl.BlockSpec((owners, per, some, width), lambda g, here=here: (0, 0, here(g), 0)),
+             *[pl.BlockSpec((ranks, m, some, width), lambda g, here=here: (0, 0, here(g), 0)) for m in parts],
+             stat_spec, stat_spec, pl.BlockSpec((some, width), lambda g, here=here: (here(g), 0)),
+             pl.BlockSpec((2, rows, some, modes), lambda g, here=here: (0, 0, here(g), 0)), *lon_b, *lat_specs],
+            (shape((rows, n * some, width), BF), shape((rows, 2, width), F32), *[shape((n * some, 128), F32)] * 2),
+            (image_part, fixed((rows, 2, width)), *[pl.BlockSpec((some, 128), lambda g: (g, 0))] * 2),
+            scratch, 56, 0.01,
+        )
+        grads.append(grad.reshape(owners, per, n * some, width))
+        lines.append(line_sums)
+        first_sums.append(sums_here)
+        at += n
+        if i < len(cuts) - 1:
+            freq, came, grads[i] = lax.optimization_barrier((freq, came, grads[i]))
+            grads[i] = lax.all_to_all(grads[i], sp, 0, 0, tiled=True)
+    weights = weights + came.astype(F32)
+    came = lax.ppermute(lax.dynamic_index_in_dim(weights, sent_half, 0, False).astype(BF), every, steps_second)
+    first_gain_sum, first_shift_sum = (jnp.concatenate(sums_here, 0) for sums_here in zip(*first_sums))
+    lines = sum(lines)
     def with_bias(full, bias):
         bias = jnp.sum(bias, 1).reshape(2, BLOCK)
         return jnp.concatenate([weight_pair(full), bias[:, :, None]], 2)
@@ -660,19 +714,13 @@
         [jnp.sum(gain_sum, 1), jnp.sum(shift_sum, 1), jnp.sum(cot_sum, 1), jnp.sum(bias_sum, 1), jnp.sum(share)[None]]
     )
     grads, lines, results, came = lax.optimization_barrier((grads, lines, results, came))
-    weights = weights + came.astype(F32)
-    weights = jnp.moveaxis(weights[0] + trade(weights[1].astype(BF), "t", 2, tp).astype(F32), 1, 0)
+    weights = jnp.moveaxis(lax.dynamic_index_in_dim(weights, own_half, 0, False) + came.astype(F32), 1, 0)
     bit = 2
     while bit < inner:
         weights = weights.reshape(-1, 2, *weights.shape[1:])
         weights, theirs = halves(weights.swapaxes(0, 1), bit)
         weights = weights + trade(theirs.astype(BF), sp, bit, owners).astype(F32)
         bit *= 2
-    expand_sum, project_sum = sum(
-        trade(lax.dynamic_index_in_dim(weights, z ^ k, 0, False).astype(BF), "z", k, planes).astype(F32)
-        for k in range(1, planes)
-    ) + lax.dynamic_index_in_dim(weights, z, 0, False)
-    project_sum = project_sum.T
     line = per * width
     feature_sums = jnp.stack([jnp.sum(first_gain_sum, 1) * keep, jnp.sum(first_shift_sum, 1) * keep]).reshape(-1)
     tail = jnp.concatenate(
@@ -680,8 +728,16 @@
          jnp.broadcast_to(jnp.concatenate([feature_sums, early]), (owners, 2 * mine + early.shape[0]))], 1
     )
     tail = lax.all_to_all(tail, sp, 0, 0, tiled=True)
-    tail, grads = lax.optimization_barrier((tail, grads))
-    grads = lax.all_to_all(grads.reshape(owners, per, mine, width), sp, 0, 0, tiled=True)
+    tail, grads, weights = lax.optimization_barrier((tail, grads, weights))
+    def along_z(weights, bit):
+        weights = weights.reshape(-1, 2, *weights.shape[1:])
+        side = (z // bit) % 2
+        theirs = lax.dynamic_index_in_dim(weights, 1 - side, 1, False).astype(BF)
+        return lax.dynamic_index_in_dim(weights, side, 1, False) + trade(theirs, "z", bit, planes).astype(F32)
+
+    weights = along_z(weights, 1)
+    grads[-1] = lax.all_to_all(grads[-1], sp, 0, 0, tiled=True)
+    grads[-1], weights = lax.optimization_barrier((grads[-1], weights))
     cuts = [2 * line, 2 * line + filters.shape[1], 2 * line + filters.shape[1] + 2 * mine]
     lines, filters, feature_sums, early = jnp.split(tail, cuts, axis=1)
     lines = jnp.sum(lines.reshape(planes, inner, -1), 1).reshape(-1)
@@ -711,11 +767,14 @@
     patch_spec = pl.BlockSpec((1, per, mine, width), lambda i: (i // inner, 0, i % inner, 0))
     patches_grad = run(
         "finish", functools.partial(finish_kernel, feats), (owners,),
-        (grads, patches, stats[:, :, 0, None], stats[:, :, 1, None], fixes[:, :, 0], fixes[:, :, 1]),
-        [pl.BlockSpec((1, per, mine, width), lambda i: (i, 0, 0, 0)), patch_spec, *[one_spec] * 4],
-        shape((snaps, per, quarter, width), F32), patch_spec, [], 48, 11,
-    )
-
+        (patches, stats[:, :, 0, None], stats[:, :, 1, None], fixes[:, :, 0], fixes[:, :, 1], *grads),
+        [patch_spec, *[one_spec] * 4,
+         *[pl.BlockSpec((1, per, grad.shape[2], width), lambda i: (i, 0, 0, 0)) for grad in grads]],
+        shape((snaps, per, quarter, width), F32), patch_spec, [], 48, 100,
+    )
+
+    expand_sum, project_sum = along_z(weights, 2)[0]
+    project_sum = project_sum.T
     return (
         result, patches_grad, last[0], last[1], filters[0, ..., :BLOCK], filters[0, ..., BLOCK],
         filters[1, ..., :BLOCK], filters[1, ..., BLOCK],

time: 696 us -> 681 us (0.978)
  blocking collectives: 37 us -> 17.7 us
  Pallas kernels: 254 us -> 269 us
  starting transfers between devices: 97.3 us -> 106 us
  other arithmetic: 37.4 us -> 29.9 us
    ppermute x7 -> x4, waiting for transfers between devices: 98.8 us -> 31 us  [trade(): return lax.ppermute(theirs, axes, [(a, a ^ bit) for a in range(size)])]
    all_to_all x1 -> x3, waiting for transfers between devices: 0.01 us -> 24.5 us  [the longest x1 12 us: per_device(): grads[i] = lax.all_to_all(grads[i], sp, 0, 0, tiled=True)]
    ppermute x8, waiting for transfers between devices: 1.82 us -> 24.9 us  [send_results(): lax.ppermute(rows_out[2 * k + part], every, route(k, part, True))]
    all_to_all x1 -> x0, blocking collectives: 19.3 us -> none  [per_device(): tail = lax.all_to_all(tail, sp, 0, 0, tiled=True)]
    pallas_call x12 -> x14, Pallas kernels: 254 us -> 269 us  [run(): return call(*scalars, *ins)]
    ppermute x0 -> x2, waiting for transfers between devices: none -> 14.8 us  [the longest x1 14.8 us: per_device(): lax.ppermute(lax.dynamic_index_in_dim(weights, sent_half, 0, False).astyp...]
    unnamed x117 -> x103, local copies, waits for them, and re-layouts: 20 us -> 9.01 us
    all_to_all x1 -> x3, starting transfers between devices: 4.95 us -> 15.2 us  [the longest x1 6.23 us: per_device(): grads[i] = lax.all_to_all(grads[i], sp, 0, 0, tiled=True)]
  transfers between devices with their start and end apart: 39 -> 40, of which waited for: 10 -> 15; matrix products, arithmetic and copies ran while one was open for 12% -> 12% of each run, Pallas kernels for 34% -> 37%
where the time goes in v5:
time: 681 us; the launch traced here: 670 us
  Pallas kernels  269 us (40%)
  waiting for transfers between devices  175 us (26%)
  starting transfers between devices  106 us (16%)
  local copies, waits for them, and re-layouts  54.5 us (8%)
  other arithmetic  29.9 us (4%)
  between operations  18.2 us (3%)
  blocking collectives  17.7 us (3%)
    pallas_call x14, Pallas kernels, run(): return call(*scalars, *ins)  269 us
    all_to_all x4, starting transfers between devices, exchange(): return lax.all_to_all(array, ('t', 'y', 'j'), 0, 0, tiled=True)  31 us
    ppermute x4, waiting for transfers between devices, trade(): return lax.ppermute(theirs, axes, [(a, a ^ bit) for a in range(size)])  31 us
    all_to_all x4, waiting for transfers between devices, exchange(): return lax.all_to_all(array, ('t', 'y', 'j'), 0, 0, tiled=True)  28.8 us
    ppermute x7, waiting for transfers between devices, per_device(): lax.ppermute(piece, sp, [(a, a ^ k) for a in range(owners)])  25.7 us
    ppermute x8, waiting for transfers between devices, send_results(): lax.ppermute(rows_out[2 * k + part], every, route(k, part, True))  24.9 us
    all_gather x1, waiting for transfers between devices, per_device(): wp = lax.all_gather(project_weight, 't', tiled=True)  24.4 us
    ppermute x8, starting transfers between devices, send_results(): lax.ppermute(rows_out[2 * k + part], every, route(k, part, True))  20.1 us
  transfers between devices with their start and end apart: 40, of which 15 were waited for; matrix products, arithmetic and copies ran while one was open for 12% of the time, Pallas kernels for 37%

profile of v5, /device:TPU:2, one launch (start us, length us, event | category | flops | bytes accessed | tf_op | source)
XLA Modules:
  0.0 670.3 jit_solution(3039716598547323313)
XLA Ops:
  8.0 2.4 copy.233
  10.4 2.8 fusion.15
  13.1 2.6 pad_maximum_fusion
  15.8 6.0 all-to-all-start
  23.4 11.6 %all-reduce = f32[5376]{0:T(1024)S(1)} all-reduce(f32[5376]{0:T(1024)S(1)} %dynamic-update-slice), channel_id=4, replica_groups=mesh['z'=4,'y'=2,'j'=1,'t'=4] {'t'}, use_global_device_ids=true, to_apply=%add | all-reduce | flops 5376 | bytes 43008
  35.1 3.3 convert_reduce_fusion
  38.4 4.2 fusion.1
  44.9 6.1 all-gather
  52.0 4.0 dynamic-slice_bitcast_fusion
  56.0 7.0 %copy.234 = bf16[4,768,768]{2,1,0:T(8,128)(2,1)} copy(bf16[4,768,768]{1,2,0:T(8,128)(2,1)} %bitcast.194) | data formatting | bytes 9437184 | tf_op jit(solution)/shard_map/transpose | solution.py:476
  63.1 24.4 %all-gather.6.cloned.1.call-done = bf16[3072,768]{0,1:T(8,128)(2,1)} async-done(((bf16[768,768]{0,1:T(8,128)(2,1)}), bf16[3072,768]{0,1:T(8,128)(2,1)}) %all-gather.6.cloned.1.call-update) | async-done | bytes 4718608 | tf_op jit(solution)/shard_map/all_gather | solution.py:475
  89.5 1.7 broadcast_in_dim.70.refs_8_
  91.4 1.8 collective-permute-start.6
  96.0 3.6 collective-permute-start.2
  100.3 3.4 collective-permute-start
  104.9 25.6 %collective-permute-done.2 = f32[12,2,256]{2,1,0:T(2,128)S(1)} collective-permute-done((f32[12,2,256]{2,1,0:T(2,128)S(1)}, f32[12,2,256]{2,1,0:T(2,128)S(1)}, u32[]{:S(2)}, u32[]{:S(2)}) %collective-permute-start.2) | collective-permute-done | bytes 24608 | tf_op jit(solution)/shard_map/ppermute | solution.py:484
  131.9 2.9 collective-permute-start.7
  135.1 3.5 collective-permute-start.9
  140.3 20.2 %spectrum.1.spec = bf16[2,96,96,128]{3,2,1,0:T(8,128)(2,1)} custom-call(bf16[8,12,96,256]{3,2,1,0:T(8,128)(2,1)} %all-to-all-done.pieces, f32[96,1,256]{2,1,0:T(1,128)} %get-tuple-element.394.mean.refs_2_, f32[96,1,256]{2,1,0:T(1,128)} %get-tuple-element.393.rstd.refs_3_, f32[96,256]{1,0:T(8,128)} %broadcast_in_dim.71.scale.refs_4_, ...), custom_call_target="tpu_custom_call" | custom-call | flops 22000001024 | bytes 74800000 | tf_op jit(solution)/shard_map/spectrum/pallas_call | solution.py:409
  162.0 14.6 %filter.1 = (bf16[2,96,96,128]{3,2,1,0:T(8,128)(2,1)}, bf16[2,96,96,128]{3,2,1,0:T(8,128)(2,1)}, bf16[2,96,96,128]{3,2,1,0:T(8,128)(2,1)}, bf16[2,96,96,128]{3,2,1,0:T(8,128)(2,1)}, f32[8,256]{1,0:T(8,128)}) custom-call(bf16[2,96,96,128]{3,2,1,0:T(8,128)(2,1)} %spectrum.1.spec, bf16[192,192]{1,0:T(8,128)(2,1)} %maximum_maximum_fusion.w1, ...), custom_call_target="tpu_custom_call" | custom-call | flops 16999999488 | bytes 57800000 | tf_op jit(solution)/shard_map/filter/pallas_call | solution.py:409
  176.6 13.4 %section.1 = (bf16[8,6,96,256]{3,2,1,0:T(8,128)(2,1)}, bf16[8,6,96,256]{3,2,1,0:T(8,128)(2,1)}) custom-call(bf16[8,12,96,256]{3,2,1,0:T(8,128)(2,1)} %all-to-all-done.pieces, f32[96,1,256]{2,1,0:T(1,128)} %get-tuple-element.394.mean.refs_2_, f32[96,1,256]{2,1,0:T(1,128)} %get-tuple-element.393.rstd.refs_3_, f32[96,256]{1,0:T(8,128)} %broadcast_in_dim.71.scale.refs_4_, ...), custom_call_target="tpu_custom_call" | custom-call | flops 16999999488 | bytes 57800000 | tf_op jit(solution)/shard_map/section/pallas_call | solution.py:409
  190.0 13.6 %all-to-all-start.1 = ((bf16[8,6,96,256]{3,2,1,0:T(8,128)(2,1)}), bf16[8,6,96,256]{3,2,1,0:T(8,128)(2,1)}, u32[]{:S(2)}, u32[]{:S(2)}) async-start(bf16[8,6,96,256]{3,2,1,0:T(8,128)(2,1)} %get-tuple-element.169), calls=%async_computation.1 | async-start | bytes 4718592 | tf_op jit(solution)/shard_map/all_to_all | solution.py:566
  204.2 6.6 copy.246.refs_6_
  210.8 20.3 %all-to-all-done.1.refs_4_.refs_0_ = bf16[8,6,96,256]{3,2,1,0:T(8,128)(2,1)} async-done(((bf16[8,6,96,256]{3,2,1,0:T(8,128)(2,1)}), bf16[8,6,96,256]{3,2,1,0:T(8,128)(2,1)}, u32[]{:S(2)}, u32[]{:S(2)}) %all-to-all-start.1) | async-done | bytes 2359328 | tf_op jit(solution)/shard_map/all_to_all | solution.py:566
  231.2 5.8 all-to-all-start.2
  237.0 2.1 collective-permute-start.11
  239.1 3.1 collective-permute-start.12
  244.5 35.5 %feed.2 = (bf16[768,3072]{1,0:T(8,128)(2,1)}, bf16[3072,3072]{1,0:T(8,128)(2,1)}, bf16[3072,3072]{1,0:T(8,128)(2,1)}, bf16[768,3072]{1,0:T(8,128)(2,1)}, bf16[8,...) custom-call(s32[4]{0:T(128)} %pad_add_fusion.2.place, ...), custom_call_target="tpu_custom_call" | custom-call | flops 43000000512 | bytes 146200000 | tf_op jit(solution)/shard_map/feed/pallas_call | solution.py:409
  280.0 8.5 %all-to-all-done.2.refs_4_.refs_1_ = bf16[8,6,96,256]{3,2,1,0:T(8,128)(2,1)} async-done(((bf16[8,6,96,256]{3,2,1,0:T(8,128)(2,1)}), bf16[8,6,96,256]{3,2,1,0:T(8,128)(2,1)}, u32[]{:S(2)}, u32[]{:S(2)}) %all-to-all-start.2) | async-done | bytes 2359328 | tf_op jit(solution)/shard_map/all_to_all | solution.py:566
  288.5 7.2 %all-to-all-start.3 = ((bf16[8,6,96,256]{3,2,1,0:T(8,128)(2,1)}), bf16[8,6,96,256]{3,2,1,0:T(8,128)(2,1)}, u32[]{:S(2)}, u32[]{:S(2)}) async-start(bf16[8,6,96,256]{3,2,1,0:T(8,128)(2,1)} %get-tuple-element.199), calls=%async_computation.3 | async-start | bytes 4718592 | tf_op jit(solution)/shard_map/all_to_all | solution.py:566
  295.7 35.5 %feed.3 = (bf16[768,3072]{1,0:T(8,128)(2,1)}, bf16[3072,3072]{1,0:T(8,128)(2,1)}, bf16[3072,3072]{1,0:T(8,128)(2,1)}, bf16[768,3072]{1,0:T(8,128)(2,1)}, bf16[8,...) custom-call(s32[4]{0:T(128)} %pad_add_fusion.2.place, ...), custom_call_target="tpu_custom_call", output_to_operand_aliasing={{0}: (12, {}), {1}: (13, {}), {2}: (14, {}), {3}: (15, {})} | custom-call | flops 43000000512 | bytes 146200000 | tf_op jit(solution)/shard_map/feed/pallas_call | solution.py:409
  331.3 4.4 all-to-all-start.4
  336.7 24.1 %result.1 = (bf16[192,1536]{1,0:T(8,128)(2,1)}, bf16[192,1536]{1,0:T(8,128)(2,1)}, bf16[192,1536]{1,0:T(8,128)(2,1)}, bf16[192,1536]{1,0:T(8,128)(2,1)}, bf16[19...) custom-call(s32[4]{0:T(128)} %pad_add_fusion.2.place, ...), custom_call_target="tpu_custom_call" | custom-call | flops 10000000 | bytes 34000 | tf_op jit(solution)/shard_map/result/pallas_call | solution.py:409
  360.8 1.9 collective-permute-start.15
  362.7 2.6 collective-permute-start.17
  365.4 2.6 collective-permute-start.18
  368.6 41.5 %weights.1 = (bf16[2,2,768,768]{3,2,1,0:T(8,128)(2,1)}, f32[2,2,768,768]{3,2,1,0:T(8,128)}, f32[3072,128]{1,0:T(8,128)}, f32[768,128]{1,0:T(8,128)}) custom-call(s32[4]{0:T(128)} %pad_add_fusion.3.order, bf16[768,3072]{1,0:T(8,128)(2,1)} %get-tuple-element.215.normal, bf16[3072,3072]{1,0:T(8,128)(2,1)} %get-tuple-element.216.pre, ...), custom_call_target="tpu_custom_call" | custom-call | flops 10000000 | bytes 34000 | tf_op jit(solution)/shard_map/weights/pallas_call | solution.py:409
  411.1 2.6 collective-permute-done.18.refs_3_
  414.3 16.6 %spectrum_back.1.freq = bf16[2,96,96,128]{3,2,1,0:T(8,128)(2,1)} custom-call(bf16[8,6,96,256]{3,2,1,0:T(8,128)(2,1)} %all-to-all-done.3.refs_0_, bf16[8,6,96,256]{3,2,1,0:T(8,128)(2,1)} %all-to-all-done.4.refs_1_, bf16[256,256]{1,0:T(8,128)(2,1)} %constant.399.clone.refs_2_, bf16[256,256]{1,0:T(8,128)(2,1)} %constant.400.clone.refs_3_, ...), custom_call_target="tpu_custom_call" | custom-call | flops 10000000 | bytes 34000 | tf_op jit(solution)/shard_map/spectrum_back/pallas_call | solution.py:409
  430.9 10.0 %add.419 = (f32[2,2,4,96,768]{4,3,2,1,0:T(8,128)}, bf16[2,2,4,96,768]{4,3,2,1,0:T(8,128)(2,1)}) custom-call(s32[2]{0:T(128)} %pad_add_fusion.4.side, f32[2,2,768,768]{3,2,1,0:T(8,128)} %get-tuple-element.231.kept, bf16[2,2,768,768]{3,2,1,0:T(8,128)(2,1)} %collective-permute-done.19.came), custom_call_target="tpu_custom_call" | custom-call | flops 10000000 | bytes 34000 | tf_op jit(solution)/shard_map/add/pallas_call | solution.py:409
  441.9 2.6 collective-permute-start.20
  444.5 4.2 collective-permute-start.21
  448.7 6.1 collective-permute-start.23
  454.8 19.3 %filter_back.1 = (bf16[2,96,96,128]{3,2,1,0:T(8,128)(2,1)}, f32[192,192]{1,0:T(8,128)}, f32[192,192]{1,0:T(8,128)}, f32[192,128]{1,0:T(8,128)}, f32[192,128]{1,0:T(8,128)}) custom-call(bf16[2,96,96,128]{3,2,1,0:T(8,128)(2,1)} %spectrum_back.1.freq, bf16[2,96,96,128]{3,2,1,0:T(8,128)(2,1)} %spectrum.1.spec, bf16[2,96,96,128]{3,2,1,0:T(8,128)(2,1)} %get-tuple-element.236.mid, ...), custom_call_target="tpu_custom_call" | custom-call | flops 10000000 | bytes 34000 | tf_op jit(solution)/shard_map/filter_back/pallas_call | solution.py:409
  474.1 19.8 %collective-permute-done.21.refs_5_ = bf16[192,1536]{1,0:T(8,128)(2,1)S(1)} collective-permute-done((bf16[192,1536]{1,0:T(8,128)(2,1)}, bf16[192,1536]{1,0:T(8,128)(2,1)S(1)}, u32[]{:S(2)}, u32[]{:S(2)}) %collective-permute-start.21) | collective-permute-done | bytes 589856 | tf_op jit(solution)/shard_map/ppermute | solution.py:613
  496.2 10.4 %last.2 = (bf16[96,48,256]{2,1,0:T(8,128)(2,1)}, f32[96,2,256]{2,1,0:T(2,128)}, f32[48,128]{1,0:T(8,128)}, f32[48,128]{1,0:T(8,128)}) custom-call(bf16[8,12,96,256]{3,2,1,0:T(8,128)(2,1)} %all-to-all-done.pieces, bf16[8,6,96,256]{3,2,1,0:T(8,128)(2,1)} %all-to-all-done.3.refs_0_, bf16[8,6,96,256]{3,2,1,0:T(8,128)(2,1)} %all-to-all-done.4.refs_1_, ...), custom_call_target="tpu_custom_call" | custom-call | flops 10000000 | bytes 34000 | tf_op jit(solution)/shard_map/last/pallas_call | solution.py:409
  506.6 6.2 all-to-all-start.5
  517.0 3.6 convert_add_fusion
  520.7 2.2 copy-done
  523.0 2.1 collective-permute-start.25
  526.5 10.5 %last.3 = (bf16[96,48,256]{2,1,0:T(8,128)(2,1)}, f32[96,2,256]{2,1,0:T(2,128)}, f32[48,128]{1,0:T(8,128)}, f32[48,128]{1,0:T(8,128)}) custom-call(bf16[8,12,96,256]{3,2,1,0:T(8,128)(2,1)} %all-to-all-done.pieces, bf16[8,6,96,256]{3,2,1,0:T(8,128)(2,1)} %all-to-all-done.3.refs_0_, bf16[8,6,96,256]{3,2,1,0:T(8,128)(2,1)} %all-to-all-done.4.refs_1_, ...), custom_call_target="tpu_custom_call" | custom-call | flops 10000000 | bytes 34000 | tf_op jit(solution)/shard_map/last/pallas_call | solution.py:409
  540.6 14.8 %collective-permute-done.25 = bf16[2,4,96,768]{3,2,1,0:T(8,128)(2,1)} collective-permute-done((bf16[2,4,96,768]{3,2,1,0:T(8,128)(2,1)S(1)}, bf16[2,4,96,768]{3,2,1,0:T(8,128)(2,1)}, u32[]{:S(2)}, u32[]{:S(2)}) %collective-permute-start.25) | collective-permute-done | bytes 1179680 | tf_op jit(solution)/shard_map/ppermute | solution.py:704
  555.4 12.0 %all-to-all-done.5.refs_0_ = bf16[8,12,48,256]{3,2,1,0:T(8,128)(2,1)} async-done(((bf16[8,12,48,256]{3,2,1,0:T(8,128)(2,1)}), bf16[8,12,48,256]{3,2,1,0:T(8,128)(2,1)}, u32[]{:S(2)}, u32[]{:S(2)}) %all-to-all-start.5) | async-done | bytes 2359328 | tf_op jit(solution)/shard_map/all_to_all | solution.py:702
  568.9 4.4 all-to-all-start.6
  573.3 3.7 fusion.2
  577.0 11.3 %all-to-all-done.6 = f32[8,1,16369]{2,1,0:T(1,128)S(1)} async-done(((f32[8,1,16369]{2,1,0:T(1,128)}), f32[8,1,16369]{2,1,0:T(1,128)S(1)}, u32[]{:S(2)}, u32[]{:S(2)}) %all-to-all-start.6) | async-done | bytes 523840 | tf_op jit(solution)/shard_map/all_to_all | solution.py:730
  588.6 4.6 all-to-all-start.7
  595.8 6.9 %widen.1 = f32[4,12,192,256]{3,2,1,0:T(8,128)} custom-call(s32[4]{0:T(128)} %pad_add_fusion.slot, s32[2]{0:T(128)} %pad_add_fusion.1.starts, bf16[192,1536]{1,0:T(8,128)(2,1)} %copy-done.31, bf16[192,1536]{1,0:T(8,128)(2,1)} %copy-done.32, bf16[192,1536]{1,0:T(8,128)(2,1)} %copy-done.33, bf16[192,1536]{1,0:T(8,128)(2,1)} %collective-permute-done.18.refs_3_, ...), custom_call_target="tpu_custom_call" | custom-call | flops 8000000000 | bytes 27200000 | tf_op jit(solution)/shard_map/widen/pallas_call | solution.py:409
  603.8 2.2 fusion.4
  605.9 2.0 collective-permute-start.28
  611.2 3.4 collective-permute-done.27
  617.8 26.5 %collective-permute-done.28 = bf16[2,2,96,768]{3,2,1,0:T(8,128)(2,1)} collective-permute-done((bf16[2,2,96,768]{3,2,1,0:T(8,128)(2,1)}, bf16[2,2,96,768]{3,2,1,0:T(8,128)(2,1)}, u32[]{:S(2)}, u32[]{:S(2)}) %collective-permute-start.28) | collective-permute-done | bytes 589856 | tf_op jit(solution)/shard_map/ppermute | solution.py:642
  646.7 2.8 collective-permute-start.29
  649.5 10.6 %finish.1 = f32[4,12,192,256]{3,2,1,0:T(8,128)} custom-call(bf16[4,12,192,256]{3,2,1,0:T(8,128)(2,1)} %patches.1, f32[4,12,1,256]{3,2,1,0:T(1,128)} %copy.260.mean, f32[4,12,1,256]{3,2,1,0:T(1,128)} %copy.261.rstd, f32[4,12,1,256]{3,2,1,0:T(1,128)} %get-tuple-element.401.one, f32[4,12,1,256]{3,2,1,0:T(1,128)} %get-tuple-element.400.two, ...), custom_call_target="tpu_custom_call" | custom-call | flops 99999997952 | bytes 340000000 | tf_op jit(solution)/shard_map/finish/pallas_call | solution.py:409
  (272 shorter events, 50.4 us)
Async XLA Ops:
  7.2 48.8 %all-gather.8.cloned.1.call-start = ((), (), s32[]{:S(2)}) async-start(), calls=%async_computation.9 | async-start | bytes 5898240 | tf_op jit(solution)/shard_map/all_gather | solution.py:474
  7.9 79.5 %all-gather.6.cloned.1.call-start = ((), (), s32[]{:S(2)}) async-start(), calls=%async_computation.8 | async-start | bytes 5898240 | tf_op jit(solution)/shard_map/all_gather | solution.py:475
  15.7 7.3 %copy-start.24 = (f32[192]{0:T(256)S(1)}, f32[192]{0:T(256)}, u32[]{:S(2)}) copy-start(f32[192]{0:T(256)} %param.35) | copy-start | bytes 2308
  15.7 7.3 %copy-start.25 = (f32[192]{0:T(256)S(1)}, f32[192]{0:T(256)}, u32[]{:S(2)}) copy-start(f32[192]{0:T(256)} %param.36) | copy-start | bytes 2308
  15.7 7.3 %copy-start.26 = (f32[192]{0:T(256)S(1)}, f32[192]{0:T(256)}, u32[]{:S(2)}) copy-start(f32[192]{0:T(256)} %param.40) | copy-start | bytes 2308
  15.8 19.3 %copy-start.17 = (bf16[2,2,96,96]{3,2,1,0:T(8,128)(2,1)S(1)}, bf16[2,2,96,96]{3,2,1,0:T(8,128)(2,1)}, u32[]{:S(2)}) copy-start(bf16[2,2,96,96]{3,2,1,0:T(8,128)(2,1)} %param.33) | copy-start | bytes 221188
  15.8 19.3 %copy-start.18 = (bf16[2,2,96,96]{3,2,1,0:T(8,128)(2,1)S(1)}, bf16[2,2,96,96]{3,2,1,0:T(8,128)(2,1)}, u32[]{:S(2)}) copy-start(bf16[2,2,96,96]{3,2,1,0:T(8,128)(2,1)} %param.31) | copy-start | bytes 221188
  15.8 116.2 %all-to-all-start = ((bf16[8,12,96,256]{3,2,1,0:T(8,128)(2,1)}), bf16[8,12,96,256]{3,2,1,0:T(8,128)(2,1)}, u32[]{:S(2)}, u32[]{:S(2)}) async-start(bf16[8,12,96,256]{3,2,1,0:T(8,128)(2,1)} %bitcast.190), calls=%async_computation | async-start | bytes 9437184 | tf_op jit(solution)/shard_map/all_to_all | solution.py:445
  35.1 8.1 %copy-start.29 = (f32[192]{0:T(256)S(1)}, f32[192]{0:T(256)}, u32[]{:S(2)}) copy-start(f32[192]{0:T(256)} %param.30) | copy-start | bytes 2308
  38.4 13.0 %copy-start.30 = (f32[192]{0:T(256)S(1)}, f32[192]{0:T(256)}, u32[]{:S(2)}) copy-start(f32[192]{0:T(256)} %param.29) | copy-start | bytes 2308
  44.0 12.0 %copy-start.21 = (f32[96]{0:T(128)}, f32[96]{0:T(128)S(1)}, u32[]{:S(2)}) copy-start(f32[96]{0:T(128)S(1)} %get-tuple-element.360) | copy-start | bytes 1156
  56.0 48.6 %copy-start.27 = (f32[2,2,96]{2,1,0:T(2,128)S(1)}, f32[2,2,96]{2,1,0:T(2,128)}, u32[]{:S(2)}) copy-start(f32[2,2,96]{2,1,0:T(2,128)} %param.32) | copy-start | bytes 4612
  56.0 48.6 %copy-start.28 = (f32[2,2,96]{2,1,0:T(2,128)S(1)}, f32[2,2,96]{2,1,0:T(2,128)}, u32[]{:S(2)}) copy-start(f32[2,2,96]{2,1,0:T(2,128)} %param.34) | copy-start | bytes 4612
  91.4 8.9 %collective-permute-start.6 = (f32[12,2,256]{2,1,0:T(2,128)S(1)}, f32[12,2,256]{2,1,0:T(2,128)S(1)}, u32[]{:S(2)}, u32[]{:S(2)}) collective-permute-start(f32[12,2,256]{2,1,0:T(2,128)S(1)} %bitcast.244), channel_id=1, source_target_pairs={{0,4},{4,0},{8,12},{12,8},{16,20},{20,16},{24,28},{28,24},{1,5},{5... | collective-permute-start | bytes 73736 | tf_op jit(solution)/shard_map/ppermute | solution.py:484
  93.2 10.4 %collective-permute-start.4 = (f32[12,2,256]{2,1,0:T(2,128)S(1)}, f32[12,2,256]{2,1,0:T(2,128)S(1)}, u32[]{:S(2)}, u32[]{:S(2)}) collective-permute-start(f32[12,2,256]{2,1,0:T(2,128)S(1)} %bitcast.243), channel_id=1, source_target_pairs={{0,12},{4,8},{8,4},{12,0},{16,28},{20,24},{24,20},{28,16},{1,13},{... | collective-permute-start | bytes 73736 | tf_op jit(solution)/shard_map/ppermute | solution.py:484
  95.6 9.2 %collective-permute-start.5 = (f32[12,2,256]{2,1,0:T(2,128)S(1)}, f32[12,2,256]{2,1,0:T(2,128)S(1)}, u32[]{:S(2)}, u32[]{:S(2)}) collective-permute-start(f32[12,2,256]{2,1,0:T(2,128)S(1)} %bitcast.238), channel_id=1, source_target_pairs={{0,8},{4,12},{8,0},{12,4},{16,24},{20,28},{24,16},{28,20},{1,9},{5... | collective-permute-start | bytes 73736 | tf_op jit(solution)/shard_map/ppermute | solution.py:484
  96.0 34.5 %collective-permute-start.2 = (f32[12,2,256]{2,1,0:T(2,128)S(1)}, f32[12,2,256]{2,1,0:T(2,128)S(1)}, u32[]{:S(2)}, u32[]{:S(2)}) collective-permute-start(f32[12,2,256]{2,1,0:T(2,128)S(1)} %bitcast.239), channel_id=1, source_target_pairs={{0,20},{4,16},{8,28},{12,24},{16,4},{20,0},{24,12},{28,8},{1,21},{... | collective-permute-start | bytes 73736 | tf_op jit(solution)/shard_map/ppermute | solution.py:484
  99.7 30.8 %collective-permute-start.3 = (f32[12,2,256]{2,1,0:T(2,128)S(1)}, f32[12,2,256]{2,1,0:T(2,128)S(1)}, u32[]{:S(2)}, u32[]{:S(2)}) collective-permute-start(f32[12,2,256]{2,1,0:T(2,128)S(1)} %bitcast.240), channel_id=1, source_target_pairs={{0,16},{4,20},{8,24},{12,28},{16,0},{20,4},{24,8},{28,12},{1,17},{... | collective-permute-start | bytes 73736 | tf_op jit(solution)/shard_map/ppermute | solution.py:484
  100.3 30.2 %collective-permute-start = (f32[12,2,256]{2,1,0:T(2,128)S(1)}, f32[12,2,256]{2,1,0:T(2,128)S(1)}, u32[]{:S(2)}, u32[]{:S(2)}) collective-permute-start(f32[12,2,256]{2,1,0:T(2,128)S(1)} %bitcast.242), channel_id=1, source_target_pairs={{0,28},{4,24},{8,20},{12,16},{16,12},{20,8},{24,4},{28,0},{1,29},{... | collective-permute-start | bytes 73736 | tf_op jit(solution)/shard_map/ppermute | solution.py:484
  103.7 26.8 %collective-permute-start.1 = (f32[12,2,256]{2,1,0:T(2,128)S(1)}, f32[12,2,256]{2,1,0:T(2,128)S(1)}, u32[]{:S(2)}, u32[]{:S(2)}) collective-permute-start(f32[12,2,256]{2,1,0:T(2,128)S(1)} %bitcast.241), channel_id=1, source_target_pairs={{0,24},{4,28},{8,16},{12,20},{16,8},{20,12},{24,0},{28,4},{1,25},{... | collective-permute-start | bytes 73736 | tf_op jit(solution)/shard_map/ppermute | solution.py:484
  131.9 44.7 %collective-permute-start.7 = (bf16[6,192,256]{2,1,0:T(8,128)(2,1)}, bf16[6,192,256]{2,1,0:T(8,128)(2,1)}, u32[]{:S(2)}, u32[]{:S(2)}) collective-permute-start(bf16[6,192,256]{2,1,0:T(8,128)(2,1)} %get-tuple-element.160), channel_id=1, source_target_pairs={{0,0},{1,16},{2,8},{3,24},{4,4},{5,20},{6,12},{7,28},{8,2},{9,18},... | collective-permute-start | bytes 1769480 | tf_op jit(solution)/shard_map/ppermute | solution.py:516
  134.9 41.7 %collective-permute-start.8 = (bf16[6,192,256]{2,1,0:T(8,128)(2,1)}, bf16[6,192,256]{2,1,0:T(8,128)(2,1)}, u32[]{:S(2)}, u32[]{:S(2)}) collective-permute-start(bf16[6,192,256]{2,1,0:T(8,128)(2,1)} %get-tuple-element.161), channel_id=1, source_target_pairs={{0,8},{1,24},{2,16},{3,0},{4,12},{5,28},{6,20},{7,4},{8,10},{9,26}... | collective-permute-start | bytes 1769480 | tf_op jit(solution)/shard_map/ppermute | solution.py:516
  135.1 41.5 %collective-permute-start.9 = (bf16[6,192,256]{2,1,0:T(8,128)(2,1)}, bf16[6,192,256]{2,1,0:T(8,128)(2,1)}, u32[]{:S(2)}, u32[]{:S(2)}) collective-permute-start(bf16[6,192,256]{2,1,0:T(8,128)(2,1)} %get-tuple-element.162), channel_id=1, source_target_pairs={{0,16},{1,0},{2,24},{3,8},{4,20},{5,4},{6,28},{7,12},{8,18},{9,2},... | collective-permute-start | bytes 1769480 | tf_op jit(solution)/shard_map/ppermute | solution.py:516
  138.7 38.0 %collective-permute-start.10 = (bf16[6,192,256]{2,1,0:T(8,128)(2,1)}, bf16[6,192,256]{2,1,0:T(8,128)(2,1)}, u32[]{:S(2)}, u32[]{:S(2)}) collective-permute-start(bf16[6,192,256]{2,1,0:T(8,128)(2,1)} %get-tuple-element.163), channel_id=1, source_target_pairs={{0,24},{1,8},{2,0},{3,16},{4,28},{5,12},{6,4},{7,20},{8,26},{9,10}... | collective-permute-start | bytes 1769480 | tf_op jit(solution)/shard_map/ppermute | solution.py:516
  190.0 41.2 %all-to-all-start.1 = ((bf16[8,6,96,256]{3,2,1,0:T(8,128)(2,1)}), bf16[8,6,96,256]{3,2,1,0:T(8,128)(2,1)}, u32[]{:S(2)}, u32[]{:S(2)}) async-start(bf16[8,6,96,256]{3,2,1,0:T(8,128)(2,1)} %get-tuple-element.169), calls=%async_computation.1 | async-start | bytes 4718592 | tf_op jit(solution)/shard_map/all_to_all | solution.py:566
  231.2 57.3 %all-to-all-start.2 = ((bf16[8,6,96,256]{3,2,1,0:T(8,128)(2,1)}), bf16[8,6,96,256]{3,2,1,0:T(8,128)(2,1)}, u32[]{:S(2)}, u32[]{:S(2)}) async-start(bf16[8,6,96,256]{3,2,1,0:T(8,128)(2,1)} %get-tuple-element.178), calls=%async_computation.2 | async-start | bytes 4718592 | tf_op jit(solution)/shard_map/all_to_all | solution.py:566
  237.0 58.7 %collective-permute-start.11 = (bf16[6,192,256]{2,1,0:T(8,128)(2,1)}, bf16[6,192,256]{2,1,0:T(8,128)(2,1)}, u32[]{:S(2)}, u32[]{:S(2)}) collective-permute-start(bf16[6,192,256]{2,1,0:T(8,128)(2,1)} %get-tuple-element.174), channel_id=1, source_target_pairs={{0,2},{1,18},{2,10},{3,26},{4,6},{5,22},{6,14},{7,30},{8,0},{9,16}... | collective-permute-start | bytes 1769480 | tf_op jit(solution)/shard_map/ppermute | solution.py:578
  239.1 56.6 %collective-permute-start.12 = (bf16[6,192,256]{2,1,0:T(8,128)(2,1)S(1)}, bf16[6,192,256]{2,1,0:T(8,128)(2,1)}, u32[]{:S(2)}, u32[]{:S(2)}) collective-permute-start(bf16[6,192,256]{2,1,0:T(8,128)(2,1)S(1)} %get-tuple-element.175), channel_id=1, source_target_pairs={{0,10},{1,26},{2,18},{3,2},{4,14},{5,30},{6,22},{7,6},{8,8},{9,24}... | collective-permute-start | bytes 1769480 | tf_op jit(solution)/shard_map/ppermute | solution.py:578
  242.2 53.5 %collective-permute-start.13 = (bf16[6,192,256]{2,1,0:T(8,128)(2,1)S(1)}, bf16[6,192,256]{2,1,0:T(8,128)(2,1)}, u32[]{:S(2)}, u32[]{:S(2)}) collective-permute-start(bf16[6,192,256]{2,1,0:T(8,128)(2,1)S(1)} %get-tuple-element.176), channel_id=1, source_target_pairs={{0,18},{1,2},{2,26},{3,10},{4,22},{5,6},{6,30},{7,14},{8,16},{9,0}... | collective-permute-start | bytes 1769480 | tf_op jit(solution)/shard_map/ppermute | solution.py:578
  243.0 52.7 %collective-permute-start.14 = (bf16[6,192,256]{2,1,0:T(8,128)(2,1)S(1)}, bf16[6,192,256]{2,1,0:T(8,128)(2,1)}, u32[]{:S(2)}, u32[]{:S(2)}) collective-permute-start(bf16[6,192,256]{2,1,0:T(8,128)(2,1)S(1)} %get-tuple-element.177), channel_id=1, source_target_pairs={{0,26},{1,10},{2,2},{3,18},{4,30},{5,14},{6,6},{7,22},{8,24},{9,8}... | collective-permute-start | bytes 1769480 | tf_op jit(solution)/shard_map/ppermute | solution.py:578
  288.5 42.8 %all-to-all-start.3 = ((bf16[8,6,96,256]{3,2,1,0:T(8,128)(2,1)}), bf16[8,6,96,256]{3,2,1,0:T(8,128)(2,1)}, u32[]{:S(2)}, u32[]{:S(2)}) async-start(bf16[8,6,96,256]{3,2,1,0:T(8,128)(2,1)} %get-tuple-element.199), calls=%async_computation.3 | async-start | bytes 4718592 | tf_op jit(solution)/shard_map/all_to_all | solution.py:566
  331.3 82.4 %all-to-all-start.4 = ((bf16[8,6,96,256]{3,2,1,0:T(8,128)(2,1)}), bf16[8,6,96,256]{3,2,1,0:T(8,128)(2,1)}, u32[]{:S(2)}, u32[]{:S(2)}) async-start(bf16[8,6,96,256]{3,2,1,0:T(8,128)(2,1)} %get-tuple-element.201), calls=%async_computation.4 | async-start | bytes 4718592 | tf_op jit(solution)/shard_map/all_to_all | solution.py:566
  360.8 49.3 %collective-permute-start.15 = (bf16[192,1536]{1,0:T(8,128)(2,1)}, bf16[192,1536]{1,0:T(8,128)(2,1)S(1)}, u32[]{:S(2)}, u32[]{:S(2)}) collective-permute-start(bf16[192,1536]{1,0:T(8,128)(2,1)} %get-tuple-element.220), channel_id=1, source_target_pairs={{0,0},{16,1},{8,2},{24,3},{4,4},{20,5},{12,6},{28,7},{2,8},{18,9},... | collective-permute-start | bytes 1769480 | tf_op jit(solution)/shard_map/ppermute | solution.py:613
  362.7 47.4 %collective-permute-start.16 = (bf16[192,1536]{1,0:T(8,128)(2,1)}, bf16[192,1536]{1,0:T(8,128)(2,1)S(1)}, u32[]{:S(2)}, u32[]{:S(2)}) collective-permute-start(bf16[192,1536]{1,0:T(8,128)(2,1)} %get-tuple-element.221), channel_id=1, source_target_pairs={{2,0},{18,1},{10,2},{26,3},{6,4},{22,5},{14,6},{30,7},{0,8},{16,9}... | collective-permute-start | bytes 1769480 | tf_op jit(solution)/shard_map/ppermute | solution.py:613
  362.7 48.4 %collective-permute-start.17 = (bf16[192,1536]{1,0:T(8,128)(2,1)}, bf16[192,1536]{1,0:T(8,128)(2,1)S(1)}, u32[]{:S(2)}, u32[]{:S(2)}) collective-permute-start(bf16[192,1536]{1,0:T(8,128)(2,1)} %get-tuple-element.222), channel_id=1, source_target_pairs={{8,0},{24,1},{16,2},{0,3},{12,4},{28,5},{20,6},{4,7},{10,8},{26,9}... | collective-permute-start | bytes 1769480 | tf_op jit(solution)/shard_map/ppermute | solution.py:613
  365.4 48.4 %collective-permute-start.18 = (bf16[192,1536]{1,0:T(8,128)(2,1)}, bf16[192,1536]{1,0:T(8,128)(2,1)}, u32[]{:S(2)}, u32[]{:S(2)}) collective-permute-start(bf16[192,1536]{1,0:T(8,128)(2,1)} %get-tuple-element.223), channel_id=1, source_target_pairs={{10,0},{26,1},{18,2},{2,3},{14,4},{30,5},{22,6},{6,7},{8,8},{24,9}... | collective-permute-start | bytes 1769480 | tf_op jit(solution)/shard_map/ppermute | solution.py:613
  410.1 20.8 %copy-start.31 = (bf16[192,1536]{1,0:T(8,128)(2,1)}, bf16[192,1536]{1,0:T(8,128)(2,1)S(1)}, u32[]{:S(2)}) copy-start(bf16[192,1536]{1,0:T(8,128)(2,1)S(1)} %collective-permute-done.15.refs_0_) | copy-start | bytes 1769476
  410.1 20.8 %copy-start.32 = (bf16[192,1536]{1,0:T(8,128)(2,1)}, bf16[192,1536]{1,0:T(8,128)(2,1)S(1)}, u32[]{:S(2)}) copy-start(bf16[192,1536]{1,0:T(8,128)(2,1)S(1)} %collective-permute-done.16.refs_1_) | copy-start | bytes 1769476
  411.1 19.8 %copy-start.33 = (bf16[192,1536]{1,0:T(8,128)(2,1)}, bf16[192,1536]{1,0:T(8,128)(2,1)S(1)}, u32[]{:S(2)}) copy-start(bf16[192,1536]{1,0:T(8,128)(2,1)S(1)} %collective-permute-done.17.refs_2_) | copy-start | bytes 1769476
  413.7 17.2 %collective-permute-start.19 = (bf16[2,2,768,768]{3,2,1,0:T(8,128)(2,1)}, bf16[2,2,768,768]{3,2,1,0:T(8,128)(2,1)}, u32[]{:S(2)}, u32[]{:S(2)}) collective-permute-start(bf16[2,2,768,768]{3,2,1,0:T(8,128)(2,1)} %get-tuple-element.229), channel_id=1, source_target_pairs={{0,1},{1,0},{2,3},{3,2},{4,5},{5,4},{6,7},{7,6},{8,9},{9,8},{10,11... | collective-permute-start | bytes 14155784 | tf_op jit(solution)/shard_map/ppermute | solution.py:633
  441.0 65.6 %collective-permute-start.24 = (bf16[2,2,4,96,768]{4,3,2,1,0:T(8,128)(2,1)}, bf16[2,2,4,96,768]{4,3,2,1,0:T(8,128)(2,1)}, u32[]{:S(2)}, u32[]{:S(2)}) collective-permute-start(bf16[2,2,4,96,768]{4,3,2,1,0:T(8,128)(2,1)} %get-tuple-element.249), channel_id=1, source_target_pairs={{0,2},{1,5},{2,0},{3,7},{4,6},{5,1},{6,4},{7,3},{8,10},{9,13},{10,... | collective-permute-start | bytes 7077896 | tf_op jit(solution)/shard_map/ppermute | solution.py:671
  441.9 32.2 %collective-permute-start.20 = (bf16[192,1536]{1,0:T(8,128)(2,1)}, bf16[192,1536]{1,0:T(8,128)(2,1)S(1)}, u32[]{:S(2)}, u32[]{:S(2)}) collective-permute-start(bf16[192,1536]{1,0:T(8,128)(2,1)} %get-tuple-element.244), channel_id=1, source_target_pairs={{16,0},{0,1},{24,2},{8,3},{20,4},{4,5},{28,6},{12,7},{18,8},{2,9},... | collective-permute-start | bytes 1769480 | tf_op jit(solution)/shard_map/ppermute | solution.py:613
  444.5 49.4 %collective-permute-start.21 = (bf16[192,1536]{1,0:T(8,128)(2,1)}, bf16[192,1536]{1,0:T(8,128)(2,1)S(1)}, u32[]{:S(2)}, u32[]{:S(2)}) collective-permute-start(bf16[192,1536]{1,0:T(8,128)(2,1)} %get-tuple-element.245), channel_id=1, source_target_pairs={{18,0},{2,1},{26,2},{10,3},{22,4},{6,5},{30,6},{14,7},{16,8},{0,9}... | collective-permute-start | bytes 1769480 | tf_op jit(solution)/shard_map/ppermute | solution.py:613
  448.7 46.7 %collective-permute-start.22 = (bf16[192,1536]{1,0:T(8,128)(2,1)}, bf16[192,1536]{1,0:T(8,128)(2,1)S(1)}, u32[]{:S(2)}, u32[]{:S(2)}) collective-permute-start(bf16[192,1536]{1,0:T(8,128)(2,1)} %get-tuple-element.246), channel_id=1, source_target_pairs={{24,0},{8,1},{0,2},{16,3},{28,4},{12,5},{4,6},{20,7},{26,8},{10,9}... | collective-permute-start | bytes 1769480 | tf_op jit(solution)/shard_map/ppermute | solution.py:613
  448.7 46.7 %collective-permute-start.23 = (bf16[192,1536]{1,0:T(8,128)(2,1)}, bf16[192,1536]{1,0:T(8,128)(2,1)}, u32[]{:S(2)}, u32[]{:S(2)}) collective-permute-start(bf16[192,1536]{1,0:T(8,128)(2,1)} %get-tuple-element.247), channel_id=1, source_target_pairs={{26,0},{10,1},{2,2},{18,3},{30,4},{14,5},{6,6},{22,7},{24,8},{8,9}... | collective-permute-start | bytes 1769480 | tf_op jit(solution)/shard_map/ppermute | solution.py:613
  474.1 21.3 %copy-start.34 = (bf16[192,1536]{1,0:T(8,128)(2,1)}, bf16[192,1536]{1,0:T(8,128)(2,1)S(1)}, u32[]{:S(2)}) copy-start(bf16[192,1536]{1,0:T(8,128)(2,1)S(1)} %collective-permute-done.20.refs_4_) | copy-start | bytes 1769476
  506.6 7.4 %copy-start.2 = (f32[3072,128]{1,0:T(8,128)S(1)}, f32[3072,128]{1,0:T(8,128)}, u32[]{:S(2)}) copy-start(f32[3072,128]{1,0:T(8,128)} %get-tuple-element.288) | copy-start | bytes 4718596
  506.6 60.8 %all-to-all-start.5 = ((bf16[8,12,48,256]{3,2,1,0:T(8,128)(2,1)}), bf16[8,12,48,256]{3,2,1,0:T(8,128)(2,1)}, u32[]{:S(2)}, u32[]{:S(2)}) async-start(bf16[8,12,48,256]{3,2,1,0:T(8,128)(2,1)} %bitcast.199), calls=%async_computation.5 | async-start | bytes 4718592 | tf_op jit(solution)/shard_map/all_to_all | solution.py:702
  517.0 8.1 %copy-start.14 = (f32[192,128]{1,0:T(8,128)S(1)}, f32[192,128]{1,0:T(8,128)}, u32[]{:S(2)}) copy-start(f32[192,128]{1,0:T(8,128)} %get-tuple-element.278) | copy-start | bytes 294916
  517.0 8.4 %copy-start.13 = (f32[192,128]{1,0:T(8,128)S(1)}, f32[192,128]{1,0:T(8,128)}, u32[]{:S(2)}) copy-start(f32[192,128]{1,0:T(8,128)} %get-tuple-element.276) | copy-start | bytes 294916
  523.0 32.4 %collective-permute-start.25 = (bf16[2,4,96,768]{3,2,1,0:T(8,128)(2,1)S(1)}, bf16[2,4,96,768]{3,2,1,0:T(8,128)(2,1)}, u32[]{:S(2)}, u32[]{:S(2)}) collective-permute-start(bf16[2,4,96,768]{3,2,1,0:T(8,128)(2,1)S(1)} %fusion.3), channel_id=1, source_target_pairs={{0,4},{1,3},{2,6},{3,1},{4,0},{5,7},{6,2},{7,5},{8,12},{9,11},{10,... | collective-permute-start | bytes 3538952 | tf_op jit(solution)/shard_map/ppermute | solution.py:704
  526.4 10.6 %copy-start.16 = (f32[48,128]{1,0:T(8,128)S(1)}, f32[48,128]{1,0:T(8,128)}, u32[]{:S(2)}) copy-start(f32[48,128]{1,0:T(8,128)} %get-tuple-element.279) | copy-start | bytes 73732
  526.4 11.4 %copy-start.15 = (f32[48,128]{1,0:T(8,128)S(1)}, f32[48,128]{1,0:T(8,128)}, u32[]{:S(2)}) copy-start(f32[48,128]{1,0:T(8,128)} %get-tuple-element.281) | copy-start | bytes 73732
  526.4 12.2 %copy-start.22 = (f32[96]{0:T(128)S(1)}, f32[96]{0:T(128)}, u32[]{:S(2)}) copy-start(f32[96]{0:T(128)} %copy-done.21) | copy-start | bytes 1156
  526.4 12.4 %copy-start.12 = (f32[96,2,256]{2,1,0:T(2,128)S(1)}, f32[96,2,256]{2,1,0:T(2,128)}, u32[]{:S(2)}) copy-start(f32[96,2,256]{2,1,0:T(2,128)} %get-tuple-element.254) | copy-start | bytes 589828
  568.9 19.4 %all-to-all-start.6 = ((f32[8,1,16369]{2,1,0:T(1,128)}), f32[8,1,16369]{2,1,0:T(1,128)S(1)}, u32[]{:S(2)}, u32[]{:S(2)}) async-start(f32[8,1,16369]{2,1,0:T(1,128)} %all_to_all.35), calls=%async_computation.6 | async-start | bytes 1048576 | tf_op jit(solution)/shard_map/all_to_all | solution.py:730
  573.3 20.0 %copy-start.6 = (f32[4,12,1,256]{3,0,1,2:T(4,128)S(1)}, f32[4,12,1,256]{3,0,1,2:T(4,128)}, u32[]{:S(2)}) copy-start(f32[4,12,1,256]{3,0,1,2:T(4,128)} %copy-done.5) | copy-start | bytes 147460
  573.3 20.6 %copy-start.4 = (f32[4,12,1,256]{3,0,1,2:T(4,128)S(1)}, f32[4,12,1,256]{3,0,1,2:T(4,128)}, u32[]{:S(2)}) copy-start(f32[4,12,1,256]{3,0,1,2:T(4,128)} %copy-done.3) | copy-start | bytes 147460
  588.6 58.0 %all-to-all-start.7 = ((bf16[8,12,48,256]{3,2,1,0:T(8,128)(2,1)}), bf16[8,12,48,256]{3,2,1,0:T(8,128)(2,1)}, u32[]{:S(2)}, u32[]{:S(2)}) async-start(bf16[8,12,48,256]{3,2,1,0:T(8,128)(2,1)} %bitcast.70), calls=%async_computation.7 | async-start | bytes 4718592 | tf_op jit(solution)/shard_map/all_to_all | solution.py:739
  602.7 41.6 %copy-start.1 = (f32[4,2,96,768]{3,2,0,1:T(8,128)S(1)}, f32[4,2,96,768]{3,2,0,1:T(8,128)}, u32[]{:S(2)}) copy-start(f32[4,2,96,768]{3,2,0,1:T(8,128)} %fusion.2) | copy-start | bytes 7077892
  603.7 5.4 collective-permute-start.26
  605.9 38.4 %collective-permute-start.28 = (bf16[2,2,96,768]{3,2,1,0:T(8,128)(2,1)}, bf16[2,2,96,768]{3,2,1,0:T(8,128)(2,1)}, u32[]{:S(2)}, u32[]{:S(2)}) collective-permute-start(bf16[2,2,96,768]{3,2,1,0:T(8,128)(2,1)} %fusion.4), channel_id=1, source_target_pairs={{0,8},{8,0},{16,24},{24,16},{1,9},{9,1},{17,25},{25,17},{2,10},{10... | collective-permute-start | bytes 1769480 | tf_op jit(solution)/shard_map/ppermute | solution.py:642
  609.1 5.6 collective-permute-start.27
  646.7 14.5 %collective-permute-start.29 = (bf16[1,2,96,768]{3,2,1,0:T(8,128)(2,1)S(1)}, bf16[1,2,96,768]{3,2,1,0:T(8,128)(2,1)S(1)}, u32[]{:S(2)}, u32[]{:S(2)}) collective-permute-start(bf16[1,2,96,768]{3,2,1,0:T(8,128)(2,1)S(1)} %dynamic-slice_convert_fusion.1), channel_id=1, source_target_pairs={{0,16},{8,24},{16,0},{24,8},{1,17},{9,25},{17,1},{25,9},{2,18},{10... | collective-permute-start | bytes 884744 | tf_op jit(solution)/shard_map/ppermute | solution.py:642
  (14 other events, 65.0 us)
Sparse Core Ops, SparseCore 0:
  9.6 38.0 all-gather.7
  49.8 37.5 all-gather.5

commit v6 on v5

--- a/solution.py
+++ b/solution.py
@@ -351,15 +351,11 @@
 
 
 def add_kernel(side, kept, came, mine, theirs):
-    blocks = mine.shape[2]
-    value = [
-        (kept[i, 0] + came[i, 0].astype(F32)).reshape(blocks, 2, -1, mine.shape[4]) for i in range(2)
-    ]
-    own, other = [[jnp.where(side[0] == bit, v[:, 1], v[:, 0]) for v in value] for bit in (1, 0)]
-    even = side[1] == 0
     for i in range(2):
-        mine[i, 0] = jnp.where(even, value[0][:, i], own[i])
-        theirs[i, 0] = jnp.where(even, value[1][:, i], other[i]).astype(BF)
+        value = (kept[i, 0] + came[i, 0].astype(F32)).reshape(mine.shape[2], 2, -1, mine.shape[4])
+        odd = side[0] == 1
+        mine[i, 0] = jnp.where(odd, value[:, 1], value[:, 0])
+        theirs[i, 0] = jnp.where(odd, value[:, 0], value[:, 1]).astype(BF)
 
 
 def widen_kernel(parts, slot, starts, *refs):
@@ -631,7 +627,7 @@
             )
             sgrad, sent, results, rows_out = lax.optimization_barrier((sgrad, sent, results, rows_out))
             came = lax.ppermute(sent, "t", [(a, a ^ 1) for a in range(tp)])
-            send_results((2, 3))
+            send_results((2,))
         sgrads.append(sgrad)
         sums.append((s0, s1))
         received.append(section)
@@ -651,7 +647,7 @@
         [*part_specs, *lon_f, *lat_specs], shape(mine_modes, BF), modes_spec, scratch, 48, 0.01,
     )
     freq, came = lax.optimization_barrier((freq, came))
-    side = jnp.stack([me % 2, t % 2]).astype(jnp.int32)
+    side = (me % 2).astype(jnp.int32).reshape(1)
     strip = feats // owners
     third = hidden_local // 3
     halves_shape = (2, 2, owners // 2, strip, hidden_local)
@@ -661,14 +657,9 @@
         [pl.BlockSpec((half, 1, feats, third), lambda kind, i, _: (0, kind, 0, i))] * 2,
         (shape(halves_shape, F32), shape(halves_shape, BF)), (halves_block, halves_block), [], 48, 0.01, (side,),
     )
-    steps_first = [
-        (rank, rank ^ 2 if rank % 2 == 0 else rank ^ tp) for rank in range(planes * inner * tp)
-    ]
-    steps_second = [(rank, rank ^ tp if rank % 2 == 0 else rank ^ 2) for rank in range(planes * inner * tp)]
-    own_half = jnp.where(t % 2 == 0, me % 2, 0)
-    sent_half = jnp.where(t % 2 == 0, 1 - me % 2, 1)
-    freq, theirs, weights = lax.optimization_barrier((freq, theirs, weights))
-    came = lax.ppermute(theirs, every, steps_first)
+    freq, theirs, weights, results, rows_out = lax.optimization_barrier((freq, theirs, weights, results, rows_out))
+    send_results((3,))
+    came = trade(theirs, sp, 1, owners)
     freq, inner_grad, outer_grad, inner_bias_grad, outer_bias_grad = run(
         "filter_back", filter_back_kernel, (lats // step,), (to_blocks(freq), spec, mid, slope, bend, w1, w2),
         [*[block_spec] * 5, square_spec, square_spec],
@@ -698,10 +689,10 @@
         first_sums.append(sums_here)
         at += n
         if i < len(cuts) - 1:
-            freq, came, grads[i] = lax.optimization_barrier((freq, came, grads[i]))
+            freq, came = lax.optimization_barrier((freq, came))
             grads[i] = lax.all_to_all(grads[i], sp, 0, 0, tiled=True)
     weights = weights + came.astype(F32)
-    came = lax.ppermute(lax.dynamic_index_in_dim(weights, sent_half, 0, False).astype(BF), every, steps_second)
+    came = trade(weights[1].astype(BF), "t", 2, tp)
     first_gain_sum, first_shift_sum = (jnp.concatenate(sums_here, 0) for sums_here in zip(*first_sums))
     lines = sum(lines)
     def with_bias(full, bias):
@@ -714,7 +705,7 @@
         [jnp.sum(gain_sum, 1), jnp.sum(shift_sum, 1), jnp.sum(cot_sum, 1), jnp.sum(bias_sum, 1), jnp.sum(share)[None]]
     )
     grads, lines, results, came = lax.optimization_barrier((grads, lines, results, came))
-    weights = jnp.moveaxis(lax.dynamic_index_in_dim(weights, own_half, 0, False) + came.astype(F32), 1, 0)
+    weights = jnp.moveaxis(weights[0] + came.astype(F32), 1, 0)
     bit = 2
     while bit < inner:
         weights = weights.reshape(-1, 2, *weights.shape[1:])

time: 681 us -> 662 us (0.972)
  waiting for transfers between devices: 175 us -> 152 us
    ppermute x4 -> x6, waiting for transfers between devices: 31 us -> 57.6 us  [trade(): return lax.ppermute(theirs, axes, [(a, a ^ bit) for a in range(size)])]
    ppermute x8, waiting for transfers between devices: 24.9 us -> 3.89 us  [send_results(): lax.ppermute(rows_out[2 * k + part], every, route(k, part, True))]
    ppermute x2 -> x0, waiting for transfers between devices: 14.8 us -> none  [the longest x1 14.8 us: per_device(): lax.ppermute(lax.dynamic_index_in_dim(weights, sent_half, 0, False).astyp...]
    all_to_all x1, waiting for transfers between devices: 12 us -> 0.01 us  [per_device(): grads[i] = lax.all_to_all(grads[i], sp, 0, 0, tiled=True)]
  transfers between devices with their start and end apart: 40 -> 40, of which waited for: 15 -> 12; matrix products, arithmetic and copies ran while one was open for 12% -> 12% of each run, Pallas kernels for 37% -> 39%
where the time goes in v6:
time: 662 us; the launch traced here: 649 us
  Pallas kernels  269 us (41%)
  waiting for transfers between devices  152 us (23%)
  starting transfers between devices  107 us (16%)
  local copies, waits for them, and re-layouts  54.7 us (8%)
  other arithmetic  29.3 us (4%)
  between operations  18.5 us (3%)
  blocking collectives  17.7 us (3%)
    pallas_call x14, Pallas kernels, run(): return call(*scalars, *ins)  269 us
    ppermute x6, waiting for transfers between devices, trade(): return lax.ppermute(theirs, axes, [(a, a ^ bit) for a in range(size)])  57.6 us
    all_to_all x4, starting transfers between devices, exchange(): return lax.all_to_all(array, ('t', 'y', 'j'), 0, 0, tiled=True)  30.3 us
    all_to_all x4, waiting for transfers between devices, exchange(): return lax.all_to_all(array, ('t', 'y', 'j'), 0, 0, tiled=True)  28.8 us
    ppermute x7, waiting for transfers between devices, per_device(): lax.ppermute(piece, sp, [(a, a ^ k) for a in range(owners)])  25.6 us
    all_gather x1, waiting for transfers between devices, per_device(): wp = lax.all_gather(project_weight, 't', tiled=True)  24.4 us
    ppermute x8, starting transfers between devices, send_results(): lax.ppermute(rows_out[2 * k + part], every, route(k, part, True))  14.4 us
  transfers between devices with their start and end apart: 40, of which 12 were waited for; matrix products, arithmetic and copies ran while one was open for 12% of the time, Pallas kernels for 39%

profile of v6, /device:TPU:2, one launch (start us, length us, event | category | flops | bytes accessed | tf_op | source)
XLA Modules:
  0.0 648.5 jit_solution(8794821651323145550)
XLA Ops:
  8.0 2.4 copy.233
  10.4 2.8 fusion.16
  13.1 2.6 pad_maximum_fusion
  15.8 6.0 all-to-all-start
  23.4 11.6 %all-reduce = f32[5376]{0:T(1024)S(1)} all-reduce(f32[5376]{0:T(1024)S(1)} %dynamic-update-slice), channel_id=4, replica_groups=mesh['z'=4,'y'=2,'j'=1,'t'=4] {'t'}, use_global_device_ids=true, to_apply=%add | all-reduce | flops 5376 | bytes 43008
  35.1 3.3 convert_reduce_fusion
  38.4 4.2 fusion.1
  44.9 6.1 all-gather
  52.0 4.0 dynamic-slice_bitcast_fusion
  56.0 7.0 %copy.234 = bf16[4,768,768]{2,1,0:T(8,128)(2,1)} copy(bf16[4,768,768]{1,2,0:T(8,128)(2,1)} %bitcast.195) | data formatting | bytes 9437184 | tf_op jit(solution)/shard_map/transpose | solution.py:472
  63.0 24.4 %all-gather.6.cloned.1.call-done = bf16[3072,768]{0,1:T(8,128)(2,1)} async-done(((bf16[768,768]{0,1:T(8,128)(2,1)}), bf16[3072,768]{0,1:T(8,128)(2,1)}) %all-gather.6.cloned.1.call-update) | async-done | bytes 4718608 | tf_op jit(solution)/shard_map/all_gather | solution.py:471
  89.5 1.7 broadcast_in_dim.70.refs_8_
  91.4 1.8 collective-permute-start.6
  96.0 3.6 collective-permute-start.2
  100.3 3.4 collective-permute-start
  104.9 25.6 %collective-permute-done.2 = f32[12,2,256]{2,1,0:T(2,128)S(1)} collective-permute-done((f32[12,2,256]{2,1,0:T(2,128)S(1)}, f32[12,2,256]{2,1,0:T(2,128)S(1)}, u32[]{:S(2)}, u32[]{:S(2)}) %collective-permute-start.2) | collective-permute-done | bytes 24608 | tf_op jit(solution)/shard_map/ppermute | solution.py:480
  131.9 2.9 collective-permute-start.7
  135.1 3.5 collective-permute-start.9
  140.6 20.2 %spectrum.1.spec = bf16[2,96,96,128]{3,2,1,0:T(8,128)(2,1)} custom-call(bf16[8,12,96,256]{3,2,1,0:T(8,128)(2,1)} %all-to-all-done.pieces, f32[96,1,256]{2,1,0:T(1,128)} %get-tuple-element.408.mean.refs_2_, f32[96,1,256]{2,1,0:T(1,128)} %get-tuple-element.407.rstd.refs_3_, f32[96,256]{1,0:T(8,128)} %broadcast_in_dim.71.scale.refs_4_, ...), custom_call_target="tpu_custom_call" | custom-call | flops 22000001024 | bytes 74800000 | tf_op jit(solution)/shard_map/spectrum/pallas_call | solution.py:405
  162.3 14.6 %filter.1 = (bf16[2,96,96,128]{3,2,1,0:T(8,128)(2,1)}, bf16[2,96,96,128]{3,2,1,0:T(8,128)(2,1)}, bf16[2,96,96,128]{3,2,1,0:T(8,128)(2,1)}, bf16[2,96,96,128]{3,2,1,0:T(8,128)(2,1)}, f32[8,256]{1,0:T(8,128)}) custom-call(bf16[2,96,96,128]{3,2,1,0:T(8,128)(2,1)} %spectrum.1.spec, bf16[192,192]{1,0:T(8,128)(2,1)} %maximum_maximum_fusion.w1, ...), custom_call_target="tpu_custom_call" | custom-call | flops 16999999488 | bytes 57800000 | tf_op jit(solution)/shard_map/filter/pallas_call | solution.py:405
  176.9 13.4 %section.1 = (bf16[8,6,96,256]{3,2,1,0:T(8,128)(2,1)}, bf16[8,6,96,256]{3,2,1,0:T(8,128)(2,1)}) custom-call(bf16[8,12,96,256]{3,2,1,0:T(8,128)(2,1)} %all-to-all-done.pieces, f32[96,1,256]{2,1,0:T(1,128)} %get-tuple-element.408.mean.refs_2_, f32[96,1,256]{2,1,0:T(1,128)} %get-tuple-element.407.rstd.refs_3_, f32[96,256]{1,0:T(8,128)} %broadcast_in_dim.71.scale.refs_4_, ...), custom_call_target="tpu_custom_call" | custom-call | flops 16999999488 | bytes 57800000 | tf_op jit(solution)/shard_map/section/pallas_call | solution.py:405
  190.4 13.2 %all-to-all-start.1 = ((bf16[8,6,96,256]{3,2,1,0:T(8,128)(2,1)}), bf16[8,6,96,256]{3,2,1,0:T(8,128)(2,1)}, u32[]{:S(2)}, u32[]{:S(2)}) async-start(bf16[8,6,96,256]{3,2,1,0:T(8,128)(2,1)} %get-tuple-element.176), calls=%async_computation.1 | async-start | bytes 4718592 | tf_op jit(solution)/shard_map/all_to_all | solution.py:562
  204.1 6.6 %copy.246.refs_6_ = bf16[3072,768]{1,0:T(8,128)(2,1)} copy(bf16[3072,768]{0,1:T(8,128)(2,1)} %all-gather.6.cloned.1.call-done) | data formatting | bytes 9437184 | tf_op jit(solution)/shard_map/optimization_barrier | solution.py:474
  210.7 20.4 %all-to-all-done.1.refs_4_.refs_0_ = bf16[8,6,96,256]{3,2,1,0:T(8,128)(2,1)} async-done(((bf16[8,6,96,256]{3,2,1,0:T(8,128)(2,1)}), bf16[8,6,96,256]{3,2,1,0:T(8,128)(2,1)}, u32[]{:S(2)}, u32[]{:S(2)}) %all-to-all-start.1) | async-done | bytes 2359328 | tf_op jit(solution)/shard_map/all_to_all | solution.py:562
  231.1 5.8 all-to-all-start.2
  236.9 2.1 collective-permute-start.11
  239.1 3.1 collective-permute-start.12
  244.5 35.5 %feed.2 = (bf16[768,3072]{1,0:T(8,128)(2,1)}, bf16[3072,3072]{1,0:T(8,128)(2,1)}, bf16[3072,3072]{1,0:T(8,128)(2,1)}, bf16[768,3072]{1,0:T(8,128)(2,1)}, bf16[8,...) custom-call(s32[4]{0:T(128)} %pad_add_fusion.2.place, ...), custom_call_target="tpu_custom_call" | custom-call | flops 43000000512 | bytes 146200000 | tf_op jit(solution)/shard_map/feed/pallas_call | solution.py:405
  280.0 8.4 %all-to-all-done.2.refs_4_.refs_1_ = bf16[8,6,96,256]{3,2,1,0:T(8,128)(2,1)} async-done(((bf16[8,6,96,256]{3,2,1,0:T(8,128)(2,1)}), bf16[8,6,96,256]{3,2,1,0:T(8,128)(2,1)}, u32[]{:S(2)}, u32[]{:S(2)}) %all-to-all-start.2) | async-done | bytes 2359328 | tf_op jit(solution)/shard_map/all_to_all | solution.py:562
  288.4 7.0 %all-to-all-start.3 = ((bf16[8,6,96,256]{3,2,1,0:T(8,128)(2,1)}), bf16[8,6,96,256]{3,2,1,0:T(8,128)(2,1)}, u32[]{:S(2)}, u32[]{:S(2)}) async-start(bf16[8,6,96,256]{3,2,1,0:T(8,128)(2,1)} %get-tuple-element.206), calls=%async_computation.3 | async-start | bytes 4718592 | tf_op jit(solution)/shard_map/all_to_all | solution.py:562
  295.4 35.7 %feed.3 = (bf16[768,3072]{1,0:T(8,128)(2,1)}, bf16[3072,3072]{1,0:T(8,128)(2,1)}, bf16[3072,3072]{1,0:T(8,128)(2,1)}, bf16[768,3072]{1,0:T(8,128)(2,1)}, bf16[8,...) custom-call(s32[4]{0:T(128)} %pad_add_fusion.2.place, ...), custom_call_target="tpu_custom_call", output_to_operand_aliasing={{0}: (12, {}), {1}: (13, {}), {2}: (14, {}), {3}: (15, {})} | custom-call | flops 43000000512 | bytes 146200000 | tf_op jit(solution)/shard_map/feed/pallas_call | solution.py:405
  331.2 4.3 all-to-all-start.4
  336.5 24.1 %result.1 = (bf16[192,1536]{1,0:T(8,128)(2,1)}, bf16[192,1536]{1,0:T(8,128)(2,1)}, bf16[192,1536]{1,0:T(8,128)(2,1)}, bf16[192,1536]{1,0:T(8,128)(2,1)}, bf16[19...) custom-call(s32[4]{0:T(128)} %pad_add_fusion.2.place, ...), custom_call_target="tpu_custom_call" | custom-call | flops 10000000 | bytes 34000 | tf_op jit(solution)/shard_map/result/pallas_call | solution.py:405
  360.6 1.9 collective-permute-start.15
  362.6 2.7 collective-permute-start.17
  365.3 2.7 collective-permute-start.18
  368.6 41.5 %weights.1 = (bf16[2,2,768,768]{3,2,1,0:T(8,128)(2,1)}, f32[2,2,768,768]{3,2,1,0:T(8,128)}, f32[3072,128]{1,0:T(8,128)}, f32[768,128]{1,0:T(8,128)}) custom-call(s32[4]{0:T(128)} %pad_add_fusion.3.order, bf16[768,3072]{1,0:T(8,128)(2,1)} %get-tuple-element.222.normal, bf16[3072,3072]{1,0:T(8,128)(2,1)} %get-tuple-element.223.pre, ...), custom_call_target="tpu_custom_call" | custom-call | flops 10000000 | bytes 34000 | tf_op jit(solution)/shard_map/weights/pallas_call | solution.py:405
  411.0 3.0 collective-permute-done.18.refs_3_
  414.0 1.9 collective-permute-start.20
  415.9 4.2 collective-permute-start.21
  420.1 16.5 %spectrum_back.1.freq = bf16[2,96,96,128]{3,2,1,0:T(8,128)(2,1)} custom-call(bf16[8,6,96,256]{3,2,1,0:T(8,128)(2,1)} %all-to-all-done.3.refs_0_, bf16[8,6,96,256]{3,2,1,0:T(8,128)(2,1)} %all-to-all-done.4.refs_1_, bf16[256,256]{1,0:T(8,128)(2,1)} %constant.383.clone.refs_2_, bf16[256,256]{1,0:T(8,128)(2,1)} %constant.384.clone.refs_3_, ...), custom_call_target="tpu_custom_call" | custom-call | flops 10000000 | bytes 34000 | tf_op jit(solution)/shard_map/spectrum_back/pallas_call | solution.py:405
  436.7 9.3 %add.403 = (f32[2,2,4,96,768]{4,3,2,1,0:T(8,128)}, bf16[2,2,4,96,768]{4,3,2,1,0:T(8,128)(2,1)}) custom-call(s32[1]{0:T(128)} %bitcast.67.side, f32[2,2,768,768]{3,2,1,0:T(8,128)} %get-tuple-element.238.kept, bf16[2,2,768,768]{3,2,1,0:T(8,128)(2,1)} %collective-permute-done.19.came), custom_call_target="tpu_custom_call" | custom-call | flops 10000000 | bytes 34000 | tf_op jit(solution)/shard_map/add/pallas_call | solution.py:405
  447.0 1.6 collective-permute-start.24
  448.6 19.2 %filter_back.1 = (bf16[2,96,96,128]{3,2,1,0:T(8,128)(2,1)}, f32[192,192]{1,0:T(8,128)}, f32[192,192]{1,0:T(8,128)}, f32[192,128]{1,0:T(8,128)}, f32[192,128]{1,0:T(8,128)}) custom-call(bf16[2,96,96,128]{3,2,1,0:T(8,128)(2,1)} %spectrum_back.1.freq, bf16[2,96,96,128]{3,2,1,0:T(8,128)(2,1)} %spectrum.1.spec, bf16[2,96,96,128]{3,2,1,0:T(8,128)(2,1)} %get-tuple-element.251.mid, ...), custom_call_target="tpu_custom_call" | custom-call | flops 10000000 | bytes 34000 | tf_op jit(solution)/shard_map/filter_back/pallas_call | solution.py:405
  468.9 10.4 %last.2 = (bf16[96,48,256]{2,1,0:T(8,128)(2,1)}, f32[96,2,256]{2,1,0:T(2,128)}, f32[48,128]{1,0:T(8,128)}, f32[48,128]{1,0:T(8,128)}) custom-call(bf16[8,12,96,256]{3,2,1,0:T(8,128)(2,1)} %all-to-all-done.pieces, bf16[8,6,96,256]{3,2,1,0:T(8,128)(2,1)} %all-to-all-done.3.refs_0_, bf16[8,6,96,256]{3,2,1,0:T(8,128)(2,1)} %all-to-all-done.4.refs_1_, ...), custom_call_target="tpu_custom_call" | custom-call | flops 10000000 | bytes 34000 | tf_op jit(solution)/shard_map/last/pallas_call | solution.py:405
  479.3 8.0 %all-to-all-start.5 = ((bf16[8,12,48,256]{3,2,1,0:T(8,128)(2,1)}), bf16[8,12,48,256]{3,2,1,0:T(8,128)(2,1)}, u32[]{:S(2)}, u32[]{:S(2)}) async-start(bf16[8,12,48,256]{3,2,1,0:T(8,128)(2,1)} %bitcast.200), calls=%async_computation.5 | async-start | bytes 4718592 | tf_op jit(solution)/shard_map/all_to_all | solution.py:693
  491.6 22.4 %collective-permute-done.24 = bf16[2,2,4,96,768]{4,3,2,1,0:T(8,128)(2,1)} collective-permute-done((bf16[2,2,4,96,768]{4,3,2,1,0:T(8,128)(2,1)}, bf16[2,2,4,96,768]{4,3,2,1,0:T(8,128)(2,1)}, u32[]{:S(2)}, u32[]{:S(2)}) %collective-permute-start.24) | collective-permute-done | bytes 2359328 | tf_op jit(solution)/shard_map/ppermute | solution.py:638
  513.9 3.6 convert_add_fusion
  517.6 2.2 copy-done
  519.9 1.6 collective-permute-start.25
  522.9 10.5 %last.3 = (bf16[96,48,256]{2,1,0:T(8,128)(2,1)}, f32[96,2,256]{2,1,0:T(2,128)}, f32[48,128]{1,0:T(8,128)}, f32[48,128]{1,0:T(8,128)}) custom-call(bf16[8,12,96,256]{3,2,1,0:T(8,128)(2,1)} %all-to-all-done.pieces, bf16[8,6,96,256]{3,2,1,0:T(8,128)(2,1)} %all-to-all-done.3.refs_0_, bf16[8,6,96,256]{3,2,1,0:T(8,128)(2,1)} %all-to-all-done.4.refs_1_, ...), custom_call_target="tpu_custom_call" | custom-call | flops 10000000 | bytes 34000 | tf_op jit(solution)/shard_map/last/pallas_call | solution.py:405
  537.0 8.8 %collective-permute-done.25 = bf16[2,4,96,768]{3,2,1,0:T(8,128)(2,1)} collective-permute-done((bf16[2,4,96,768]{3,2,1,0:T(8,128)(2,1)S(1)}, bf16[2,4,96,768]{3,2,1,0:T(8,128)(2,1)}, u32[]{:S(2)}, u32[]{:S(2)}) %collective-permute-start.25) | collective-permute-done | bytes 1179680 | tf_op jit(solution)/shard_map/ppermute | solution.py:638
  547.4 8.3 %all-to-all-start.6 = ((f32[8,1,16369]{2,1,0:T(1,128)}), f32[8,1,16369]{2,1,0:T(1,128)S(1)}, u32[]{:S(2)}, u32[]{:S(2)}) async-start(f32[8,1,16369]{2,1,0:T(1,128)} %all_to_all.35), calls=%async_computation.6 | async-start | bytes 1048576 | tf_op jit(solution)/shard_map/all_to_all | solution.py:721
  555.6 3.7 fusion.3
  559.3 9.5 %all-to-all-done.6 = f32[8,1,16369]{2,1,0:T(1,128)S(1)} async-done(((f32[8,1,16369]{2,1,0:T(1,128)}), f32[8,1,16369]{2,1,0:T(1,128)S(1)}, u32[]{:S(2)}, u32[]{:S(2)}) %all-to-all-start.6) | async-done | bytes 523840 | tf_op jit(solution)/shard_map/all_to_all | solution.py:721
  569.1 4.6 all-to-all-start.7
  576.2 6.9 %widen.1 = f32[4,12,192,256]{3,2,1,0:T(8,128)} custom-call(s32[4]{0:T(128)} %pad_add_fusion.slot, s32[2]{0:T(128)} %pad_add_fusion.1.starts, bf16[192,1536]{1,0:T(8,128)(2,1)} %copy-done.31, bf16[192,1536]{1,0:T(8,128)(2,1)} %copy-done.32, bf16[192,1536]{1,0:T(8,128)(2,1)} %copy-done.33, bf16[192,1536]{1,0:T(8,128)(2,1)} %collective-permute-done.18.refs_3_, ...), custom_call_target="tpu_custom_call" | custom-call | flops 8000000000 | bytes 27200000 | tf_op jit(solution)/shard_map/widen/pallas_call | solution.py:405
  584.2 2.2 fusion.5
  586.4 2.0 collective-permute-start.28
  593.1 2.0 collective-permute-done.27
  598.3 24.4 %collective-permute-done.28 = bf16[2,2,96,768]{3,2,1,0:T(8,128)(2,1)} collective-permute-done((bf16[2,2,96,768]{3,2,1,0:T(8,128)(2,1)}, bf16[2,2,96,768]{3,2,1,0:T(8,128)(2,1)}, u32[]{:S(2)}, u32[]{:S(2)}) %collective-permute-start.28) | collective-permute-done | bytes 589856 | tf_op jit(solution)/shard_map/ppermute | solution.py:638
  623.9 1.9 all-to-all-done.7.refs_1_
  625.8 2.7 collective-permute-start.29
  628.6 10.6 %finish.1 = f32[4,12,192,256]{3,2,1,0:T(8,128)} custom-call(bf16[4,12,192,256]{3,2,1,0:T(8,128)(2,1)} %patches.1, f32[4,12,1,256]{3,2,1,0:T(1,128)} %copy.260.mean, f32[4,12,1,256]{3,2,1,0:T(1,128)} %copy.261.rstd, f32[4,12,1,256]{3,2,1,0:T(1,128)} %get-tuple-element.415.one, f32[4,12,1,256]{3,2,1,0:T(1,128)} %get-tuple-element.414.two, ...), custom_call_target="tpu_custom_call" | custom-call | flops 99999997952 | bytes 340000000 | tf_op jit(solution)/shard_map/finish/pallas_call | solution.py:405
  (271 shorter events, 48.0 us)
Async XLA Ops:
  7.2 48.8 %all-gather.8.cloned.1.call-start = ((), (), s32[]{:S(2)}) async-start(), calls=%async_computation.9 | async-start | bytes 5898240 | tf_op jit(solution)/shard_map/all_gather | solution.py:470
  7.9 79.5 %all-gather.6.cloned.1.call-start = ((), (), s32[]{:S(2)}) async-start(), calls=%async_computation.8 | async-start | bytes 5898240 | tf_op jit(solution)/shard_map/all_gather | solution.py:471
  15.8 19.3 %copy-start.17 = (bf16[2,2,96,96]{3,2,1,0:T(8,128)(2,1)S(1)}, bf16[2,2,96,96]{3,2,1,0:T(8,128)(2,1)}, u32[]{:S(2)}) copy-start(bf16[2,2,96,96]{3,2,1,0:T(8,128)(2,1)} %param.33) | copy-start | bytes 221188
  15.8 19.3 %copy-start.18 = (bf16[2,2,96,96]{3,2,1,0:T(8,128)(2,1)S(1)}, bf16[2,2,96,96]{3,2,1,0:T(8,128)(2,1)}, u32[]{:S(2)}) copy-start(bf16[2,2,96,96]{3,2,1,0:T(8,128)(2,1)} %param.31) | copy-start | bytes 221188
  15.8 116.2 %all-to-all-start = ((bf16[8,12,96,256]{3,2,1,0:T(8,128)(2,1)}), bf16[8,12,96,256]{3,2,1,0:T(8,128)(2,1)}, u32[]{:S(2)}, u32[]{:S(2)}) async-start(bf16[8,12,96,256]{3,2,1,0:T(8,128)(2,1)} %bitcast.191), calls=%async_computation | async-start | bytes 9437184 | tf_op jit(solution)/shard_map/all_to_all | solution.py:441
  38.4 13.0 %copy-start.30 = (f32[192]{0:T(256)S(1)}, f32[192]{0:T(256)}, u32[]{:S(2)}) copy-start(f32[192]{0:T(256)} %param.29) | copy-start | bytes 2308
  44.0 12.0 %copy-start.21 = (f32[96]{0:T(128)}, f32[96]{0:T(128)S(1)}, u32[]{:S(2)}) copy-start(f32[96]{0:T(128)S(1)} %get-tuple-element.374) | copy-start | bytes 1156
  56.0 48.7 %copy-start.27 = (f32[2,2,96]{2,1,0:T(2,128)S(1)}, f32[2,2,96]{2,1,0:T(2,128)}, u32[]{:S(2)}) copy-start(f32[2,2,96]{2,1,0:T(2,128)} %param.32) | copy-start | bytes 4612
  56.0 48.7 %copy-start.28 = (f32[2,2,96]{2,1,0:T(2,128)S(1)}, f32[2,2,96]{2,1,0:T(2,128)}, u32[]{:S(2)}) copy-start(f32[2,2,96]{2,1,0:T(2,128)} %param.34) | copy-start | bytes 4612
  91.4 8.9 %collective-permute-start.6 = (f32[12,2,256]{2,1,0:T(2,128)S(1)}, f32[12,2,256]{2,1,0:T(2,128)S(1)}, u32[]{:S(2)}, u32[]{:S(2)}) collective-permute-start(f32[12,2,256]{2,1,0:T(2,128)S(1)} %bitcast.245), channel_id=1, source_target_pairs={{0,4},{4,0},{8,12},{12,8},{16,20},{20,16},{24,28},{28,24},{1,5},{5... | collective-permute-start | bytes 73736 | tf_op jit(solution)/shard_map/ppermute | solution.py:480
  93.2 10.5 %collective-permute-start.4 = (f32[12,2,256]{2,1,0:T(2,128)S(1)}, f32[12,2,256]{2,1,0:T(2,128)S(1)}, u32[]{:S(2)}, u32[]{:S(2)}) collective-permute-start(f32[12,2,256]{2,1,0:T(2,128)S(1)} %bitcast.244), channel_id=1, source_target_pairs={{0,12},{4,8},{8,4},{12,0},{16,28},{20,24},{24,20},{28,16},{1,13},{... | collective-permute-start | bytes 73736 | tf_op jit(solution)/shard_map/ppermute | solution.py:480
  95.7 9.3 %collective-permute-start.5 = (f32[12,2,256]{2,1,0:T(2,128)S(1)}, f32[12,2,256]{2,1,0:T(2,128)S(1)}, u32[]{:S(2)}, u32[]{:S(2)}) collective-permute-start(f32[12,2,256]{2,1,0:T(2,128)S(1)} %bitcast.239), channel_id=1, source_target_pairs={{0,8},{4,12},{8,0},{12,4},{16,24},{20,28},{24,16},{28,20},{1,9},{5... | collective-permute-start | bytes 73736 | tf_op jit(solution)/shard_map/ppermute | solution.py:480
  96.0 34.5 %collective-permute-start.2 = (f32[12,2,256]{2,1,0:T(2,128)S(1)}, f32[12,2,256]{2,1,0:T(2,128)S(1)}, u32[]{:S(2)}, u32[]{:S(2)}) collective-permute-start(f32[12,2,256]{2,1,0:T(2,128)S(1)} %bitcast.240), channel_id=1, source_target_pairs={{0,20},{4,16},{8,28},{12,24},{16,4},{20,0},{24,12},{28,8},{1,21},{... | collective-permute-start | bytes 73736 | tf_op jit(solution)/shard_map/ppermute | solution.py:480
  99.7 30.8 %collective-permute-start.3 = (f32[12,2,256]{2,1,0:T(2,128)S(1)}, f32[12,2,256]{2,1,0:T(2,128)S(1)}, u32[]{:S(2)}, u32[]{:S(2)}) collective-permute-start(f32[12,2,256]{2,1,0:T(2,128)S(1)} %bitcast.241), channel_id=1, source_target_pairs={{0,16},{4,20},{8,24},{12,28},{16,0},{20,4},{24,8},{28,12},{1,17},{... | collective-permute-start | bytes 73736 | tf_op jit(solution)/shard_map/ppermute | solution.py:480
  100.3 30.2 %collective-permute-start = (f32[12,2,256]{2,1,0:T(2,128)S(1)}, f32[12,2,256]{2,1,0:T(2,128)S(1)}, u32[]{:S(2)}, u32[]{:S(2)}) collective-permute-start(f32[12,2,256]{2,1,0:T(2,128)S(1)} %bitcast.243), channel_id=1, source_target_pairs={{0,28},{4,24},{8,20},{12,16},{16,12},{20,8},{24,4},{28,0},{1,29},{... | collective-permute-start | bytes 73736 | tf_op jit(solution)/shard_map/ppermute | solution.py:480
  103.7 26.8 %collective-permute-start.1 = (f32[12,2,256]{2,1,0:T(2,128)S(1)}, f32[12,2,256]{2,1,0:T(2,128)S(1)}, u32[]{:S(2)}, u32[]{:S(2)}) collective-permute-start(f32[12,2,256]{2,1,0:T(2,128)S(1)} %bitcast.242), channel_id=1, source_target_pairs={{0,24},{4,28},{8,16},{12,20},{16,8},{20,12},{24,0},{28,4},{1,25},{... | collective-permute-start | bytes 73736 | tf_op jit(solution)/shard_map/ppermute | solution.py:480
  131.9 45.0 %collective-permute-start.7 = (bf16[6,192,256]{2,1,0:T(8,128)(2,1)}, bf16[6,192,256]{2,1,0:T(8,128)(2,1)}, u32[]{:S(2)}, u32[]{:S(2)}) collective-permute-start(bf16[6,192,256]{2,1,0:T(8,128)(2,1)} %get-tuple-element.167), channel_id=1, source_target_pairs={{0,0},{1,16},{2,8},{3,24},{4,4},{5,20},{6,12},{7,28},{8,2},{9,18},... | collective-permute-start | bytes 1769480 | tf_op jit(solution)/shard_map/ppermute | solution.py:512
  134.9 42.0 %collective-permute-start.8 = (bf16[6,192,256]{2,1,0:T(8,128)(2,1)}, bf16[6,192,256]{2,1,0:T(8,128)(2,1)}, u32[]{:S(2)}, u32[]{:S(2)}) collective-permute-start(bf16[6,192,256]{2,1,0:T(8,128)(2,1)} %get-tuple-element.168), channel_id=1, source_target_pairs={{0,8},{1,24},{2,16},{3,0},{4,12},{5,28},{6,20},{7,4},{8,10},{9,26}... | collective-permute-start | bytes 1769480 | tf_op jit(solution)/shard_map/ppermute | solution.py:512
  135.1 41.8 %collective-permute-start.9 = (bf16[6,192,256]{2,1,0:T(8,128)(2,1)}, bf16[6,192,256]{2,1,0:T(8,128)(2,1)}, u32[]{:S(2)}, u32[]{:S(2)}) collective-permute-start(bf16[6,192,256]{2,1,0:T(8,128)(2,1)} %get-tuple-element.169), channel_id=1, source_target_pairs={{0,16},{1,0},{2,24},{3,8},{4,20},{5,4},{6,28},{7,12},{8,18},{9,2},... | collective-permute-start | bytes 1769480 | tf_op jit(solution)/shard_map/ppermute | solution.py:512
  138.6 38.3 %collective-permute-start.10 = (bf16[6,192,256]{2,1,0:T(8,128)(2,1)}, bf16[6,192,256]{2,1,0:T(8,128)(2,1)}, u32[]{:S(2)}, u32[]{:S(2)}) collective-permute-start(bf16[6,192,256]{2,1,0:T(8,128)(2,1)} %get-tuple-element.170), channel_id=1, source_target_pairs={{0,24},{1,8},{2,0},{3,16},{4,28},{5,12},{6,4},{7,20},{8,26},{9,10}... | collective-permute-start | bytes 1769480 | tf_op jit(solution)/shard_map/ppermute | solution.py:512
  190.4 40.7 %all-to-all-start.1 = ((bf16[8,6,96,256]{3,2,1,0:T(8,128)(2,1)}), bf16[8,6,96,256]{3,2,1,0:T(8,128)(2,1)}, u32[]{:S(2)}, u32[]{:S(2)}) async-start(bf16[8,6,96,256]{3,2,1,0:T(8,128)(2,1)} %get-tuple-element.176), calls=%async_computation.1 | async-start | bytes 4718592 | tf_op jit(solution)/shard_map/all_to_all | solution.py:562
  231.1 57.3 %all-to-all-start.2 = ((bf16[8,6,96,256]{3,2,1,0:T(8,128)(2,1)}), bf16[8,6,96,256]{3,2,1,0:T(8,128)(2,1)}, u32[]{:S(2)}, u32[]{:S(2)}) async-start(bf16[8,6,96,256]{3,2,1,0:T(8,128)(2,1)} %get-tuple-element.185), calls=%async_computation.2 | async-start | bytes 4718592 | tf_op jit(solution)/shard_map/all_to_all | solution.py:562
  236.9 58.4 %collective-permute-start.11 = (bf16[6,192,256]{2,1,0:T(8,128)(2,1)}, bf16[6,192,256]{2,1,0:T(8,128)(2,1)}, u32[]{:S(2)}, u32[]{:S(2)}) collective-permute-start(bf16[6,192,256]{2,1,0:T(8,128)(2,1)} %get-tuple-element.181), channel_id=1, source_target_pairs={{0,2},{1,18},{2,10},{3,26},{4,6},{5,22},{6,14},{7,30},{8,0},{9,16}... | collective-permute-start | bytes 1769480 | tf_op jit(solution)/shard_map/ppermute | solution.py:574
  239.1 56.3 %collective-permute-start.12 = (bf16[6,192,256]{2,1,0:T(8,128)(2,1)S(1)}, bf16[6,192,256]{2,1,0:T(8,128)(2,1)}, u32[]{:S(2)}, u32[]{:S(2)}) collective-permute-start(bf16[6,192,256]{2,1,0:T(8,128)(2,1)S(1)} %get-tuple-element.182), channel_id=1, source_target_pairs={{0,10},{1,26},{2,18},{3,2},{4,14},{5,30},{6,22},{7,6},{8,8},{9,24}... | collective-permute-start | bytes 1769480 | tf_op jit(solution)/shard_map/ppermute | solution.py:574
  242.2 53.2 %collective-permute-start.13 = (bf16[6,192,256]{2,1,0:T(8,128)(2,1)S(1)}, bf16[6,192,256]{2,1,0:T(8,128)(2,1)}, u32[]{:S(2)}, u32[]{:S(2)}) collective-permute-start(bf16[6,192,256]{2,1,0:T(8,128)(2,1)S(1)} %get-tuple-element.183), channel_id=1, source_target_pairs={{0,18},{1,2},{2,26},{3,10},{4,22},{5,6},{6,30},{7,14},{8,16},{9,0}... | collective-permute-start | bytes 1769480 | tf_op jit(solution)/shard_map/ppermute | solution.py:574
  243.0 52.4 %collective-permute-start.14 = (bf16[6,192,256]{2,1,0:T(8,128)(2,1)S(1)}, bf16[6,192,256]{2,1,0:T(8,128)(2,1)}, u32[]{:S(2)}, u32[]{:S(2)}) collective-permute-start(bf16[6,192,256]{2,1,0:T(8,128)(2,1)S(1)} %get-tuple-element.184), channel_id=1, source_target_pairs={{0,26},{1,10},{2,2},{3,18},{4,30},{5,14},{6,6},{7,22},{8,24},{9,8}... | collective-permute-start | bytes 1769480 | tf_op jit(solution)/shard_map/ppermute | solution.py:574
  288.4 42.7 %all-to-all-start.3 = ((bf16[8,6,96,256]{3,2,1,0:T(8,128)(2,1)}), bf16[8,6,96,256]{3,2,1,0:T(8,128)(2,1)}, u32[]{:S(2)}, u32[]{:S(2)}) async-start(bf16[8,6,96,256]{3,2,1,0:T(8,128)(2,1)} %get-tuple-element.206), calls=%async_computation.3 | async-start | bytes 4718592 | tf_op jit(solution)/shard_map/all_to_all | solution.py:562
  331.2 82.9 %all-to-all-start.4 = ((bf16[8,6,96,256]{3,2,1,0:T(8,128)(2,1)}), bf16[8,6,96,256]{3,2,1,0:T(8,128)(2,1)}, u32[]{:S(2)}, u32[]{:S(2)}) async-start(bf16[8,6,96,256]{3,2,1,0:T(8,128)(2,1)} %get-tuple-element.208), calls=%async_computation.4 | async-start | bytes 4718592 | tf_op jit(solution)/shard_map/all_to_all | solution.py:562
  360.6 49.4 %collective-permute-start.15 = (bf16[192,1536]{1,0:T(8,128)(2,1)}, bf16[192,1536]{1,0:T(8,128)(2,1)S(1)}, u32[]{:S(2)}, u32[]{:S(2)}) collective-permute-start(bf16[192,1536]{1,0:T(8,128)(2,1)} %get-tuple-element.227), channel_id=1, source_target_pairs={{0,0},{16,1},{8,2},{24,3},{4,4},{20,5},{12,6},{28,7},{2,8},{18,9},... | collective-permute-start | bytes 1769480 | tf_op jit(solution)/shard_map/ppermute | solution.py:609
  362.6 47.5 %collective-permute-start.16 = (bf16[192,1536]{1,0:T(8,128)(2,1)}, bf16[192,1536]{1,0:T(8,128)(2,1)S(1)}, u32[]{:S(2)}, u32[]{:S(2)}) collective-permute-start(bf16[192,1536]{1,0:T(8,128)(2,1)} %get-tuple-element.228), channel_id=1, source_target_pairs={{2,0},{18,1},{10,2},{26,3},{6,4},{22,5},{14,6},{30,7},{0,8},{16,9}... | collective-permute-start | bytes 1769480 | tf_op jit(solution)/shard_map/ppermute | solution.py:609
  362.6 48.4 %collective-permute-start.17 = (bf16[192,1536]{1,0:T(8,128)(2,1)}, bf16[192,1536]{1,0:T(8,128)(2,1)S(1)}, u32[]{:S(2)}, u32[]{:S(2)}) collective-permute-start(bf16[192,1536]{1,0:T(8,128)(2,1)} %get-tuple-element.229), channel_id=1, source_target_pairs={{8,0},{24,1},{16,2},{0,3},{12,4},{28,5},{20,6},{4,7},{10,8},{26,9}... | collective-permute-start | bytes 1769480 | tf_op jit(solution)/shard_map/ppermute | solution.py:609
  365.3 48.7 %collective-permute-start.18 = (bf16[192,1536]{1,0:T(8,128)(2,1)}, bf16[192,1536]{1,0:T(8,128)(2,1)}, u32[]{:S(2)}, u32[]{:S(2)}) collective-permute-start(bf16[192,1536]{1,0:T(8,128)(2,1)} %get-tuple-element.230), channel_id=1, source_target_pairs={{10,0},{26,1},{18,2},{2,3},{14,4},{30,5},{22,6},{6,7},{8,8},{24,9}... | collective-permute-start | bytes 1769480 | tf_op jit(solution)/shard_map/ppermute | solution.py:609
  410.1 26.5 %copy-start.31 = (bf16[192,1536]{1,0:T(8,128)(2,1)}, bf16[192,1536]{1,0:T(8,128)(2,1)S(1)}, u32[]{:S(2)}) copy-start(bf16[192,1536]{1,0:T(8,128)(2,1)S(1)} %collective-permute-done.15.refs_0_) | copy-start | bytes 1769476
  410.1 26.5 %copy-start.32 = (bf16[192,1536]{1,0:T(8,128)(2,1)}, bf16[192,1536]{1,0:T(8,128)(2,1)S(1)}, u32[]{:S(2)}) copy-start(bf16[192,1536]{1,0:T(8,128)(2,1)S(1)} %collective-permute-done.16.refs_1_) | copy-start | bytes 1769476
  411.0 25.6 %copy-start.33 = (bf16[192,1536]{1,0:T(8,128)(2,1)}, bf16[192,1536]{1,0:T(8,128)(2,1)S(1)}, u32[]{:S(2)}) copy-start(bf16[192,1536]{1,0:T(8,128)(2,1)S(1)} %collective-permute-done.17.refs_2_) | copy-start | bytes 1769476
  414.0 22.7 %collective-permute-start.19 = (bf16[2,2,768,768]{3,2,1,0:T(8,128)(2,1)}, bf16[2,2,768,768]{3,2,1,0:T(8,128)(2,1)}, u32[]{:S(2)}, u32[]{:S(2)}) collective-permute-start(bf16[2,2,768,768]{3,2,1,0:T(8,128)(2,1)} %get-tuple-element.236), channel_id=1, source_target_pairs={{0,1},{1,0},{2,3},{3,2},{4,5},{5,4},{6,7},{7,6},{8,9},{9,8},{10,11... | collective-permute-start | bytes 14155784 | tf_op jit(solution)/shard_map/ppermute | solution.py:629
  414.0 32.0 %collective-permute-start.20 = (bf16[192,1536]{1,0:T(8,128)(2,1)}, bf16[192,1536]{1,0:T(8,128)(2,1)}, u32[]{:S(2)}, u32[]{:S(2)}) collective-permute-start(bf16[192,1536]{1,0:T(8,128)(2,1)} %get-tuple-element.246), channel_id=1, source_target_pairs={{16,0},{0,1},{24,2},{8,3},{20,4},{4,5},{28,6},{12,7},{18,8},{2,9},... | collective-permute-start | bytes 1769480 | tf_op jit(solution)/shard_map/ppermute | solution.py:609
  415.9 30.2 %collective-permute-start.21 = (bf16[192,1536]{1,0:T(8,128)(2,1)}, bf16[192,1536]{1,0:T(8,128)(2,1)}, u32[]{:S(2)}, u32[]{:S(2)}) collective-permute-start(bf16[192,1536]{1,0:T(8,128)(2,1)} %get-tuple-element.247), channel_id=1, source_target_pairs={{18,0},{2,1},{26,2},{10,3},{22,4},{6,5},{30,6},{14,7},{16,8},{0,9}... | collective-permute-start | bytes 1769480 | tf_op jit(solution)/shard_map/ppermute | solution.py:609
  436.7 9.4 %copy-start.36 = (bf16[192,1536]{1,0:T(8,128)(2,1)S(1)}, bf16[192,1536]{1,0:T(8,128)(2,1)}, u32[]{:S(2)}) copy-start(bf16[192,1536]{1,0:T(8,128)(2,1)} %get-tuple-element.262) | copy-start | bytes 1769476
  446.0 21.8 %collective-permute-start.22 = (bf16[192,1536]{1,0:T(8,128)(2,1)}, bf16[192,1536]{1,0:T(8,128)(2,1)S(1)}, u32[]{:S(2)}, u32[]{:S(2)}) collective-permute-start(bf16[192,1536]{1,0:T(8,128)(2,1)} %get-tuple-element.261), channel_id=1, source_target_pairs={{24,0},{8,1},{0,2},{16,3},{28,4},{12,5},{4,6},{20,7},{26,8},{10,9}... | collective-permute-start | bytes 1769480 | tf_op jit(solution)/shard_map/ppermute | solution.py:609
  446.1 21.8 %collective-permute-start.23 = (bf16[192,1536]{1,0:T(8,128)(2,1)S(1)}, bf16[192,1536]{1,0:T(8,128)(2,1)S(1)}, u32[]{:S(2)}, u32[]{:S(2)}) collective-permute-start(bf16[192,1536]{1,0:T(8,128)(2,1)S(1)} %copy-done.36), channel_id=1, source_target_pairs={{26,0},{10,1},{2,2},{18,3},{30,4},{14,5},{6,6},{22,7},{24,8},{8,9}... | collective-permute-start | bytes 1769480 | tf_op jit(solution)/shard_map/ppermute | solution.py:609
  447.0 66.9 %collective-permute-start.24 = (bf16[2,2,4,96,768]{4,3,2,1,0:T(8,128)(2,1)}, bf16[2,2,4,96,768]{4,3,2,1,0:T(8,128)(2,1)}, u32[]{:S(2)}, u32[]{:S(2)}) collective-permute-start(bf16[2,2,4,96,768]{4,3,2,1,0:T(8,128)(2,1)} %get-tuple-element.265), channel_id=1, source_target_pairs={{0,4},{4,0},{8,12},{12,8},{16,20},{20,16},{24,28},{28,24},{1,5},{5... | collective-permute-start | bytes 7077896 | tf_op jit(solution)/shard_map/ppermute | solution.py:638
  479.3 8.7 %copy-start.8 = (f32[768,128]{1,0:T(8,128)S(1)}, f32[768,128]{1,0:T(8,128)}, u32[]{:S(2)}) copy-start(f32[768,128]{1,0:T(8,128)} %get-tuple-element.297) | copy-start | bytes 1179652
  479.3 8.9 %copy-start.7 = (f32[768,128]{1,0:T(8,128)S(1)}, f32[768,128]{1,0:T(8,128)}, u32[]{:S(2)}) copy-start(f32[768,128]{1,0:T(8,128)} %get-tuple-element.299) | copy-start | bytes 1179652
  479.3 8.9 %copy-start.9 = (f32[768,128]{1,0:T(8,128)S(1)}, f32[768,128]{1,0:T(8,128)}, u32[]{:S(2)}) copy-start(f32[768,128]{1,0:T(8,128)} %get-tuple-element.300) | copy-start | bytes 1179652
  479.3 9.0 %copy-start.11 = (f32[768,128]{1,0:T(8,128)S(1)}, f32[768,128]{1,0:T(8,128)}, u32[]{:S(2)}) copy-start(f32[768,128]{1,0:T(8,128)} %get-tuple-element.301) | copy-start | bytes 1179652
  479.3 9.2 %copy-start.2 = (f32[3072,128]{1,0:T(8,128)S(1)}, f32[3072,128]{1,0:T(8,128)}, u32[]{:S(2)}) copy-start(f32[3072,128]{1,0:T(8,128)} %get-tuple-element.302) | copy-start | bytes 4718596
  479.3 66.5 %all-to-all-start.5 = ((bf16[8,12,48,256]{3,2,1,0:T(8,128)(2,1)}), bf16[8,12,48,256]{3,2,1,0:T(8,128)(2,1)}, u32[]{:S(2)}, u32[]{:S(2)}) async-start(bf16[8,12,48,256]{3,2,1,0:T(8,128)(2,1)} %bitcast.200), calls=%async_computation.5 | async-start | bytes 4718592 | tf_op jit(solution)/shard_map/all_to_all | solution.py:693
  491.5 30.0 %copy-start.14 = (f32[192,128]{1,0:T(8,128)S(1)}, f32[192,128]{1,0:T(8,128)}, u32[]{:S(2)}) copy-start(f32[192,128]{1,0:T(8,128)} %get-tuple-element.292) | copy-start | bytes 294916
  491.6 30.3 %copy-start.13 = (f32[192,128]{1,0:T(8,128)S(1)}, f32[192,128]{1,0:T(8,128)}, u32[]{:S(2)}) copy-start(f32[192,128]{1,0:T(8,128)} %get-tuple-element.290) | copy-start | bytes 294916
  519.9 26.0 %collective-permute-start.25 = (bf16[2,4,96,768]{3,2,1,0:T(8,128)(2,1)S(1)}, bf16[2,4,96,768]{3,2,1,0:T(8,128)(2,1)}, u32[]{:S(2)}, u32[]{:S(2)}) collective-permute-start(bf16[2,4,96,768]{3,2,1,0:T(8,128)(2,1)S(1)} %fusion.4), channel_id=1, source_target_pairs={{0,2},{1,3},{2,0},{3,1},{4,6},{5,7},{6,4},{7,5},{8,10},{9,11},{10,... | collective-permute-start | bytes 3538952 | tf_op jit(solution)/shard_map/ppermute | solution.py:638
  522.8 10.6 %copy-start.16 = (f32[48,128]{1,0:T(8,128)S(1)}, f32[48,128]{1,0:T(8,128)}, u32[]{:S(2)}) copy-start(f32[48,128]{1,0:T(8,128)} %get-tuple-element.293) | copy-start | bytes 73732
  522.9 11.4 %copy-start.15 = (f32[48,128]{1,0:T(8,128)S(1)}, f32[48,128]{1,0:T(8,128)}, u32[]{:S(2)}) copy-start(f32[48,128]{1,0:T(8,128)} %get-tuple-element.295) | copy-start | bytes 73732
  522.9 12.3 %copy-start.22 = (f32[96]{0:T(128)S(1)}, f32[96]{0:T(128)}, u32[]{:S(2)}) copy-start(f32[96]{0:T(128)} %copy-done.21) | copy-start | bytes 1156
  522.9 12.4 %copy-start.12 = (f32[96,2,256]{2,1,0:T(2,128)S(1)}, f32[96,2,256]{2,1,0:T(2,128)}, u32[]{:S(2)}) copy-start(f32[96,2,256]{2,1,0:T(2,128)} %get-tuple-element.268) | copy-start | bytes 589828
  547.4 21.4 %all-to-all-start.6 = ((f32[8,1,16369]{2,1,0:T(1,128)}), f32[8,1,16369]{2,1,0:T(1,128)S(1)}, u32[]{:S(2)}, u32[]{:S(2)}) async-start(f32[8,1,16369]{2,1,0:T(1,128)} %all_to_all.35), calls=%async_computation.6 | async-start | bytes 1048576 | tf_op jit(solution)/shard_map/all_to_all | solution.py:721
  555.6 18.1 %copy-start.6 = (f32[4,12,1,256]{3,0,1,2:T(4,128)S(1)}, f32[4,12,1,256]{3,0,1,2:T(4,128)}, u32[]{:S(2)}) copy-start(f32[4,12,1,256]{3,0,1,2:T(4,128)} %copy-done.5) | copy-start | bytes 147460
  555.6 18.8 %copy-start.4 = (f32[4,12,1,256]{3,0,1,2:T(4,128)S(1)}, f32[4,12,1,256]{3,0,1,2:T(4,128)}, u32[]{:S(2)}) copy-start(f32[4,12,1,256]{3,0,1,2:T(4,128)} %copy-done.3) | copy-start | bytes 147460
  569.1 56.7 %all-to-all-start.7 = ((bf16[8,12,48,256]{3,2,1,0:T(8,128)(2,1)}), bf16[8,12,48,256]{3,2,1,0:T(8,128)(2,1)}, u32[]{:S(2)}, u32[]{:S(2)}) async-start(bf16[8,12,48,256]{3,2,1,0:T(8,128)(2,1)} %bitcast.69), calls=%async_computation.7 | async-start | bytes 4718592 | tf_op jit(solution)/shard_map/all_to_all | solution.py:730
  583.2 39.5 %copy-start.1 = (f32[4,2,96,768]{3,2,0,1:T(8,128)S(1)}, f32[4,2,96,768]{3,2,0,1:T(8,128)}, u32[]{:S(2)}) copy-start(f32[4,2,96,768]{3,2,0,1:T(8,128)} %fusion.3) | copy-start | bytes 7077892
  584.1 5.3 collective-permute-start.26
  586.4 36.3 %collective-permute-start.28 = (bf16[2,2,96,768]{3,2,1,0:T(8,128)(2,1)}, bf16[2,2,96,768]{3,2,1,0:T(8,128)(2,1)}, u32[]{:S(2)}, u32[]{:S(2)}) collective-permute-start(bf16[2,2,96,768]{3,2,1,0:T(8,128)(2,1)} %fusion.5), channel_id=1, source_target_pairs={{0,8},{8,0},{16,24},{24,16},{1,9},{9,1},{17,25},{25,17},{2,10},{10... | collective-permute-start | bytes 1769480 | tf_op jit(solution)/shard_map/ppermute | solution.py:638
  589.5 5.6 collective-permute-start.27
  625.8 13.3 %collective-permute-start.29 = (bf16[1,2,96,768]{3,2,1,0:T(8,128)(2,1)S(1)}, bf16[1,2,96,768]{3,2,1,0:T(8,128)(2,1)S(1)}, u32[]{:S(2)}, u32[]{:S(2)}) collective-permute-start(bf16[1,2,96,768]{3,2,1,0:T(8,128)(2,1)S(1)} %dynamic-slice_convert_fusion), channel_id=1, source_target_pairs={{0,16},{8,24},{16,0},{24,8},{1,17},{9,25},{17,1},{25,9},{2,18},{10... | collective-permute-start | bytes 884744 | tf_op jit(solution)/shard_map/ppermute | solution.py:638
  (14 other events, 69.7 us)
Sparse Core Ops, SparseCore 0:
  9.6 38.0 all-gather.7
  49.8 37.5 all-gather.5

commit v7 on v6

--- a/solution.py
+++ b/solution.py
@@ -370,15 +370,10 @@
                 out[0, starts[part] + row] = piece[:, row * width : (row + 1) * width].astype(F32)
 
 
-def finish_kernel(feats, patches, mean, rstd, one, two, *refs):
-    grads, out = refs[:-1], refs[-1]
+def finish_kernel(feats, grad, patches, mean, rstd, one, two, *refs):
+    out = refs[-1]
     normed = (patches[0].astype(F32) - mean[0]) * rstd[0]
-    fix = rstd[0] * (one[0] + normed * two[0]) * (1.0 / feats)
-    at = 0
-    for grad in grads:
-        here = slice(at, at + grad.shape[2])
-        out[0, :, here] = grad[0].astype(F32) - fix[:, here]
-        at += grad.shape[2]
+    out[0] = grad[0].astype(F32) - rstd[0] * (one[0] + normed * two[0]) * (1.0 / feats)
 
 
 def whole(shape):
@@ -438,6 +433,7 @@
     shape = jax.ShapeDtypeStruct
 
     pieces = patches.reshape(snaps, per, inner, mine, width).swapaxes(1, 2).reshape(owners, per, mine, width)
+    pieces, expand_weight, project_weight = lax.optimization_barrier((pieces, expand_weight, project_weight))
     pieces = lax.all_to_all(pieces, sp, 0, 0, tiled=True)
 
     held = Rows(per, inner, tp)
@@ -549,7 +545,6 @@
         (*[shape(block_modes, BF)] * 4, shape((8, 2 * modes), F32)),
         (block_spec, block_spec, block_spec, block_spec, fixed((8, 2 * modes))), [], 48, 17,
     )
-    kept, late, cots[0] = lax.optimization_barrier((kept, late, cots[0]))
     part_specs = [pl.BlockSpec((ranks, n, some, width), lambda g, *_: (0, 0, g, 0)) for n in parts]
     sections = run(
         "section", functools.partial(section_kernel, order), grid,
@@ -557,6 +552,8 @@
         [piece_spec, stat_spec, stat_spec, feat_spec, feat_spec, modes_spec, *lon_b, *lat_specs],
         [shape((ranks, n, mine, width), BF) for n in parts], part_specs, scratch, 56, 17,
     )
+
+    sections, late, cots[0] = lax.optimization_barrier((sections, late, cots[0]))
 
     def exchange(array):
         return lax.all_to_all(array, ("t", "y", "j"), 0, 0, tiled=True)
@@ -755,15 +752,22 @@
         pl.BlockSpec((1, per, quarter, width), lambda i, s, _: (s[i], 0, 0, 0)), [], 32, 8, (slot, starts),
     )
     one_spec = pl.BlockSpec((1, per, 1, width), lambda i: (i // inner, 0, 0, 0))
-    patch_spec = pl.BlockSpec((1, per, mine, width), lambda i: (i // inner, 0, i % inner, 0))
-    patches_grad = run(
-        "finish", functools.partial(finish_kernel, feats), (owners,),
-        (patches, stats[:, :, 0, None], stats[:, :, 1, None], fixes[:, :, 0], fixes[:, :, 1], *grads),
-        [patch_spec, *[one_spec] * 4,
-         *[pl.BlockSpec((1, per, grad.shape[2], width), lambda i: (i, 0, 0, 0)) for grad in grads]],
-        shape((snaps, per, quarter, width), F32), patch_spec, [], 48, 100,
-    )
-
+    any_out = pl.BlockSpec(memory_space=pl.ANY)
+    written = []
+    for i, grad in enumerate(grads):
+        n = grad.shape[2]
+        part_spec = pl.BlockSpec(
+            (1, per, n, width), lambda g, i=i, n=n: (g // inner, 0, g % inner * (mine // n) + i, 0)
+        )
+        written = [run(
+            "finish", functools.partial(finish_kernel, feats), (owners,),
+            (grad, patches, stats[:, :, 0, None], stats[:, :, 1, None], fixes[:, :, 0], fixes[:, :, 1], *written),
+            [pl.BlockSpec((1, per, n, width), lambda g: (g, 0, 0, 0)), part_spec, *[one_spec] * 4,
+             *[any_out] * len(written)],
+            shape((snaps, per, quarter, width), F32), part_spec, [], 48, 100 if i == len(grads) - 1 else 5,
+            aliases={6: 0} if written else None,
+        )]
+    patches_grad = written[0]
     expand_sum, project_sum = along_z(weights, 2)[0]
     project_sum = project_sum.T
     return (

time: 662 us -> 655 us (0.989)
    ppermute x7, waiting for transfers between devices: 25.6 us -> 15.7 us  [per_device(): lax.ppermute(piece, sp, [(a, a ^ k) for a in range(owners)])]
    all_to_all x4, starting transfers between devices: 30.3 us -> 22.7 us  [exchange(): return lax.all_to_all(array, ('t', 'y', 'j'), 0, 0, tiled=True)]
    pallas_call x14 -> x15, Pallas kernels: 269 us -> 273 us  [run(): return call(*scalars, *ins)]
  transfers between devices with their start and end apart: 40 -> 40, of which waited for: 12 -> 14; matrix products, arithmetic and copies ran while one was open for 12% -> 11% of each run, Pallas kernels for 39% -> 42%
where the time goes in v7:
time: 655 us; the launch traced here: 643 us
  Pallas kernels  273 us (42%)
  waiting for transfers between devices  148 us (23%)
  starting transfers between devices  102 us (16%)
  local copies, waits for them, and re-layouts  52.7 us (8%)
  other arithmetic  29.6 us (5%)
  blocking collectives  20.2 us (3%)
  between operations  18.3 us (3%)
    pallas_call x15, Pallas kernels, run(): return call(*scalars, *ins)  273 us
    ppermute x6, waiting for transfers between devices, trade(): return lax.ppermute(theirs, axes, [(a, a ^ bit) for a in range(size)])  59.1 us
    all_gather x1, waiting for transfers between devices, per_device(): wp = lax.all_gather(project_weight, 't', tiled=True)  28.7 us
    all_to_all x4, waiting for transfers between devices, exchange(): return lax.all_to_all(array, ('t', 'y', 'j'), 0, 0, tiled=True)  27.6 us
    all_to_all x4, starting transfers between devices, exchange(): return lax.all_to_all(array, ('t', 'y', 'j'), 0, 0, tiled=True)  22.7 us
    ppermute x8, starting transfers between devices, send_results(): lax.ppermute(rows_out[2 * k + part], every, route(k, part, True))  15.7 us
    ppermute x7, waiting for transfers between devices, per_device(): lax.ppermute(piece, sp, [(a, a ^ k) for a in range(owners)])  15.7 us
    ppermute x7, starting transfers between devices, per_device(): lax.ppermute(piece, sp, [(a, a ^ k) for a in range(owners)])  15.3 us
  transfers between devices with their start and end apart: 40, of which 14 were waited for; matrix products, arithmetic and copies ran while one was open for 11% of the time, Pallas kernels for 42%

profile of v7, /device:TPU:2, one launch (start us, length us, event | category | flops | bytes accessed | tf_op | source)
XLA Modules:
  0.0 643.0 jit_solution(13578717457237550907)
XLA Ops:
  7.2 2.8 fusion.16
  10.0 2.6 pad_maximum_fusion
  14.3 6.0 all-to-all-start
  21.9 11.5 %all-reduce = f32[5376]{0:T(1024)S(1)} all-reduce(f32[5376]{0:T(1024)S(1)} %dynamic-update-slice), channel_id=4, replica_groups=mesh['z'=4,'y'=2,'j'=1,'t'=4] {'t'}, use_global_device_ids=true, to_apply=%add | all-reduce | flops 5376 | bytes 43008
  33.5 3.3 convert_reduce_fusion
  36.9 4.2 fusion.1
  43.4 8.8 %all-gather = f32[8,4,12,256]{3,1,2,0:T(4,128)S(1)} all-gather(f32[2,4,12,256]{3,1,2,0:T(4,128)S(1)} %copy.239), channel_id=2, replica_groups=mesh['z'=4,'y'=2,'j'=1,'t'=4] {'t'}, dimensions={0}, use_global_device_ids=true | all-gather | bytes 491520 | tf_op jit(solution)/shard_map/all_gather | solution.py:456
  53.1 4.0 dynamic-slice_bitcast_fusion
  57.2 6.7 %copy.245 = bf16[4,768,768]{2,1,0:T(8,128)(2,1)} copy(bf16[4,768,768]{1,2,0:T(8,128)(2,1)} %bitcast.195) | data formatting | bytes 9437184 | tf_op jit(solution)/shard_map/transpose | solution.py:468
  63.9 28.7 %all-gather.6.cloned.1.call-done = bf16[3072,768]{0,1:T(8,128)(2,1)} async-done(((bf16[768,768]{0,1:T(8,128)(2,1)}), bf16[3072,768]{0,1:T(8,128)(2,1)}) %all-gather.6.cloned.1.call-update) | async-done | bytes 4718608 | tf_op jit(solution)/shard_map/all_gather | solution.py:467
  94.7 1.7 broadcast_in_dim.70.refs_8_
  96.6 1.8 collective-permute-start.6
  101.2 3.6 collective-permute-start.2
  105.5 6.4 collective-permute-start
  113.9 15.7 %collective-permute-done.2 = f32[12,2,256]{2,1,0:T(2,128)S(1)} collective-permute-done((f32[12,2,256]{2,1,0:T(2,128)S(1)}, f32[12,2,256]{2,1,0:T(2,128)S(1)}, u32[]{:S(2)}, u32[]{:S(2)}) %collective-permute-start.2) | collective-permute-done | bytes 24608 | tf_op jit(solution)/shard_map/ppermute | solution.py:476
  131.0 2.9 collective-permute-start.7
  134.0 3.3 collective-permute-start.9
  139.2 20.2 %spectrum.1.spec = bf16[2,96,96,128]{3,2,1,0:T(8,128)(2,1)} custom-call(bf16[8,12,96,256]{3,2,1,0:T(8,128)(2,1)} %all-to-all-done.pieces, f32[96,1,256]{2,1,0:T(1,128)} %get-tuple-element.416.mean.refs_2_, f32[96,1,256]{2,1,0:T(1,128)} %get-tuple-element.415.rstd.refs_3_, f32[96,256]{1,0:T(8,128)} %broadcast_in_dim.71.scale.refs_4_, ...), custom_call_target="tpu_custom_call" | custom-call | flops 22000001024 | bytes 74800000 | tf_op jit(solution)/shard_map/spectrum/pallas_call | solution.py:400
  160.9 14.6 %filter.1 = (bf16[2,96,96,128]{3,2,1,0:T(8,128)(2,1)}, bf16[2,96,96,128]{3,2,1,0:T(8,128)(2,1)}, bf16[2,96,96,128]{3,2,1,0:T(8,128)(2,1)}, bf16[2,96,96,128]{3,2,1,0:T(8,128)(2,1)}, f32[8,256]{1,0:T(8,128)}) custom-call(bf16[2,96,96,128]{3,2,1,0:T(8,128)(2,1)} %spectrum.1.spec, bf16[192,192]{1,0:T(8,128)(2,1)} %maximum_maximum_fusion.w1, ...), custom_call_target="tpu_custom_call" | custom-call | flops 16999999488 | bytes 57800000 | tf_op jit(solution)/shard_map/filter/pallas_call | solution.py:400
  175.5 13.4 %section.1 = (bf16[8,6,96,256]{3,2,1,0:T(8,128)(2,1)}, bf16[8,6,96,256]{3,2,1,0:T(8,128)(2,1)}) custom-call(bf16[8,12,96,256]{3,2,1,0:T(8,128)(2,1)} %all-to-all-done.pieces, f32[96,1,256]{2,1,0:T(1,128)} %get-tuple-element.416.mean.refs_2_, f32[96,1,256]{2,1,0:T(1,128)} %get-tuple-element.415.rstd.refs_3_, f32[96,256]{1,0:T(8,128)} %broadcast_in_dim.71.scale.refs_4_, ...), custom_call_target="tpu_custom_call" | custom-call | flops 16999999488 | bytes 57800000 | tf_op jit(solution)/shard_map/section/pallas_call | solution.py:400
  188.9 5.8 all-to-all-start.1
  195.4 6.6 %copy.257.refs_6_ = bf16[3072,768]{1,0:T(8,128)(2,1)} copy(bf16[3072,768]{0,1:T(8,128)(2,1)} %all-gather.6.cloned.1.call-done) | data formatting | bytes 9437184 | tf_op jit(solution)/shard_map/optimization_barrier | solution.py:470
  202.0 20.8 %all-to-all-done.1.refs_4_.refs_0_ = bf16[8,6,96,256]{3,2,1,0:T(8,128)(2,1)} async-done(((bf16[8,6,96,256]{3,2,1,0:T(8,128)(2,1)}), bf16[8,6,96,256]{3,2,1,0:T(8,128)(2,1)}, u32[]{:S(2)}, u32[]{:S(2)}) %all-to-all-start.1) | async-done | bytes 2359328 | tf_op jit(solution)/shard_map/all_to_all | solution.py:559
  222.8 5.3 all-to-all-start.2
  228.7 4.6 collective-permute-start.12
  233.3 2.5 collective-permute-start.13
  237.3 35.5 %feed.2 = (bf16[768,3072]{1,0:T(8,128)(2,1)}, bf16[3072,3072]{1,0:T(8,128)(2,1)}, bf16[3072,3072]{1,0:T(8,128)(2,1)}, bf16[768,3072]{1,0:T(8,128)(2,1)}, bf16[8,...) custom-call(s32[4]{0:T(128)} %pad_add_fusion.2.place, ...), custom_call_target="tpu_custom_call" | custom-call | flops 43000000512 | bytes 146200000 | tf_op jit(solution)/shard_map/feed/pallas_call | solution.py:400
  272.7 6.8 %all-to-all-done.2.refs_4_.refs_1_ = bf16[8,6,96,256]{3,2,1,0:T(8,128)(2,1)} async-done(((bf16[8,6,96,256]{3,2,1,0:T(8,128)(2,1)}), bf16[8,6,96,256]{3,2,1,0:T(8,128)(2,1)}, u32[]{:S(2)}, u32[]{:S(2)}) %all-to-all-start.2) | async-done | bytes 2359328 | tf_op jit(solution)/shard_map/all_to_all | solution.py:559
  279.6 7.2 %all-to-all-start.3 = ((bf16[8,6,96,256]{3,2,1,0:T(8,128)(2,1)}), bf16[8,6,96,256]{3,2,1,0:T(8,128)(2,1)}, u32[]{:S(2)}, u32[]{:S(2)}) async-start(bf16[8,6,96,256]{3,2,1,0:T(8,128)(2,1)} %get-tuple-element.214), calls=%async_computation.3 | async-start | bytes 4718592 | tf_op jit(solution)/shard_map/all_to_all | solution.py:559
  286.8 35.7 %feed.3 = (bf16[768,3072]{1,0:T(8,128)(2,1)}, bf16[3072,3072]{1,0:T(8,128)(2,1)}, bf16[3072,3072]{1,0:T(8,128)(2,1)}, bf16[768,3072]{1,0:T(8,128)(2,1)}, bf16[8,...) custom-call(s32[4]{0:T(128)} %pad_add_fusion.2.place, ...), custom_call_target="tpu_custom_call", output_to_operand_aliasing={{0}: (12, {}), {1}: (13, {}), {2}: (14, {}), {3}: (15, {})} | custom-call | flops 43000000512 | bytes 146200000 | tf_op jit(solution)/shard_map/feed/pallas_call | solution.py:400
  322.5 4.3 all-to-all-start.4
  327.9 24.1 %result.1 = (bf16[192,1536]{1,0:T(8,128)(2,1)}, bf16[192,1536]{1,0:T(8,128)(2,1)}, bf16[192,1536]{1,0:T(8,128)(2,1)}, bf16[192,1536]{1,0:T(8,128)(2,1)}, bf16[19...) custom-call(s32[4]{0:T(128)} %pad_add_fusion.2.place, ...), custom_call_target="tpu_custom_call" | custom-call | flops 10000000 | bytes 34000 | tf_op jit(solution)/shard_map/result/pallas_call | solution.py:400
  352.0 1.9 collective-permute-start.15
  354.0 3.6 collective-permute-start.17
  357.5 2.7 collective-permute-start.18
  360.8 41.5 %weights.1 = (bf16[2,2,768,768]{3,2,1,0:T(8,128)(2,1)}, f32[2,2,768,768]{3,2,1,0:T(8,128)}, f32[3072,128]{1,0:T(8,128)}, f32[768,128]{1,0:T(8,128)}) custom-call(s32[4]{0:T(128)} %pad_add_fusion.3.order, bf16[768,3072]{1,0:T(8,128)(2,1)} %get-tuple-element.230.normal, bf16[3072,3072]{1,0:T(8,128)(2,1)} %get-tuple-element.231.pre, ...), custom_call_target="tpu_custom_call" | custom-call | flops 10000000 | bytes 34000 | tf_op jit(solution)/shard_map/weights/pallas_call | solution.py:400
  402.7 4.9 collective-permute-done.18.refs_3_
  407.7 1.7 collective-permute-start.20
  410.4 16.6 %spectrum_back.1.freq = bf16[2,96,96,128]{3,2,1,0:T(8,128)(2,1)} custom-call(bf16[8,6,96,256]{3,2,1,0:T(8,128)(2,1)} %all-to-all-done.3.refs_0_, bf16[8,6,96,256]{3,2,1,0:T(8,128)(2,1)} %all-to-all-done.4.refs_1_, bf16[256,256]{1,0:T(8,128)(2,1)} %constant.383.clone.refs_2_, bf16[256,256]{1,0:T(8,128)(2,1)} %constant.384.clone.refs_3_, ...), custom_call_target="tpu_custom_call" | custom-call | flops 10000000 | bytes 34000 | tf_op jit(solution)/shard_map/spectrum_back/pallas_call | solution.py:400
  427.0 9.3 %add.403 = (f32[2,2,4,96,768]{4,3,2,1,0:T(8,128)}, bf16[2,2,4,96,768]{4,3,2,1,0:T(8,128)(2,1)}) custom-call(s32[1]{0:T(128)} %bitcast.67.side, f32[2,2,768,768]{3,2,1,0:T(8,128)} %get-tuple-element.246.kept, bf16[2,2,768,768]{3,2,1,0:T(8,128)(2,1)} %collective-permute-done.19.came), custom_call_target="tpu_custom_call" | custom-call | flops 10000000 | bytes 34000 | tf_op jit(solution)/shard_map/add/pallas_call | solution.py:400
  436.3 4.0 collective-permute-start.22
  441.1 2.0 collective-permute-start.24
  443.1 19.2 %filter_back.1 = (bf16[2,96,96,128]{3,2,1,0:T(8,128)(2,1)}, f32[192,192]{1,0:T(8,128)}, f32[192,192]{1,0:T(8,128)}, f32[192,128]{1,0:T(8,128)}, f32[192,128]{1,0:T(8,128)}) custom-call(bf16[2,96,96,128]{3,2,1,0:T(8,128)(2,1)} %spectrum_back.1.freq, bf16[2,96,96,128]{3,2,1,0:T(8,128)(2,1)} %spectrum.1.spec, bf16[2,96,96,128]{3,2,1,0:T(8,128)(2,1)} %get-tuple-element.259.mid, ...), custom_call_target="tpu_custom_call" | custom-call | flops 10000000 | bytes 34000 | tf_op jit(solution)/shard_map/filter_back/pallas_call | solution.py:400
  463.4 10.4 %last.2 = (bf16[96,48,256]{2,1,0:T(8,128)(2,1)}, f32[96,2,256]{2,1,0:T(2,128)}, f32[48,128]{1,0:T(8,128)}, f32[48,128]{1,0:T(8,128)}) custom-call(bf16[8,12,96,256]{3,2,1,0:T(8,128)(2,1)} %all-to-all-done.pieces, bf16[8,6,96,256]{3,2,1,0:T(8,128)(2,1)} %all-to-all-done.3.refs_0_, bf16[8,6,96,256]{3,2,1,0:T(8,128)(2,1)} %all-to-all-done.4.refs_1_, ...), custom_call_target="tpu_custom_call" | custom-call | flops 10000000 | bytes 34000 | tf_op jit(solution)/shard_map/last/pallas_call | solution.py:400
  473.8 6.7 %all-to-all-start.5 = ((bf16[8,12,48,256]{3,2,1,0:T(8,128)(2,1)}), bf16[8,12,48,256]{3,2,1,0:T(8,128)(2,1)}, u32[]{:S(2)}, u32[]{:S(2)}) async-start(bf16[8,12,48,256]{3,2,1,0:T(8,128)(2,1)} %bitcast.200), calls=%async_computation.5 | async-start | bytes 4718592 | tf_op jit(solution)/shard_map/all_to_all | solution.py:690
  484.7 24.0 %collective-permute-done.24 = bf16[2,2,4,96,768]{4,3,2,1,0:T(8,128)(2,1)} collective-permute-done((bf16[2,2,4,96,768]{4,3,2,1,0:T(8,128)(2,1)}, bf16[2,2,4,96,768]{4,3,2,1,0:T(8,128)(2,1)}, u32[]{:S(2)}, u32[]{:S(2)}) %collective-permute-start.24) | collective-permute-done | bytes 2359328 | tf_op jit(solution)/shard_map/ppermute | solution.py:635
  508.7 3.6 convert_add_fusion
  512.3 2.2 copy-done
  514.6 3.0 collective-permute-start.25
  519.1 10.5 %last.3 = (bf16[96,48,256]{2,1,0:T(8,128)(2,1)}, f32[96,2,256]{2,1,0:T(2,128)}, f32[48,128]{1,0:T(8,128)}, f32[48,128]{1,0:T(8,128)}) custom-call(bf16[8,12,96,256]{3,2,1,0:T(8,128)(2,1)} %all-to-all-done.pieces, bf16[8,6,96,256]{3,2,1,0:T(8,128)(2,1)} %all-to-all-done.3.refs_0_, bf16[8,6,96,256]{3,2,1,0:T(8,128)(2,1)} %all-to-all-done.4.refs_1_, ...), custom_call_target="tpu_custom_call" | custom-call | flops 10000000 | bytes 34000 | tf_op jit(solution)/shard_map/last/pallas_call | solution.py:400
  533.2 10.5 %collective-permute-done.25 = bf16[2,4,96,768]{3,2,1,0:T(8,128)(2,1)} collective-permute-done((bf16[2,4,96,768]{3,2,1,0:T(8,128)(2,1)S(1)}, bf16[2,4,96,768]{3,2,1,0:T(8,128)(2,1)}, u32[]{:S(2)}, u32[]{:S(2)}) %collective-permute-start.25) | collective-permute-done | bytes 1179680 | tf_op jit(solution)/shard_map/ppermute | solution.py:635
  545.2 4.6 all-to-all-start.6
  549.9 3.7 fusion.3
  553.6 9.6 %all-to-all-done.6 = f32[8,1,16369]{2,1,0:T(1,128)S(1)} async-done(((f32[8,1,16369]{2,1,0:T(1,128)}), f32[8,1,16369]{2,1,0:T(1,128)S(1)}, u32[]{:S(2)}, u32[]{:S(2)}) %all-to-all-start.6) | async-done | bytes 523840 | tf_op jit(solution)/shard_map/all_to_all | solution.py:718
  563.5 4.6 all-to-all-start.7
  570.6 6.9 %widen.1 = f32[4,12,192,256]{3,2,1,0:T(8,128)} custom-call(s32[4]{0:T(128)} %pad_add_fusion.slot, s32[2]{0:T(128)} %pad_add_fusion.1.starts, bf16[192,1536]{1,0:T(8,128)(2,1)} %copy-done.31, bf16[192,1536]{1,0:T(8,128)(2,1)} %copy-done.32, bf16[192,1536]{1,0:T(8,128)(2,1)} %copy-done.33, bf16[192,1536]{1,0:T(8,128)(2,1)} %collective-permute-done.18.refs_3_, ...), custom_call_target="tpu_custom_call" | custom-call | flops 8000000000 | bytes 27200000 | tf_op jit(solution)/shard_map/widen/pallas_call | solution.py:400
  579.0 2.0 collective-permute-start.26
  585.5 3.5 collective-permute-done.28
  592.2 7.4 %finish.2.refs_0_ = f32[4,12,192,256]{3,2,1,0:T(8,128)} custom-call(bf16[8,12,48,256]{3,2,1,0:T(8,128)(2,1)} %all-to-all-done.5.grad, bf16[4,12,192,256]{3,2,1,0:T(8,128)(2,1)} %patches.3, f32[4,12,1,256]{3,2,1,0:T(1,128)} %copy.273.mean, f32[4,12,1,256]{3,2,1,0:T(1,128)} %copy.274.rstd, f32[4,12,1,256]{3,2,1,0:T(1,128)} %get-tuple-element.423.one, ...), custom_call_target="tpu_custom_call" | custom-call | flops 5000000000 | bytes 17000000 | tf_op jit(solution)/shard_map/finish/pallas_call | solution.py:400
  599.6 17.6 %collective-permute-done.26 = bf16[2,2,96,768]{3,2,1,0:T(8,128)(2,1)S(1)} collective-permute-done((bf16[2,2,96,768]{3,2,1,0:T(8,128)(2,1)S(1)}, bf16[2,2,96,768]{3,2,1,0:T(8,128)(2,1)S(1)}, u32[]{:S(2)}, u32[]{:S(2)}) %collective-permute-start.26) | collective-permute-done | bytes 589856 | tf_op jit(solution)/shard_map/ppermute | solution.py:635
  618.6 1.8 all-to-all-done.7.grad
  620.4 2.8 collective-permute-start.29
  623.2 7.3 %finish.3 = f32[4,12,192,256]{3,2,1,0:T(8,128)} custom-call(bf16[8,12,48,256]{3,2,1,0:T(8,128)(2,1)} %all-to-all-done.7.grad, bf16[4,12,192,256]{3,2,1,0:T(8,128)(2,1)} %patches.3, f32[4,12,1,256]{3,2,1,0:T(1,128)} %copy.273.mean, f32[4,12,1,256]{3,2,1,0:T(1,128)} %copy.274.rstd, ...), custom_call_target="tpu_custom_call", output_to_operand_aliasing={{}: (6, {})} | custom-call | flops 99999997952 | bytes 340000000 | tf_op jit(solution)/shard_map/finish/pallas_call | solution.py:400
  630.6 3.3 collective-permute-done.29
  (272 shorter events, 50.0 us)
Async XLA Ops:
  7.2 49.9 %all-gather.8.cloned.1.call-start = ((), (), s32[]{:S(2)}) async-start(), calls=%async_computation.9 | async-start | bytes 5898240 | tf_op jit(solution)/shard_map/all_gather | solution.py:466
  12.6 80.0 %all-gather.6.cloned.1.call-start = ((), (), s32[]{:S(2)}) async-start(), calls=%async_computation.8 | async-start | bytes 5898240 | tf_op jit(solution)/shard_map/all_gather | solution.py:467
  14.2 19.2 %copy-start.17 = (bf16[2,2,96,96]{3,2,1,0:T(8,128)(2,1)S(1)}, bf16[2,2,96,96]{3,2,1,0:T(8,128)(2,1)}, u32[]{:S(2)}) copy-start(bf16[2,2,96,96]{3,2,1,0:T(8,128)(2,1)} %param.33) | copy-start | bytes 221188
  14.2 19.2 %copy-start.18 = (bf16[2,2,96,96]{3,2,1,0:T(8,128)(2,1)S(1)}, bf16[2,2,96,96]{3,2,1,0:T(8,128)(2,1)}, u32[]{:S(2)}) copy-start(bf16[2,2,96,96]{3,2,1,0:T(8,128)(2,1)} %param.31) | copy-start | bytes 221188
  14.3 116.7 %all-to-all-start = ((bf16[8,12,96,256]{3,2,1,0:T(8,128)(2,1)}), bf16[8,12,96,256]{3,2,1,0:T(8,128)(2,1)}, u32[]{:S(2)}, u32[]{:S(2)}) async-start(bf16[8,12,96,256]{3,2,1,0:T(8,128)(2,1)} %bitcast.191), calls=%async_computation | async-start | bytes 9437184 | tf_op jit(solution)/shard_map/all_to_all | solution.py:437
  33.5 8.2 %copy-start.29 = (f32[192]{0:T(256)S(1)}, f32[192]{0:T(256)}, u32[]{:S(2)}) copy-start(f32[192]{0:T(256)} %param.30) | copy-start | bytes 2308
  36.9 15.7 %copy-start.30 = (f32[192]{0:T(256)S(1)}, f32[192]{0:T(256)}, u32[]{:S(2)}) copy-start(f32[192]{0:T(256)} %param.29) | copy-start | bytes 2308
  42.5 14.6 %copy-start.21 = (f32[96]{0:T(128)}, f32[96]{0:T(128)S(1)}, u32[]{:S(2)}) copy-start(f32[96]{0:T(128)S(1)} %get-tuple-element.382) | copy-start | bytes 1156
  57.1 56.5 %copy-start.27 = (f32[2,2,96]{2,1,0:T(2,128)S(1)}, f32[2,2,96]{2,1,0:T(2,128)}, u32[]{:S(2)}) copy-start(f32[2,2,96]{2,1,0:T(2,128)} %param.32) | copy-start | bytes 4612
  57.1 56.5 %copy-start.28 = (f32[2,2,96]{2,1,0:T(2,128)S(1)}, f32[2,2,96]{2,1,0:T(2,128)}, u32[]{:S(2)}) copy-start(f32[2,2,96]{2,1,0:T(2,128)} %param.34) | copy-start | bytes 4612
  96.6 8.9 %collective-permute-start.6 = (f32[12,2,256]{2,1,0:T(2,128)S(1)}, f32[12,2,256]{2,1,0:T(2,128)S(1)}, u32[]{:S(2)}, u32[]{:S(2)}) collective-permute-start(f32[12,2,256]{2,1,0:T(2,128)S(1)} %bitcast.245), channel_id=1, source_target_pairs={{0,4},{4,0},{8,12},{12,8},{16,20},{20,16},{24,28},{28,24},{1,5},{5... | collective-permute-start | bytes 73736 | tf_op jit(solution)/shard_map/ppermute | solution.py:476
  98.4 13.5 %collective-permute-start.4 = (f32[12,2,256]{2,1,0:T(2,128)S(1)}, f32[12,2,256]{2,1,0:T(2,128)S(1)}, u32[]{:S(2)}, u32[]{:S(2)}) collective-permute-start(f32[12,2,256]{2,1,0:T(2,128)S(1)} %bitcast.244), channel_id=1, source_target_pairs={{0,12},{4,8},{8,4},{12,0},{16,28},{20,24},{24,20},{28,16},{1,13},{... | collective-permute-start | bytes 73736 | tf_op jit(solution)/shard_map/ppermute | solution.py:476
  100.8 13.0 %collective-permute-start.5 = (f32[12,2,256]{2,1,0:T(2,128)S(1)}, f32[12,2,256]{2,1,0:T(2,128)S(1)}, u32[]{:S(2)}, u32[]{:S(2)}) collective-permute-start(f32[12,2,256]{2,1,0:T(2,128)S(1)} %bitcast.239), channel_id=1, source_target_pairs={{0,8},{4,12},{8,0},{12,4},{16,24},{20,28},{24,16},{28,20},{1,9},{5... | collective-permute-start | bytes 73736 | tf_op jit(solution)/shard_map/ppermute | solution.py:476
  101.2 28.3 %collective-permute-start.2 = (f32[12,2,256]{2,1,0:T(2,128)S(1)}, f32[12,2,256]{2,1,0:T(2,128)S(1)}, u32[]{:S(2)}, u32[]{:S(2)}) collective-permute-start(f32[12,2,256]{2,1,0:T(2,128)S(1)} %bitcast.240), channel_id=1, source_target_pairs={{0,20},{4,16},{8,28},{12,24},{16,4},{20,0},{24,12},{28,8},{1,21},{... | collective-permute-start | bytes 73736 | tf_op jit(solution)/shard_map/ppermute | solution.py:476
  104.9 24.7 %collective-permute-start.3 = (f32[12,2,256]{2,1,0:T(2,128)S(1)}, f32[12,2,256]{2,1,0:T(2,128)S(1)}, u32[]{:S(2)}, u32[]{:S(2)}) collective-permute-start(f32[12,2,256]{2,1,0:T(2,128)S(1)} %bitcast.241), channel_id=1, source_target_pairs={{0,16},{4,20},{8,24},{12,28},{16,0},{20,4},{24,8},{28,12},{1,17},{... | collective-permute-start | bytes 73736 | tf_op jit(solution)/shard_map/ppermute | solution.py:476
  105.5 24.1 %collective-permute-start = (f32[12,2,256]{2,1,0:T(2,128)S(1)}, f32[12,2,256]{2,1,0:T(2,128)S(1)}, u32[]{:S(2)}, u32[]{:S(2)}) collective-permute-start(f32[12,2,256]{2,1,0:T(2,128)S(1)} %bitcast.243), channel_id=1, source_target_pairs={{0,28},{4,24},{8,20},{12,16},{16,12},{20,8},{24,4},{28,0},{1,29},{... | collective-permute-start | bytes 73736 | tf_op jit(solution)/shard_map/ppermute | solution.py:476
  111.9 17.7 %collective-permute-start.1 = (f32[12,2,256]{2,1,0:T(2,128)S(1)}, f32[12,2,256]{2,1,0:T(2,128)S(1)}, u32[]{:S(2)}, u32[]{:S(2)}) collective-permute-start(f32[12,2,256]{2,1,0:T(2,128)S(1)} %bitcast.242), channel_id=1, source_target_pairs={{0,24},{4,28},{8,16},{12,20},{16,8},{20,12},{24,0},{28,4},{1,25},{... | collective-permute-start | bytes 73736 | tf_op jit(solution)/shard_map/ppermute | solution.py:476
  131.0 57.9 %collective-permute-start.7 = (bf16[6,192,256]{2,1,0:T(8,128)(2,1)}, bf16[6,192,256]{2,1,0:T(8,128)(2,1)}, u32[]{:S(2)}, u32[]{:S(2)}) collective-permute-start(bf16[6,192,256]{2,1,0:T(8,128)(2,1)} %get-tuple-element.176), channel_id=1, source_target_pairs={{0,0},{1,16},{2,8},{3,24},{4,4},{5,20},{6,12},{7,28},{8,2},{9,18},... | collective-permute-start | bytes 1769480 | tf_op jit(solution)/shard_map/ppermute | solution.py:508
  133.9 55.0 %collective-permute-start.8 = (bf16[6,192,256]{2,1,0:T(8,128)(2,1)}, bf16[6,192,256]{2,1,0:T(8,128)(2,1)}, u32[]{:S(2)}, u32[]{:S(2)}) collective-permute-start(bf16[6,192,256]{2,1,0:T(8,128)(2,1)} %get-tuple-element.177), channel_id=1, source_target_pairs={{0,8},{1,24},{2,16},{3,0},{4,12},{5,28},{6,20},{7,4},{8,10},{9,26}... | collective-permute-start | bytes 1769480 | tf_op jit(solution)/shard_map/ppermute | solution.py:508
  134.0 54.9 %collective-permute-start.9 = (bf16[6,192,256]{2,1,0:T(8,128)(2,1)}, bf16[6,192,256]{2,1,0:T(8,128)(2,1)}, u32[]{:S(2)}, u32[]{:S(2)}) collective-permute-start(bf16[6,192,256]{2,1,0:T(8,128)(2,1)} %get-tuple-element.178), channel_id=1, source_target_pairs={{0,16},{1,0},{2,24},{3,8},{4,20},{5,4},{6,28},{7,12},{8,18},{9,2},... | collective-permute-start | bytes 1769480 | tf_op jit(solution)/shard_map/ppermute | solution.py:508
  137.3 51.7 %collective-permute-start.10 = (bf16[6,192,256]{2,1,0:T(8,128)(2,1)}, bf16[6,192,256]{2,1,0:T(8,128)(2,1)}, u32[]{:S(2)}, u32[]{:S(2)}) collective-permute-start(bf16[6,192,256]{2,1,0:T(8,128)(2,1)} %get-tuple-element.179), channel_id=1, source_target_pairs={{0,24},{1,8},{2,0},{3,16},{4,28},{5,12},{6,4},{7,20},{8,26},{9,10}... | collective-permute-start | bytes 1769480 | tf_op jit(solution)/shard_map/ppermute | solution.py:508
  188.9 33.8 %all-to-all-start.1 = ((bf16[8,6,96,256]{3,2,1,0:T(8,128)(2,1)}), bf16[8,6,96,256]{3,2,1,0:T(8,128)(2,1)}, u32[]{:S(2)}, u32[]{:S(2)}) async-start(bf16[8,6,96,256]{3,2,1,0:T(8,128)(2,1)} %get-tuple-element.184), calls=%async_computation.1 | async-start | bytes 4718592 | tf_op jit(solution)/shard_map/all_to_all | solution.py:559
  222.8 56.8 %all-to-all-start.2 = ((bf16[8,6,96,256]{3,2,1,0:T(8,128)(2,1)}), bf16[8,6,96,256]{3,2,1,0:T(8,128)(2,1)}, u32[]{:S(2)}, u32[]{:S(2)}) async-start(bf16[8,6,96,256]{3,2,1,0:T(8,128)(2,1)} %get-tuple-element.193), calls=%async_computation.2 | async-start | bytes 4718592 | tf_op jit(solution)/shard_map/all_to_all | solution.py:559
  228.1 58.7 %collective-permute-start.11 = (bf16[6,192,256]{2,1,0:T(8,128)(2,1)}, bf16[6,192,256]{2,1,0:T(8,128)(2,1)}, u32[]{:S(2)}, u32[]{:S(2)}) collective-permute-start(bf16[6,192,256]{2,1,0:T(8,128)(2,1)} %get-tuple-element.189), channel_id=1, source_target_pairs={{0,2},{1,18},{2,10},{3,26},{4,6},{5,22},{6,14},{7,30},{8,0},{9,16}... | collective-permute-start | bytes 1769480 | tf_op jit(solution)/shard_map/ppermute | solution.py:571
  228.7 58.1 %collective-permute-start.12 = (bf16[6,192,256]{2,1,0:T(8,128)(2,1)S(1)}, bf16[6,192,256]{2,1,0:T(8,128)(2,1)}, u32[]{:S(2)}, u32[]{:S(2)}) collective-permute-start(bf16[6,192,256]{2,1,0:T(8,128)(2,1)S(1)} %get-tuple-element.190), channel_id=1, source_target_pairs={{0,10},{1,26},{2,18},{3,2},{4,14},{5,30},{6,22},{7,6},{8,8},{9,24}... | collective-permute-start | bytes 1769480 | tf_op jit(solution)/shard_map/ppermute | solution.py:571
  233.3 53.5 %collective-permute-start.13 = (bf16[6,192,256]{2,1,0:T(8,128)(2,1)S(1)}, bf16[6,192,256]{2,1,0:T(8,128)(2,1)}, u32[]{:S(2)}, u32[]{:S(2)}) collective-permute-start(bf16[6,192,256]{2,1,0:T(8,128)(2,1)S(1)} %get-tuple-element.191), channel_id=1, source_target_pairs={{0,18},{1,2},{2,26},{3,10},{4,22},{5,6},{6,30},{7,14},{8,16},{9,0}... | collective-permute-start | bytes 1769480 | tf_op jit(solution)/shard_map/ppermute | solution.py:571
  235.8 51.0 %collective-permute-start.14 = (bf16[6,192,256]{2,1,0:T(8,128)(2,1)S(1)}, bf16[6,192,256]{2,1,0:T(8,128)(2,1)}, u32[]{:S(2)}, u32[]{:S(2)}) collective-permute-start(bf16[6,192,256]{2,1,0:T(8,128)(2,1)S(1)} %get-tuple-element.192), channel_id=1, source_target_pairs={{0,26},{1,10},{2,2},{3,18},{4,30},{5,14},{6,6},{7,22},{8,24},{9,8}... | collective-permute-start | bytes 1769480 | tf_op jit(solution)/shard_map/ppermute | solution.py:571
  279.6 43.0 %all-to-all-start.3 = ((bf16[8,6,96,256]{3,2,1,0:T(8,128)(2,1)}), bf16[8,6,96,256]{3,2,1,0:T(8,128)(2,1)}, u32[]{:S(2)}, u32[]{:S(2)}) async-start(bf16[8,6,96,256]{3,2,1,0:T(8,128)(2,1)} %get-tuple-element.214), calls=%async_computation.3 | async-start | bytes 4718592 | tf_op jit(solution)/shard_map/all_to_all | solution.py:559
  322.5 85.1 %all-to-all-start.4 = ((bf16[8,6,96,256]{3,2,1,0:T(8,128)(2,1)}), bf16[8,6,96,256]{3,2,1,0:T(8,128)(2,1)}, u32[]{:S(2)}, u32[]{:S(2)}) async-start(bf16[8,6,96,256]{3,2,1,0:T(8,128)(2,1)} %get-tuple-element.216), calls=%async_computation.4 | async-start | bytes 4718592 | tf_op jit(solution)/shard_map/all_to_all | solution.py:559
  352.0 50.3 %collective-permute-start.15 = (bf16[192,1536]{1,0:T(8,128)(2,1)}, bf16[192,1536]{1,0:T(8,128)(2,1)S(1)}, u32[]{:S(2)}, u32[]{:S(2)}) collective-permute-start(bf16[192,1536]{1,0:T(8,128)(2,1)} %get-tuple-element.235), channel_id=1, source_target_pairs={{0,0},{16,1},{8,2},{24,3},{4,4},{20,5},{12,6},{28,7},{2,8},{18,9},... | collective-permute-start | bytes 1769480 | tf_op jit(solution)/shard_map/ppermute | solution.py:606
  353.9 48.4 %collective-permute-start.16 = (bf16[192,1536]{1,0:T(8,128)(2,1)}, bf16[192,1536]{1,0:T(8,128)(2,1)S(1)}, u32[]{:S(2)}, u32[]{:S(2)}) collective-permute-start(bf16[192,1536]{1,0:T(8,128)(2,1)} %get-tuple-element.236), channel_id=1, source_target_pairs={{2,0},{18,1},{10,2},{26,3},{6,4},{22,5},{14,6},{30,7},{0,8},{16,9}... | collective-permute-start | bytes 1769480 | tf_op jit(solution)/shard_map/ppermute | solution.py:606
  354.0 48.8 %collective-permute-start.17 = (bf16[192,1536]{1,0:T(8,128)(2,1)}, bf16[192,1536]{1,0:T(8,128)(2,1)S(1)}, u32[]{:S(2)}, u32[]{:S(2)}) collective-permute-start(bf16[192,1536]{1,0:T(8,128)(2,1)} %get-tuple-element.237), channel_id=1, source_target_pairs={{8,0},{24,1},{16,2},{0,3},{12,4},{28,5},{20,6},{4,7},{10,8},{26,9}... | collective-permute-start | bytes 1769480 | tf_op jit(solution)/shard_map/ppermute | solution.py:606
  357.5 50.1 %collective-permute-start.18 = (bf16[192,1536]{1,0:T(8,128)(2,1)}, bf16[192,1536]{1,0:T(8,128)(2,1)}, u32[]{:S(2)}, u32[]{:S(2)}) collective-permute-start(bf16[192,1536]{1,0:T(8,128)(2,1)} %get-tuple-element.238), channel_id=1, source_target_pairs={{10,0},{26,1},{18,2},{2,3},{14,4},{30,5},{22,6},{6,7},{8,8},{24,9}... | collective-permute-start | bytes 1769480 | tf_op jit(solution)/shard_map/ppermute | solution.py:606
  402.3 24.7 %copy-start.31 = (bf16[192,1536]{1,0:T(8,128)(2,1)}, bf16[192,1536]{1,0:T(8,128)(2,1)S(1)}, u32[]{:S(2)}) copy-start(bf16[192,1536]{1,0:T(8,128)(2,1)S(1)} %collective-permute-done.15.refs_0_) | copy-start | bytes 1769476
  402.3 24.7 %copy-start.32 = (bf16[192,1536]{1,0:T(8,128)(2,1)}, bf16[192,1536]{1,0:T(8,128)(2,1)S(1)}, u32[]{:S(2)}) copy-start(bf16[192,1536]{1,0:T(8,128)(2,1)S(1)} %collective-permute-done.16.refs_1_) | copy-start | bytes 1769476
  402.7 24.3 %copy-start.33 = (bf16[192,1536]{1,0:T(8,128)(2,1)}, bf16[192,1536]{1,0:T(8,128)(2,1)S(1)}, u32[]{:S(2)}) copy-start(bf16[192,1536]{1,0:T(8,128)(2,1)S(1)} %collective-permute-done.17.refs_2_) | copy-start | bytes 1769476
  407.6 19.4 %collective-permute-start.19 = (bf16[2,2,768,768]{3,2,1,0:T(8,128)(2,1)}, bf16[2,2,768,768]{3,2,1,0:T(8,128)(2,1)}, u32[]{:S(2)}, u32[]{:S(2)}) collective-permute-start(bf16[2,2,768,768]{3,2,1,0:T(8,128)(2,1)} %get-tuple-element.244), channel_id=1, source_target_pairs={{0,1},{1,0},{2,3},{3,2},{4,5},{5,4},{6,7},{7,6},{8,9},{9,8},{10,11... | collective-permute-start | bytes 14155784 | tf_op jit(solution)/shard_map/ppermute | solution.py:626
  407.7 28.7 %collective-permute-start.20 = (bf16[192,1536]{1,0:T(8,128)(2,1)}, bf16[192,1536]{1,0:T(8,128)(2,1)}, u32[]{:S(2)}, u32[]{:S(2)}) collective-permute-start(bf16[192,1536]{1,0:T(8,128)(2,1)} %get-tuple-element.254), channel_id=1, source_target_pairs={{16,0},{0,1},{24,2},{8,3},{20,4},{4,5},{28,6},{12,7},{18,8},{2,9},... | collective-permute-start | bytes 1769480 | tf_op jit(solution)/shard_map/ppermute | solution.py:606
  409.3 27.0 %collective-permute-start.21 = (bf16[192,1536]{1,0:T(8,128)(2,1)}, bf16[192,1536]{1,0:T(8,128)(2,1)}, u32[]{:S(2)}, u32[]{:S(2)}) collective-permute-start(bf16[192,1536]{1,0:T(8,128)(2,1)} %get-tuple-element.255), channel_id=1, source_target_pairs={{18,0},{2,1},{26,2},{10,3},{22,4},{6,5},{30,6},{14,7},{16,8},{0,9}... | collective-permute-start | bytes 1769480 | tf_op jit(solution)/shard_map/ppermute | solution.py:606
  427.0 13.2 %copy-start.36 = (bf16[192,1536]{1,0:T(8,128)(2,1)S(1)}, bf16[192,1536]{1,0:T(8,128)(2,1)}, u32[]{:S(2)}) copy-start(bf16[192,1536]{1,0:T(8,128)(2,1)} %get-tuple-element.270) | copy-start | bytes 1769476
  436.3 26.0 %collective-permute-start.22 = (bf16[192,1536]{1,0:T(8,128)(2,1)}, bf16[192,1536]{1,0:T(8,128)(2,1)S(1)}, u32[]{:S(2)}, u32[]{:S(2)}) collective-permute-start(bf16[192,1536]{1,0:T(8,128)(2,1)} %get-tuple-element.269), channel_id=1, source_target_pairs={{24,0},{8,1},{0,2},{16,3},{28,4},{12,5},{4,6},{20,7},{26,8},{10,9}... | collective-permute-start | bytes 1769480 | tf_op jit(solution)/shard_map/ppermute | solution.py:606
  440.3 22.1 %collective-permute-start.23 = (bf16[192,1536]{1,0:T(8,128)(2,1)S(1)}, bf16[192,1536]{1,0:T(8,128)(2,1)S(1)}, u32[]{:S(2)}, u32[]{:S(2)}) collective-permute-start(bf16[192,1536]{1,0:T(8,128)(2,1)S(1)} %copy-done.36), channel_id=1, source_target_pairs={{26,0},{10,1},{2,2},{18,3},{30,4},{14,5},{6,6},{22,7},{24,8},{8,9}... | collective-permute-start | bytes 1769480 | tf_op jit(solution)/shard_map/ppermute | solution.py:606
  441.1 67.6 %collective-permute-start.24 = (bf16[2,2,4,96,768]{4,3,2,1,0:T(8,128)(2,1)}, bf16[2,2,4,96,768]{4,3,2,1,0:T(8,128)(2,1)}, u32[]{:S(2)}, u32[]{:S(2)}) collective-permute-start(bf16[2,2,4,96,768]{4,3,2,1,0:T(8,128)(2,1)} %get-tuple-element.273), channel_id=1, source_target_pairs={{0,4},{4,0},{8,12},{12,8},{16,20},{20,16},{24,28},{28,24},{1,5},{5... | collective-permute-start | bytes 7077896 | tf_op jit(solution)/shard_map/ppermute | solution.py:635
  473.8 7.3 %copy-start.8 = (f32[768,128]{1,0:T(8,128)S(1)}, f32[768,128]{1,0:T(8,128)}, u32[]{:S(2)}) copy-start(f32[768,128]{1,0:T(8,128)} %get-tuple-element.305) | copy-start | bytes 1179652
  473.8 7.5 %copy-start.7 = (f32[768,128]{1,0:T(8,128)S(1)}, f32[768,128]{1,0:T(8,128)}, u32[]{:S(2)}) copy-start(f32[768,128]{1,0:T(8,128)} %get-tuple-element.307) | copy-start | bytes 1179652
  473.8 7.5 %copy-start.9 = (f32[768,128]{1,0:T(8,128)S(1)}, f32[768,128]{1,0:T(8,128)}, u32[]{:S(2)}) copy-start(f32[768,128]{1,0:T(8,128)} %get-tuple-element.308) | copy-start | bytes 1179652
  473.8 7.7 %copy-start.11 = (f32[768,128]{1,0:T(8,128)S(1)}, f32[768,128]{1,0:T(8,128)}, u32[]{:S(2)}) copy-start(f32[768,128]{1,0:T(8,128)} %get-tuple-element.309) | copy-start | bytes 1179652
  473.8 7.9 %copy-start.1 = (f32[3072,128]{1,0:T(8,128)S(1)}, f32[3072,128]{1,0:T(8,128)}, u32[]{:S(2)}) copy-start(f32[3072,128]{1,0:T(8,128)} %get-tuple-element.310) | copy-start | bytes 4718596
  473.8 69.9 %all-to-all-start.5 = ((bf16[8,12,48,256]{3,2,1,0:T(8,128)(2,1)}), bf16[8,12,48,256]{3,2,1,0:T(8,128)(2,1)}, u32[]{:S(2)}, u32[]{:S(2)}) async-start(bf16[8,12,48,256]{3,2,1,0:T(8,128)(2,1)} %bitcast.200), calls=%async_computation.5 | async-start | bytes 4718592 | tf_op jit(solution)/shard_map/all_to_all | solution.py:690
  484.7 33.0 %copy-start.14 = (f32[192,128]{1,0:T(8,128)S(1)}, f32[192,128]{1,0:T(8,128)}, u32[]{:S(2)}) copy-start(f32[192,128]{1,0:T(8,128)} %get-tuple-element.300) | copy-start | bytes 294916
  484.7 33.3 %copy-start.13 = (f32[192,128]{1,0:T(8,128)S(1)}, f32[192,128]{1,0:T(8,128)}, u32[]{:S(2)}) copy-start(f32[192,128]{1,0:T(8,128)} %get-tuple-element.298) | copy-start | bytes 294916
  514.6 29.1 %collective-permute-start.25 = (bf16[2,4,96,768]{3,2,1,0:T(8,128)(2,1)S(1)}, bf16[2,4,96,768]{3,2,1,0:T(8,128)(2,1)}, u32[]{:S(2)}, u32[]{:S(2)}) collective-permute-start(bf16[2,4,96,768]{3,2,1,0:T(8,128)(2,1)S(1)} %fusion.4), channel_id=1, source_target_pairs={{0,2},{1,3},{2,0},{3,1},{4,6},{5,7},{6,4},{7,5},{8,10},{9,11},{10,... | collective-permute-start | bytes 3538952 | tf_op jit(solution)/shard_map/ppermute | solution.py:635
  519.0 10.6 %copy-start.16 = (f32[48,128]{1,0:T(8,128)S(1)}, f32[48,128]{1,0:T(8,128)}, u32[]{:S(2)}) copy-start(f32[48,128]{1,0:T(8,128)} %get-tuple-element.301) | copy-start | bytes 73732
  519.0 11.4 %copy-start.15 = (f32[48,128]{1,0:T(8,128)S(1)}, f32[48,128]{1,0:T(8,128)}, u32[]{:S(2)}) copy-start(f32[48,128]{1,0:T(8,128)} %get-tuple-element.303) | copy-start | bytes 73732
  519.0 12.3 %copy-start.22 = (f32[96]{0:T(128)S(1)}, f32[96]{0:T(128)}, u32[]{:S(2)}) copy-start(f32[96]{0:T(128)} %copy-done.21) | copy-start | bytes 1156
  519.1 12.4 %copy-start.12 = (f32[96,2,256]{2,1,0:T(2,128)S(1)}, f32[96,2,256]{2,1,0:T(2,128)}, u32[]{:S(2)}) copy-start(f32[96,2,256]{2,1,0:T(2,128)} %get-tuple-element.276) | copy-start | bytes 589828
  545.2 18.0 %all-to-all-start.6 = ((f32[8,1,16369]{2,1,0:T(1,128)}), f32[8,1,16369]{2,1,0:T(1,128)S(1)}, u32[]{:S(2)}, u32[]{:S(2)}) async-start(f32[8,1,16369]{2,1,0:T(1,128)} %all_to_all.35), calls=%async_computation.6 | async-start | bytes 1048576 | tf_op jit(solution)/shard_map/all_to_all | solution.py:718
  549.8 18.8 %copy-start.6 = (f32[4,12,1,256]{3,0,1,2:T(4,128)S(1)}, f32[4,12,1,256]{3,0,1,2:T(4,128)}, u32[]{:S(2)}) copy-start(f32[4,12,1,256]{3,0,1,2:T(4,128)} %copy-done.5) | copy-start | bytes 147460
  549.8 19.5 %copy-start.4 = (f32[4,12,1,256]{3,0,1,2:T(4,128)S(1)}, f32[4,12,1,256]{3,0,1,2:T(4,128)}, u32[]{:S(2)}) copy-start(f32[4,12,1,256]{3,0,1,2:T(4,128)} %copy-done.3) | copy-start | bytes 147460
  563.5 56.9 %all-to-all-start.7 = ((bf16[8,12,48,256]{3,2,1,0:T(8,128)(2,1)}), bf16[8,12,48,256]{3,2,1,0:T(8,128)(2,1)}, u32[]{:S(2)}, u32[]{:S(2)}) async-start(bf16[8,12,48,256]{3,2,1,0:T(8,128)(2,1)} %bitcast.69), calls=%async_computation.7 | async-start | bytes 4718592 | tf_op jit(solution)/shard_map/all_to_all | solution.py:727
  579.0 38.2 %collective-permute-start.26 = (bf16[2,2,96,768]{3,2,1,0:T(8,128)(2,1)S(1)}, bf16[2,2,96,768]{3,2,1,0:T(8,128)(2,1)S(1)}, u32[]{:S(2)}, u32[]{:S(2)}) collective-permute-start(bf16[2,2,96,768]{3,2,1,0:T(8,128)(2,1)S(1)} %fusion.5), channel_id=1, source_target_pairs={{0,8},{8,0},{16,24},{24,16},{1,9},{9,1},{17,25},{25,17},{2,10},{10... | collective-permute-start | bytes 1769480 | tf_op jit(solution)/shard_map/ppermute | solution.py:635
  581.9 1.4 collective-permute-start.27
  583.3 5.7 collective-permute-start.28
  620.4 13.5 %collective-permute-start.29 = (bf16[1,2,96,768]{3,2,1,0:T(8,128)(2,1)S(1)}, bf16[1,2,96,768]{3,2,1,0:T(8,128)(2,1)S(1)}, u32[]{:S(2)}, u32[]{:S(2)}) collective-permute-start(bf16[1,2,96,768]{3,2,1,0:T(8,128)(2,1)S(1)} %dynamic-slice_convert_fusion), channel_id=1, source_target_pairs={{0,16},{8,24},{16,0},{24,8},{1,17},{9,25},{17,1},{25,9},{2,18},{10... | collective-permute-start | bytes 884744 | tf_op jit(solution)/shard_map/ppermute | solution.py:635
  (14 other events, 61.6 us)
Sparse Core Ops, SparseCore 0:
  12.8 40.1 all-gather.7
  55.1 37.4 all-gather.5

commit v8 on v7

--- a/solution.py
+++ b/solution.py
@@ -127,7 +127,7 @@
         total = total + dot(parts[1], table_hi)
     total = total + dot(parts[0], table_hi)
     for c in range(2):
-        lons[c] = total[:, c * modes : (c + 1) * modes]
+        lons[c, : rows * feats] = total[:, c * modes : (c + 1) * modes]
     for f in range(0, feats, 2):
         pair = []
         for g in (f, f + 1):
@@ -148,7 +148,7 @@
             for c in range(2):
                 lons[c, pl.ds(g, rows, stride=feats), :] = out[c * rows : (c + 1) * rows, i * modes : (i + 1) * modes]
     table_hi, table_lo = table
-    value = jnp.concatenate([lons[0], lons[1]], axis=1).astype(BF)
+    value = jnp.concatenate([lons[c, : rows * feats] for c in range(2)], axis=1).astype(BF)
     return dot(value, table_hi) + dot(value, table_lo)
 
 
@@ -157,7 +157,7 @@
     rows, feats, width = mixed.shape
     parts = split(mixed.reshape(rows * feats, width))
     plane_forward(parts, (hi[...], lo[...]), lat[...], lons, spectra)
-    spec[...] = spectra[...].reshape(spec.shape).astype(BF)
+    spec[...] = spectra[: math.prod(spec.shape[:3])].reshape(spec.shape).astype(BF)
 
 
 def join_lines(parts):
@@ -174,7 +174,7 @@
     else:
         value = value.reshape(rows * feats, width)
     plane_forward((value,), (hi[...], lo[...]), lat[...], lons, spectra)
-    freq[...] = spectra[...].reshape(freq.shape).astype(BF)
+    freq[...] = spectra[: math.prod(freq.shape[:3])].reshape(freq.shape).astype(BF)
 
 
 def two_modes(ref, ky):
@@ -226,7 +226,7 @@
 
 def section_kernel(order, pieces, mean, rstd, scale, shift, kept, hi, lo, lat, *refs):
     outs, (lons, spectra) = refs[:-2], refs[-2:]
-    spectra[...] = kept[...].astype(F32).reshape(spectra.shape)
+    spectra[: math.prod(kept.shape[:3])] = kept[...].astype(F32).reshape(-1, kept.shape[3])
     value = collect(pieces, order)
     mixed = (value - mean[...]) * rstd[...] * scale[...] + shift[...]
     spectral = plane_inverse((hi[...], lo[...]), lat[...], lons, spectra)
@@ -240,7 +240,7 @@
 
 def last_kernel(order, n, pieces, *refs):
     sgrad, (mean, rstd, scale, freq, hi, lo, lat, out, sums, gain_sum, shift_sum, lons, spectra) = refs[:n], refs[n:]
-    spectra[...] = freq[...].astype(F32).reshape(spectra.shape)
+    spectra[: math.prod(freq.shape[:3])] = freq[...].astype(F32).reshape(-1, freq.shape[3])
     normed = (collect(pieces, order) - mean[...]) * rstd[...]
     grad = join_lines(sgrad).astype(F32)
     mixed = grad + plane_inverse((hi[...], lo[...]), lat[...], lons, spectra).reshape(grad.shape)
@@ -516,8 +516,8 @@
     image_spec = pl.BlockSpec((rows, some, width), lambda g, *_: (0, g, 0))
     modes_spec = pl.BlockSpec((2, rows, some, modes), lambda g, *_: (0, 0, g, 0))
     scratch = [
-        pltpu.VMEM((2, rows * some, modes), F32),
-        pltpu.VMEM((2 * rows * some, modes), F32),
+        pltpu.VMEM((2, (rows + 1) * some, modes), F32),
+        pltpu.VMEM(((2 * rows + 1) * some, modes), F32),
     ]
     mine_modes = (2, rows, mine, modes)
     spec = run(
@@ -535,7 +535,7 @@
 
     spec = to_blocks(spec)
     lats = rows // cut
-    step = 8
+    step = 16 if lats % 16 == 0 else 8
     block_modes = (2, lats, BLOCK, modes)
     block_spec = pl.BlockSpec((2, step, BLOCK, modes), lambda g: (0, g, 0, 0))
     square_spec, lane_spec = whole((2 * BLOCK, 2 * BLOCK)), whole((2 * BLOCK, 2 * modes))

time: 655 us -> 652 us (level)
  no operation moved by 1% of the time
where the time goes in v8:
time: 652 us; the launch traced here: 640 us
  Pallas kernels  268 us (41%)
  waiting for transfers between devices  147 us (23%)
  starting transfers between devices  104 us (16%)
  local copies, waits for them, and re-layouts  52.7 us (8%)
  other arithmetic  29.6 us (5%)
  blocking collectives  20.2 us (3%)
  between operations  18.5 us (3%)
    pallas_call x15, Pallas kernels, run(): return call(*scalars, *ins)  268 us
    ppermute x6, waiting for transfers between devices, trade(): return lax.ppermute(theirs, axes, [(a, a ^ bit) for a in range(size)])  58.5 us
    all_gather x1, waiting for transfers between devices, per_device(): wp = lax.all_gather(project_weight, 't', tiled=True)  28.7 us
    all_to_all x4, waiting for transfers between devices, exchange(): return lax.all_to_all(array, ('t', 'y', 'j'), 0, 0, tiled=True)  27.6 us
    all_to_all x4, starting transfers between devices, exchange(): return lax.all_to_all(array, ('t', 'y', 'j'), 0, 0, tiled=True)  22.5 us
    ppermute x8, starting transfers between devices, send_results(): lax.ppermute(rows_out[2 * k + part], every, route(k, part, True))  15.8 us
    ppermute x7, waiting for transfers between devices, per_device(): lax.ppermute(piece, sp, [(a, a ^ k) for a in range(owners)])  15.7 us
    ppermute x7, starting transfers between devices, per_device(): lax.ppermute(piece, sp, [(a, a ^ k) for a in range(owners)])  15.3 us
  transfers between devices with their start and end apart: 40, of which 14 were waited for; matrix products, arithmetic and copies ran while one was open for 11% of the time, Pallas kernels for 42%

profile of v8, /device:TPU:2, one launch (start us, length us, event | category | flops | bytes accessed | tf_op | source)
XLA Modules:
  0.0 640.0 jit_solution(14304219466432515267)
XLA Ops:
  7.2 2.8 fusion.16
  10.0 2.6 pad_maximum_fusion
  14.3 6.0 all-to-all-start
  21.9 11.5 %all-reduce = f32[5376]{0:T(1024)S(1)} all-reduce(f32[5376]{0:T(1024)S(1)} %dynamic-update-slice), channel_id=4, replica_groups=mesh['z'=4,'y'=2,'j'=1,'t'=4] {'t'}, use_global_device_ids=true, to_apply=%add | all-reduce | flops 5376 | bytes 43008
  33.5 3.3 convert_reduce_fusion
  36.9 4.2 fusion.1
  43.4 8.8 %all-gather = f32[8,4,12,256]{3,1,2,0:T(4,128)S(1)} all-gather(f32[2,4,12,256]{3,1,2,0:T(4,128)S(1)} %copy.239), channel_id=2, replica_groups=mesh['z'=4,'y'=2,'j'=1,'t'=4] {'t'}, dimensions={0}, use_global_device_ids=true | all-gather | bytes 491520 | tf_op jit(solution)/shard_map/all_gather | solution.py:456
  53.1 4.0 dynamic-slice_bitcast_fusion
  57.2 6.7 %copy.245 = bf16[4,768,768]{2,1,0:T(8,128)(2,1)} copy(bf16[4,768,768]{1,2,0:T(8,128)(2,1)} %bitcast.195) | data formatting | bytes 9437184 | tf_op jit(solution)/shard_map/transpose | solution.py:468
  63.9 28.7 %all-gather.6.cloned.1.call-done = bf16[3072,768]{0,1:T(8,128)(2,1)} async-done(((bf16[768,768]{0,1:T(8,128)(2,1)}), bf16[3072,768]{0,1:T(8,128)(2,1)}) %all-gather.6.cloned.1.call-update) | async-done | bytes 4718608 | tf_op jit(solution)/shard_map/all_gather | solution.py:467
  94.7 1.7 broadcast_in_dim.70.refs_8_
  96.6 1.8 collective-permute-start.6
  101.2 3.6 collective-permute-start.2
  105.5 6.4 collective-permute-start
  113.9 15.7 %collective-permute-done.2 = f32[12,2,256]{2,1,0:T(2,128)S(1)} collective-permute-done((f32[12,2,256]{2,1,0:T(2,128)S(1)}, f32[12,2,256]{2,1,0:T(2,128)S(1)}, u32[]{:S(2)}, u32[]{:S(2)}) %collective-permute-start.2) | collective-permute-done | bytes 24608 | tf_op jit(solution)/shard_map/ppermute | solution.py:476
  131.0 2.9 collective-permute-start.7
  134.0 3.3 collective-permute-start.9
  139.4 20.2 %spectrum.1.spec = bf16[2,96,96,128]{3,2,1,0:T(8,128)(2,1)} custom-call(bf16[8,12,96,256]{3,2,1,0:T(8,128)(2,1)} %all-to-all-done.pieces, f32[96,1,256]{2,1,0:T(1,128)} %get-tuple-element.416.mean.refs_2_, f32[96,1,256]{2,1,0:T(1,128)} %get-tuple-element.415.rstd.refs_3_, f32[96,256]{1,0:T(8,128)} %broadcast_in_dim.71.scale.refs_4_, ...), custom_call_target="tpu_custom_call" | custom-call | flops 22000001024 | bytes 74800000 | tf_op jit(solution)/shard_map/spectrum/pallas_call | solution.py:400
  161.2 12.2 %filter.1 = (bf16[2,96,96,128]{3,2,1,0:T(8,128)(2,1)}, bf16[2,96,96,128]{3,2,1,0:T(8,128)(2,1)}, bf16[2,96,96,128]{3,2,1,0:T(8,128)(2,1)}, bf16[2,96,96,128]{3,2,1,0:T(8,128)(2,1)}, f32[8,256]{1,0:T(8,128)}) custom-call(bf16[2,96,96,128]{3,2,1,0:T(8,128)(2,1)} %spectrum.1.spec, bf16[192,192]{1,0:T(8,128)(2,1)} %maximum_maximum_fusion.w1, ...), custom_call_target="tpu_custom_call" | custom-call | flops 16999999488 | bytes 57800000 | tf_op jit(solution)/shard_map/filter/pallas_call | solution.py:400
  173.4 13.4 %section.1 = (bf16[8,6,96,256]{3,2,1,0:T(8,128)(2,1)}, bf16[8,6,96,256]{3,2,1,0:T(8,128)(2,1)}) custom-call(bf16[8,12,96,256]{3,2,1,0:T(8,128)(2,1)} %all-to-all-done.pieces, f32[96,1,256]{2,1,0:T(1,128)} %get-tuple-element.416.mean.refs_2_, f32[96,1,256]{2,1,0:T(1,128)} %get-tuple-element.415.rstd.refs_3_, f32[96,256]{1,0:T(8,128)} %broadcast_in_dim.71.scale.refs_4_, ...), custom_call_target="tpu_custom_call" | custom-call | flops 16999999488 | bytes 57800000 | tf_op jit(solution)/shard_map/section/pallas_call | solution.py:400
  186.8 5.8 all-to-all-start.1
  193.3 6.6 %copy.257.refs_6_ = bf16[3072,768]{1,0:T(8,128)(2,1)} copy(bf16[3072,768]{0,1:T(8,128)(2,1)} %all-gather.6.cloned.1.call-done) | data formatting | bytes 9437184 | tf_op jit(solution)/shard_map/optimization_barrier | solution.py:470
  199.9 20.8 %all-to-all-done.1.refs_4_.refs_0_ = bf16[8,6,96,256]{3,2,1,0:T(8,128)(2,1)} async-done(((bf16[8,6,96,256]{3,2,1,0:T(8,128)(2,1)}), bf16[8,6,96,256]{3,2,1,0:T(8,128)(2,1)}, u32[]{:S(2)}, u32[]{:S(2)}) %all-to-all-start.1) | async-done | bytes 2359328 | tf_op jit(solution)/shard_map/all_to_all | solution.py:559
  220.6 5.3 all-to-all-start.2
  226.6 4.6 collective-permute-start.12
  231.2 2.5 collective-permute-start.13
  235.1 35.5 %feed.2 = (bf16[768,3072]{1,0:T(8,128)(2,1)}, bf16[3072,3072]{1,0:T(8,128)(2,1)}, bf16[3072,3072]{1,0:T(8,128)(2,1)}, bf16[768,3072]{1,0:T(8,128)(2,1)}, bf16[8,...) custom-call(s32[4]{0:T(128)} %pad_add_fusion.2.place, ...), custom_call_target="tpu_custom_call" | custom-call | flops 43000000512 | bytes 146200000 | tf_op jit(solution)/shard_map/feed/pallas_call | solution.py:400
  270.6 6.8 %all-to-all-done.2.refs_4_.refs_1_ = bf16[8,6,96,256]{3,2,1,0:T(8,128)(2,1)} async-done(((bf16[8,6,96,256]{3,2,1,0:T(8,128)(2,1)}), bf16[8,6,96,256]{3,2,1,0:T(8,128)(2,1)}, u32[]{:S(2)}, u32[]{:S(2)}) %all-to-all-start.2) | async-done | bytes 2359328 | tf_op jit(solution)/shard_map/all_to_all | solution.py:559
  277.4 7.0 %all-to-all-start.3 = ((bf16[8,6,96,256]{3,2,1,0:T(8,128)(2,1)}), bf16[8,6,96,256]{3,2,1,0:T(8,128)(2,1)}, u32[]{:S(2)}, u32[]{:S(2)}) async-start(bf16[8,6,96,256]{3,2,1,0:T(8,128)(2,1)} %get-tuple-element.214), calls=%async_computation.3 | async-start | bytes 4718592 | tf_op jit(solution)/shard_map/all_to_all | solution.py:559
  284.4 35.7 %feed.3 = (bf16[768,3072]{1,0:T(8,128)(2,1)}, bf16[3072,3072]{1,0:T(8,128)(2,1)}, bf16[3072,3072]{1,0:T(8,128)(2,1)}, bf16[768,3072]{1,0:T(8,128)(2,1)}, bf16[8,...) custom-call(s32[4]{0:T(128)} %pad_add_fusion.2.place, ...), custom_call_target="tpu_custom_call", output_to_operand_aliasing={{0}: (12, {}), {1}: (13, {}), {2}: (14, {}), {3}: (15, {})} | custom-call | flops 43000000512 | bytes 146200000 | tf_op jit(solution)/shard_map/feed/pallas_call | solution.py:400
  320.2 4.3 all-to-all-start.4
  325.5 24.1 %result.1 = (bf16[192,1536]{1,0:T(8,128)(2,1)}, bf16[192,1536]{1,0:T(8,128)(2,1)}, bf16[192,1536]{1,0:T(8,128)(2,1)}, bf16[192,1536]{1,0:T(8,128)(2,1)}, bf16[19...) custom-call(s32[4]{0:T(128)} %pad_add_fusion.2.place, ...), custom_call_target="tpu_custom_call" | custom-call | flops 10000000 | bytes 34000 | tf_op jit(solution)/shard_map/result/pallas_call | solution.py:400
  349.6 1.9 collective-permute-start.15
  351.6 3.6 collective-permute-start.17
  355.2 2.6 collective-permute-start.18
  358.4 41.5 %weights.1 = (bf16[2,2,768,768]{3,2,1,0:T(8,128)(2,1)}, f32[2,2,768,768]{3,2,1,0:T(8,128)}, f32[3072,128]{1,0:T(8,128)}, f32[768,128]{1,0:T(8,128)}) custom-call(s32[4]{0:T(128)} %pad_add_fusion.3.order, bf16[768,3072]{1,0:T(8,128)(2,1)} %get-tuple-element.230.normal, bf16[3072,3072]{1,0:T(8,128)(2,1)} %get-tuple-element.231.pre, ...), custom_call_target="tpu_custom_call" | custom-call | flops 10000000 | bytes 34000 | tf_op jit(solution)/shard_map/weights/pallas_call | solution.py:400
  400.4 4.9 collective-permute-done.18.refs_3_
  405.3 1.7 collective-permute-start.20
  408.0 16.6 %spectrum_back.1.freq = bf16[2,96,96,128]{3,2,1,0:T(8,128)(2,1)} custom-call(bf16[8,6,96,256]{3,2,1,0:T(8,128)(2,1)} %all-to-all-done.3.refs_0_, bf16[8,6,96,256]{3,2,1,0:T(8,128)(2,1)} %all-to-all-done.4.refs_1_, bf16[256,256]{1,0:T(8,128)(2,1)} %constant.383.clone.refs_2_, bf16[256,256]{1,0:T(8,128)(2,1)} %constant.384.clone.refs_3_, ...), custom_call_target="tpu_custom_call" | custom-call | flops 10000000 | bytes 34000 | tf_op jit(solution)/shard_map/spectrum_back/pallas_call | solution.py:400
  424.7 9.3 %add.403 = (f32[2,2,4,96,768]{4,3,2,1,0:T(8,128)}, bf16[2,2,4,96,768]{4,3,2,1,0:T(8,128)(2,1)}) custom-call(s32[1]{0:T(128)} %bitcast.67.side, f32[2,2,768,768]{3,2,1,0:T(8,128)} %get-tuple-element.246.kept, bf16[2,2,768,768]{3,2,1,0:T(8,128)(2,1)} %collective-permute-done.19.came), custom_call_target="tpu_custom_call" | custom-call | flops 10000000 | bytes 34000 | tf_op jit(solution)/shard_map/add/pallas_call | solution.py:400
  434.0 4.0 collective-permute-start.22
  438.8 2.0 collective-permute-start.24
  440.8 16.7 %filter_back.1 = (bf16[2,96,96,128]{3,2,1,0:T(8,128)(2,1)}, f32[192,192]{1,0:T(8,128)}, f32[192,192]{1,0:T(8,128)}, f32[192,128]{1,0:T(8,128)}, f32[192,128]{1,0:T(8,128)}) custom-call(bf16[2,96,96,128]{3,2,1,0:T(8,128)(2,1)} %spectrum_back.1.freq, bf16[2,96,96,128]{3,2,1,0:T(8,128)(2,1)} %spectrum.1.spec, bf16[2,96,96,128]{3,2,1,0:T(8,128)(2,1)} %get-tuple-element.259.mid, ...), custom_call_target="tpu_custom_call" | custom-call | flops 10000000 | bytes 34000 | tf_op jit(solution)/shard_map/filter_back/pallas_call | solution.py:400
  458.6 10.3 %last.2 = (bf16[96,48,256]{2,1,0:T(8,128)(2,1)}, f32[96,2,256]{2,1,0:T(2,128)}, f32[48,128]{1,0:T(8,128)}, f32[48,128]{1,0:T(8,128)}) custom-call(bf16[8,12,96,256]{3,2,1,0:T(8,128)(2,1)} %all-to-all-done.pieces, bf16[8,6,96,256]{3,2,1,0:T(8,128)(2,1)} %all-to-all-done.3.refs_0_, bf16[8,6,96,256]{3,2,1,0:T(8,128)(2,1)} %all-to-all-done.4.refs_1_, ...), custom_call_target="tpu_custom_call" | custom-call | flops 10000000 | bytes 34000 | tf_op jit(solution)/shard_map/last/pallas_call | solution.py:400
  468.9 9.1 %all-to-all-start.5 = ((bf16[8,12,48,256]{3,2,1,0:T(8,128)(2,1)}), bf16[8,12,48,256]{3,2,1,0:T(8,128)(2,1)}, u32[]{:S(2)}, u32[]{:S(2)}) async-start(bf16[8,12,48,256]{3,2,1,0:T(8,128)(2,1)} %bitcast.200), calls=%async_computation.5 | async-start | bytes 4718592 | tf_op jit(solution)/shard_map/all_to_all | solution.py:690
  482.2 24.2 %collective-permute-done.24 = bf16[2,2,4,96,768]{4,3,2,1,0:T(8,128)(2,1)} collective-permute-done((bf16[2,2,4,96,768]{4,3,2,1,0:T(8,128)(2,1)}, bf16[2,2,4,96,768]{4,3,2,1,0:T(8,128)(2,1)}, u32[]{:S(2)}, u32[]{:S(2)}) %collective-permute-start.24) | collective-permute-done | bytes 2359328 | tf_op jit(solution)/shard_map/ppermute | solution.py:635
  506.5 3.6 convert_add_fusion
  510.1 2.2 copy-done
  512.4 3.0 collective-permute-start.25
  516.8 10.4 %last.3 = (bf16[96,48,256]{2,1,0:T(8,128)(2,1)}, f32[96,2,256]{2,1,0:T(2,128)}, f32[48,128]{1,0:T(8,128)}, f32[48,128]{1,0:T(8,128)}) custom-call(bf16[8,12,96,256]{3,2,1,0:T(8,128)(2,1)} %all-to-all-done.pieces, bf16[8,6,96,256]{3,2,1,0:T(8,128)(2,1)} %all-to-all-done.3.refs_0_, bf16[8,6,96,256]{3,2,1,0:T(8,128)(2,1)} %all-to-all-done.4.refs_1_, ...), custom_call_target="tpu_custom_call" | custom-call | flops 10000000 | bytes 34000 | tf_op jit(solution)/shard_map/last/pallas_call | solution.py:400
  530.7 10.7 %collective-permute-done.25 = bf16[2,4,96,768]{3,2,1,0:T(8,128)(2,1)} collective-permute-done((bf16[2,4,96,768]{3,2,1,0:T(8,128)(2,1)S(1)}, bf16[2,4,96,768]{3,2,1,0:T(8,128)(2,1)}, u32[]{:S(2)}, u32[]{:S(2)}) %collective-permute-start.25) | collective-permute-done | bytes 1179680 | tf_op jit(solution)/shard_map/ppermute | solution.py:635
  542.9 4.5 all-to-all-start.6
  547.5 3.7 fusion.3
  551.2 9.4 %all-to-all-done.6 = f32[8,1,16369]{2,1,0:T(1,128)S(1)} async-done(((f32[8,1,16369]{2,1,0:T(1,128)}), f32[8,1,16369]{2,1,0:T(1,128)S(1)}, u32[]{:S(2)}, u32[]{:S(2)}) %all-to-all-start.6) | async-done | bytes 523840 | tf_op jit(solution)/shard_map/all_to_all | solution.py:718
  560.9 4.6 all-to-all-start.7
  568.1 6.9 %widen.1 = f32[4,12,192,256]{3,2,1,0:T(8,128)} custom-call(s32[4]{0:T(128)} %pad_add_fusion.slot, s32[2]{0:T(128)} %pad_add_fusion.1.starts, bf16[192,1536]{1,0:T(8,128)(2,1)} %copy-done.31, bf16[192,1536]{1,0:T(8,128)(2,1)} %copy-done.32, bf16[192,1536]{1,0:T(8,128)(2,1)} %copy-done.33, bf16[192,1536]{1,0:T(8,128)(2,1)} %collective-permute-done.18.refs_3_, ...), custom_call_target="tpu_custom_call" | custom-call | flops 8000000000 | bytes 27200000 | tf_op jit(solution)/shard_map/widen/pallas_call | solution.py:400
  576.5 2.0 collective-permute-start.26
  583.1 3.3 collective-permute-done.28
  589.6 7.4 %finish.2.refs_0_ = f32[4,12,192,256]{3,2,1,0:T(8,128)} custom-call(bf16[8,12,48,256]{3,2,1,0:T(8,128)(2,1)} %all-to-all-done.5.grad, bf16[4,12,192,256]{3,2,1,0:T(8,128)(2,1)} %patches.3, f32[4,12,1,256]{3,2,1,0:T(1,128)} %copy.273.mean, f32[4,12,1,256]{3,2,1,0:T(1,128)} %copy.274.rstd, f32[4,12,1,256]{3,2,1,0:T(1,128)} %get-tuple-element.423.one, ...), custom_call_target="tpu_custom_call" | custom-call | flops 5000000000 | bytes 17000000 | tf_op jit(solution)/shard_map/finish/pallas_call | solution.py:400
  597.0 17.2 %collective-permute-done.26 = bf16[2,2,96,768]{3,2,1,0:T(8,128)(2,1)S(1)} collective-permute-done((bf16[2,2,96,768]{3,2,1,0:T(8,128)(2,1)S(1)}, bf16[2,2,96,768]{3,2,1,0:T(8,128)(2,1)S(1)}, u32[]{:S(2)}, u32[]{:S(2)}) %collective-permute-start.26) | collective-permute-done | bytes 589856 | tf_op jit(solution)/shard_map/ppermute | solution.py:635
  615.6 1.9 all-to-all-done.7.grad
  617.6 2.8 collective-permute-start.29
  620.4 7.3 %finish.3 = f32[4,12,192,256]{3,2,1,0:T(8,128)} custom-call(bf16[8,12,48,256]{3,2,1,0:T(8,128)(2,1)} %all-to-all-done.7.grad, bf16[4,12,192,256]{3,2,1,0:T(8,128)(2,1)} %patches.3, f32[4,12,1,256]{3,2,1,0:T(1,128)} %copy.273.mean, f32[4,12,1,256]{3,2,1,0:T(1,128)} %copy.274.rstd, ...), custom_call_target="tpu_custom_call", output_to_operand_aliasing={{}: (6, {})} | custom-call | flops 99999997952 | bytes 340000000 | tf_op jit(solution)/shard_map/finish/pallas_call | solution.py:400
  627.7 2.9 collective-permute-done.29
  (272 shorter events, 50.5 us)
Async XLA Ops:
  7.2 49.9 %all-gather.8.cloned.1.call-start = ((), (), s32[]{:S(2)}) async-start(), calls=%async_computation.9 | async-start | bytes 5898240 | tf_op jit(solution)/shard_map/all_gather | solution.py:466
  12.6 80.0 %all-gather.6.cloned.1.call-start = ((), (), s32[]{:S(2)}) async-start(), calls=%async_computation.8 | async-start | bytes 5898240 | tf_op jit(solution)/shard_map/all_gather | solution.py:467
  14.2 19.2 %copy-start.17 = (bf16[2,2,96,96]{3,2,1,0:T(8,128)(2,1)S(1)}, bf16[2,2,96,96]{3,2,1,0:T(8,128)(2,1)}, u32[]{:S(2)}) copy-start(bf16[2,2,96,96]{3,2,1,0:T(8,128)(2,1)} %param.33) | copy-start | bytes 221188
  14.2 19.2 %copy-start.18 = (bf16[2,2,96,96]{3,2,1,0:T(8,128)(2,1)S(1)}, bf16[2,2,96,96]{3,2,1,0:T(8,128)(2,1)}, u32[]{:S(2)}) copy-start(bf16[2,2,96,96]{3,2,1,0:T(8,128)(2,1)} %param.31) | copy-start | bytes 221188
  14.3 116.7 %all-to-all-start = ((bf16[8,12,96,256]{3,2,1,0:T(8,128)(2,1)}), bf16[8,12,96,256]{3,2,1,0:T(8,128)(2,1)}, u32[]{:S(2)}, u32[]{:S(2)}) async-start(bf16[8,12,96,256]{3,2,1,0:T(8,128)(2,1)} %bitcast.191), calls=%async_computation | async-start | bytes 9437184 | tf_op jit(solution)/shard_map/all_to_all | solution.py:437
  36.9 15.7 %copy-start.30 = (f32[192]{0:T(256)S(1)}, f32[192]{0:T(256)}, u32[]{:S(2)}) copy-start(f32[192]{0:T(256)} %param.29) | copy-start | bytes 2308
  42.5 14.6 %copy-start.21 = (f32[96]{0:T(128)}, f32[96]{0:T(128)S(1)}, u32[]{:S(2)}) copy-start(f32[96]{0:T(128)S(1)} %get-tuple-element.382) | copy-start | bytes 1156
  57.1 56.5 %copy-start.27 = (f32[2,2,96]{2,1,0:T(2,128)S(1)}, f32[2,2,96]{2,1,0:T(2,128)}, u32[]{:S(2)}) copy-start(f32[2,2,96]{2,1,0:T(2,128)} %param.32) | copy-start | bytes 4612
  57.1 56.5 %copy-start.28 = (f32[2,2,96]{2,1,0:T(2,128)S(1)}, f32[2,2,96]{2,1,0:T(2,128)}, u32[]{:S(2)}) copy-start(f32[2,2,96]{2,1,0:T(2,128)} %param.34) | copy-start | bytes 4612
  96.6 8.9 %collective-permute-start.6 = (f32[12,2,256]{2,1,0:T(2,128)S(1)}, f32[12,2,256]{2,1,0:T(2,128)S(1)}, u32[]{:S(2)}, u32[]{:S(2)}) collective-permute-start(f32[12,2,256]{2,1,0:T(2,128)S(1)} %bitcast.245), channel_id=1, source_target_pairs={{0,4},{4,0},{8,12},{12,8},{16,20},{20,16},{24,28},{28,24},{1,5},{5... | collective-permute-start | bytes 73736 | tf_op jit(solution)/shard_map/ppermute | solution.py:476
  98.4 13.5 %collective-permute-start.4 = (f32[12,2,256]{2,1,0:T(2,128)S(1)}, f32[12,2,256]{2,1,0:T(2,128)S(1)}, u32[]{:S(2)}, u32[]{:S(2)}) collective-permute-start(f32[12,2,256]{2,1,0:T(2,128)S(1)} %bitcast.244), channel_id=1, source_target_pairs={{0,12},{4,8},{8,4},{12,0},{16,28},{20,24},{24,20},{28,16},{1,13},{... | collective-permute-start | bytes 73736 | tf_op jit(solution)/shard_map/ppermute | solution.py:476
  100.8 13.0 %collective-permute-start.5 = (f32[12,2,256]{2,1,0:T(2,128)S(1)}, f32[12,2,256]{2,1,0:T(2,128)S(1)}, u32[]{:S(2)}, u32[]{:S(2)}) collective-permute-start(f32[12,2,256]{2,1,0:T(2,128)S(1)} %bitcast.239), channel_id=1, source_target_pairs={{0,8},{4,12},{8,0},{12,4},{16,24},{20,28},{24,16},{28,20},{1,9},{5... | collective-permute-start | bytes 73736 | tf_op jit(solution)/shard_map/ppermute | solution.py:476
  101.2 28.3 %collective-permute-start.2 = (f32[12,2,256]{2,1,0:T(2,128)S(1)}, f32[12,2,256]{2,1,0:T(2,128)S(1)}, u32[]{:S(2)}, u32[]{:S(2)}) collective-permute-start(f32[12,2,256]{2,1,0:T(2,128)S(1)} %bitcast.240), channel_id=1, source_target_pairs={{0,20},{4,16},{8,28},{12,24},{16,4},{20,0},{24,12},{28,8},{1,21},{... | collective-permute-start | bytes 73736 | tf_op jit(solution)/shard_map/ppermute | solution.py:476
  104.9 24.7 %collective-permute-start.3 = (f32[12,2,256]{2,1,0:T(2,128)S(1)}, f32[12,2,256]{2,1,0:T(2,128)S(1)}, u32[]{:S(2)}, u32[]{:S(2)}) collective-permute-start(f32[12,2,256]{2,1,0:T(2,128)S(1)} %bitcast.241), channel_id=1, source_target_pairs={{0,16},{4,20},{8,24},{12,28},{16,0},{20,4},{24,8},{28,12},{1,17},{... | collective-permute-start | bytes 73736 | tf_op jit(solution)/shard_map/ppermute | solution.py:476
  105.5 24.1 %collective-permute-start = (f32[12,2,256]{2,1,0:T(2,128)S(1)}, f32[12,2,256]{2,1,0:T(2,128)S(1)}, u32[]{:S(2)}, u32[]{:S(2)}) collective-permute-start(f32[12,2,256]{2,1,0:T(2,128)S(1)} %bitcast.243), channel_id=1, source_target_pairs={{0,28},{4,24},{8,20},{12,16},{16,12},{20,8},{24,4},{28,0},{1,29},{... | collective-permute-start | bytes 73736 | tf_op jit(solution)/shard_map/ppermute | solution.py:476
  111.9 17.7 %collective-permute-start.1 = (f32[12,2,256]{2,1,0:T(2,128)S(1)}, f32[12,2,256]{2,1,0:T(2,128)S(1)}, u32[]{:S(2)}, u32[]{:S(2)}) collective-permute-start(f32[12,2,256]{2,1,0:T(2,128)S(1)} %bitcast.242), channel_id=1, source_target_pairs={{0,24},{4,28},{8,16},{12,20},{16,8},{20,12},{24,0},{28,4},{1,25},{... | collective-permute-start | bytes 73736 | tf_op jit(solution)/shard_map/ppermute | solution.py:476
  131.0 55.8 %collective-permute-start.7 = (bf16[6,192,256]{2,1,0:T(8,128)(2,1)}, bf16[6,192,256]{2,1,0:T(8,128)(2,1)}, u32[]{:S(2)}, u32[]{:S(2)}) collective-permute-start(bf16[6,192,256]{2,1,0:T(8,128)(2,1)} %get-tuple-element.176), channel_id=1, source_target_pairs={{0,0},{1,16},{2,8},{3,24},{4,4},{5,20},{6,12},{7,28},{8,2},{9,18},... | collective-permute-start | bytes 1769480 | tf_op jit(solution)/shard_map/ppermute | solution.py:508
  133.9 52.8 %collective-permute-start.8 = (bf16[6,192,256]{2,1,0:T(8,128)(2,1)}, bf16[6,192,256]{2,1,0:T(8,128)(2,1)}, u32[]{:S(2)}, u32[]{:S(2)}) collective-permute-start(bf16[6,192,256]{2,1,0:T(8,128)(2,1)} %get-tuple-element.177), channel_id=1, source_target_pairs={{0,8},{1,24},{2,16},{3,0},{4,12},{5,28},{6,20},{7,4},{8,10},{9,26}... | collective-permute-start | bytes 1769480 | tf_op jit(solution)/shard_map/ppermute | solution.py:508
  134.0 52.8 %collective-permute-start.9 = (bf16[6,192,256]{2,1,0:T(8,128)(2,1)}, bf16[6,192,256]{2,1,0:T(8,128)(2,1)}, u32[]{:S(2)}, u32[]{:S(2)}) collective-permute-start(bf16[6,192,256]{2,1,0:T(8,128)(2,1)} %get-tuple-element.178), channel_id=1, source_target_pairs={{0,16},{1,0},{2,24},{3,8},{4,20},{5,4},{6,28},{7,12},{8,18},{9,2},... | collective-permute-start | bytes 1769480 | tf_op jit(solution)/shard_map/ppermute | solution.py:508
  137.3 49.5 %collective-permute-start.10 = (bf16[6,192,256]{2,1,0:T(8,128)(2,1)}, bf16[6,192,256]{2,1,0:T(8,128)(2,1)}, u32[]{:S(2)}, u32[]{:S(2)}) collective-permute-start(bf16[6,192,256]{2,1,0:T(8,128)(2,1)} %get-tuple-element.179), channel_id=1, source_target_pairs={{0,24},{1,8},{2,0},{3,16},{4,28},{5,12},{6,4},{7,20},{8,26},{9,10}... | collective-permute-start | bytes 1769480 | tf_op jit(solution)/shard_map/ppermute | solution.py:508
  186.8 33.8 %all-to-all-start.1 = ((bf16[8,6,96,256]{3,2,1,0:T(8,128)(2,1)}), bf16[8,6,96,256]{3,2,1,0:T(8,128)(2,1)}, u32[]{:S(2)}, u32[]{:S(2)}) async-start(bf16[8,6,96,256]{3,2,1,0:T(8,128)(2,1)} %get-tuple-element.184), calls=%async_computation.1 | async-start | bytes 4718592 | tf_op jit(solution)/shard_map/all_to_all | solution.py:559
  220.6 56.8 %all-to-all-start.2 = ((bf16[8,6,96,256]{3,2,1,0:T(8,128)(2,1)}), bf16[8,6,96,256]{3,2,1,0:T(8,128)(2,1)}, u32[]{:S(2)}, u32[]{:S(2)}) async-start(bf16[8,6,96,256]{3,2,1,0:T(8,128)(2,1)} %get-tuple-element.193), calls=%async_computation.2 | async-start | bytes 4718592 | tf_op jit(solution)/shard_map/all_to_all | solution.py:559
  226.0 58.4 %collective-permute-start.11 = (bf16[6,192,256]{2,1,0:T(8,128)(2,1)}, bf16[6,192,256]{2,1,0:T(8,128)(2,1)}, u32[]{:S(2)}, u32[]{:S(2)}) collective-permute-start(bf16[6,192,256]{2,1,0:T(8,128)(2,1)} %get-tuple-element.189), channel_id=1, source_target_pairs={{0,2},{1,18},{2,10},{3,26},{4,6},{5,22},{6,14},{7,30},{8,0},{9,16}... | collective-permute-start | bytes 1769480 | tf_op jit(solution)/shard_map/ppermute | solution.py:571
  226.6 57.8 %collective-permute-start.12 = (bf16[6,192,256]{2,1,0:T(8,128)(2,1)S(1)}, bf16[6,192,256]{2,1,0:T(8,128)(2,1)}, u32[]{:S(2)}, u32[]{:S(2)}) collective-permute-start(bf16[6,192,256]{2,1,0:T(8,128)(2,1)S(1)} %get-tuple-element.190), channel_id=1, source_target_pairs={{0,10},{1,26},{2,18},{3,2},{4,14},{5,30},{6,22},{7,6},{8,8},{9,24}... | collective-permute-start | bytes 1769480 | tf_op jit(solution)/shard_map/ppermute | solution.py:571
  231.2 53.2 %collective-permute-start.13 = (bf16[6,192,256]{2,1,0:T(8,128)(2,1)S(1)}, bf16[6,192,256]{2,1,0:T(8,128)(2,1)}, u32[]{:S(2)}, u32[]{:S(2)}) collective-permute-start(bf16[6,192,256]{2,1,0:T(8,128)(2,1)S(1)} %get-tuple-element.191), channel_id=1, source_target_pairs={{0,18},{1,2},{2,26},{3,10},{4,22},{5,6},{6,30},{7,14},{8,16},{9,0}... | collective-permute-start | bytes 1769480 | tf_op jit(solution)/shard_map/ppermute | solution.py:571
  233.6 50.8 %collective-permute-start.14 = (bf16[6,192,256]{2,1,0:T(8,128)(2,1)S(1)}, bf16[6,192,256]{2,1,0:T(8,128)(2,1)}, u32[]{:S(2)}, u32[]{:S(2)}) collective-permute-start(bf16[6,192,256]{2,1,0:T(8,128)(2,1)S(1)} %get-tuple-element.192), channel_id=1, source_target_pairs={{0,26},{1,10},{2,2},{3,18},{4,30},{5,14},{6,6},{7,22},{8,24},{9,8}... | collective-permute-start | bytes 1769480 | tf_op jit(solution)/shard_map/ppermute | solution.py:571
  277.4 42.7 %all-to-all-start.3 = ((bf16[8,6,96,256]{3,2,1,0:T(8,128)(2,1)}), bf16[8,6,96,256]{3,2,1,0:T(8,128)(2,1)}, u32[]{:S(2)}, u32[]{:S(2)}) async-start(bf16[8,6,96,256]{3,2,1,0:T(8,128)(2,1)} %get-tuple-element.214), calls=%async_computation.3 | async-start | bytes 4718592 | tf_op jit(solution)/shard_map/all_to_all | solution.py:559
  320.2 85.1 %all-to-all-start.4 = ((bf16[8,6,96,256]{3,2,1,0:T(8,128)(2,1)}), bf16[8,6,96,256]{3,2,1,0:T(8,128)(2,1)}, u32[]{:S(2)}, u32[]{:S(2)}) async-start(bf16[8,6,96,256]{3,2,1,0:T(8,128)(2,1)} %get-tuple-element.216), calls=%async_computation.4 | async-start | bytes 4718592 | tf_op jit(solution)/shard_map/all_to_all | solution.py:559
  349.6 50.3 %collective-permute-start.15 = (bf16[192,1536]{1,0:T(8,128)(2,1)}, bf16[192,1536]{1,0:T(8,128)(2,1)S(1)}, u32[]{:S(2)}, u32[]{:S(2)}) collective-permute-start(bf16[192,1536]{1,0:T(8,128)(2,1)} %get-tuple-element.235), channel_id=1, source_target_pairs={{0,0},{16,1},{8,2},{24,3},{4,4},{20,5},{12,6},{28,7},{2,8},{18,9},... | collective-permute-start | bytes 1769480 | tf_op jit(solution)/shard_map/ppermute | solution.py:606
  351.5 48.4 %collective-permute-start.16 = (bf16[192,1536]{1,0:T(8,128)(2,1)}, bf16[192,1536]{1,0:T(8,128)(2,1)S(1)}, u32[]{:S(2)}, u32[]{:S(2)}) collective-permute-start(bf16[192,1536]{1,0:T(8,128)(2,1)} %get-tuple-element.236), channel_id=1, source_target_pairs={{2,0},{18,1},{10,2},{26,3},{6,4},{22,5},{14,6},{30,7},{0,8},{16,9}... | collective-permute-start | bytes 1769480 | tf_op jit(solution)/shard_map/ppermute | solution.py:606
  351.6 48.8 %collective-permute-start.17 = (bf16[192,1536]{1,0:T(8,128)(2,1)}, bf16[192,1536]{1,0:T(8,128)(2,1)S(1)}, u32[]{:S(2)}, u32[]{:S(2)}) collective-permute-start(bf16[192,1536]{1,0:T(8,128)(2,1)} %get-tuple-element.237), channel_id=1, source_target_pairs={{8,0},{24,1},{16,2},{0,3},{12,4},{28,5},{20,6},{4,7},{10,8},{26,9}... | collective-permute-start | bytes 1769480 | tf_op jit(solution)/shard_map/ppermute | solution.py:606
  355.2 50.1 %collective-permute-start.18 = (bf16[192,1536]{1,0:T(8,128)(2,1)}, bf16[192,1536]{1,0:T(8,128)(2,1)}, u32[]{:S(2)}, u32[]{:S(2)}) collective-permute-start(bf16[192,1536]{1,0:T(8,128)(2,1)} %get-tuple-element.238), channel_id=1, source_target_pairs={{10,0},{26,1},{18,2},{2,3},{14,4},{30,5},{22,6},{6,7},{8,8},{24,9}... | collective-permute-start | bytes 1769480 | tf_op jit(solution)/shard_map/ppermute | solution.py:606
  399.9 24.7 %copy-start.31 = (bf16[192,1536]{1,0:T(8,128)(2,1)}, bf16[192,1536]{1,0:T(8,128)(2,1)S(1)}, u32[]{:S(2)}) copy-start(bf16[192,1536]{1,0:T(8,128)(2,1)S(1)} %collective-permute-done.15.refs_0_) | copy-start | bytes 1769476
  400.0 24.7 %copy-start.32 = (bf16[192,1536]{1,0:T(8,128)(2,1)}, bf16[192,1536]{1,0:T(8,128)(2,1)S(1)}, u32[]{:S(2)}) copy-start(bf16[192,1536]{1,0:T(8,128)(2,1)S(1)} %collective-permute-done.16.refs_1_) | copy-start | bytes 1769476
  400.4 24.3 %copy-start.33 = (bf16[192,1536]{1,0:T(8,128)(2,1)}, bf16[192,1536]{1,0:T(8,128)(2,1)S(1)}, u32[]{:S(2)}) copy-start(bf16[192,1536]{1,0:T(8,128)(2,1)S(1)} %collective-permute-done.17.refs_2_) | copy-start | bytes 1769476
  405.3 19.4 %collective-permute-start.19 = (bf16[2,2,768,768]{3,2,1,0:T(8,128)(2,1)}, bf16[2,2,768,768]{3,2,1,0:T(8,128)(2,1)}, u32[]{:S(2)}, u32[]{:S(2)}) collective-permute-start(bf16[2,2,768,768]{3,2,1,0:T(8,128)(2,1)} %get-tuple-element.244), channel_id=1, source_target_pairs={{0,1},{1,0},{2,3},{3,2},{4,5},{5,4},{6,7},{7,6},{8,9},{9,8},{10,11... | collective-permute-start | bytes 14155784 | tf_op jit(solution)/shard_map/ppermute | solution.py:626
  405.3 28.7 %collective-permute-start.20 = (bf16[192,1536]{1,0:T(8,128)(2,1)}, bf16[192,1536]{1,0:T(8,128)(2,1)}, u32[]{:S(2)}, u32[]{:S(2)}) collective-permute-start(bf16[192,1536]{1,0:T(8,128)(2,1)} %get-tuple-element.254), channel_id=1, source_target_pairs={{16,0},{0,1},{24,2},{8,3},{20,4},{4,5},{28,6},{12,7},{18,8},{2,9},... | collective-permute-start | bytes 1769480 | tf_op jit(solution)/shard_map/ppermute | solution.py:606
  406.9 27.0 %collective-permute-start.21 = (bf16[192,1536]{1,0:T(8,128)(2,1)}, bf16[192,1536]{1,0:T(8,128)(2,1)}, u32[]{:S(2)}, u32[]{:S(2)}) collective-permute-start(bf16[192,1536]{1,0:T(8,128)(2,1)} %get-tuple-element.255), channel_id=1, source_target_pairs={{18,0},{2,1},{26,2},{10,3},{22,4},{6,5},{30,6},{14,7},{16,8},{0,9}... | collective-permute-start | bytes 1769480 | tf_op jit(solution)/shard_map/ppermute | solution.py:606
  424.7 13.3 %copy-start.36 = (bf16[192,1536]{1,0:T(8,128)(2,1)S(1)}, bf16[192,1536]{1,0:T(8,128)(2,1)}, u32[]{:S(2)}) copy-start(bf16[192,1536]{1,0:T(8,128)(2,1)} %get-tuple-element.270) | copy-start | bytes 1769476
  434.0 23.6 %collective-permute-start.22 = (bf16[192,1536]{1,0:T(8,128)(2,1)}, bf16[192,1536]{1,0:T(8,128)(2,1)S(1)}, u32[]{:S(2)}, u32[]{:S(2)}) collective-permute-start(bf16[192,1536]{1,0:T(8,128)(2,1)} %get-tuple-element.269), channel_id=1, source_target_pairs={{24,0},{8,1},{0,2},{16,3},{28,4},{12,5},{4,6},{20,7},{26,8},{10,9}... | collective-permute-start | bytes 1769480 | tf_op jit(solution)/shard_map/ppermute | solution.py:606
  437.9 19.6 %collective-permute-start.23 = (bf16[192,1536]{1,0:T(8,128)(2,1)S(1)}, bf16[192,1536]{1,0:T(8,128)(2,1)S(1)}, u32[]{:S(2)}, u32[]{:S(2)}) collective-permute-start(bf16[192,1536]{1,0:T(8,128)(2,1)S(1)} %copy-done.36), channel_id=1, source_target_pairs={{26,0},{10,1},{2,2},{18,3},{30,4},{14,5},{6,6},{22,7},{24,8},{8,9}... | collective-permute-start | bytes 1769480 | tf_op jit(solution)/shard_map/ppermute | solution.py:606
  438.8 67.6 %collective-permute-start.24 = (bf16[2,2,4,96,768]{4,3,2,1,0:T(8,128)(2,1)}, bf16[2,2,4,96,768]{4,3,2,1,0:T(8,128)(2,1)}, u32[]{:S(2)}, u32[]{:S(2)}) collective-permute-start(bf16[2,2,4,96,768]{4,3,2,1,0:T(8,128)(2,1)} %get-tuple-element.273), channel_id=1, source_target_pairs={{0,4},{4,0},{8,12},{12,8},{16,20},{20,16},{24,28},{28,24},{1,5},{5... | collective-permute-start | bytes 7077896 | tf_op jit(solution)/shard_map/ppermute | solution.py:635
  468.9 9.8 %copy-start.8 = (f32[768,128]{1,0:T(8,128)S(1)}, f32[768,128]{1,0:T(8,128)}, u32[]{:S(2)}) copy-start(f32[768,128]{1,0:T(8,128)} %get-tuple-element.305) | copy-start | bytes 1179652
  468.9 9.8 %copy-start.10 = (f32[768,128]{1,0:T(8,128)S(1)}, f32[768,128]{1,0:T(8,128)}, u32[]{:S(2)}) copy-start(f32[768,128]{1,0:T(8,128)} %get-tuple-element.306) | copy-start | bytes 1179652
  468.9 9.9 %copy-start.7 = (f32[768,128]{1,0:T(8,128)S(1)}, f32[768,128]{1,0:T(8,128)}, u32[]{:S(2)}) copy-start(f32[768,128]{1,0:T(8,128)} %get-tuple-element.307) | copy-start | bytes 1179652
  468.9 9.9 %copy-start.9 = (f32[768,128]{1,0:T(8,128)S(1)}, f32[768,128]{1,0:T(8,128)}, u32[]{:S(2)}) copy-start(f32[768,128]{1,0:T(8,128)} %get-tuple-element.308) | copy-start | bytes 1179652
  468.9 10.1 %copy-start.11 = (f32[768,128]{1,0:T(8,128)S(1)}, f32[768,128]{1,0:T(8,128)}, u32[]{:S(2)}) copy-start(f32[768,128]{1,0:T(8,128)} %get-tuple-element.309) | copy-start | bytes 1179652
  468.9 10.3 %copy-start.1 = (f32[3072,128]{1,0:T(8,128)S(1)}, f32[3072,128]{1,0:T(8,128)}, u32[]{:S(2)}) copy-start(f32[3072,128]{1,0:T(8,128)} %get-tuple-element.310) | copy-start | bytes 4718596
  468.9 72.5 %all-to-all-start.5 = ((bf16[8,12,48,256]{3,2,1,0:T(8,128)(2,1)}), bf16[8,12,48,256]{3,2,1,0:T(8,128)(2,1)}, u32[]{:S(2)}, u32[]{:S(2)}) async-start(bf16[8,12,48,256]{3,2,1,0:T(8,128)(2,1)} %bitcast.200), calls=%async_computation.5 | async-start | bytes 4718592 | tf_op jit(solution)/shard_map/all_to_all | solution.py:690
  482.2 33.2 %copy-start.14 = (f32[192,128]{1,0:T(8,128)S(1)}, f32[192,128]{1,0:T(8,128)}, u32[]{:S(2)}) copy-start(f32[192,128]{1,0:T(8,128)} %get-tuple-element.300) | copy-start | bytes 294916
  482.2 33.5 %copy-start.13 = (f32[192,128]{1,0:T(8,128)S(1)}, f32[192,128]{1,0:T(8,128)}, u32[]{:S(2)}) copy-start(f32[192,128]{1,0:T(8,128)} %get-tuple-element.298) | copy-start | bytes 294916
  512.4 29.0 %collective-permute-start.25 = (bf16[2,4,96,768]{3,2,1,0:T(8,128)(2,1)S(1)}, bf16[2,4,96,768]{3,2,1,0:T(8,128)(2,1)}, u32[]{:S(2)}, u32[]{:S(2)}) collective-permute-start(bf16[2,4,96,768]{3,2,1,0:T(8,128)(2,1)S(1)} %fusion.4), channel_id=1, source_target_pairs={{0,2},{1,3},{2,0},{3,1},{4,6},{5,7},{6,4},{7,5},{8,10},{9,11},{10,... | collective-permute-start | bytes 3538952 | tf_op jit(solution)/shard_map/ppermute | solution.py:635
  516.7 10.4 %copy-start.16 = (f32[48,128]{1,0:T(8,128)S(1)}, f32[48,128]{1,0:T(8,128)}, u32[]{:S(2)}) copy-start(f32[48,128]{1,0:T(8,128)} %get-tuple-element.301) | copy-start | bytes 73732
  516.7 11.3 %copy-start.15 = (f32[48,128]{1,0:T(8,128)S(1)}, f32[48,128]{1,0:T(8,128)}, u32[]{:S(2)}) copy-start(f32[48,128]{1,0:T(8,128)} %get-tuple-element.303) | copy-start | bytes 73732
  516.7 12.1 %copy-start.22 = (f32[96]{0:T(128)S(1)}, f32[96]{0:T(128)}, u32[]{:S(2)}) copy-start(f32[96]{0:T(128)} %copy-done.21) | copy-start | bytes 1156
  516.7 12.2 %copy-start.12 = (f32[96,2,256]{2,1,0:T(2,128)S(1)}, f32[96,2,256]{2,1,0:T(2,128)}, u32[]{:S(2)}) copy-start(f32[96,2,256]{2,1,0:T(2,128)} %get-tuple-element.276) | copy-start | bytes 589828
  542.9 17.7 %all-to-all-start.6 = ((f32[8,1,16369]{2,1,0:T(1,128)}), f32[8,1,16369]{2,1,0:T(1,128)S(1)}, u32[]{:S(2)}, u32[]{:S(2)}) async-start(f32[8,1,16369]{2,1,0:T(1,128)} %all_to_all.35), calls=%async_computation.6 | async-start | bytes 1048576 | tf_op jit(solution)/shard_map/all_to_all | solution.py:718
  547.5 18.7 %copy-start.6 = (f32[4,12,1,256]{3,0,1,2:T(4,128)S(1)}, f32[4,12,1,256]{3,0,1,2:T(4,128)}, u32[]{:S(2)}) copy-start(f32[4,12,1,256]{3,0,1,2:T(4,128)} %copy-done.5) | copy-start | bytes 147460
  547.5 19.4 %copy-start.4 = (f32[4,12,1,256]{3,0,1,2:T(4,128)S(1)}, f32[4,12,1,256]{3,0,1,2:T(4,128)}, u32[]{:S(2)}) copy-start(f32[4,12,1,256]{3,0,1,2:T(4,128)} %copy-done.3) | copy-start | bytes 147460
  560.9 56.6 %all-to-all-start.7 = ((bf16[8,12,48,256]{3,2,1,0:T(8,128)(2,1)}), bf16[8,12,48,256]{3,2,1,0:T(8,128)(2,1)}, u32[]{:S(2)}, u32[]{:S(2)}) async-start(bf16[8,12,48,256]{3,2,1,0:T(8,128)(2,1)} %bitcast.69), calls=%async_computation.7 | async-start | bytes 4718592 | tf_op jit(solution)/shard_map/all_to_all | solution.py:727
  576.5 37.8 %collective-permute-start.26 = (bf16[2,2,96,768]{3,2,1,0:T(8,128)(2,1)S(1)}, bf16[2,2,96,768]{3,2,1,0:T(8,128)(2,1)S(1)}, u32[]{:S(2)}, u32[]{:S(2)}) collective-permute-start(bf16[2,2,96,768]{3,2,1,0:T(8,128)(2,1)S(1)} %fusion.5), channel_id=1, source_target_pairs={{0,8},{8,0},{16,24},{24,16},{1,9},{9,1},{17,25},{25,17},{2,10},{10... | collective-permute-start | bytes 1769480 | tf_op jit(solution)/shard_map/ppermute | solution.py:635
  579.3 1.4 collective-permute-start.27
  580.7 5.7 collective-permute-start.28
  617.6 13.0 %collective-permute-start.29 = (bf16[1,2,96,768]{3,2,1,0:T(8,128)(2,1)S(1)}, bf16[1,2,96,768]{3,2,1,0:T(8,128)(2,1)S(1)}, u32[]{:S(2)}, u32[]{:S(2)}) collective-permute-start(bf16[1,2,96,768]{3,2,1,0:T(8,128)(2,1)S(1)} %dynamic-slice_convert_fusion), channel_id=1, source_target_pairs={{0,16},{8,24},{16,0},{24,8},{1,17},{9,25},{17,1},{25,9},{2,18},{10... | collective-permute-start | bytes 884744 | tf_op jit(solution)/shard_map/ppermute | solution.py:635
  (14 other events, 65.0 us)
Sparse Core Ops, SparseCore 0:
  12.8 40.1 all-gather.7
  55.1 37.4 all-gather.5
